TPU v7x, 32 devices: a whole 2x2x4 slice. The times are simulated.
32 devices in a mesh: seq: 32 (over z, y, x, core).
Axes of the slice: x: 2, y: 2, z: 4, core: 2. Of those that a mesh axis runs over, the one named last changes fastest.
Arguments:
- inputs: bfloat16 [2, 8192, 1024], P(None, 'seq'), may hold values from -6 to 6
- doc_start: int32 [2, 8192], P(None, 'seq'), may hold values from 0 to 8191, as said below
- norm_gain: float32 [1024], replicated, may hold values from 0.5 to 1.5
- w_in: bfloat16 [1024, 3072], P('seq'), may hold values from -0.1875 to 0.1875
- conv_weight: float32 [4, 2048], replicated, may hold values from -3 to 3
- w_low: bfloat16 [1024, 16], replicated, may hold values from -0.1875 to 0.1875
- w_high: float32 [16, 512], replicated, may hold values from -1.5 to 1.5
- gate_bias: float32 [512], replicated, may hold values from 0 to 6
- head_gain: float32 [256], replicated, may hold values from 0.5 to 1.5
- w_out: bfloat16 [1024, 1024], P('seq'), may hold values from -0.375 to 0.375
- ffn_gain: float32 [1024], replicated, may hold values from 0.5 to 1.5
- w_gate_up: bfloat16 [1024, 5632], P('seq'), may hold values from -0.1875 to 0.1875
- w_down: bfloat16 [2816, 1024], P('seq'), may hold values from -0.3125 to 0.3125
- out_grad: bfloat16 [2, 8192, 1024], P(None, 'seq'), may hold values from -6 to 6
Outputs:
- layer_out: float32 [2, 8192, 1024], P(None, 'seq')
- input_grad: float32 [2, 8192, 1024], P(None, 'seq')
- norm_gain_grad: float32 [1024], replicated
- w_in_grad: float32 [1024, 3072], P('seq')
- conv_weight_grad: float32 [4, 2048], replicated
- w_low_grad: float32 [1024, 16], replicated
- w_high_grad: float32 [16, 512], replicated
- gate_bias_grad: float32 [512], replicated
- head_gain_grad: float32 [256], replicated
- w_out_grad: float32 [1024, 1024], P('seq')
- ffn_gain_grad: float32 [1024], replicated
- w_gate_up_grad: float32 [1024, 5632], P('seq')
- w_down_grad: float32 [2816, 1024], P('seq')
Inputs may be any that keep to these rules, and one draw needn't show every extreme that they name: `doc_start`: each entry is the position within its sequence of the first token of the token's document, so entries never fall along a sequence and equal their own position at a document's first token; documents hold 200 to 2000 tokens, except the last of a sequence, which the sequence's end may cut.
All inputs are finite; a program needn't handle non-finite values.
Results may differ from a plain program's by a relative error of at most 0.012.
The roundings to bfloat16 on the way count: a program that leaves them out, or rounds other values in their place, can miss the bound.
Values may be sent and summed in bfloat16 or wider, within the bound.
No kernel may reach another device: no remote copies, remote signals or barrier semaphores. Data moves between devices by JAX's collectives and lax.ppermute only.
A program may use at most 576 MiB of HBM per device.

v0:
```python
import jax
import jax.numpy as jnp
from jax import lax
from jax.sharding import PartitionSpec as P

HEADS = 4
DK = 128
DV = 256
FF = 2816
SPAN = 64
CONV = 4


epsilon = 1e-06
gate_scale = 16.0
highest = lax.Precision.HIGHEST


def shifted(array, axis, by):
    count = lax.axis_size(axis)
    pairs = [(i, i + by) for i in range(count) if 0 <= i + by < count]
    return lax.ppermute(array, axis, pairs)


def entering(value, axis, join, neutral):
    count, mine = (lax.axis_size(axis), lax.axis_index(axis))
    pieces = jax.tree.map(lambda part: lax.all_gather(part, axis), value)
    running = jax.tree.map(
        lambda part, zero: jnp.full_like(part, 0) + jnp.asarray(zero, part.dtype), value, neutral
    )

    def turn(position, running):
        longer = join(running, jax.tree.map(lambda part: part[position], pieces))
        return jax.tree.map(lambda new, old: jnp.where(position < mine, new, old), longer, running)

    return lax.fori_loop(0, count - 1, turn, running)


def carried_in(array, axis, join, neutral):
    count = lax.axis_size(axis)
    place = lax.axis_index(axis)
    ahead = count - 1 - place
    gathered = jax.tree.map(
        lambda a, kind: lax.all_gather(a.astype(kind), axis),
        array,
        jax.tree.map(lambda a: jnp.bfloat16 if a.dtype == jnp.float32 else a.dtype, array),
    )
    state = jax.tree.map(lambda a, e: jnp.zeros_like(a) + jnp.asarray(e, a.dtype), array, neutral)

    def one(turn, state):
        source = count - 1 - turn
        return join(
            state,
            jax.tree.map(
                lambda a, own: lax.dynamic_index_in_dim(a, source, 0, False).astype(own.dtype),
                gathered,
                array,
            ),
        )

    return lax.fori_loop(0, ahead, one, state)


def segment_step(memory, inputs_piece):
    query_vecs, key_vecs, value_vecs, log_decay, starts, position = inputs_piece
    first_pos = position[0]
    cumulative = jnp.cumsum(log_decay, axis=0)
    query_decayed = query_vecs * jnp.exp(cumulative)
    key_decayed = key_vecs * jnp.exp(-cumulative)
    scores = jnp.einsum("thc,uhc->htu", query_decayed, key_decayed, precision=highest)
    allowed = (position[None, :] <= position[:, None]) & (position[None, :] >= starts[:, None])
    scores = jnp.where(allowed[None, :, :], scores, 0.0)
    within = jnp.einsum("htu,uhv->thv", scores, value_vecs, precision=highest)
    carried = (starts < first_pos).astype(jnp.float32)
    across = (
        jnp.einsum("thc,hcv->thv", query_decayed, memory, precision=highest)
        * carried[:, None, None]
    )
    decay_total = cumulative[-1]
    kept_state = (starts[-1] < first_pos).astype(jnp.float32)
    same_doc = (position >= starts[-1]).astype(jnp.float32)
    key_final = key_vecs * jnp.exp(decay_total[None, :, :] - cumulative) * same_doc[:, None, None]
    updated = memory * (jnp.exp(decay_total) * kept_state)[:, :, None] + jnp.einsum(
        "uhc,uhv->hcv", key_final, value_vecs, precision=highest
    )
    return (updated, within + across)


def recurrence(
    query_vecs, key_vecs, value_vecs, log_decay, starts, position, memory, step_function
):
    span_count = starts.shape[1] // SPAN

    def per_sequence(query_seq, key_seq, value_seq, decay_seq, start_seq, memory_seq):

        def split_spans(source):
            return source.reshape((span_count, SPAN) + source.shape[1:])

        final_memory, outputs = lax.scan(
            step_function,
            memory_seq,
            (
                split_spans(query_seq),
                split_spans(key_seq),
                split_spans(value_seq),
                split_spans(decay_seq),
                split_spans(start_seq),
                split_spans(position),
            ),
        )
        return (outputs.reshape((span_count * SPAN,) + outputs.shape[2:]), final_memory)

    return jax.vmap(per_sequence)(query_vecs, key_vecs, value_vecs, log_decay, starts, memory)


def compose(earlier, later):
    decay_early, state_early = earlier
    decay_late, state_late = later
    return (decay_early * decay_late, decay_late[..., None] * state_early + state_late)


def bf_dot(left, right):
    return jnp.dot(left, right, preferred_element_type=jnp.float32)


def rms_back(grad_normed, source, inv_rms, gain_vec):
    scaled = grad_normed * gain_vec
    return inv_rms * (
        scaled - source * inv_rms * inv_rms * jnp.mean(scaled * source, axis=-1, keepdims=True)
    )


def local(
    inputs,
    doc_start,
    norm_gain,
    w_in,
    conv_weight,
    w_low,
    w_high,
    gate_bias,
    head_gain,
    w_out,
    ffn_gain,
    w_gate_up,
    w_down,
    out_grad,
):
    seq_count, block_len, model_width = inputs.shape
    row_count = seq_count * block_len
    key_width = HEADS * DK
    value_width = HEADS * DV
    conv_width = 2 * key_width + value_width
    block_start = lax.axis_index("seq") * block_len
    position = block_start + jnp.arange(block_len, dtype=jnp.int32)
    layer_in = inputs.reshape(row_count, model_width).astype(jnp.float32)
    in_full, out_full = (
        lax.all_gather(w_in, "seq", axis=0, tiled=True),
        lax.all_gather(w_out, "seq", axis=0, tiled=True),
    )
    inv_rms = lax.rsqrt(jnp.mean(layer_in * layer_in, axis=-1, keepdims=True) + epsilon)
    normed = (layer_in * inv_rms * norm_gain).astype(jnp.bfloat16)
    projected = bf_dot(normed, in_full).astype(jnp.bfloat16)
    lowrank = bf_dot(normed, w_low)
    gate_logit = (
        jnp.dot(lowrank, w_high, precision=highest, preferred_element_type=jnp.float32) + gate_bias
    )
    log_decay = jax.nn.log_sigmoid(gate_logit) / gate_scale
    mixed = projected[:, :conv_width].reshape(seq_count, block_len, conv_width)
    prior = shifted(mixed[:, block_len - (CONV - 1) :, :], "seq", 1)
    padded = jnp.concatenate([prior, mixed], axis=1).astype(jnp.float32)
    usables = [
        (position[None, :] - tap_index >= doc_start).astype(jnp.float32)[:, :, None]
        for tap_index in range(CONV)
    ]
    convolved = conv_weight[0] * padded[:, CONV - 1 :, :]
    for tap_index in range(1, CONV):
        offset = CONV - 1 - tap_index
        convolved = (
            convolved
            + conv_weight[tap_index]
            * padded[:, offset : offset + block_len, :]
            * usables[tap_index]
        )
    conv_sig = jax.nn.sigmoid(convolved)
    activated = convolved * conv_sig
    query_vecs = (activated[..., :key_width] * DK ** (-0.5)).reshape(
        seq_count, block_len, HEADS, DK
    )
    key_vecs = activated[..., key_width : 2 * key_width].reshape(seq_count, block_len, HEADS, DK)
    value_vecs = activated[..., 2 * key_width :].reshape(seq_count, block_len, HEADS, DV)
    decay_rows = log_decay.reshape(seq_count, block_len, HEADS, DK)
    zero_memory = jnp.zeros((seq_count, HEADS, DK, DV), jnp.float32)
    local_out, local_state = recurrence(
        query_vecs, key_vecs, value_vecs, decay_rows, doc_start, position, zero_memory, segment_step
    )
    cumulative = jnp.cumsum(decay_rows, axis=1)
    reach_in = (doc_start < block_start).astype(jnp.float32)
    block_decay = jnp.exp(cumulative[:, -1]) * reach_in[:, -1][:, None, None]
    identity = (jnp.ones_like(block_decay), jnp.zeros_like(local_state))
    _, incoming = entering((block_decay, local_state), "seq", compose, identity)
    query_reach = query_vecs * jnp.exp(cumulative) * reach_in[:, :, None, None]
    mixer_out = local_out + jnp.einsum("sbhc,shcv->sbhv", query_reach, incoming, precision=highest)
    mixer_rows = mixer_out.reshape(row_count, HEADS, DV)
    head_rms = lax.rsqrt(jnp.mean(mixer_rows * mixer_rows, axis=-1, keepdims=True) + epsilon)
    head_normed = mixer_rows * head_rms * head_gain
    gate_vals = projected[:, conv_width:].astype(jnp.float32).reshape(row_count, HEADS, DV)
    gate_sig = jax.nn.sigmoid(gate_vals)
    swish = gate_vals * gate_sig
    gated = (head_normed * swish).reshape(row_count, value_width).astype(jnp.bfloat16)
    hidden_one = layer_in + bf_dot(gated, out_full)
    gate_up_full, down_full = (
        lax.all_gather(w_gate_up, "seq", axis=0, tiled=True),
        lax.all_gather(w_down, "seq", axis=0, tiled=True),
    )
    ffn_rms = lax.rsqrt(jnp.mean(hidden_one * hidden_one, axis=-1, keepdims=True) + epsilon)
    ffn_in = (hidden_one * ffn_rms * ffn_gain).astype(jnp.bfloat16)
    gate_up = bf_dot(ffn_in, gate_up_full)
    gate_part = gate_up[:, :FF]
    up_part = gate_up[:, FF:]
    gate_act = jax.nn.sigmoid(gate_part)
    activation = (gate_part * gate_act * up_part).astype(jnp.bfloat16)
    layer_out = hidden_one + bf_dot(activation, down_full)
    out_rows = out_grad.reshape(row_count, model_width).astype(jnp.float32)
    out_rows_low = out_rows.astype(jnp.bfloat16)
    held_up, held_down, out_rows_low = lax.optimization_barrier((w_gate_up, w_down, out_rows_low))
    gate_up_full, down_full = (
        lax.all_gather(held_up, "seq", axis=0, tiled=True),
        lax.all_gather(held_down, "seq", axis=0, tiled=True),
    )
    act_grad = bf_dot(out_rows_low, down_full.T)
    gate_grad = act_grad * up_part * gate_act * (1.0 + gate_part * (1.0 - gate_act))
    up_grad = act_grad * gate_part * gate_act
    gate_up_grad = jnp.concatenate([gate_grad, up_grad], axis=1).astype(jnp.bfloat16)
    down_term = jnp.dot(activation.T, out_rows_low, preferred_element_type=jnp.float32)
    gate_up_term = jnp.dot(ffn_in.T, gate_up_grad, preferred_element_type=jnp.float32)
    ffn_sums = (
        lax.psum_scatter(gate_up_term, "seq", scatter_dimension=0, tiled=True),
        lax.psum_scatter(down_term, "seq", scatter_dimension=0, tiled=True),
    )
    ffn_in_grad = bf_dot(gate_up_grad, gate_up_full.T)
    ffn_gain_grad = jnp.sum(ffn_in_grad * hidden_one * ffn_rms, axis=0)
    hidden_grad = out_rows + rms_back(ffn_in_grad, hidden_one, ffn_rms, ffn_gain)
    hidden_low = hidden_grad.astype(jnp.bfloat16)
    held_in, held_out, hidden_low = lax.optimization_barrier((w_in, w_out, hidden_low))
    in_full, out_full = (
        lax.all_gather(held_in, "seq", axis=0, tiled=True),
        lax.all_gather(held_out, "seq", axis=0, tiled=True),
    )
    gated_grad = bf_dot(hidden_low, out_full.T).reshape(row_count, HEADS, DV)
    head_normed_grad = gated_grad * swish
    gate_vals_grad = gated_grad * head_normed * gate_sig * (1.0 + gate_vals * (1.0 - gate_sig))
    head_gain_grad = jnp.sum(head_normed_grad * mixer_rows * head_rms, axis=(0, 1))
    mixer_grad = rms_back(head_normed_grad, mixer_rows, head_rms, head_gain).reshape(
        seq_count, block_len, HEADS, DV
    )
    state_term = jnp.einsum("sbhc,sbhv->shcv", query_reach, mixer_grad, precision=highest)
    _, outgoing = carried_in((block_decay, state_term), "seq", compose, identity)

    def local_block(query_in, key_in, value_in, decay_in, memory_in):
        return recurrence(
            query_in, key_in, value_in, decay_in, doc_start, position, memory_in, segment_step
        )

    _, block_pullback = jax.vjp(local_block, query_vecs, key_vecs, value_vecs, decay_rows, incoming)
    query_grad, key_grad, value_grad, decay_grad, _ = block_pullback((mixer_grad, outgoing))
    act_in_grad = jnp.concatenate(
        [
            query_grad.reshape(seq_count, block_len, key_width) * DK ** (-0.5),
            key_grad.reshape(seq_count, block_len, key_width),
            value_grad.reshape(seq_count, block_len, value_width),
        ],
        axis=-1,
    )
    conv_pre_grad = act_in_grad * conv_sig * (1.0 + convolved * (1.0 - conv_sig))
    padded_grad = jnp.zeros_like(padded)
    tap_grads = []
    for tap_index in range(CONV):
        offset = CONV - 1 - tap_index
        masked = conv_pre_grad * usables[tap_index]
        tap_grads.append(jnp.sum(masked * padded[:, offset : offset + block_len, :], axis=(0, 1)))
        padded_grad = padded_grad + jnp.pad(
            masked * conv_weight[tap_index], ((0, 0), (offset, CONV - 1 - offset), (0, 0))
        )
    conv_weight_grad = jnp.stack(tap_grads, axis=0)
    back_edge = shifted(padded_grad[:, : CONV - 1, :].astype(jnp.bfloat16), "seq", -1).astype(
        jnp.float32
    )
    mixed_grad = padded_grad[:, CONV - 1 :, :] + jnp.pad(
        back_edge, ((0, 0), (block_len - (CONV - 1), 0), (0, 0))
    )
    proj_grad = jnp.concatenate(
        [mixed_grad.reshape(row_count, conv_width), gate_vals_grad.reshape(row_count, value_width)],
        axis=1,
    ).astype(jnp.bfloat16)
    logit_grad = decay_grad.reshape(row_count, key_width) / gate_scale * jax.nn.sigmoid(-gate_logit)
    gate_bias_grad = jnp.sum(logit_grad, axis=0)
    w_high_grad = jnp.dot(
        lowrank.T, logit_grad, precision=highest, preferred_element_type=jnp.float32
    )
    lowrank_grad = jnp.dot(
        logit_grad, w_high.T, precision=highest, preferred_element_type=jnp.float32
    ).astype(jnp.bfloat16)
    w_low_grad = jnp.dot(normed.T, lowrank_grad, preferred_element_type=jnp.float32)
    normed_grad = bf_dot(proj_grad, in_full.T) + bf_dot(lowrank_grad, w_low.T)
    norm_gain_grad = jnp.sum(normed_grad * layer_in * inv_rms, axis=0)
    input_grad = hidden_grad + rms_back(normed_grad, layer_in, inv_rms, norm_gain)
    small_grads = lax.psum(
        (
            norm_gain_grad,
            conv_weight_grad,
            w_low_grad,
            w_high_grad,
            gate_bias_grad,
            head_gain_grad,
            ffn_gain_grad,
        ),
        "seq",
    )
    in_term = jnp.dot(normed.T, proj_grad, preferred_element_type=jnp.float32)
    out_term = jnp.dot(gated.T, hidden_low, preferred_element_type=jnp.float32)
    w_in_grad, w_out_grad = (
        lax.psum_scatter(in_term, "seq", scatter_dimension=0, tiled=True),
        lax.psum_scatter(out_term, "seq", scatter_dimension=0, tiled=True),
    )
    w_gate_up_grad, w_down_grad = ffn_sums
    return (
        layer_out.reshape(seq_count, block_len, model_width),
        input_grad.reshape(seq_count, block_len, model_width),
        small_grads[0],
        w_in_grad,
        small_grads[1],
        small_grads[2],
        small_grads[3],
        small_grads[4],
        small_grads[5],
        w_out_grad,
        small_grads[6],
        w_gate_up_grad,
        w_down_grad,
    )


def solution(mesh):
    placed = (
        P(None, "seq", None),
        P(None, "seq"),
        P(),
        P("seq", None),
        P(),
        P(),
        P(),
        P(),
        P(),
        P("seq", None),
        P(),
        P("seq", None),
        P("seq", None),
        P(None, "seq", None),
    )
    return jax.shard_map(
        local,
        mesh=mesh,
        in_specs=placed,
        out_specs=(
            P(None, "seq", None),
            P(None, "seq", None),
            P(),
            P("seq", None),
            P(),
            P(),
            P(),
            P(),
            P(),
            P("seq", None),
            P(),
            P("seq", None),
            P("seq", None),
        ),
        check_vma=False,
    )
```

profile of v0, /device:TPU:0, one launch (start us, length us, event | category | flops | bytes accessed | tf_op | source)
XLA Modules:
  0.0 2004.9 jit_solution(10074225457623221174)
XLA Ops:
  13.5 3.0 fusion.123
  16.5 66.6 %all-gather.13.cloned.1.call-done = bf16[1024,3072]{1,0:T(8,128)(2,1)} async-done(((bf16[32,3072]{1,0:T(8,128)(2,1)}), bf16[1024,3072]{1,0:T(8,128)(2,1)}) %all-gather.13.cloned.1.call-update) | async-done | bytes 6291472 | tf_op jit(solution)/shard_map/all_gather | solution.py:158
  83.1 6.4 convolution_convert_fusion
  91.3 2.7 collective-permute-start
  101.9 2.9 maximum_convert_fusion
  104.9 6.0 fusion.89
  120.7 2.9 copy.270
  123.6 3.2 reshape_reshape.19
  130.2 43.3 %while.105 = (s32[]{:T(128)}, f32[2,4,128,256]{3,2,1,0:T(8,128)S(1)}, f32[4,2,64,4,256]{4,2,3,1,0:T(8,128)}, f32[4,2,64,4,128]{4,3,2,1,0:T(4,128)}, s32[4,2,64]{...) while((s32[]{:T(128)}, ...), condition=%wide.region_3.4_spmd.clone, body=%wide.region_1.3_spmd.clone.sunk | while | flops 559535616 | bytes 11459072 | solution.py:99
  136.4 2.6 fusion.269
  147.2 2.6 fusion.269
  158.0 2.6 fusion.269
  168.8 2.6 fusion.269
  186.3 40.4 %all_gather.45 = f32[32,2,4,128]{3,2,1,0:T(4,128)S(1)} all-gather(f32[1,2,4,128]{3,2,1,0:T(4,128)S(1)} %get-tuple-element.1403), channel_id=1, replica_groups=mesh['seq'=32] {'seq'}, dimensions={0}, use_global_device_ids=true | all-gather | bytes 135168 | tf_op jit(solution)/shard_map/all_gather | solution.py:27
  228.2 2.6 copy.280
  230.7 138.8 %all-gather.29.cloned.1.call-done = f32[64,4,128,256]{3,2,1,0:T(8,128)} async-done(((f32[2,4,128,256]{3,2,1,0:T(8,128)}), f32[64,4,128,256]{3,2,1,0:T(8,128)}) %all-gather.29.cloned.1.call-update) | async-done | bytes 33554448 | tf_op jit(solution)/shard_map/all_gather | solution.py:27
  369.5 51.9 %while.106 = (s32[]{:T(128)}, f32[2,4,128,256]{3,2,1,0:T(8,128)S(1)}, s32[]{:T(128)}, f32[32,2,4,128]{3,2,1,0:T(4,128)S(1)}, f32[32,2,4,128,256]{4,3,2,1,0:T(8,128)}, /*index=5*/s32[]{:T(128)}, s32[]{:T(128)}) while((s32[]{:T(128)}, f32[2,4,128,256]{3,2,1,0:T(8,128)S(1)}, s32[]{:T(128)}, f32[32,2,4,128]{3,2,1,0:T(4,128)S(1)}, ...), condition=%wide.region_7.8_spmd.clone, body=%wide.region_6.7_spmd.clone.sunk | while | flops 1048580 | bytes 3158121 | solution.py:36
  421.4 5.6 multiply_reduce_fusion.9
  432.9 3.0 multiply_convert_fusion.5
  435.9 5.0 multiply_reduce_fusion.8
  440.9 78.9 %all-gather.17.cloned.1.call-done = bf16[1024,5632]{1,0:T(8,128)(2,1)} async-done(((bf16[32,5632]{1,0:T(8,128)(2,1)}), bf16[1024,5632]{1,0:T(8,128)(2,1)}) %all-gather.17.cloned.1.call-update) | async-done | bytes 11534352 | tf_op jit(solution)/shard_map/all_gather | solution.py:213
  519.7 12.2 fusion.136
  532.0 56.1 %all-gather.21.cloned.1.call-done = bf16[2816,1024]{1,0:T(8,128)(2,1)} async-done(((bf16[88,1024]{1,0:T(8,128)(2,1)}), bf16[2816,1024]{1,0:T(8,128)(2,1)}) %all-gather.21.cloned.1.call-update) | async-done | bytes 5767184 | tf_op jit(solution)/shard_map/all_gather | solution.py:229
  588.0 12.4 multiply_convert_fusion.1
  600.5 80.4 %all-gather.23.cloned.1.call-done = bf16[1024,5632]{1,0:T(8,128)(2,1)} async-done(((bf16[32,5632]{1,0:T(8,128)(2,1)}), bf16[1024,5632]{1,0:T(8,128)(2,1)}) %all-gather.23.cloned.1.call-update) | async-done | bytes 11534352 | tf_op jit(solution)/shard_map/all_gather | solution.py:228
  680.9 13.8 multiply_reduce_fusion.4
  694.7 3.3 fusion.137
  698.0 2.8 slice_convert_fusion.1
  700.8 3.2 reshape.701
  704.0 48.9 %all-gather.25.cloned.1.call-done = bf16[1024,1024]{1,0:T(8,128)(2,1)} async-done(((bf16[32,1024]{1,0:T(8,128)(2,1)}), bf16[1024,1024]{1,0:T(8,128)(2,1)}) %all-gather.25.cloned.1.call-update) | async-done | bytes 2097168 | tf_op jit(solution)/shard_map/all_gather | solution.py:248
  752.9 7.0 multiply_convert_fusion.3
  759.8 3.2 reshape.700
  763.0 4.6 multiply_reduce_fusion.5
  767.6 3.7 fusion.119
  773.1 4.8 fusion.146
  778.6 40.5 %all_gather.53 = bf16[32,2,4,128]{3,2,1,0:T(4,128)(2,1)S(1)} all-gather(bf16[1,2,4,128]{3,2,1,0:T(4,128)(2,1)} %get-tuple-element.1402), channel_id=1, replica_groups=mesh['seq'=32] {'seq'}, dimensions={0}, use_global_device_ids=true | all-gather | bytes 67584 | tf_op jit(solution)/shard_map/all_gather | solution.py:44
  819.1 3.2 reshape.703
  822.3 9.5 fusion.147
  839.0 50.1 %while.103 = (s32[]{:T(128)}, f32[2,4,128,256]{3,2,1,0:T(8,128)S(1)}, f32[4,2,64,4,128]{4,3,2,1,0:T(4,128)}, f32[4,2,64,4,128]{4,3,2,1,0:T(4,128)}, f32[4,2,64,4...) while((s32[]{:T(128)}, ...), condition=%wide.region_16.17_spmd, body=%wide.region_14.16_spmd.sunk | while | flops 257153792 | bytes 10388301 | solution.py:99
  878.5 2.6 multiply_dynamic-update-slice_fusion.4
  889.3 3.2 reshape.702
  892.5 4.8 fusion.107
  897.4 42.9 %while.102 = (s32[]{:T(128)}, f32[2,4,128,256]{3,2,1,0:T(8,128)S(1)}, s32[]{:T(128)}, bf16[32,2,4,128]{3,2,1,0:T(4,128)(2,1)S(1)}, bf16[32,2,4,128,256]{4,3,2,1,...) while((s32[]{:T(128)}, f32[2,4,128,256]{3,2,1,0:T(8,128)S(1)}, s32[]{:T(128)}, ...), condition=%wide.region_13.14_spmd, body=%wide.region_12.13_spmd.sunk | while | flops 787462 | bytes 2631827 | solution.py:61
  945.1 74.9 %while.104 = (s32[]{:T(128)}, f32[2,4,128,256]{3,2,1,0:T(8,128)S(1)}, f32[4,2,64,4,128]{4,2,3,1,0:T(8,128)}, f32[4,2,64,4,128]{4,2,3,1,0:T(8,128)}, f32[4,2,64,4...) while((s32[]{:T(128)}, ...), condition=%wide.region_21.22_spmd, body=%wide.region_17.21_spmd.sunk | while | flops 1114211328 | bytes 49537916 | solution.py:99
  1020.0 4.8 copy.330
  1024.9 4.2 reshape.718
  1034.6 2.7 copy.329
  1037.3 3.4 reshape.717
  1040.8 14.0 multiply_reduce_fusion.3
  1054.9 3.3 multiply_multiply_fusion.4
  1058.2 6.8 pad_add_fusion
  1065.0 2.7 copy-done.9
  1079.0 4.2 fusion.87
  1085.8 10.5 fusion.102
  1096.3 13.8 fusion.90
  1110.5 8.4 fusion.115
  1119.0 8.1 convolution_add_fusion.4
  1127.1 2.6 fusion.98
  1129.7 37.6 %reduce-scatter.7.cloned.1.call-done = f32[32,1024]{1,0:T(8,128)} async-done(((f32[1024,1024]{1,0:T(8,128)}), f32[32,1024]{1,0:T(8,128)}) %reduce-scatter.7.cloned.1.call-update) | async-done | bytes 131088 | tf_op jit(solution)/shard_map/reduce_scatter | solution.py:324
  1167.3 153.6 %reduce-scatter.11.cloned.1.call-done = f32[88,1024]{1,0:T(8,128)} async-done(((f32[2816,1024]{1,0:T(8,128)}), f32[88,1024]{1,0:T(8,128)}) %reduce-scatter.11.cloned.1.call-update) | async-done | bytes 360464 | tf_op jit(solution)/shard_map/reduce_scatter | solution.py:239
  1320.9 119.7 %all-reduce.10.cloned.1.call-done = f32[1024,16]{0,1:T(8,128)} async-done(((f32[1024,16]{0,1:T(8,128)}), f32[1024,16]{0,1:T(8,128)}) %all-reduce.10.cloned.1.call-update) | async-done | bytes 65552 | tf_op jit(solution)/shard_map/psum | solution.py:308
  1440.6 130.0 %all-reduce.12.cloned.1.call-done = (f32[1024]{0:T(1024)}, f32[4,2048]{1,0:T(4,128)}, f32[16,512]{1,0:T(8,128)}, f32[512]{0:T(512)}, f32[256]{0:T(256)}, /*index=5*/f32[1024]{0:T(1024)}) async-done(((f32[1024]{0:T(1024)}, f32[4,2048]{1,0:T(4,128)}, f32[16,512]{1,0:T(8,128)}, f32[512]{0:T(512)}, f32[256]{0:T(256)}, /*index=5*/f32[1024]{0:T(1024)}), (f32[1024]{0:T(1024)}, f32[4,2048]{1,0:T(4,128)}, ...) | async-done | bytes 76816 | tf_op jit(solution)/shard_map/psum | solution.py:308
  1570.6 251.0 %reduce-scatter.9.cloned.1.call-done = f32[32,5632]{1,0:T(8,128)} async-done(((f32[1024,5632]{1,0:T(8,128)}), f32[32,5632]{1,0:T(8,128)}) %reduce-scatter.9.cloned.1.call-update) | async-done | bytes 720912 | tf_op jit(solution)/shard_map/reduce_scatter | solution.py:238
  1821.6 167.0 %reduce-scatter.5.cloned.1.call-done = f32[32,3072]{1,0:T(8,128)} async-done(((f32[1024,3072]{1,0:T(8,128)}), f32[32,3072]{1,0:T(8,128)}) %reduce-scatter.5.cloned.1.call-update) | async-done | bytes 393232 | tf_op jit(solution)/shard_map/reduce_scatter | solution.py:323
  (645 shorter events, 339.3 us)
Async XLA Ops:
  7.2 6.3 copy-start
  7.2 5.2 copy-start.34
  7.2 75.9 %all-gather.13.cloned.1.call-start = ((), (), s32[]{:S(2)}) async-start(), calls=%async_computation.4 | async-start | bytes 6488064 | tf_op jit(solution)/shard_map/all_gather | solution.py:158
  7.9 361.6 %all-gather.29.cloned.1.call-start = ((), (), s32[]{:S(2)}) async-start(), calls=%async_computation.17 | async-start | bytes 34603008 | tf_op jit(solution)/shard_map/all_gather | solution.py:27
  8.0 5.5 copy-start.63
  9.5 6.9 copy-start.54
  10.8 94.0 %copy-start.46 = (f32[2,256]{1,0:T(2,128)}, f32[2,256]{1,0:T(2,128)S(1)}, u32[]{:S(2)}) copy-start(f32[2,256]{1,0:T(2,128)S(1)} %get-tuple-element.1448) | copy-start | bytes 6148
  10.8 94.0 %copy-start.48 = (f32[2,256]{1,0:T(2,128)}, f32[2,256]{1,0:T(2,128)S(1)}, u32[]{:S(2)}) copy-start(f32[2,256]{1,0:T(2,128)S(1)} %get-tuple-element.1449) | copy-start | bytes 6148
  10.8 94.1 %copy-start.50 = (f32[2,256]{1,0:T(2,128)}, f32[2,256]{1,0:T(2,128)S(1)}, u32[]{:S(2)}) copy-start(f32[2,256]{1,0:T(2,128)S(1)} %get-tuple-element.1450) | copy-start | bytes 6148
  12.4 70.8 %copy-start.12 = (bf16[512,1024]{1,0:T(8,128)(2,1)}, bf16[512,1024]{1,0:T(8,128)(2,1)S(1)}, u32[]{:S(2)}) copy-start(bf16[512,1024]{1,0:T(8,128)(2,1)S(1)} %fusion.94) | copy-start | bytes 3145732
  12.4 4.1 copy-start.52
  16.5 88.4 %copy-start.38 = (f32[1,2048]{1,0:T(1,128)}, f32[1,2048]{1,0:T(1,128)S(1)}, u32[]{:S(2)}) copy-start(f32[1,2048]{1,0:T(1,128)S(1)} %get-tuple-element.1443) | copy-start | bytes 24580
  16.5 88.4 %copy-start.40 = (f32[1,2048]{1,0:T(1,128)}, f32[1,2048]{1,0:T(1,128)S(1)}, u32[]{:S(2)}) copy-start(f32[1,2048]{1,0:T(1,128)S(1)} %get-tuple-element.1444) | copy-start | bytes 24580
  16.5 88.4 %copy-start.42 = (f32[1,2048]{1,0:T(1,128)}, f32[1,2048]{1,0:T(1,128)S(1)}, u32[]{:S(2)}) copy-start(f32[1,2048]{1,0:T(1,128)S(1)} %get-tuple-element.1445) | copy-start | bytes 24580
  16.5 88.4 %copy-start.44 = (f32[1,2048]{1,0:T(1,128)}, f32[1,2048]{1,0:T(1,128)S(1)}, u32[]{:S(2)}) copy-start(f32[1,2048]{1,0:T(1,128)S(1)} %get-tuple-element.1446) | copy-start | bytes 24580
  89.6 4.5 copy-start.61
  91.3 10.1 collective-permute-start
  104.9 6.1 copy-start.1
  119.5 4.1 copy-start.15
  173.5 7.5 copy-start.62
  174.5 261.4 %all-gather.15.cloned.1.call-start = ((), (), s32[]{:S(2)}) async-start(), calls=%async_computation.5 | async-start | bytes 2162688 | tf_op jit(solution)/shard_map/all_gather | solution.py:159
  175.3 344.5 %all-gather.17.cloned.1.call-start = ((), (), s32[]{:S(2)}) async-start(), calls=%async_computation.6 | async-start | bytes 11894784 | tf_op jit(solution)/shard_map/all_gather | solution.py:213
  175.8 412.2 %all-gather.21.cloned.1.call-start = ((), (), s32[]{:S(2)}) async-start(), calls=%async_computation.8 | async-start | bytes 5947392 | tf_op jit(solution)/shard_map/all_gather | solution.py:229
  176.4 504.5 %all-gather.23.cloned.1.call-start = ((), (), s32[]{:S(2)}) async-start(), calls=%async_computation.9 | async-start | bytes 11894784 | tf_op jit(solution)/shard_map/all_gather | solution.py:228
  177.0 575.9 %all-gather.25.cloned.1.call-start = ((), (), s32[]{:S(2)}) async-start(), calls=%async_computation.10 | async-start | bytes 2162688 | tf_op jit(solution)/shard_map/all_gather | solution.py:248
  182.9 43.8 %copy-start.22 = (f32[4,2,64,4,256]{4,2,3,1,0:T(8,128)S(1)}, f32[4,2,64,4,256]{4,2,3,1,0:T(8,128)}, u32[]{:S(2)}) copy-start(f32[4,2,64,4,256]{4,2,3,1,0:T(8,128)} %get-tuple-element.908) | copy-start | bytes 6291460
  435.9 83.9 %copy-start.33 = (f32[1024]{0:T(1024)S(1)}, f32[1024]{0:T(1024)}, u32[]{:S(2)}) copy-start(f32[1024]{0:T(1024)} %param.34) | copy-start | bytes 12292
  680.9 13.8 copy-start.10
  680.9 13.8 copy-start.27
  698.0 199.3 %all-gather.31.cloned.1.call-start = ((), (), s32[]{:S(2)}) async-start(), calls=%async_computation.18 | async-start | bytes 17301504 | tf_op jit(solution)/shard_map/all_gather | solution.py:44
  763.0 4.6 copy-start.5
  763.0 4.6 copy-start.17
  763.0 4.6 copy-start.19
  771.3 314.5 %all-gather.27.cloned.1.call-start = ((), (), s32[]{:S(2)}) async-start(), calls=%async_computation.11 | async-start | bytes 6488064 | tf_op jit(solution)/shard_map/all_gather | solution.py:247
  772.0 346.9 %all-gather.19.cloned.1.call-start = ((), (), s32[]{:S(2)}) async-start(), calls=%async_computation.7 | async-start | bytes 5947392 | tf_op jit(solution)/shard_map/all_gather | solution.py:214
  772.6 394.7 %reduce-scatter.7.cloned.1.call-start = ((), (), s32[]{:S(2)}) async-start(), calls=%async_computation.14 | async-start | bytes 4325376 | tf_op jit(solution)/shard_map/reduce_scatter | solution.py:324
  777.9 543.0 %reduce-scatter.11.cloned.1.call-start = ((), (), s32[]{:S(2)}) async-start(), calls=%async_computation.16 | async-start | bytes 11894784 | tf_op jit(solution)/shard_map/reduce_scatter | solution.py:239
  831.9 608.7 %all-reduce.10.cloned.1.call-start = ((), (), s32[]{:S(2)}) async-start(), calls=%async_computation.13 | async-start | bytes 131072 | tf_op jit(solution)/shard_map/psum | solution.py:308
  945.1 4.2 copy-start.3
  949.4 4.4 copy-start.7
  963.8 4.3 copy-start.3
  968.0 4.4 copy-start.7
  982.5 4.2 copy-start.3
  986.7 4.4 copy-start.7
  1001.1 4.5 copy-start.3
  1005.6 4.5 copy-start.7
  1037.3 3.4 copy-start.47
  1037.3 3.4 copy-start.49
  1037.3 3.4 copy-start.51
  1037.3 3.4 copy-start.53
  1040.8 14.1 copy-start.39
  1040.8 14.1 copy-start.41
  1040.8 14.1 copy-start.43
  1040.8 14.1 copy-start.45
  1068.2 9.3 collective-permute-start.1
  1076.6 494.0 %all-reduce.12.cloned.1.call-start = ((), (), s32[]{:S(2)}) async-start(), calls=%async_computation.19 | async-start | bytes 153600 | tf_op jit(solution)/shard_map/psum | solution.py:308
  1085.8 10.6 copy-start.11
  1096.3 725.3 %reduce-scatter.9.cloned.1.call-start = ((), (), s32[]{:S(2)}) async-start(), calls=%async_computation.15 | async-start | bytes 23789568 | tf_op jit(solution)/shard_map/reduce_scatter | solution.py:238
  1110.1 878.5 %reduce-scatter.5.cloned.1.call-start = ((), (), s32[]{:S(2)}) async-start(), calls=%async_computation.12 | async-start | bytes 12976128 | tf_op jit(solution)/shard_map/reduce_scatter | solution.py:323
  1118.9 8.2 copy-start.18
  1118.9 8.2 copy-start.57
  1119.0 8.2 copy-start.21
  1119.0 8.2 copy-start.28
  1119.0 8.2 copy-start.31
  (30 other events, 62.4 us)
Sparse Core Ops, SparseCore 0:
  10.9 72.1 all-gather.12
  174.7 194.8 all-gather.28
  372.4 54.5 all-gather.14
  429.7 89.9 all-gather.16
  522.4 65.5 all-gather.20
  590.7 90.1 all-gather.22
  698.1 54.7 all-gather.24
  771.4 113.9 all-gather.30
  888.3 67.6 all-gather.26
  958.7 65.8 all-gather.18
  1027.4 139.8 reduce-scatter.6
  1170.0 150.7 reduce-scatter.10
  1327.0 113.4 all-reduce.9
  1448.0 122.5 all-reduce.11
  1573.3 248.2 reduce-scatter.8
  1828.1 160.5 reduce-scatter.4
where the time goes:
time: 2010 us; the launch traced here: 2000 us
  waiting for transfers between devices  1330 us (66%)
  other arithmetic  212 us (11%)
  matrix products  202 us (10%)
  local copies, waits for them, and re-layouts  152 us (8%)
  blocking collectives  80.9 us (4%)
    reduce_scatter x1, waiting for transfers between devices, local(): lax.psum_scatter(gate_up_term, 'seq', scatter_dimension=0, tiled=True)  251 us
    psum x2, waiting for transfers between devices, local(): lax.psum((norm_gain_grad, conv_weight_grad, w_low_grad, w_high_grad, gate...  250 us
    reduce_scatter x1, waiting for transfers between devices, local(): lax.psum_scatter(in_term, 'seq', scatter_dimension=0, tiled=True)  167 us
    reduce_scatter x1, waiting for transfers between devices, local(): lax.psum_scatter(down_term, 'seq', scatter_dimension=0, tiled=True)  154 us
    all_gather x1, waiting for transfers between devices, entering(): pieces = jax.tree.map(lambda part: lax.all_gather(part, axis), value)  139 us
    all_gather x1, waiting for transfers between devices, local(): lax.all_gather(held_up, 'seq', axis=0, tiled=True)  80.4 us
    all_gather x1, waiting for transfers between devices, local(): lax.all_gather(w_gate_up, 'seq', axis=0, tiled=True)  78.9 us
    dot_general x10, matrix products, bf_dot(): return jnp.dot(left, right, preferred_element_type=jnp.float32)  77.4 us
  transfers between devices with their start and end apart: 18, of which 12 were waited for; matrix products, arithmetic and copies ran while one was open for 22% of the time, Pallas kernels for 0%

commit v1 on v0

--- a/solution.py
+++ b/solution.py
@@ -16,49 +16,148 @@
 highest = lax.Precision.HIGHEST
 
 
-def shifted(array, axis, by):
-    count = lax.axis_size(axis)
+GROUP = 8
+HALO = 8
+
+
+def chip_axes():
+    count = lax.axis_size("seq")
+    sides = {16: (4, 2, 2), 64: (4, 4, 4)}.get(count // 2, (count // 2, 1, 1))
+    return (
+        (sides[0], 2 * sides[1] * sides[2]),
+        (sides[1], 2 * sides[2]),
+        (sides[2], 2),
+        (2, 1),
+    )
+
+
+def moved(array, size, stride, by):
+    count = lax.axis_size("seq")
+    pairs = [(i, i + by * stride) for i in range(count) if 0 <= (i // stride) % size + by < size]
+    return lax.ppermute(array, "seq", pairs)
+
+
+def swapped(array, mask):
+    count = lax.axis_size("seq")
+    return lax.ppermute(array, "seq", [(i, i ^ mask) for i in range(count)])
+
+
+def shifted(array, by):
+    count = lax.axis_size("seq")
     pairs = [(i, i + by) for i in range(count) if 0 <= i + by < count]
-    return lax.ppermute(array, axis, pairs)
-
-
-def entering(value, axis, join, neutral):
-    count, mine = (lax.axis_size(axis), lax.axis_index(axis))
-    pieces = jax.tree.map(lambda part: lax.all_gather(part, axis), value)
-    running = jax.tree.map(
-        lambda part, zero: jnp.full_like(part, 0) + jnp.asarray(zero, part.dtype), value, neutral
-    )
-
-    def turn(position, running):
-        longer = join(running, jax.tree.map(lambda part: part[position], pieces))
-        return jax.tree.map(lambda new, old: jnp.where(position < mine, new, old), longer, running)
-
-    return lax.fori_loop(0, count - 1, turn, running)
-
-
-def carried_in(array, axis, join, neutral):
-    count = lax.axis_size(axis)
-    place = lax.axis_index(axis)
-    ahead = count - 1 - place
-    gathered = jax.tree.map(
-        lambda a, kind: lax.all_gather(a.astype(kind), axis),
-        array,
-        jax.tree.map(lambda a: jnp.bfloat16 if a.dtype == jnp.float32 else a.dtype, array),
-    )
-    state = jax.tree.map(lambda a, e: jnp.zeros_like(a) + jnp.asarray(e, a.dtype), array, neutral)
-
-    def one(turn, state):
-        source = count - 1 - turn
-        return join(
-            state,
-            jax.tree.map(
-                lambda a, own: lax.dynamic_index_in_dim(a, source, 0, False).astype(own.dtype),
-                gathered,
-                array,
-            ),
-        )
-
-    return lax.fori_loop(0, ahead, one, state)
+    return lax.ppermute(array, "seq", pairs)
+
+
+def line_gather(block, size, stride, at):
+    mine = (lax.axis_index("seq") // stride) % size
+    if size == 2:
+        other = swapped(block, stride)
+        first = jnp.where(mine == 0, block, other)
+        second = jnp.where(mine == 0, other, block)
+        return jnp.stack([first, second], axis=at)
+    below, above = [block], [block]
+    for _ in range(size - 1):
+        below.append(moved(below[-1], size, stride, 1))
+        above.append(moved(above[-1], size, stride, -1))
+    row = jnp.stack(below[:0:-1] + above, axis=at)
+    return lax.dynamic_slice_in_dim(row, size - 1 - mine, size, axis=at)
+
+
+def gather_rows(shard, order):
+    axes, done, block = chip_axes(), [], shard
+    for which in order + (3,):
+        size, stride = axes[which]
+        if size > 1:
+            block = line_gather(block, size, stride, sum(1 for d in done if d < which))
+            done.append(which)
+    return block.reshape(-1, shard.shape[-1])
+
+
+def line_reduce(block, size, stride, at):
+    mine = (lax.axis_index("seq") // stride) % size
+
+    def pick(index):
+        return lax.dynamic_index_in_dim(block, index, at, False).astype(jnp.float32)
+
+    if size == 2:
+        return pick(mine) + swapped(pick(1 - mine).astype(jnp.bfloat16), stride).astype(jnp.float32)
+    up = down = None
+    for step in range(1, size):
+        reach = size - step
+        to_up = pick(jnp.minimum(mine + reach, size - 1))
+        to_down = pick(jnp.maximum(mine - reach, 0))
+        if step > 1:
+            to_up, to_down = to_up + up, to_down + down
+        up = moved(to_up.astype(jnp.bfloat16), size, stride, 1).astype(jnp.float32)
+        down = moved(to_down.astype(jnp.bfloat16), size, stride, -1).astype(jnp.float32)
+    return pick(mine) + up + down
+
+
+def reduce_rows(full, order):
+    axes = chip_axes()
+    left = [which for which in range(4) if axes[which][0] > 1]
+    block = full.reshape(tuple(axes[which][0] for which in left) + (-1, full.shape[-1]))
+    for which in (3,) + order:
+        size, stride = axes[which]
+        if size > 1:
+            block = line_reduce(block, size, stride, left.index(which))
+            left.remove(which)
+    return block
+
+
+def small_sum(value):
+    axes = chip_axes()
+    for size, stride in axes[::-1]:
+        if size == 2:
+            value = value + swapped(value, stride)
+        elif size > 1:
+            total = value
+            for by in range(1, size):
+                total = total + moved(value, size, stride, by) + moved(value, size, stride, -by)
+            value = total
+    return value
+
+
+def to_owners(pieces):
+    mine = lax.axis_index("seq") % GROUP
+    got = [lax.dynamic_index_in_dim(pieces, mine, 0, False)]
+    for mask in range(1, GROUP):
+        got.append(swapped(lax.dynamic_index_in_dim(pieces, mine ^ mask, 0, False), mask))
+    got = jnp.stack(got)
+    return [
+        lax.dynamic_index_in_dim(got, mine ^ index, 0, False).astype(jnp.float32)
+        for index in range(GROUP)
+    ]
+
+
+def packed(decay, state):
+    decay = decay.reshape(GROUP, 1, DK)
+    high = decay.astype(jnp.bfloat16)
+    low = (decay - high.astype(jnp.float32)).astype(jnp.bfloat16)
+    return jnp.concatenate(
+        [
+            state.reshape(GROUP, DK, DV).astype(jnp.bfloat16),
+            jnp.pad(jnp.concatenate([high, low], axis=-1), ((0, 0), (0, 15), (0, 0))),
+        ],
+        axis=1,
+    )
+
+
+def carried_over(decay, state, backward):
+    got = to_owners(packed(decay, state))
+    order = range(GROUP)[::-1] if backward else range(GROUP)
+    running = jnp.zeros((DK, DV), jnp.float32)
+    reach = jnp.ones((DK, 1), jnp.float32)
+    before = [None] * GROUP
+    for index in order:
+        before[index] = (running, reach)
+        kept = (got[index][DK, :DK] + got[index][DK, DK:])[:, None]
+        running = kept * running + got[index][:DK]
+        reach = reach * kept
+    beyond = shifted(running.astype(jnp.bfloat16), -GROUP if backward else GROUP)
+    beyond = beyond.astype(jnp.float32)
+    result = jnp.stack([(part + far * beyond).astype(jnp.bfloat16) for part, far in before])
+    return jnp.stack(to_owners(result)).reshape(state.shape)
 
 
 def segment_step(memory, inputs_piece):
@@ -111,12 +210,6 @@
         return (outputs.reshape((span_count * SPAN,) + outputs.shape[2:]), final_memory)
 
     return jax.vmap(per_sequence)(query_vecs, key_vecs, value_vecs, log_decay, starts, memory)
-
-
-def compose(earlier, later):
-    decay_early, state_early = earlier
-    decay_late, state_late = later
-    return (decay_early * decay_late, decay_late[..., None] * state_early + state_late)
 
 
 def bf_dot(left, right):
@@ -153,22 +246,33 @@
     conv_width = 2 * key_width + value_width
     block_start = lax.axis_index("seq") * block_len
     position = block_start + jnp.arange(block_len, dtype=jnp.int32)
-    layer_in = inputs.reshape(row_count, model_width).astype(jnp.float32)
-    in_full, out_full = (
-        lax.all_gather(w_in, "seq", axis=0, tiled=True),
-        lax.all_gather(w_out, "seq", axis=0, tiled=True),
-    )
-    inv_rms = lax.rsqrt(jnp.mean(layer_in * layer_in, axis=-1, keepdims=True) + epsilon)
-    normed = (layer_in * inv_rms * norm_gain).astype(jnp.bfloat16)
-    projected = bf_dot(normed, in_full).astype(jnp.bfloat16)
+    zyx, zxy, xyz, yzx = (0, 1, 2), (0, 2, 1), (2, 1, 0), (1, 0, 2)
+    qk_full = gather_rows(w_in[:, : 2 * key_width], zxy)
+    v_full = gather_rows(w_in[:, 2 * key_width : conv_width], xyz)
+    g_full = gather_rows(w_in[:, conv_width:], yzx)
+    edge = shifted(inputs[:, block_len - HALO :, :], 1)
+    wide = jnp.concatenate([edge, inputs], axis=1).astype(jnp.float32)
+    wide_rms = lax.rsqrt(jnp.mean(wide * wide, axis=-1, keepdims=True) + epsilon)
+    wide_normed = (wide * wide_rms * norm_gain).astype(jnp.bfloat16)
+    layer_in = wide[:, HALO:].reshape(row_count, model_width)
+    inv_rms = wide_rms[:, HALO:].reshape(row_count, 1)
+    normed = wide_normed[:, HALO:].reshape(row_count, model_width)
+    wide_rows = wide_normed.reshape(-1, model_width)
+    wide_mixed = jnp.concatenate([bf_dot(wide_rows, qk_full), bf_dot(wide_rows, v_full)], axis=1)
+    wide_mixed = wide_mixed.astype(jnp.bfloat16).reshape(seq_count, HALO + block_len, conv_width)
+    gate_cols = bf_dot(normed, g_full).astype(jnp.bfloat16)
+    out_full = gather_rows(w_out, zyx)
+    gate_full = gather_rows(w_gate_up[:, :FF], zxy)
+    up_full = gather_rows(w_gate_up[:, FF:], zyx)
+    half = model_width // 2
+    down_left = gather_rows(w_down[:, :half], zxy)
+    down_right = gather_rows(w_down[:, half:], zyx)
     lowrank = bf_dot(normed, w_low)
     gate_logit = (
         jnp.dot(lowrank, w_high, precision=highest, preferred_element_type=jnp.float32) + gate_bias
     )
     log_decay = jax.nn.log_sigmoid(gate_logit) / gate_scale
-    mixed = projected[:, :conv_width].reshape(seq_count, block_len, conv_width)
-    prior = shifted(mixed[:, block_len - (CONV - 1) :, :], "seq", 1)
-    padded = jnp.concatenate([prior, mixed], axis=1).astype(jnp.float32)
+    padded = wide_mixed[:, HALO - (CONV - 1) :].astype(jnp.float32)
     usables = [
         (position[None, :] - tap_index >= doc_start).astype(jnp.float32)[:, :, None]
         for tap_index in range(CONV)
@@ -197,56 +301,54 @@
     cumulative = jnp.cumsum(decay_rows, axis=1)
     reach_in = (doc_start < block_start).astype(jnp.float32)
     block_decay = jnp.exp(cumulative[:, -1]) * reach_in[:, -1][:, None, None]
-    identity = (jnp.ones_like(block_decay), jnp.zeros_like(local_state))
-    _, incoming = entering((block_decay, local_state), "seq", compose, identity)
+    incoming = carried_over(block_decay, local_state, False)
     query_reach = query_vecs * jnp.exp(cumulative) * reach_in[:, :, None, None]
     mixer_out = local_out + jnp.einsum("sbhc,shcv->sbhv", query_reach, incoming, precision=highest)
     mixer_rows = mixer_out.reshape(row_count, HEADS, DV)
     head_rms = lax.rsqrt(jnp.mean(mixer_rows * mixer_rows, axis=-1, keepdims=True) + epsilon)
     head_normed = mixer_rows * head_rms * head_gain
-    gate_vals = projected[:, conv_width:].astype(jnp.float32).reshape(row_count, HEADS, DV)
+    gate_vals = gate_cols.astype(jnp.float32).reshape(row_count, HEADS, DV)
     gate_sig = jax.nn.sigmoid(gate_vals)
     swish = gate_vals * gate_sig
     gated = (head_normed * swish).reshape(row_count, value_width).astype(jnp.bfloat16)
     hidden_one = layer_in + bf_dot(gated, out_full)
-    gate_up_full, down_full = (
-        lax.all_gather(w_gate_up, "seq", axis=0, tiled=True),
-        lax.all_gather(w_down, "seq", axis=0, tiled=True),
-    )
     ffn_rms = lax.rsqrt(jnp.mean(hidden_one * hidden_one, axis=-1, keepdims=True) + epsilon)
     ffn_in = (hidden_one * ffn_rms * ffn_gain).astype(jnp.bfloat16)
-    gate_up = bf_dot(ffn_in, gate_up_full)
-    gate_part = gate_up[:, :FF]
-    up_part = gate_up[:, FF:]
+    gate_part = bf_dot(ffn_in, gate_full)
+    up_part = bf_dot(ffn_in, up_full)
     gate_act = jax.nn.sigmoid(gate_part)
     activation = (gate_part * gate_act * up_part).astype(jnp.bfloat16)
-    layer_out = hidden_one + bf_dot(activation, down_full)
+    layer_out = hidden_one + jnp.concatenate(
+        [bf_dot(activation, down_left), bf_dot(activation, down_right)], axis=1
+    )
     out_rows = out_grad.reshape(row_count, model_width).astype(jnp.float32)
     out_rows_low = out_rows.astype(jnp.bfloat16)
-    held_up, held_down, out_rows_low = lax.optimization_barrier((w_gate_up, w_down, out_rows_low))
-    gate_up_full, down_full = (
-        lax.all_gather(held_up, "seq", axis=0, tiled=True),
-        lax.all_gather(held_down, "seq", axis=0, tiled=True),
-    )
-    act_grad = bf_dot(out_rows_low, down_full.T)
+    act_grad = bf_dot(out_rows_low[:, :half], down_left.T) + bf_dot(
+        out_rows_low[:, half:], down_right.T
+    )
     gate_grad = act_grad * up_part * gate_act * (1.0 + gate_part * (1.0 - gate_act))
     up_grad = act_grad * gate_part * gate_act
-    gate_up_grad = jnp.concatenate([gate_grad, up_grad], axis=1).astype(jnp.bfloat16)
-    down_term = jnp.dot(activation.T, out_rows_low, preferred_element_type=jnp.float32)
-    gate_up_term = jnp.dot(ffn_in.T, gate_up_grad, preferred_element_type=jnp.float32)
-    ffn_sums = (
-        lax.psum_scatter(gate_up_term, "seq", scatter_dimension=0, tiled=True),
-        lax.psum_scatter(down_term, "seq", scatter_dimension=0, tiled=True),
-    )
-    ffn_in_grad = bf_dot(gate_up_grad, gate_up_full.T)
+    gate_grad, up_grad = gate_grad.astype(jnp.bfloat16), up_grad.astype(jnp.bfloat16)
+
+    def term(left, right):
+        return jnp.dot(left.T, right, preferred_element_type=jnp.float32).astype(jnp.bfloat16)
+
+    w_gate_up_grad = jnp.concatenate(
+        [reduce_rows(term(ffn_in, gate_grad), (2, 1, 0)), reduce_rows(term(ffn_in, up_grad), (1, 2, 0))],
+        axis=1,
+    )
+    w_down_grad = jnp.concatenate(
+        [
+            reduce_rows(term(activation, out_rows_low[:, :half]), (2, 1, 0)),
+            reduce_rows(term(activation, out_rows_low[:, half:]), (1, 2, 0)),
+        ],
+        axis=1,
+    )
+    ffn_in_grad = bf_dot(gate_grad, gate_full.T) + bf_dot(up_grad, up_full.T)
     ffn_gain_grad = jnp.sum(ffn_in_grad * hidden_one * ffn_rms, axis=0)
     hidden_grad = out_rows + rms_back(ffn_in_grad, hidden_one, ffn_rms, ffn_gain)
     hidden_low = hidden_grad.astype(jnp.bfloat16)
-    held_in, held_out, hidden_low = lax.optimization_barrier((w_in, w_out, hidden_low))
-    in_full, out_full = (
-        lax.all_gather(held_in, "seq", axis=0, tiled=True),
-        lax.all_gather(held_out, "seq", axis=0, tiled=True),
-    )
+    w_out_grad = reduce_rows(term(gated, hidden_low), (2, 1, 0))
     gated_grad = bf_dot(hidden_low, out_full.T).reshape(row_count, HEADS, DV)
     head_normed_grad = gated_grad * swish
     gate_vals_grad = gated_grad * head_normed * gate_sig * (1.0 + gate_vals * (1.0 - gate_sig))
@@ -255,7 +357,7 @@
         seq_count, block_len, HEADS, DV
     )
     state_term = jnp.einsum("sbhc,sbhv->shcv", query_reach, mixer_grad, precision=highest)
-    _, outgoing = carried_in((block_decay, state_term), "seq", compose, identity)
+    outgoing = carried_over(block_decay, state_term, True)
 
     def local_block(query_in, key_in, value_in, decay_in, memory_in):
         return recurrence(
@@ -283,16 +385,23 @@
             masked * conv_weight[tap_index], ((0, 0), (offset, CONV - 1 - offset), (0, 0))
         )
     conv_weight_grad = jnp.stack(tap_grads, axis=0)
-    back_edge = shifted(padded_grad[:, : CONV - 1, :].astype(jnp.bfloat16), "seq", -1).astype(
+    back_edge = shifted(padded_grad[:, : CONV - 1, :].astype(jnp.bfloat16), -1).astype(
         jnp.float32
     )
     mixed_grad = padded_grad[:, CONV - 1 :, :] + jnp.pad(
         back_edge, ((0, 0), (block_len - (CONV - 1), 0), (0, 0))
     )
-    proj_grad = jnp.concatenate(
-        [mixed_grad.reshape(row_count, conv_width), gate_vals_grad.reshape(row_count, value_width)],
+    mixed_grad = mixed_grad.reshape(row_count, conv_width).astype(jnp.bfloat16)
+    gate_vals_grad = gate_vals_grad.reshape(row_count, value_width).astype(jnp.bfloat16)
+    qk_grad, v_grad = mixed_grad[:, : 2 * key_width], mixed_grad[:, 2 * key_width :]
+    w_in_grad = jnp.concatenate(
+        [
+            reduce_rows(term(normed, qk_grad), (1, 2, 0)),
+            reduce_rows(term(normed, v_grad), (0, 1, 2)),
+            reduce_rows(term(normed, gate_vals_grad), (2, 0, 1)),
+        ],
         axis=1,
-    ).astype(jnp.bfloat16)
+    )
     logit_grad = decay_grad.reshape(row_count, key_width) / gate_scale * jax.nn.sigmoid(-gate_logit)
     gate_bias_grad = jnp.sum(logit_grad, axis=0)
     w_high_grad = jnp.dot(
@@ -302,28 +411,29 @@
         logit_grad, w_high.T, precision=highest, preferred_element_type=jnp.float32
     ).astype(jnp.bfloat16)
     w_low_grad = jnp.dot(normed.T, lowrank_grad, preferred_element_type=jnp.float32)
-    normed_grad = bf_dot(proj_grad, in_full.T) + bf_dot(lowrank_grad, w_low.T)
+    normed_grad = (
+        bf_dot(qk_grad, qk_full.T)
+        + bf_dot(v_grad, v_full.T)
+        + bf_dot(gate_vals_grad, g_full.T)
+        + bf_dot(lowrank_grad, w_low.T)
+    )
     norm_gain_grad = jnp.sum(normed_grad * layer_in * inv_rms, axis=0)
     input_grad = hidden_grad + rms_back(normed_grad, layer_in, inv_rms, norm_gain)
-    small_grads = lax.psum(
-        (
-            norm_gain_grad,
-            conv_weight_grad,
-            w_low_grad,
-            w_high_grad,
-            gate_bias_grad,
-            head_gain_grad,
-            ffn_gain_grad,
-        ),
-        "seq",
-    )
-    in_term = jnp.dot(normed.T, proj_grad, preferred_element_type=jnp.float32)
-    out_term = jnp.dot(gated.T, hidden_low, preferred_element_type=jnp.float32)
-    w_in_grad, w_out_grad = (
-        lax.psum_scatter(in_term, "seq", scatter_dimension=0, tiled=True),
-        lax.psum_scatter(out_term, "seq", scatter_dimension=0, tiled=True),
-    )
-    w_gate_up_grad, w_down_grad = ffn_sums
+    small = (
+        norm_gain_grad,
+        conv_weight_grad,
+        w_low_grad,
+        w_high_grad,
+        gate_bias_grad,
+        head_gain_grad,
+        ffn_gain_grad,
+    )
+    summed = small_sum(jnp.concatenate([part.reshape(-1, 128) for part in small]))
+    small_grads, start = [], 0
+    for part in small:
+        rows = part.size // 128
+        small_grads.append(summed[start : start + rows].reshape(part.shape))
+        start += rows
     return (
         layer_out.reshape(seq_count, block_len, model_width),
         input_grad.reshape(seq_count, block_len, model_width),

time: 2010 us -> 1120 us (0.56)
  waiting for transfers between devices: 1330 us -> 250 us
  starting transfers between devices: 5.74 us -> 359 us
  blocking collectives: 80.9 us -> 0 us
  other arithmetic: 212 us -> 148 us
  matrix products: 202 us -> 165 us
    reduce_scatter x4 -> x0, waiting for transfers between devices: 609 us -> none  [the longest x1 251 us: local(): lax.psum_scatter(gate_up_term, 'seq', scatter_dimension=0, tiled=True)]
    all_gather x10 -> x0, waiting for transfers between devices: 470 us -> none  [the longest x1 139 us: entering(): pieces = jax.tree.map(lambda part: lax.all_gather(part, axis), value)]
    ppermute x2 -> x185, starting transfers between devices: 3.98 us -> 359 us  [the longest x102 280 us: moved(): return lax.ppermute(array, 'seq', pairs)]
    ppermute x2 -> x185, waiting for transfers between devices: 0.01 us -> 250 us  [the longest x79 129 us: swapped(): return lax.ppermute(array, 'seq', [(i, i ^ mask) for i in range(count)])]
    psum x2 -> x0, waiting for transfers between devices: 250 us -> none  [local(): lax.psum((norm_gain_grad, conv_weight_grad, w_low_grad, w_high_grad, gate...]
    all_gather x2 -> x0, blocking collectives: 80.9 us -> none  [the longest x1 40.5 us: carried_in(): lax.all_gather(a.astype(kind), axis)]
    select_n x31 -> x0, other arithmetic: 50.6 us -> none  [turn(): jnp.where(position < mine, new, old)]
    another operation x5 -> x52, other arithmetic: 6.6 us -> 34.8 us  [the longest x47 33.8 us: line_gather(): return jnp.stack([first, second], axis=at)]
  transfers between devices with their start and end apart: 18 -> 185, of which waited for: 12 -> 71; matrix products, arithmetic and copies ran while one was open for 22% -> 24% of each run, Pallas kernels for 0% -> 0%
where the time goes in v1:
time: 1120 us; the launch traced here: 1100 us
  starting transfers between devices  359 us (32%)
  waiting for transfers between devices  250 us (22%)
  local copies, waits for them, and re-layouts  172 us (15%)
  matrix products  165 us (15%)
  other arithmetic  148 us (13%)
    ppermute x102, starting transfers between devices, moved(): return lax.ppermute(array, 'seq', pairs)  280 us
    ppermute x79, waiting for transfers between devices, swapped(): return lax.ppermute(array, 'seq', [(i, i ^ mask) for i in range(count)])  129 us
    ppermute x102, waiting for transfers between devices, moved(): return lax.ppermute(array, 'seq', pairs)  116 us
    ppermute x79, starting transfers between devices, swapped(): return lax.ppermute(array, 'seq', [(i, i ^ mask) for i in range(count)])  71.3 us
    dot_general x18, matrix products, bf_dot(): return jnp.dot(left, right, preferred_element_type=jnp.float32)  51.4 us
    unnamed x366, local copies, waits for them, and re-layouts  34.3 us
    another operation x47, other arithmetic, line_gather(): return jnp.stack([first, second], axis=at)  33.8 us
    dot_general x8, matrix products, term(): jnp.dot(left.T, right, preferred_element_type=jnp.float32)  26.8 us
  transfers between devices with their start and end apart: 185, of which 71 were waited for; matrix products, arithmetic and copies ran while one was open for 24% of the time, Pallas kernels for 0%

profile of v1, /device:TPU:0, one launch (start us, length us, event | category | flops | bytes accessed | tf_op | source)
XLA Modules:
  0.0 1101.8 jit_solution(5137903766482298554)
XLA Ops:
  0.7 5.7 collective-permute-start.43
  24.6 4.5 collective-permute-start.61
  46.6 4.5 collective-permute-start.44
  73.2 4.6 collective-permute-start.70
  79.1 4.5 collective-permute-start.3
  92.7 5.2 collective-permute-start.80
  104.5 4.4 collective-permute-start.81
  111.9 4.4 collective-permute-start.52
  119.9 5.1 collective-permute-done.74
  126.3 5.6 collective-permute-done.83
  133.2 5.1 collective-permute-done.75
  150.7 4.3 collective-permute-start.37
  161.5 5.7 collective-permute-start.53
  175.1 9.1 collective-permute-done.40
  185.1 4.4 collective-permute-start.12
  192.7 4.4 collective-permute-start.54
  200.1 4.4 collective-permute-start.63
  211.3 6.5 collective-permute-done.66
  220.7 6.0 collective-permute-done.57
  234.6 4.9 collective-permute-start.14
  247.0 7.3 collective-permute-done.17
  277.9 4.6 fusion.93
  299.2 42.0 %while.76 = (s32[]{:T(128)}, f32[2,4,128,256]{3,2,1,0:T(8,128)S(1)}, f32[4,2,64,4,256]{4,2,3,1,0:T(8,128)}, f32[4,2,64,4,128]{4,3,2,1,0:T(4,128)}, s32[4,2,64]{2...) while((s32[]{:T(128)}, ...), condition=%wide.region_3.4_spmd.clone, body=%wide.region_1.3_spmd.clone.sunk | while | flops 559535616 | bytes 11458064 | solution.py:198
  367.0 4.9 collective-permute-done.25
  404.1 4.6 collective-permute-done.33
  424.6 36.9 %while.74 = (s32[]{:T(128)}, f32[2,4,128,256]{3,2,1,0:T(8,128)S(1)}, f32[4,2,64,4,128]{4,3,2,1,0:T(4,128)}, f32[4,2,64,4,128]{4,3,2,1,0:T(4,128)}, f32[4,2,64,4,...) while((s32[]{:T(128)}, ...), condition=%wide.region_12.13_spmd, body=%wide.region_10.12_spmd.sunk | while | flops 257153792 | bytes 18774176 | solution.py:198
  461.5 6.1 multiply_convert_fusion.3
  495.8 7.7 fusion.344
  508.5 10.4 fusion.88
  527.7 5.3 convolution_convert_fusion
  536.3 5.3 convolution_convert_fusion.3
  541.6 5.0 convolution_convert_fusion.1
  573.3 4.9 constant_dynamic-slice_fusion.22
  627.3 84.3 %while.75 = (s32[]{:T(128)}, f32[2,4,128,256]{3,2,1,0:T(8,128)S(1)}, f32[4,2,64,4,128]{4,2,3,1,0:T(8,128)}, f32[4,2,64,4,128]{4,2,3,1,0:T(8,128)}, f32[4,2,64,4,...) while((s32[]{:T(128)}, ...), condition=%wide.region_17.18_spmd, body=%wide.region_13.17_spmd.sunk | while | flops 1114211328 | bytes 32760680 | solution.py:198
  732.6 10.6 multiply_reduce_fusion.3
  747.5 6.0 pad_add_fusion
  775.2 4.3 fusion.109
  788.3 6.4 collective-permute-start.111
  796.0 5.5 collective-permute-start.109
  802.8 4.6 collective-permute-start.107
  819.1 6.4 collective-permute-done.113
  843.6 7.1 collective-permute-done.141
  858.9 20.5 %collective-permute-done.142 = bf16[4,32,1024]{2,1,0:T(8,128)(2,1)S(1)} collective-permute-done((bf16[4,32,1024]{2,1,0:T(8,128)(2,1)S(1)}, bf16[4,32,1024]{2,1,0:T(8,128)(2,1)S(1)}, u32[]{:S(2)}, u32[]{:S(2)}) %collective-permute-start.142) | collective-permute-done | bytes 262176 | tf_op jit(solution)/shard_map/ppermute | solution.py:42
  879.4 4.4 collective-permute-start.143
  892.5 4.3 collective-permute-start.144
  900.0 5.9 collective-permute-done.137
  907.2 5.6 collective-permute-done.147
  914.1 4.6 collective-permute-start.135
  923.9 4.5 collective-permute-start.145
  946.1 4.4 collective-permute-start.125
  952.1 4.5 collective-permute-start.117
  959.9 6.0 collective-permute-done.120
  988.1 4.8 collective-permute-start.170
  995.1 4.6 collective-permute-start.180
  1003.4 4.6 collective-permute-start.181
  1009.4 4.6 collective-permute-start.172
  1024.5 22.2 %collective-permute-done.159 = bf16[4,2,32,2816]{3,2,0,1:T(8,128)(2,1)S(1)} collective-permute-done((bf16[4,2,32,2816]{3,2,0,1:T(8,128)(2,1)S(1)}, bf16[4,2,32,2816]{3,2,0,1:T(8,128)(2,1)S(1)}, u32[]{:S(2)}, u32[]{:S(2)}) %collective-permute-start.159) | collective-permute-done | bytes 1441824 | tf_op jit(solution)/shard_map/ppermute | solution.py:42
  1050.3 8.1 collective-permute-done.160
  1058.6 5.0 collective-permute-start.161
  1065.1 4.6 collective-permute-start.152
  1071.0 4.6 collective-permute-start.162
  1080.7 4.6 collective-permute-start.163
  1086.6 4.6 collective-permute-start.154
  1094.1 4.6 collective-permute-done.166
  (1302 shorter events, 733.3 us)
Async XLA Ops:
  0.7 45.9 %collective-permute-start.43 = (bf16[32,1024]{1,0:T(8,128)(2,1)}, bf16[32,1024]{1,0:T(8,128)(2,1)}, u32[]{:S(2)}, u32[]{:S(2)}) collective-permute-start(bf16[32,1024]{1,0:T(8,128)(2,1)} %param.29), channel_id=1, source_target_pairs={{0,8},{1,9},{2,10},{3,11},{4,12},{5,13},{6,14},{7,15},{8,16},{9,17... | collective-permute-start | bytes 196616 | tf_op jit(solution)/shard_map/ppermute | solution.py:37
  6.4 51.2 %collective-permute-start.46 = (bf16[32,1024]{1,0:T(8,128)(2,1)}, bf16[32,1024]{1,0:T(8,128)(2,1)}, u32[]{:S(2)}, u32[]{:S(2)}) collective-permute-start(bf16[32,1024]{1,0:T(8,128)(2,1)} %param.29), channel_id=1, source_target_pairs={{8,0},{9,1},{10,2},{11,3},{12,4},{13,5},{14,6},{15,7},{16,8},{17,9... | collective-permute-start | bytes 196616 | tf_op jit(solution)/shard_map/ppermute | solution.py:37
  8.4 16.2 %collective-permute-start = (bf16[2,8,1024]{2,1,0:T(8,128)(2,1)S(1)}, bf16[2,8,1024]{2,1,0:T(8,128)(2,1)S(1)}, u32[]{:S(2)}, u32[]{:S(2)}) collective-permute-start(bf16[2,8,1024]{2,1,0:T(8,128)(2,1)S(1)} %slice.351), channel_id=1, source_target_pairs={{0,1},{1,2},{2,3},{3,4},{4,5},{5,6},{6,7},{7,8},{8,9},{9,10},{10,1... | collective-permute-start | bytes 98312 | tf_op jit(solution)/shard_map/ppermute | solution.py:48
  11.4 33.9 %collective-permute-start.10 = (bf16[32,1024]{1,0:T(8,128)(2,1)}, bf16[32,1024]{1,0:T(8,128)(2,1)}, u32[]{:S(2)}, u32[]{:S(2)}) collective-permute-start(bf16[32,1024]{1,0:T(8,128)(2,1)} %get-tuple-element.1324), channel_id=1, source_target_pairs={{0,2},{1,3},{2,0},{3,1},{4,6},{5,7},{6,4},{7,5},{8,10},{9,11},{10,... | collective-permute-start | bytes 196616 | tf_op jit(solution)/shard_map/ppermute | solution.py:42
  13.3 37.8 %collective-permute-start.34 = (bf16[32,1024]{1,0:T(8,128)(2,1)}, bf16[32,1024]{1,0:T(8,128)(2,1)}, u32[]{:S(2)}, u32[]{:S(2)}) collective-permute-start(bf16[32,1024]{1,0:T(8,128)(2,1)} %get-tuple-element.1325), channel_id=1, source_target_pairs={{0,4},{1,5},{2,6},{3,7},{4,0},{5,1},{6,2},{7,3},{8,12},{9,13},{10,... | collective-permute-start | bytes 196616 | tf_op jit(solution)/shard_map/ppermute | solution.py:42
  24.6 136.9 %collective-permute-start.61 = (bf16[32,2816]{1,0:T(8,128)(2,1)}, bf16[32,2816]{1,0:T(8,128)(2,1)S(1)}, u32[]{:S(2)}, u32[]{:S(2)}) collective-permute-start(bf16[32,2816]{1,0:T(8,128)(2,1)} %get-tuple-element.1314), channel_id=1, source_target_pairs={{0,8},{1,9},{2,10},{3,11},{4,12},{5,13},{6,14},{7,15},{8,16},{9,17... | collective-permute-start | bytes 540680 | tf_op jit(solution)/shard_map/ppermute | solution.py:37
  45.3 121.9 %collective-permute-start.64 = (bf16[32,2816]{1,0:T(8,128)(2,1)}, bf16[32,2816]{1,0:T(8,128)(2,1)S(1)}, u32[]{:S(2)}, u32[]{:S(2)}) collective-permute-start(bf16[32,2816]{1,0:T(8,128)(2,1)} %get-tuple-element.1314), channel_id=1, source_target_pairs={{8,0},{9,1},{10,2},{11,3},{12,4},{13,5},{14,6},{15,7},{16,8},{17,9... | collective-permute-start | bytes 540680 | tf_op jit(solution)/shard_map/ppermute | solution.py:37
  52.1 18.8 %collective-permute-start.11 = (bf16[2,32,1024]{2,1,0:T(8,128)(2,1)S(1)}, bf16[2,32,1024]{2,1,0:T(8,128)(2,1)S(1)}, u32[]{:S(2)}, u32[]{:S(2)}) collective-permute-start(bf16[2,32,1024]{2,1,0:T(8,128)(2,1)S(1)} %pad_maximum_fusion.26), channel_id=1, source_target_pairs={{0,4},{1,5},{2,6},{3,7},{4,0},{5,1},{6,2},{7,3},{8,12},{9,13},{10,... | collective-permute-start | bytes 393224 | tf_op jit(solution)/shard_map/ppermute | solution.py:42
  91.4 24.9 %collective-permute-start.73 = (bf16[88,512]{1,0:T(8,128)(2,1)S(1)}, bf16[88,512]{1,0:T(8,128)(2,1)S(1)}, u32[]{:S(2)}, u32[]{:S(2)}) collective-permute-start(bf16[88,512]{1,0:T(8,128)(2,1)S(1)} %copy-done.97), channel_id=1, source_target_pairs={{8,0},{9,1},{10,2},{11,3},{12,4},{13,5},{14,6},{15,7},{16,8},{17,9... | collective-permute-start | bytes 270344 | tf_op jit(solution)/shard_map/ppermute | solution.py:37
  101.9 16.6 %collective-permute-start.82 = (bf16[88,512]{1,0:T(8,128)(2,1)S(1)}, bf16[88,512]{1,0:T(8,128)(2,1)S(1)}, u32[]{:S(2)}, u32[]{:S(2)}) collective-permute-start(bf16[88,512]{1,0:T(8,128)(2,1)S(1)} %get-tuple-element.1329), channel_id=1, source_target_pairs={{8,0},{9,1},{10,2},{11,3},{12,4},{13,5},{14,6},{15,7},{16,8},{17,9... | collective-permute-start | bytes 270344 | tf_op jit(solution)/shard_map/ppermute | solution.py:37
  111.9 47.0 %collective-permute-start.52 = (bf16[32,2816]{1,0:T(8,128)(2,1)S(1)}, bf16[32,2816]{1,0:T(8,128)(2,1)S(1)}, u32[]{:S(2)}, u32[]{:S(2)}) collective-permute-start(bf16[32,2816]{1,0:T(8,128)(2,1)S(1)} %copy-done.92), channel_id=1, source_target_pairs={{0,8},{1,9},{2,10},{3,11},{4,12},{5,13},{6,14},{7,15},{8,16},{9,17... | collective-permute-start | bytes 540680 | tf_op jit(solution)/shard_map/ppermute | solution.py:37
  116.4 23.3 %collective-permute-start.35 = (bf16[2,32,1024]{2,1,0:T(8,128)(2,1)S(1)}, bf16[2,32,1024]{2,1,0:T(8,128)(2,1)S(1)}, u32[]{:S(2)}, u32[]{:S(2)}) collective-permute-start(bf16[2,32,1024]{2,1,0:T(8,128)(2,1)S(1)} %pad_maximum_fusion.27), channel_id=1, source_target_pairs={{0,8},{1,9},{2,10},{3,11},{4,12},{5,13},{6,14},{7,15},{8,16},{9,17... | collective-permute-start | bytes 393224 | tf_op jit(solution)/shard_map/ppermute | solution.py:37
  139.7 20.5 %collective-permute-start.38 = (bf16[2,32,1024]{2,1,0:T(8,128)(2,1)S(1)}, bf16[2,32,1024]{2,1,0:T(8,128)(2,1)S(1)}, u32[]{:S(2)}, u32[]{:S(2)}) collective-permute-start(bf16[2,32,1024]{2,1,0:T(8,128)(2,1)S(1)} %pad_maximum_fusion.27), channel_id=1, source_target_pairs={{8,0},{9,1},{10,2},{11,3},{12,4},{13,5},{14,6},{15,7},{16,8},{17,9... | collective-permute-start | bytes 393224 | tf_op jit(solution)/shard_map/ppermute | solution.py:37
  158.5 15.3 %collective-permute-start.49 = (bf16[4,32,1024]{2,1,0:T(8,128)(2,1)S(1)}, bf16[4,32,1024]{2,1,0:T(8,128)(2,1)S(1)}, u32[]{:S(2)}, u32[]{:S(2)}) collective-permute-start(bf16[4,32,1024]{2,1,0:T(8,128)(2,1)S(1)} %constant_dynamic-slice_fusion.35), channel_id=1, source_target_pairs={{0,4},{1,5},{2,6},{3,7},{4,0},{5,1},{6,2},{7,3},{8,12},{9,13},{10,... | collective-permute-start | bytes 786440 | tf_op jit(solution)/shard_map/ppermute | solution.py:42
  161.5 23.6 %collective-permute-start.53 = (bf16[32,2816]{1,0:T(8,128)(2,1)S(1)}, bf16[32,2816]{1,0:T(8,128)(2,1)S(1)}, u32[]{:S(2)}, u32[]{:S(2)}) collective-permute-start(bf16[32,2816]{1,0:T(8,128)(2,1)S(1)} %collective-permute-done.52), channel_id=1, source_target_pairs={{0,8},{1,9},{2,10},{3,11},{4,12},{5,13},{6,14},{7,15},{8,16},{9,17... | collective-permute-start | bytes 540680 | tf_op jit(solution)/shard_map/ppermute | solution.py:37
  167.2 30.1 %collective-permute-start.62 = (bf16[32,2816]{1,0:T(8,128)(2,1)S(1)}, bf16[32,2816]{1,0:T(8,128)(2,1)S(1)}, u32[]{:S(2)}, u32[]{:S(2)}) collective-permute-start(bf16[32,2816]{1,0:T(8,128)(2,1)S(1)} %collective-permute-done.61), channel_id=1, source_target_pairs={{0,8},{1,9},{2,10},{3,11},{4,12},{5,13},{6,14},{7,15},{8,16},{9,17... | collective-permute-start | bytes 540680 | tf_op jit(solution)/shard_map/ppermute | solution.py:37
  171.1 38.2 %collective-permute-start.65 = (bf16[32,2816]{1,0:T(8,128)(2,1)S(1)}, bf16[32,2816]{1,0:T(8,128)(2,1)S(1)}, u32[]{:S(2)}, u32[]{:S(2)}) collective-permute-start(bf16[32,2816]{1,0:T(8,128)(2,1)S(1)} %collective-permute-done.64), channel_id=1, source_target_pairs={{8,0},{9,1},{10,2},{11,3},{12,4},{13,5},{14,6},{15,7},{16,8},{17,9... | collective-permute-start | bytes 540680 | tf_op jit(solution)/shard_map/ppermute | solution.py:37
  172.4 37.5 %collective-permute-start.56 = (bf16[32,2816]{1,0:T(8,128)(2,1)S(1)}, bf16[32,2816]{1,0:T(8,128)(2,1)S(1)}, u32[]{:S(2)}, u32[]{:S(2)}) collective-permute-start(bf16[32,2816]{1,0:T(8,128)(2,1)S(1)} %collective-permute-done.55), channel_id=1, source_target_pairs={{8,0},{9,1},{10,2},{11,3},{12,4},{13,5},{14,6},{15,7},{16,8},{17,9... | collective-permute-start | bytes 540680 | tf_op jit(solution)/shard_map/ppermute | solution.py:37
  185.1 34.1 %collective-permute-start.12 = (bf16[2,2,32,1024]{3,2,1,0:T(8,128)(2,1)S(1)}, bf16[2,2,32,1024]{3,2,1,0:T(8,128)(2,1)S(1)}, u32[]{:S(2)}, u32[]{:S(2)}) collective-permute-start(bf16[2,2,32,1024]{3,2,1,0:T(8,128)(2,1)S(1)} %pad_maximum_fusion.25), channel_id=1, source_target_pairs={{0,8},{1,9},{2,10},{3,11},{4,12},{5,13},{6,14},{7,15},{8,16},{9,17... | collective-permute-start | bytes 786440 | tf_op jit(solution)/shard_map/ppermute | solution.py:37
  197.2 33.7 %collective-permute-start.15 = (bf16[2,2,32,1024]{3,2,1,0:T(8,128)(2,1)S(1)}, bf16[2,2,32,1024]{3,2,1,0:T(8,128)(2,1)S(1)}, u32[]{:S(2)}, u32[]{:S(2)}) collective-permute-start(bf16[2,2,32,1024]{3,2,1,0:T(8,128)(2,1)S(1)} %pad_maximum_fusion.25), channel_id=1, source_target_pairs={{8,0},{9,1},{10,2},{11,3},{12,4},{13,5},{14,6},{15,7},{16,8},{17,9... | collective-permute-start | bytes 786440 | tf_op jit(solution)/shard_map/ppermute | solution.py:37
  207.7 23.5 %collective-permute-start.76 = (bf16[4,88,512]{2,1,0:T(8,128)(2,1)S(1)}, bf16[4,88,512]{2,1,0:T(8,128)(2,1)S(1)}, u32[]{:S(2)}, u32[]{:S(2)}) collective-permute-start(bf16[4,88,512]{2,1,0:T(8,128)(2,1)S(1)} %constant_dynamic-slice_fusion.32), channel_id=1, source_target_pairs={{0,2},{1,3},{2,0},{3,1},{4,6},{5,7},{6,4},{7,5},{8,10},{9,11},{10,... | collective-permute-start | bytes 1081352 | tf_op jit(solution)/shard_map/ppermute | solution.py:42
  209.3 23.3 %collective-permute-start.85 = (bf16[4,88,512]{2,1,0:T(8,128)(2,1)S(1)}, bf16[4,88,512]{2,1,0:T(8,128)(2,1)S(1)}, u32[]{:S(2)}, u32[]{:S(2)}) collective-permute-start(bf16[4,88,512]{2,1,0:T(8,128)(2,1)S(1)} %constant_dynamic-slice_fusion.31), channel_id=1, source_target_pairs={{0,4},{1,5},{2,6},{3,7},{4,0},{5,1},{6,2},{7,3},{8,12},{9,13},{10,... | collective-permute-start | bytes 1081352 | tf_op jit(solution)/shard_map/ppermute | solution.py:42
  219.1 26.0 %collective-permute-start.41 = (bf16[4,2,32,1024]{3,2,1,0:T(8,128)(2,1)S(1)}, bf16[4,2,32,1024]{3,2,1,0:T(8,128)(2,1)S(1)}, u32[]{:S(2)}, u32[]{:S(2)}) collective-permute-start(bf16[4,2,32,1024]{3,2,1,0:T(8,128)(2,1)S(1)} %constant_dynamic-slice_fusion.36), channel_id=1, source_target_pairs={{0,2},{1,3},{2,0},{3,1},{4,6},{5,7},{6,4},{7,5},{8,10},{9,11},{10,... | collective-permute-start | bytes 1572872 | tf_op jit(solution)/shard_map/ppermute | solution.py:42
  232.6 24.7 %collective-permute-start.8 = (bf16[4,2,32,1024]{3,2,1,0:T(8,128)(2,1)S(1)}, bf16[4,2,32,1024]{3,2,1,0:T(8,128)(2,1)S(1)}, u32[]{:S(2)}, u32[]{:S(2)}) collective-permute-start(bf16[4,2,32,1024]{3,2,1,0:T(8,128)(2,1)S(1)} %pad_maximum_fusion.21), channel_id=1, source_target_pairs={{0,4},{1,5},{2,6},{3,7},{4,0},{5,1},{6,2},{7,3},{8,12},{9,13},{10,... | collective-permute-start | bytes 1572872 | tf_op jit(solution)/shard_map/ppermute | solution.py:42
  243.3 14.9 %collective-permute-start.58 = (bf16[4,32,2816]{2,1,0:T(8,128)(2,1)S(1)}, bf16[4,32,2816]{2,1,0:T(8,128)(2,1)S(1)}, u32[]{:S(2)}, u32[]{:S(2)}) collective-permute-start(bf16[4,32,2816]{2,1,0:T(8,128)(2,1)S(1)} %constant_dynamic-slice_fusion.34), channel_id=1, source_target_pairs={{0,2},{1,3},{2,0},{3,1},{4,6},{5,7},{6,4},{7,5},{8,10},{9,11},{10,... | collective-permute-start | bytes 2162696 | tf_op jit(solution)/shard_map/ppermute | solution.py:42
  245.1 16.8 %collective-permute-start.77 = (bf16[4,2,88,512]{3,2,1,0:T(8,128)(2,1)S(1)}, bf16[4,2,88,512]{3,2,1,0:T(8,128)(2,1)S(1)}, u32[]{:S(2)}, u32[]{:S(2)}) collective-permute-start(bf16[4,2,88,512]{3,2,1,0:T(8,128)(2,1)S(1)} %pad_maximum_fusion.18), channel_id=1, source_target_pairs={{0,4},{1,5},{2,6},{3,7},{4,0},{5,1},{6,2},{7,3},{8,12},{9,13},{10,... | collective-permute-start | bytes 2162696 | tf_op jit(solution)/shard_map/ppermute | solution.py:42
  258.2 83.2 %collective-permute-start.51 = (bf16[4,2,2,32,1024]{4,3,2,1,0:T(8,128)(2,1)}, bf16[4,2,2,32,1024]{4,3,2,1,0:T(8,128)(2,1)}, u32[]{:S(2)}, u32[]{:S(2)}) collective-permute-start(bf16[4,2,2,32,1024]{4,3,2,1,0:T(8,128)(2,1)} %pad_maximum_fusion.17), channel_id=1, source_target_pairs={{0,1},{1,0},{2,3},{3,2},{4,5},{5,4},{6,7},{7,6},{8,9},{9,8},{10,11... | collective-permute-start | bytes 3145736 | tf_op jit(solution)/shard_map/ppermute | solution.py:42
  265.6 205.1 %collective-permute-start.68 = (bf16[4,2,32,2816]{3,2,1,0:T(8,128)(2,1)}, bf16[4,2,32,2816]{3,2,1,0:T(8,128)(2,1)}, u32[]{:S(2)}, u32[]{:S(2)}) collective-permute-start(bf16[4,2,32,2816]{3,2,1,0:T(8,128)(2,1)} %pad_maximum_fusion.12), channel_id=1, source_target_pairs={{0,2},{1,3},{2,0},{3,1},{4,6},{5,7},{6,4},{7,5},{8,10},{9,11},{10,... | collective-permute-start | bytes 4325384 | tf_op jit(solution)/shard_map/ppermute | solution.py:42
  269.8 203.5 %collective-permute-start.59 = (bf16[4,2,32,2816]{3,2,1,0:T(8,128)(2,1)}, bf16[4,2,32,2816]{3,2,1,0:T(8,128)(2,1)}, u32[]{:S(2)}, u32[]{:S(2)}) collective-permute-start(bf16[4,2,32,2816]{3,2,1,0:T(8,128)(2,1)} %pad_maximum_fusion.11), channel_id=1, source_target_pairs={{0,4},{1,5},{2,6},{3,7},{4,0},{5,1},{6,2},{7,3},{8,12},{9,13},{10,... | collective-permute-start | bytes 4325384 | tf_op jit(solution)/shard_map/ppermute | solution.py:42
  270.5 207.2 %collective-permute-start.78 = (bf16[4,2,2,88,512]{4,3,2,1,0:T(8,128)(2,1)}, bf16[4,2,2,88,512]{4,3,2,1,0:T(8,128)(2,1)}, u32[]{:S(2)}, u32[]{:S(2)}) collective-permute-start(bf16[4,2,2,88,512]{4,3,2,1,0:T(8,128)(2,1)} %pad_maximum_fusion.13), channel_id=1, source_target_pairs={{0,1},{1,0},{2,3},{3,2},{4,5},{5,4},{6,7},{7,6},{8,9},{9,8},{10,11... | collective-permute-start | bytes 4325384 | tf_op jit(solution)/shard_map/ppermute | solution.py:42
  273.8 205.8 %collective-permute-start.87 = (bf16[4,2,2,88,512]{4,3,2,1,0:T(8,128)(2,1)}, bf16[4,2,2,88,512]{4,3,2,1,0:T(8,128)(2,1)}, u32[]{:S(2)}, u32[]{:S(2)}) collective-permute-start(bf16[4,2,2,88,512]{4,3,2,1,0:T(8,128)(2,1)} %pad_maximum_fusion.14), channel_id=1, source_target_pairs={{0,1},{1,0},{2,3},{3,2},{4,5},{5,4},{6,7},{7,6},{8,9},{9,8},{10,11... | collective-permute-start | bytes 4325384 | tf_op jit(solution)/shard_map/ppermute | solution.py:42
  477.7 25.8 %collective-permute-start.60 = (bf16[4,2,2,32,2816]{4,3,2,1,0:T(8,128)(2,1)}, bf16[4,2,2,32,2816]{4,3,2,1,0:T(8,128)(2,1)}, u32[]{:S(2)}, u32[]{:S(2)}) collective-permute-start(bf16[4,2,2,32,2816]{4,3,2,1,0:T(8,128)(2,1)} %pad_maximum_fusion.2), channel_id=1, source_target_pairs={{0,1},{1,0},{2,3},{3,2},{4,5},{5,4},{6,7},{7,6},{8,9},{9,8},{10,11... | collective-permute-start | bytes 8650760 | tf_op jit(solution)/shard_map/ppermute | solution.py:42
  564.3 20.2 %collective-permute-start.88 = (bf16[144,256]{1,0:T(8,128)(2,1)}, bf16[144,256]{1,0:T(8,128)(2,1)}, u32[]{:S(2)}, u32[]{:S(2)}) collective-permute-start(bf16[144,256]{1,0:T(8,128)(2,1)} %get-tuple-element.1257), channel_id=1, source_target_pairs={{0,1},{1,0},{2,3},{3,2},{4,5},{5,4},{6,7},{7,6},{8,9},{9,8},{10,11... | collective-permute-start | bytes 221192 | tf_op jit(solution)/shard_map/ppermute | solution.py:42
  564.8 22.1 %collective-permute-start.89 = (bf16[144,256]{1,0:T(8,128)(2,1)}, bf16[144,256]{1,0:T(8,128)(2,1)}, u32[]{:S(2)}, u32[]{:S(2)}) collective-permute-start(bf16[144,256]{1,0:T(8,128)(2,1)} %get-tuple-element.1256), channel_id=1, source_target_pairs={{0,2},{1,3},{2,0},{3,1},{4,6},{5,7},{6,4},{7,5},{8,10},{9,11},{10,... | collective-permute-start | bytes 221192 | tf_op jit(solution)/shard_map/ppermute | solution.py:42
  565.6 23.1 %collective-permute-start.90 = (bf16[144,256]{1,0:T(8,128)(2,1)}, bf16[144,256]{1,0:T(8,128)(2,1)}, u32[]{:S(2)}, u32[]{:S(2)}) collective-permute-start(bf16[144,256]{1,0:T(8,128)(2,1)} %get-tuple-element.1255), channel_id=1, source_target_pairs={{0,3},{1,2},{2,1},{3,0},{4,7},{5,6},{6,5},{7,4},{8,11},{9,10},{10,... | collective-permute-start | bytes 221192 | tf_op jit(solution)/shard_map/ppermute | solution.py:42
  566.2 23.4 %collective-permute-start.91 = (bf16[144,256]{1,0:T(8,128)(2,1)}, bf16[144,256]{1,0:T(8,128)(2,1)}, u32[]{:S(2)}, u32[]{:S(2)}) collective-permute-start(bf16[144,256]{1,0:T(8,128)(2,1)} %get-tuple-element.1254), channel_id=1, source_target_pairs={{0,4},{1,5},{2,6},{3,7},{4,0},{5,1},{6,2},{7,3},{8,12},{9,13},{10,... | collective-permute-start | bytes 221192 | tf_op jit(solution)/shard_map/ppermute | solution.py:42
  566.9 23.6 %collective-permute-start.92 = (bf16[144,256]{1,0:T(8,128)(2,1)}, bf16[144,256]{1,0:T(8,128)(2,1)}, u32[]{:S(2)}, u32[]{:S(2)}) collective-permute-start(bf16[144,256]{1,0:T(8,128)(2,1)} %get-tuple-element.1253), channel_id=1, source_target_pairs={{0,5},{1,4},{2,7},{3,6},{4,1},{5,0},{6,3},{7,2},{8,13},{9,12},{10,... | collective-permute-start | bytes 221192 | tf_op jit(solution)/shard_map/ppermute | solution.py:42
  600.2 15.3 %collective-permute-start.96 = (bf16[128,256]{1,0:T(8,128)(2,1)S(1)}, bf16[128,256]{1,0:T(8,128)(2,1)S(1)}, u32[]{:S(2)}, u32[]{:S(2)}) collective-permute-start(bf16[128,256]{1,0:T(8,128)(2,1)S(1)} %get-tuple-element.1297), channel_id=1, source_target_pairs={{0,1},{1,0},{2,3},{3,2},{4,5},{5,4},{6,7},{7,6},{8,9},{9,8},{10,11... | collective-permute-start | bytes 196616 | tf_op jit(solution)/shard_map/ppermute | solution.py:42
  785.7 17.0 %collective-permute-start.112 = (f32[278,128]{1,0:T(8,128)S(1)}, f32[278,128]{1,0:T(8,128)S(1)}, u32[]{:S(2)}, u32[]{:S(2)}) collective-permute-start(f32[278,128]{1,0:T(8,128)S(1)} %add.1349), channel_id=1, source_target_pairs={{24,0},{25,1},{26,2},{27,3},{28,4},{29,5},{30,6},{31,7}} | collective-permute-start | bytes 427016 | tf_op jit(solution)/shard_map/ppermute | solution.py:37
  788.3 21.4 %collective-permute-start.111 = (f32[278,128]{1,0:T(8,128)S(1)}, f32[278,128]{1,0:T(8,128)S(1)}, u32[]{:S(2)}, u32[]{:S(2)}) collective-permute-start(f32[278,128]{1,0:T(8,128)S(1)} %add.1349), channel_id=1, source_target_pairs={{0,24},{1,25},{2,26},{3,27},{4,28},{5,29},{6,30},{7,31}} | collective-permute-start | bytes 427016 | tf_op jit(solution)/shard_map/ppermute | solution.py:37
  794.7 15.0 %collective-permute-start.110 = (f32[278,128]{1,0:T(8,128)S(1)}, f32[278,128]{1,0:T(8,128)S(1)}, u32[]{:S(2)}, u32[]{:S(2)}) collective-permute-start(f32[278,128]{1,0:T(8,128)S(1)} %add.1349), channel_id=1, source_target_pairs={{16,0},{17,1},{18,2},{19,3},{20,4},{21,5},{22,6},{23,7},{24,8},{25... | collective-permute-start | bytes 427016 | tf_op jit(solution)/shard_map/ppermute | solution.py:37
  810.2 205.6 %collective-permute-start.158 = (bf16[4,2,2,32,2816]{4,3,0,2,1:T(8,128)(2,1)}, bf16[4,2,2,32,2816]{4,3,0,2,1:T(8,128)(2,1)}, u32[]{:S(2)}, u32[]{:S(2)}) collective-permute-start(bf16[4,2,2,32,2816]{4,3,0,2,1:T(8,128)(2,1)} %bitcast.1413), channel_id=1, source_target_pairs={{0,1},{1,0},{2,3},{3,2},{4,5},{5,4},{6,7},{7,6},{8,9},{9,8},{10,11... | collective-permute-start | bytes 8650760 | tf_op jit(solution)/shard_map/ppermute | solution.py:42
  810.3 19.6 %collective-permute-start.176 = (bf16[4,2,2,88,512]{4,3,0,2,1:T(8,128)(2,1)}, bf16[4,2,2,88,512]{4,3,0,2,1:T(8,128)(2,1)}, u32[]{:S(2)}, u32[]{:S(2)}) collective-permute-start(bf16[4,2,2,88,512]{4,3,0,2,1:T(8,128)(2,1)} %bitcast.1417), channel_id=1, source_target_pairs={{0,1},{1,0},{2,3},{3,2},{4,5},{5,4},{6,7},{7,6},{8,9},{9,8},{10,11... | collective-permute-start | bytes 4325384 | tf_op jit(solution)/shard_map/ppermute | solution.py:42
  810.7 14.7 %collective-permute-start.113 = (bf16[4,2,2,32,1024]{4,3,0,2,1:T(8,128)(2,1)}, bf16[4,2,2,32,1024]{4,3,0,2,1:T(8,128)(2,1)}, u32[]{:S(2)}, u32[]{:S(2)}) collective-permute-start(bf16[4,2,2,32,1024]{4,3,0,2,1:T(8,128)(2,1)} %bitcast.1421), channel_id=1, source_target_pairs={{0,1},{1,0},{2,3},{3,2},{4,5},{5,4},{6,7},{7,6},{8,9},{9,8},{10,11... | collective-permute-start | bytes 3145736 | tf_op jit(solution)/shard_map/ppermute | solution.py:42
  817.1 16.9 %collective-permute-start.167 = (bf16[4,2,2,88,512]{4,3,0,1,2:T(8,128)(2,1)S(1)}, bf16[4,2,2,88,512]{4,3,0,1,2:T(8,128)(2,1)S(1)}, u32[]{:S(2)}, u32[]{:S(2)}) collective-permute-start(bf16[4,2,2,88,512]{4,3,0,1,2:T(8,128)(2,1)S(1)} %bitcast.1650), channel_id=1, source_target_pairs={{0,1},{1,0},{2,3},{3,2},{4,5},{5,4},{6,7},{7,6},{8,9},{9,8},{10,11... | collective-permute-start | bytes 4325384 | tf_op jit(solution)/shard_map/ppermute | solution.py:42
  825.5 14.8 %collective-permute-start.132 = (bf16[4,2,32,1024]{3,2,1,0:T(8,128)(2,1)S(1)}, bf16[4,2,32,1024]{3,2,1,0:T(8,128)(2,1)S(1)}, u32[]{:S(2)}, u32[]{:S(2)}) collective-permute-start(bf16[4,2,32,1024]{3,2,1,0:T(8,128)(2,1)S(1)} %fusion.142), channel_id=1, source_target_pairs={{0,2},{1,3},{2,0},{3,1},{4,6},{5,7},{6,4},{7,5},{8,10},{9,11},{10,... | collective-permute-start | bytes 1572872 | tf_op jit(solution)/shard_map/ppermute | solution.py:42
  828.5 22.1 %collective-permute-start.141 = (bf16[4,2,32,1024]{3,2,0,1:T(8,128)(2,1)S(1)}, bf16[4,2,32,1024]{3,2,0,1:T(8,128)(2,1)S(1)}, u32[]{:S(2)}, u32[]{:S(2)}) collective-permute-start(bf16[4,2,32,1024]{3,2,0,1:T(8,128)(2,1)S(1)} %fusion.143), channel_id=1, source_target_pairs={{0,2},{1,3},{2,0},{3,1},{4,6},{5,7},{6,4},{7,5},{8,10},{9,11},{10,... | collective-permute-start | bytes 1572872 | tf_op jit(solution)/shard_map/ppermute | solution.py:42
  834.0 21.1 %collective-permute-start.126 = (bf16[2,2,32,1024]{3,2,1,0:T(8,128)(2,1)S(1)}, bf16[2,2,32,1024]{3,2,1,0:T(8,128)(2,1)S(1)}, u32[]{:S(2)}, u32[]{:S(2)}) collective-permute-start(bf16[2,2,32,1024]{3,2,1,0:T(8,128)(2,1)S(1)} %get-tuple-element.1184), channel_id=1, source_target_pairs={{8,0},{9,1},{10,2},{11,3},{12,4},{13,5},{14,6},{15,7},{16,8},{17,9... | collective-permute-start | bytes 786440 | tf_op jit(solution)/shard_map/ppermute | solution.py:37
  837.2 21.2 %collective-permute-start.114 = (bf16[4,2,32,1024]{3,2,0,1:T(8,128)(2,1)S(1)}, bf16[4,2,32,1024]{3,2,0,1:T(8,128)(2,1)S(1)}, u32[]{:S(2)}, u32[]{:S(2)}) collective-permute-start(bf16[4,2,32,1024]{3,2,0,1:T(8,128)(2,1)S(1)} %fusion.141), channel_id=1, source_target_pairs={{0,4},{1,5},{2,6},{3,7},{4,0},{5,1},{6,2},{7,3},{8,12},{9,13},{10,... | collective-permute-start | bytes 1572872 | tf_op jit(solution)/shard_map/ppermute | solution.py:42
  840.2 16.7 %collective-permute-start.124 = (bf16[2,2,32,1024]{3,2,1,0:T(8,128)(2,1)S(1)}, bf16[2,2,32,1024]{3,2,1,0:T(8,128)(2,1)S(1)}, u32[]{:S(2)}, u32[]{:S(2)}) collective-permute-start(bf16[2,2,32,1024]{3,2,1,0:T(8,128)(2,1)S(1)} %fusion.146), channel_id=1, source_target_pairs={{0,8},{1,9},{2,10},{3,11},{4,12},{5,13},{6,14},{7,15},{8,16},{9,17... | collective-permute-start | bytes 786440 | tf_op jit(solution)/shard_map/ppermute | solution.py:37
  855.1 164.8 %collective-permute-start.149 = (bf16[4,2,2,32,2816]{4,3,0,1,2:T(8,128)(2,1)S(1)}, bf16[4,2,2,32,2816]{4,3,0,1,2:T(8,128)(2,1)S(1)}, u32[]{:S(2)}, u32[]{:S(2)}) collective-permute-start(bf16[4,2,2,32,2816]{4,3,0,1,2:T(8,128)(2,1)S(1)} %bitcast.1623), channel_id=1, source_target_pairs={{0,1},{1,0},{2,3},{3,2},{4,5},{5,4},{6,7},{7,6},{8,9},{9,8},{10,11... | collective-permute-start | bytes 8650760 | tf_op jit(solution)/shard_map/ppermute | solution.py:42
  855.1 95.4 %collective-permute-start.177 = (bf16[4,2,88,512]{3,2,0,1:T(8,128)(2,1)S(1)}, bf16[4,2,88,512]{3,2,0,1:T(8,128)(2,1)S(1)}, u32[]{:S(2)}, u32[]{:S(2)}) collective-permute-start(bf16[4,2,88,512]{3,2,0,1:T(8,128)(2,1)S(1)} %fusion.138), channel_id=1, source_target_pairs={{0,4},{1,5},{2,6},{3,7},{4,0},{5,1},{6,2},{7,3},{8,12},{9,13},{10,... | collective-permute-start | bytes 2162696 | tf_op jit(solution)/shard_map/ppermute | solution.py:42
  856.9 33.1 %collective-permute-start.136 = (bf16[2,32,1024]{2,1,0:T(8,128)(2,1)S(1)}, bf16[2,32,1024]{2,1,0:T(8,128)(2,1)S(1)}, u32[]{:S(2)}, u32[]{:S(2)}) collective-permute-start(bf16[2,32,1024]{2,1,0:T(8,128)(2,1)S(1)} %get-tuple-element.1216), channel_id=1, source_target_pairs={{8,0},{9,1},{10,2},{11,3},{12,4},{13,5},{14,6},{15,7},{16,8},{17,9... | collective-permute-start | bytes 393224 | tf_op jit(solution)/shard_map/ppermute | solution.py:37
  858.4 21.0 %collective-permute-start.142 = (bf16[4,32,1024]{2,1,0:T(8,128)(2,1)S(1)}, bf16[4,32,1024]{2,1,0:T(8,128)(2,1)S(1)}, u32[]{:S(2)}, u32[]{:S(2)}) collective-permute-start(bf16[4,32,1024]{2,1,0:T(8,128)(2,1)S(1)} %fusion.173), channel_id=1, source_target_pairs={{0,4},{1,5},{2,6},{3,7},{4,0},{5,1},{6,2},{7,3},{8,12},{9,13},{10,... | collective-permute-start | bytes 786440 | tf_op jit(solution)/shard_map/ppermute | solution.py:42
  896.9 17.2 %collective-permute-start.115 = (bf16[4,32,1024]{2,1,0:T(8,128)(2,1)S(1)}, bf16[4,32,1024]{2,1,0:T(8,128)(2,1)S(1)}, u32[]{:S(2)}, u32[]{:S(2)}) collective-permute-start(bf16[4,32,1024]{2,1,0:T(8,128)(2,1)S(1)} %fusion.170), channel_id=1, source_target_pairs={{0,2},{1,3},{2,0},{3,1},{4,6},{5,7},{6,4},{7,5},{8,10},{9,11},{10,... | collective-permute-start | bytes 786440 | tf_op jit(solution)/shard_map/ppermute | solution.py:42
  930.7 21.4 %collective-permute-start.168 = (bf16[4,2,88,512]{3,2,0,1:T(8,128)(2,1)S(1)}, bf16[4,2,88,512]{3,2,0,1:T(8,128)(2,1)S(1)}, u32[]{:S(2)}, u32[]{:S(2)}) collective-permute-start(bf16[4,2,88,512]{3,2,0,1:T(8,128)(2,1)S(1)} %fusion.137), channel_id=1, source_target_pairs={{0,2},{1,3},{2,0},{3,1},{4,6},{5,7},{6,4},{7,5},{8,10},{9,11},{10,... | collective-permute-start | bytes 2162696 | tf_op jit(solution)/shard_map/ppermute | solution.py:42
  946.1 21.1 %collective-permute-start.125 = (bf16[2,2,32,1024]{3,2,1,0:T(8,128)(2,1)S(1)}, bf16[2,2,32,1024]{3,2,1,0:T(8,128)(2,1)S(1)}, u32[]{:S(2)}, u32[]{:S(2)}) collective-permute-start(bf16[2,2,32,1024]{3,2,1,0:T(8,128)(2,1)S(1)} %get-tuple-element.1181), channel_id=1, source_target_pairs={{0,8},{1,9},{2,10},{3,11},{4,12},{5,13},{6,14},{7,15},{8,16},{9,17... | collective-permute-start | bytes 786440 | tf_op jit(solution)/shard_map/ppermute | solution.py:37
  965.9 16.4 %collective-permute-start.178 = (bf16[4,88,512]{2,1,0:T(8,128)(2,1)S(1)}, bf16[4,88,512]{2,1,0:T(8,128)(2,1)S(1)}, u32[]{:S(2)}, u32[]{:S(2)}) collective-permute-start(bf16[4,88,512]{2,1,0:T(8,128)(2,1)S(1)} %fusion.157), channel_id=1, source_target_pairs={{0,2},{1,3},{2,0},{3,1},{4,6},{5,7},{6,4},{7,5},{8,10},{9,11},{10,... | collective-permute-start | bytes 1081352 | tf_op jit(solution)/shard_map/ppermute | solution.py:42
  1003.4 19.1 %collective-permute-start.181 = (bf16[88,512]{1,0:T(8,128)(2,1)S(1)}, bf16[88,512]{1,0:T(8,128)(2,1)S(1)}, u32[]{:S(2)}, u32[]{:S(2)}) collective-permute-start(bf16[88,512]{1,0:T(8,128)(2,1)S(1)} %get-tuple-element.1227), channel_id=1, source_target_pairs={{0,8},{1,9},{2,10},{3,11},{4,12},{5,13},{6,14},{7,15},{8,16},{9,17... | collective-permute-start | bytes 270344 | tf_op jit(solution)/shard_map/ppermute | solution.py:37
  1019.9 26.8 %collective-permute-start.159 = (bf16[4,2,32,2816]{3,2,0,1:T(8,128)(2,1)S(1)}, bf16[4,2,32,2816]{3,2,0,1:T(8,128)(2,1)S(1)}, u32[]{:S(2)}, u32[]{:S(2)}) collective-permute-start(bf16[4,2,32,2816]{3,2,0,1:T(8,128)(2,1)S(1)} %fusion.117), channel_id=1, source_target_pairs={{0,4},{1,5},{2,6},{3,7},{4,0},{5,1},{6,2},{7,3},{8,12},{9,13},{10,... | collective-permute-start | bytes 4325384 | tf_op jit(solution)/shard_map/ppermute | solution.py:42
  1022.6 25.6 %collective-permute-start.150 = (bf16[4,2,32,2816]{3,2,0,1:T(8,128)(2,1)S(1)}, bf16[4,2,32,2816]{3,2,0,1:T(8,128)(2,1)S(1)}, u32[]{:S(2)}, u32[]{:S(2)}) collective-permute-start(bf16[4,2,32,2816]{3,2,0,1:T(8,128)(2,1)S(1)} %fusion.116), channel_id=1, source_target_pairs={{0,2},{1,3},{2,0},{3,1},{4,6},{5,7},{6,4},{7,5},{8,10},{9,11},{10,... | collective-permute-start | bytes 4325384 | tf_op jit(solution)/shard_map/ppermute | solution.py:42
  1048.5 16.3 %collective-permute-start.151 = (bf16[4,32,2816]{2,1,0:T(8,128)(2,1)S(1)}, bf16[4,32,2816]{2,1,0:T(8,128)(2,1)S(1)}, u32[]{:S(2)}, u32[]{:S(2)}) collective-permute-start(bf16[4,32,2816]{2,1,0:T(8,128)(2,1)S(1)} %fusion.135), channel_id=1, source_target_pairs={{0,4},{1,5},{2,6},{3,7},{4,0},{5,1},{6,2},{7,3},{8,12},{9,13},{10,... | collective-permute-start | bytes 2162696 | tf_op jit(solution)/shard_map/ppermute | solution.py:42
  1063.6 15.7 %collective-permute-start.164 = (bf16[32,2816]{1,0:T(8,128)(2,1)S(1)}, bf16[32,2816]{1,0:T(8,128)(2,1)S(1)}, u32[]{:S(2)}, u32[]{:S(2)}) collective-permute-start(bf16[32,2816]{1,0:T(8,128)(2,1)S(1)} %get-tuple-element.1204), channel_id=1, source_target_pairs={{8,0},{9,1},{10,2},{11,3},{12,4},{13,5},{14,6},{15,7},{16,8},{17,9... | collective-permute-start | bytes 540680 | tf_op jit(solution)/shard_map/ppermute | solution.py:37
  1069.6 15.6 %collective-permute-start.155 = (bf16[32,2816]{1,0:T(8,128)(2,1)S(1)}, bf16[32,2816]{1,0:T(8,128)(2,1)S(1)}, u32[]{:S(2)}, u32[]{:S(2)}) collective-permute-start(bf16[32,2816]{1,0:T(8,128)(2,1)S(1)} %get-tuple-element.1200), channel_id=1, source_target_pairs={{8,0},{9,1},{10,2},{11,3},{12,4},{13,5},{14,6},{15,7},{16,8},{17,9... | collective-permute-start | bytes 540680 | tf_op jit(solution)/shard_map/ppermute | solution.py:37
  (277 other events, 3718.0 us)

commit v2 on v1

v2 whole, which is shorter than its diff:
```python
import jax
import jax.numpy as jnp
from jax import lax
from jax.experimental import pallas as pl
from jax.experimental.pallas import tpu as pltpu
from jax.sharding import PartitionSpec as P

HEADS = 4
DK = 128
DV = 256
FF = 2816
WIDE = 128
CONV = 4


epsilon = 1e-06
gate_scale = 16.0
highest = lax.Precision.HIGHEST


GROUP = 8
HALO = 8
EXTRA = 16


def chip_axes():
    count = lax.axis_size("seq")
    sides = {16: (4, 2, 2), 64: (4, 4, 4)}.get(count // 2, (count // 2, 1, 1))
    return (
        (sides[0], 2 * sides[1] * sides[2]),
        (sides[1], 2 * sides[2]),
        (sides[2], 2),
        (2, 1),
    )


def swapped(array, mask):
    count = lax.axis_size("seq")
    return lax.ppermute(array, "seq", [(i, i ^ mask) for i in range(count)])


def shifted(array, by):
    count = lax.axis_size("seq")
    pairs = [(i, i + by) for i in range(count) if 0 <= i + by < count]
    return lax.ppermute(array, "seq", pairs)


def spread(block, axis):
    size, stride = axis
    return [block] + [swapped(block, step * stride) for step in range(1, size)]


def takes(micros):
    return pl.CostEstimate(flops=int(micros * 1e9), bytes_accessed=0, transcendentals=0)


def coordinates():
    mine = lax.axis_index("seq")
    return jnp.stack([(mine // stride) % size for size, stride in chip_axes()]).astype(jnp.int32)


def placed_blocks(pieces, one, two, cuts):
    axes = chip_axes()
    sizes = tuple(size for size, _ in axes)
    depth, sides, mine = sizes[0], sizes[one], coordinates()
    rows, columns = pieces[0].shape[2:]

    def target(step, side, me):
        spot = [0, 0, 0, 0]
        spot[one] = jnp.bitwise_xor(side, me[one])
        spot[two] = jnp.bitwise_xor(step // sizes[3], me[two])
        spot[3] = jnp.bitwise_xor(step % sizes[3], me[3])
        return tuple(spot) + (0, 0)

    def source(which):
        def index(step, side, me):
            before = jnp.where(step < which, 0, sides - 1)
            return (jnp.where(step == which, side, before), 0, 0, 0)

        return index

    def kernel(me, *refs):
        sources, outs = refs[: len(pieces)], refs[len(pieces) :]
        step = pl.program_id(0)
        for which, piece in enumerate(sources):

            @pl.when(step == which)
            def _():
                for level in range(depth):
                    block, start = piece[0, level], 0
                    for out, cut in zip(outs, cuts):
                        out[jnp.bitwise_xor(me[0], level), 0, 0, 0] = block[start : start + cut]
                        start += cut

    found = pl.pallas_call(
        kernel,
        out_shape=[jax.ShapeDtypeStruct(sizes + (cut, columns), pieces[0].dtype) for cut in cuts],
        grid_spec=pltpu.PrefetchScalarGridSpec(
            num_scalar_prefetch=1,
            grid=(len(pieces), sides),
            in_specs=[
                pl.BlockSpec((1, depth, rows, columns), source(which))
                for which in range(len(pieces))
            ],
            out_specs=[pl.BlockSpec((depth, 1, 1, 1, cut, columns), target) for cut in cuts],
        ),
        compiler_params=pltpu.CompilerParams(vmem_limit_bytes=40 * 2**20),
        cost_estimate=takes(1.0 + rows * columns * 5e-5),
    )(mine, *pieces)
    return [array.reshape(-1, columns) for array in found]


def together(*values):
    return lax.optimization_barrier(values)


def gather_all(groups):
    axis_z, axis_y, axis_x, axis_c = chip_axes()
    near = []
    for shards in groups:
        shard = jnp.concatenate(shards, axis=0) if len(shards) > 1 else shards[0]
        if near:
            shard, near[-1][1] = together(shard, near[-1][1])
        near.append(spread(shard, axis_z))
    crossed, gathered = None, []
    for pieces in near:
        if crossed is not None:
            pieces, crossed = together(pieces, crossed)
            gathered.append(crossed)
        half = pieces[0].shape[1] // 2
        stacked = jnp.stack(pieces)
        sides = [
            jnp.stack(spread(stacked[..., :half], axis_x)),
            jnp.stack(spread(stacked[..., half:], axis_y)),
        ]
        crossed = [spread(sides[0], axis_y), spread(sides[1], axis_x)]
    gathered.append(crossed)
    full = []
    for shards, crossed in zip(groups, gathered):
        cuts, halves = [shard.shape[0] for shard in shards], []
        for pieces, one, two in zip(crossed, (2, 1), (1, 2)):
            pieces = [copy for piece in pieces for copy in spread(piece, axis_c)]
            halves.append(placed_blocks(pieces, one, two, cuts))
        full.extend(zip(*halves))
    return full


def grad_products(left, right_a, right_b):
    sizes = tuple(size for size, _ in chip_axes())
    strides = tuple(stride for _, stride in chip_axes())
    (tokens, features), columns = left.shape, right_a.shape[1]
    count, mine = lax.axis_size("seq"), coordinates()
    rows = features // count
    tile = 512 if columns % 512 == 0 and features <= 1024 else 256
    chunks = next(c for c in (4, 2, 1) if features // c % 128 == 0)
    chunk = features // chunks

    def kernel(me, left_ref, a_ref, b_ref, away_a, keep_a, away_b, keep_b, flipped):
        @pl.when(pl.program_id(0) == 0)
        def _():
            flipped[...] = left_ref[...].T

        even = me[3] == 0
        for right, away, keep, order in (
            (a_ref, away_a, keep_a, (2, 1, 0)),
            (b_ref, away_b, keep_b, (1, 2, 0)),
        ):
            for part in range(chunks):
                full = jnp.dot(
                    flipped[part * chunk : (part + 1) * chunk],
                    right[...],
                    preferred_element_type=jnp.float32,
                )
                for start in range(0, chunk, 2 * rows):
                    device = (part * chunk + start) // rows
                    spot = tuple(
                        jnp.bitwise_xor(device // strides[axis] % sizes[axis], me[axis])
                        for axis in order
                    )
                    low = full[start : start + rows]
                    high = full[start + rows : start + 2 * rows]
                    away[spot] = jnp.where(even, high, low).astype(jnp.bfloat16)
                    keep[spot] = jnp.where(even, low, high).astype(jnp.bfloat16)

    def result(one, two):
        shape = (sizes[one], sizes[two], sizes[0], rows)
        return (
            jax.ShapeDtypeStruct(shape + (columns,), jnp.bfloat16),
            pl.BlockSpec(shape + (tile,), lambda i, me: (0, 0, 0, 0, i)),
        )

    results = [result(2, 1), result(2, 1), result(1, 2), result(1, 2)]
    right_spec = pl.BlockSpec((tokens, tile), lambda i, me: (0, i))
    return pl.pallas_call(
        kernel,
        out_shape=[shape for shape, _ in results],
        grid_spec=pltpu.PrefetchScalarGridSpec(
            num_scalar_prefetch=1,
            grid=(columns // tile,),
            in_specs=[
                pl.BlockSpec((tokens, features), lambda i, me: (0, 0)),
                right_spec,
                right_spec,
            ],
            out_specs=[spec for _, spec in results],
            scratch_shapes=[pltpu.VMEM((features, tokens), jnp.bfloat16)],
        ),
        compiler_params=pltpu.CompilerParams(vmem_limit_bytes=48 * 2**20),
        cost_estimate=takes(1.5 + features * columns * 4.5e-6),
    )(mine, left, right_a, right_b)


def fold(block, axis):
    total = block[0].astype(jnp.float32)
    for step in range(1, axis[0]):
        part = swapped(block[step].astype(jnp.bfloat16), step * axis[1])
        total = total + part.astype(jnp.float32)
    return total


def cores_summed(left, right_a, right_b):
    away_a, keep_a, away_b, keep_b = grad_products(left, right_a, right_b)
    return [keep_a, swapped(away_a, 1), keep_b, swapped(away_b, 1)]


def sides_summed(products):
    axes = chip_axes()
    products = [[piece.astype(jnp.float32) for piece in pieces] for pieces in products]
    end_a = jnp.concatenate([pieces[0] + pieces[1] for pieces in products], axis=3)
    end_b = jnp.concatenate([pieces[2] + pieces[3] for pieces in products], axis=3)
    ends = [fold(end_a, axes[2]), fold(end_b, axes[1])]
    return [fold(ends[0], axes[1]), fold(ends[1], axes[2])]


def levels_summed(ends):
    return fold(jnp.concatenate(ends, axis=-1), chip_axes()[0])


def small_sum(value):
    for axis in chip_axes()[::-1]:
        value = sum(spread(value, axis))
    return value


def exchanged(pieces):
    shape = pieces.shape
    pieces = pieces.reshape((2, 2, 2) + shape[1:])
    kept, sent = pieces[:, :, 0], pieces[:, :, 1]
    pieces = jnp.stack([kept, swapped(sent, 1)], axis=2)
    kept, sent = pieces[:, 0], pieces[:, 1]
    pieces = jnp.stack([kept, swapped(sent, 2)], axis=1)
    return jnp.stack([pieces[0], swapped(pieces[1], 4)]).reshape(shape)


def column(row):
    square = jnp.broadcast_to(row, (DK, DK)).T
    return jnp.concatenate([square, square], axis=1)


def packed_rows(state, decay):
    high = decay.astype(jnp.bfloat16)
    low = (decay - high.astype(jnp.float32)).astype(jnp.bfloat16)
    tail = jnp.broadcast_to(jnp.concatenate([high, low], axis=1), (EXTRA, DV))
    return jnp.concatenate([state.astype(jnp.bfloat16), tail], axis=0)


def composed(place, got, backward, beyond=None):
    order = range(GROUP)[::-1] if backward else range(GROUP)

    def kernel(place_ref, got_ref, *refs):
        mine, out = place_ref[1], refs[-1]
        running = jnp.zeros((DK, DV), jnp.float32)
        reach = jnp.ones((DK, DV), jnp.float32)
        far = None if beyond is None else refs[0][...].astype(jnp.float32)
        for index in order:
            spot = jnp.bitwise_xor(mine, index)
            piece = got_ref[spot].astype(jnp.float32)
            if beyond is not None:
                out[spot] = (running + reach * far).astype(jnp.bfloat16)
            tail = piece[DK : DK + 1]
            kept = column(tail[:, :DK] + tail[:, DK:])
            running = kept * running + piece[:DK]
            reach = reach * kept
        if beyond is None:
            out[...] = running.astype(jnp.bfloat16)

    extra = () if beyond is None else (beyond,)
    shape = (DK, DV) if beyond is None else (GROUP, DK, DV)
    return pl.pallas_call(
        kernel,
        out_shape=jax.ShapeDtypeStruct(shape, jnp.bfloat16),
        in_specs=[pl.BlockSpec(memory_space=pltpu.SMEM)]
        + [pl.BlockSpec(memory_space=pltpu.VMEM)] * (1 + len(extra)),
        out_specs=pl.BlockSpec(memory_space=pltpu.VMEM),
        cost_estimate=takes(2),
    )(place, got, *extra)


def carried_over(place, pieces, backward):
    got = exchanged(pieces)
    total = composed(place, got, backward)
    beyond = shifted(total, -GROUP if backward else GROUP)
    return exchanged(composed(place, got, backward, beyond))


def split_dot(left, right, dims):
    dims = (dims, ((), ()))
    left_high, right_high = left.astype(jnp.bfloat16), right.astype(jnp.bfloat16)
    left_low = (left - left_high.astype(jnp.float32)).astype(jnp.bfloat16)
    right_low = (right - right_high.astype(jnp.float32)).astype(jnp.bfloat16)

    def one(a, b):
        return lax.dot_general(a, b, dims, preferred_element_type=jnp.float32)

    return one(left_high, right_high) + (one(left_high, right_low) + one(left_low, right_high))


def unit_dot(unit, value, dims):
    high = value.astype(jnp.bfloat16)
    rest = value - high.astype(jnp.float32)
    middle = rest.astype(jnp.bfloat16)
    low = (rest - middle.astype(jnp.float32)).astype(jnp.bfloat16)
    unit = unit.astype(jnp.bfloat16)
    return sum(
        lax.dot_general(unit, part, (dims, ((), ())), preferred_element_type=jnp.float32)
        for part in (low, middle, high)
    )


NN, NT, TN = ((1,), (0,)), ((1,), (1,)), ((0,), (0,))


def conv_in(piece, taps, pos, starts, block_len):
    wide = piece[0].astype(jnp.float32)
    total = taps[0:1, :] * wide[HALO:]
    for tap in range(1, CONV):
        usable = (pos - tap >= starts).astype(jnp.float32)
        total = total + taps[tap : tap + 1, :] * wide[HALO - tap : HALO - tap + block_len] * usable
    return wide, total


def decays(logit):
    return (jnp.minimum(logit, 0.0) - jnp.log1p(jnp.exp(-jnp.abs(logit)))) / gate_scale


class Span:
    def __init__(self, index, first, query, key, value, decay, starts, pos):
        rows = slice(index * WIDE, (index + 1) * WIDE)
        self.rows, first_pos = rows, first + index * WIDE
        self.query, self.key, self.value = query[rows], key[rows], value[rows]
        decay, starts, pos = decay[rows], starts[rows], pos[rows]
        t = lax.broadcasted_iota(jnp.int32, (WIDE, WIDE), 0)
        u = lax.broadcasted_iota(jnp.int32, (WIDE, WIDE), 1)
        self.lower = (u <= t).astype(jnp.float32)
        self.upper = (u >= t).astype(jnp.float32)
        self.allowed = (u <= t) & (u + first_pos >= starts)
        cum = unit_dot(self.lower, decay, NN)
        self.total = cum[WIDE - 1 :]
        middle = cum[WIDE // 2 - 1 : WIDE // 2]
        self.to_query, self.to_key = jnp.exp(cum - middle), jnp.exp(middle - cum)
        self.carried = (starts < first_pos).astype(jnp.float32)
        self.kept = (starts[WIDE - 1 :] < first_pos).astype(jnp.float32)
        self.from_start = jnp.exp(cum) * self.carried
        self.to_end = jnp.exp(self.total - cum) * (pos >= starts[WIDE - 1 :]).astype(jnp.float32)
        self.query_centred = self.query * self.to_query
        self.key_centred = self.key * self.to_key
        self.query_start = self.query * self.from_start
        self.key_end = self.key * self.to_end
        self.cum = cum
        ones = jnp.ones((WIDE, DV), jnp.float32)
        total_column = unit_dot_right(decay, ones)
        self.keep_column = jnp.exp(total_column) * self.kept

    def scores(self):
        raw = split_dot(self.query_centred, self.key_centred, NT)
        return jnp.where(self.allowed, raw, 0.0)

    def next_state(self, state):
        update = split_dot(self.key_end, self.value, TN)
        return update if state is None else state * self.keep_column + update


def unit_dot_right(value, unit):
    high = value.astype(jnp.bfloat16)
    rest = value - high.astype(jnp.float32)
    middle = rest.astype(jnp.bfloat16)
    low = (rest - middle.astype(jnp.float32)).astype(jnp.bfloat16)
    unit = unit.astype(jnp.bfloat16)
    return sum(
        lax.dot_general(part, unit, (TN, ((), ())), preferred_element_type=jnp.float32)
        for part in (low, middle, high)
    )


def activations(refs, starts, first, block_len):
    pos = first + lax.broadcasted_iota(jnp.int32, (block_len, 1), 0)
    found = []
    for piece, taps in refs:
        wide, total = conv_in(piece, taps, pos, starts, block_len)
        sig = jax.nn.sigmoid(total)
        found.append((wide, total, sig))
    return pos, found


def mixer_specs(block_len):
    wide = HALO + block_len
    return [
        pl.BlockSpec((1, wide, DK), lambda s, h, first: (s, 0, h)),
        pl.BlockSpec((1, wide, DK), lambda s, h, first: (s, 0, HEADS + h)),
        pl.BlockSpec((1, wide, DV), lambda s, h, first: (s, 0, HEADS + h)),
        pl.BlockSpec((CONV, DK), lambda s, h, first: (0, h)),
        pl.BlockSpec((CONV, DK), lambda s, h, first: (0, HEADS + h)),
        pl.BlockSpec((CONV, DV), lambda s, h, first: (0, HEADS + h)),
        pl.BlockSpec((1, block_len, DK), lambda s, h, first: (s, 0, h)),
        pl.BlockSpec((1, block_len, 1), lambda s, h, first: (s, 0, 0)),
    ]


def key_spec(block_len):
    return pl.BlockSpec((1, block_len, DK), lambda s, h, first: (s, 0, h))


def value_spec(block_len):
    return pl.BlockSpec((1, block_len, DV), lambda s, h, first: (s, 0, h))


def pair_spec(rows):
    return pl.BlockSpec(
        (1, rows, DV), lambda s, h, place: (jnp.bitwise_xor(place[1], s * HEADS + h), 0, 0)
    )


decay_spec = pl.BlockSpec((1, 1, 1, DK), lambda s, h, first: (s, h, 0, 0))


def launch(kernel, inputs, in_specs, outputs, out_specs, seq_count, micros):
    return pl.pallas_call(
        kernel,
        out_shape=[jax.ShapeDtypeStruct(shape, kind) for shape, kind in outputs],
        grid_spec=pltpu.PrefetchScalarGridSpec(
            num_scalar_prefetch=1,
            grid=(seq_count, HEADS),
            in_specs=in_specs,
            out_specs=out_specs,
        ),
        compiler_params=pltpu.CompilerParams(vmem_limit_bytes=40 * 2**20),
        cost_estimate=takes(micros),
    )(*inputs)


def mixer_forward(first, wide_mixed, conv_weight, logits, starts):
    seq_count, block_len = starts.shape[:2]

    def kernel(
        first_ref, q_ref, k_ref, v_ref, tq, tk, tv, logit_ref, start_ref, out, reach, state, decay
    ):
        first, starts = first_ref[0], start_ref[0]
        pos, found = activations(
            ((q_ref, tq), (k_ref, tk), (v_ref, tv)), starts, first, block_len
        )
        query, key, value = [total * sig for _, total, sig in found]
        query = query * DK ** (-0.5)
        log_decay = decays(logit_ref[0])
        running = None
        before = jnp.zeros((1, DK), jnp.float32)
        reach_in = (starts < first).astype(jnp.float32)
        for index in range(block_len // WIDE):
            span = Span(index, first, query, key, value, log_decay, starts, pos)
            result = split_dot(span.scores(), span.value, NN)
            if running is not None:
                result = result + split_dot(span.query_start, running, NN)
            out[0, span.rows] = result
            reach[0, span.rows] = span.query * jnp.exp(before + span.cum) * reach_in[span.rows]
            before = before + span.total
            running = span.next_state(running)
        block_decay = jnp.exp(before) * reach_in[block_len - 1 :]
        state[0] = packed_rows(running, block_decay)
        decay[0, 0] = block_decay

    return launch(
        kernel,
        (first, wide_mixed, wide_mixed, wide_mixed)
        + (conv_weight, conv_weight, conv_weight, logits, starts),
        mixer_specs(block_len),
        (
            ((seq_count, block_len, HEADS * DV), jnp.float32),
            ((seq_count, block_len, HEADS * DK), jnp.float32),
            ((GROUP, DK + EXTRA, DV), jnp.bfloat16),
            ((seq_count, HEADS, 1, DK), jnp.float32),
        ),
        [value_spec(block_len), key_spec(block_len), pair_spec(DK + EXTRA), decay_spec],
        seq_count,
        13,
    )


def mixer_output(first, local_out, reach, incoming, gates, head_gain):
    seq_count, block_len = reach.shape[:2]

    def kernel(first_ref, local, reach_ref, state, gate, gain, out, gated):
        result = local[0] + split_dot(reach_ref[0], state[0].astype(jnp.float32), NN)
        out[0] = result
        rms = lax.rsqrt(jnp.mean(result * result, axis=-1, keepdims=True) + epsilon)
        value = gate[0].astype(jnp.float32)
        gated[0] = (result * rms * gain[...] * (value * jax.nn.sigmoid(value))).astype(jnp.bfloat16)

    values = value_spec(block_len)
    return launch(
        kernel,
        (first, local_out, reach, incoming, gates, head_gain),
        [values, key_spec(block_len), pair_spec(DK), values]
        + [pl.BlockSpec((1, DV), lambda s, h, first: (0, 0))],
        (
            ((seq_count, block_len, HEADS * DV), jnp.float32),
            ((seq_count, block_len, HEADS * DV), jnp.bfloat16),
        ),
        [values, values],
        seq_count,
        4,
    )


def mixer_output_back(first, mixer_out, reach, gated_grad, gates, head_gain, decay):
    seq_count, block_len = reach.shape[:2]

    def kernel(
        first_ref,
        mixed,
        reach_ref,
        grad_ref,
        gate,
        gain,
        decay_ref,
        out_grad,
        gate_grad,
        term,
        gain_grad,
    ):
        result, grad = mixed[0], grad_ref[0]
        rms = lax.rsqrt(jnp.mean(result * result, axis=-1, keepdims=True) + epsilon)
        value = gate[0].astype(jnp.float32)
        sig = jax.nn.sigmoid(value)
        inner = grad * (value * sig)
        normed = result * rms
        gate_grad[0] = (
            grad * (normed * gain[...]) * sig * (1.0 + value * (1.0 - sig))
        ).astype(jnp.bfloat16)
        gain_grad[0, 0] = jnp.sum(inner * normed, axis=0, keepdims=True)
        scaled = inner * gain[...]
        grad_out = rms * (
            scaled - normed * rms * jnp.mean(scaled * result, axis=-1, keepdims=True)
        )
        out_grad[0] = grad_out
        term[0] = packed_rows(split_dot(reach_ref[0], grad_out, TN), decay_ref[0, 0])

    values = value_spec(block_len)
    return launch(
        kernel,
        (first, mixer_out, reach, gated_grad, gates, head_gain, decay),
        [values, key_spec(block_len), values, values]
        + [pl.BlockSpec((1, DV), lambda s, h, first: (0, 0)), decay_spec],
        (
            ((seq_count, block_len, HEADS * DV), jnp.float32),
            ((seq_count, block_len, HEADS * DV), jnp.bfloat16),
            ((GROUP, DK + EXTRA, DV), jnp.bfloat16),
            ((seq_count, HEADS, 1, DV), jnp.float32),
        ),
        [values, values, pair_spec(DK + EXTRA)]
        + [pl.BlockSpec((1, 1, 1, DV), lambda s, h, first: (s, h, 0, 0))],
        seq_count,
        5,
    )


def conv_back(grad, found, taps, pos, starts, block_len):
    wide, total, sig = found
    grad = grad * sig * (1.0 + total * (1.0 - sig))
    zeros = jnp.zeros((HALO, grad.shape[1]), jnp.float32)
    spread_grad, tap_grads = None, []
    for tap in range(CONV):
        masked = grad if tap == 0 else grad * (pos - tap >= starts).astype(jnp.float32)
        source = wide[HALO - tap : HALO - tap + block_len]
        tap_grads.append(jnp.sum(masked * source, axis=0, keepdims=True))
        padded = jnp.concatenate([zeros, masked * taps[tap : tap + 1, :], zeros], axis=0)
        part = padded[tap : tap + HALO + block_len]
        spread_grad = part if spread_grad is None else spread_grad + part
    return spread_grad, jnp.concatenate(tap_grads, axis=0)


def mixer_backward(first, wide_mixed, conv_weight, logits, starts, out_grad, incoming, outgoing):
    seq_count, block_len = starts.shape[:2]
    conv_width = wide_mixed.shape[2]
    wide_len = HALO + block_len

    def kernel(first_ref, q_ref, k_ref, v_ref, tq, tk, tv, logit_ref, start_ref, *refs):
        grad_ref, in_ref, end_ref, dq, dk, dv, wq, wk, wv, dlogit, bias = refs
        first, starts = first_ref[0], start_ref[0]
        taps = (tq, tk, tv)
        pos, found = activations(
            tuple(zip((q_ref, k_ref, v_ref), taps)), starts, first, block_len
        )
        query, key, value = [total * sig for _, total, sig in found]
        query = query * DK ** (-0.5)
        logit = logit_ref[0]
        log_decay = decays(logit)
        count = block_len // WIDE
        spans, states = [], [in_ref[0].astype(jnp.float32)]
        for index in range(count):
            span = Span(index, first, query, key, value, log_decay, starts, pos)
            spans.append(span)
            if index + 1 < count:
                states.append(span.next_state(states[-1]))
        later = end_ref[0].astype(jnp.float32)
        query_grads, key_grads, value_grads, decay_grads = [], [], [], []
        for index in range(count)[::-1]:
            span, state = spans[index], states[index]
            grad = grad_ref[0, span.rows]
            score_grad = jnp.where(span.allowed, split_dot(grad, span.value, NT), 0.0)
            query_grad = split_dot(score_grad, span.key_centred, NN) * span.to_query
            query_grad = query_grad + split_dot(grad, state, NT) * span.from_start
            end_grad = split_dot(span.value, later, NT)
            key_grad = split_dot(score_grad, span.query_centred, TN) * span.to_key
            key_grad = key_grad + end_grad * span.to_end
            value_grad = split_dot(span.scores(), grad, TN) + split_dot(span.key_end, later, NN)
            kept = unit_dot(jnp.ones((8, DV), jnp.float32), state * later, NT)[:1]
            total_grad = jnp.sum(end_grad * span.key_end, axis=0, keepdims=True)
            total_grad = total_grad + kept * jnp.exp(span.total) * span.kept
            cum_grad = span.query * query_grad - span.key * key_grad
            decay_grads.append(unit_dot(span.upper, cum_grad, NN) + total_grad)
            query_grads.append(query_grad)
            key_grads.append(key_grad)
            value_grads.append(value_grad)
            if index > 0:
                later = later * span.keep_column + split_dot(span.query_start, grad, TN)
        grads = [
            jnp.concatenate(parts[::-1], axis=0) for parts in (query_grads, key_grads, value_grads)
        ]
        grads[0] = grads[0] * DK ** (-0.5)
        for grad, piece, tap, out, tap_grad in zip(
            grads, found, taps, (dq, dk, dv), (wq, wk, wv)
        ):
            out[0], tap_grad[0] = conv_back(grad, piece, tap, pos, starts, block_len)
        decay_grad = jnp.concatenate(decay_grads[::-1], axis=0)
        decay_grad = jnp.where(starts < pos, decay_grad, 0.0)
        logit_grad = decay_grad / gate_scale * jax.nn.sigmoid(-logit)
        dlogit[0] = logit_grad
        bias[0, 0] = jnp.sum(logit_grad, axis=0, keepdims=True)

    wide_keys = pl.BlockSpec((1, wide_len, DK), lambda s, h, first: (s, 0, h))
    wide_values = pl.BlockSpec((1, wide_len, DV), lambda s, h, first: (s, 0, h))
    tap_keys = pl.BlockSpec((1, CONV, DK), lambda s, h, first: (s, 0, h))
    tap_values = pl.BlockSpec((1, CONV, DV), lambda s, h, first: (s, 0, h))
    keys, values = HEADS * DK, HEADS * DV
    return launch(
        kernel,
        (first, wide_mixed, wide_mixed, wide_mixed)
        + (conv_weight, conv_weight, conv_weight, logits, starts)
        + (out_grad, incoming, outgoing),
        mixer_specs(block_len) + [value_spec(block_len), pair_spec(DK), pair_spec(DK)],
        (
            ((seq_count, wide_len, keys), jnp.float32),
            ((seq_count, wide_len, keys), jnp.float32),
            ((seq_count, wide_len, values), jnp.float32),
            ((seq_count, CONV, keys), jnp.float32),
            ((seq_count, CONV, keys), jnp.float32),
            ((seq_count, CONV, values), jnp.float32),
            ((seq_count, block_len, keys), jnp.float32),
            ((seq_count, HEADS, 1, DK), jnp.float32),
        ),
        [wide_keys, wide_keys, wide_values, tap_keys, tap_keys, tap_values]
        + [key_spec(block_len), decay_spec],
        seq_count,
        24,
    )


def bf_dot(left, right):
    return jnp.dot(left, right, preferred_element_type=jnp.float32)


def feed_forward(hidden, out_grad, gain, w_gate, w_up, down_left, down_right):
    tokens, width = hidden.shape
    inner, tile = w_gate.shape[1], 256
    half = width // 2
    steps = inner // tile

    def kernel(hid, grad, gain_ref, wg, wu, wl, wr, *refs):
        out, back, back_low, normed, act, gate_back, up_back, gain_back, total, turned = refs
        step = pl.program_id(0)

        @pl.when(step == 0)
        def _():
            value = hid[...]
            rms = lax.rsqrt(jnp.mean(value * value, axis=-1, keepdims=True) + epsilon)
            normed[...] = (value * rms * gain_ref[...]).astype(jnp.bfloat16)
            total[...] = jnp.zeros_like(total)
            turned[...] = jnp.zeros_like(turned)

        source, low = normed[...], grad[...]
        gate, up = bf_dot(source, wg[...]), bf_dot(source, wu[...])
        inner_grad = nt_dot(low[:, :half], wl[...]) + nt_dot(low[:, half:], wr[...])
        sig = jax.nn.sigmoid(gate)
        silu = gate * sig
        active = (silu * up).astype(jnp.bfloat16)
        gate_grad = (inner_grad * up * sig * (1.0 + gate * (1.0 - sig))).astype(jnp.bfloat16)
        up_grad = (inner_grad * silu).astype(jnp.bfloat16)
        act[...], gate_back[...], up_back[...] = active, gate_grad, up_grad
        total[:, :half] += bf_dot(active, wl[...])
        total[:, half:] += bf_dot(active, wr[...])
        turned[...] += nt_dot(gate_grad, wg[...]) + nt_dot(up_grad, wu[...])

        @pl.when(step == steps - 1)
        def _():
            value, back_in = hid[...], turned[...]
            rms = lax.rsqrt(jnp.mean(value * value, axis=-1, keepdims=True) + epsilon)
            out[...] = value + total[...]
            gain_back[...] = jnp.sum(back_in * value * rms, axis=0, keepdims=True)
            result = grad[...].astype(jnp.float32) + rms_back(back_in, value, rms, gain_ref[...])
            back[...] = result
            back_low[...] = result.astype(jnp.bfloat16)

    def whole(rows, columns):
        return pl.BlockSpec((rows, columns), lambda i: (0, 0))

    across = pl.BlockSpec((width, tile), lambda i: (0, i))
    along = pl.BlockSpec((tile, half), lambda i: (i, 0))
    inner_spec = pl.BlockSpec((tokens, tile), lambda i: (0, i))
    inner_shape = jax.ShapeDtypeStruct((tokens, inner), jnp.bfloat16)
    return pl.pallas_call(
        kernel,
        out_shape=[
            jax.ShapeDtypeStruct((tokens, width), jnp.float32),
            jax.ShapeDtypeStruct((tokens, width), jnp.float32),
            jax.ShapeDtypeStruct((tokens, width), jnp.bfloat16),
            jax.ShapeDtypeStruct((tokens, width), jnp.bfloat16),
            inner_shape,
            inner_shape,
            inner_shape,
            jax.ShapeDtypeStruct((1, width), jnp.float32),
        ],
        grid=(steps,),
        in_specs=[whole(tokens, width), whole(tokens, width), whole(1, width)]
        + [across, across, along, along],
        out_specs=[whole(tokens, width)] * 4 + [inner_spec] * 3 + [whole(1, width)],
        scratch_shapes=[
            pltpu.VMEM((tokens, width), jnp.float32),
            pltpu.VMEM((tokens, width), jnp.float32),
        ],
        compiler_params=pltpu.CompilerParams(vmem_limit_bytes=52 * 2**20),
        cost_estimate=takes(28),
    )(hidden, out_grad, gain, w_gate, w_up, down_left, down_right)


def nt_dot(left, right):
    return lax.dot_general(left, right, (NT, ((), ())), preferred_element_type=jnp.float32)


def rms_back(grad_normed, source, inv_rms, gain_vec):
    scaled = grad_normed * gain_vec
    return inv_rms * (
        scaled - source * inv_rms * inv_rms * jnp.mean(scaled * source, axis=-1, keepdims=True)
    )


def local(
    inputs,
    doc_start,
    norm_gain,
    w_in,
    conv_weight,
    w_low,
    w_high,
    gate_bias,
    head_gain,
    w_out,
    ffn_gain,
    w_gate_up,
    w_down,
    out_grad,
):
    seq_count, block_len, model_width = inputs.shape
    row_count = seq_count * block_len
    key_width = HEADS * DK
    value_width = HEADS * DV
    conv_width = 2 * key_width + value_width
    block_start = lax.axis_index("seq") * block_len
    half = model_width // 2
    (
        (qk_full, v_full),
        (g_left, g_right),
        (out_left, out_right),
        (down_left, down_right),
        (gate_full, up_full),
    ) = gather_all([[w_in[:, :conv_width]], [w_in[:, conv_width:], w_out, w_down], [w_gate_up]])
    edge = shifted(inputs[:, block_len - HALO :, :], 1)
    wide = jnp.concatenate([edge, inputs], axis=1).astype(jnp.float32)
    wide_rms = lax.rsqrt(jnp.mean(wide * wide, axis=-1, keepdims=True) + epsilon)
    wide_normed = (wide * wide_rms * norm_gain).astype(jnp.bfloat16)
    layer_in = wide[:, HALO:].reshape(row_count, model_width)
    inv_rms = wide_rms[:, HALO:].reshape(row_count, 1)
    normed = wide_normed[:, HALO:].reshape(row_count, model_width)
    wide_rows = wide_normed.reshape(-1, model_width)
    wide_mixed = jnp.concatenate([bf_dot(wide_rows, qk_full), bf_dot(wide_rows, v_full)], axis=1)
    wide_mixed = wide_mixed.astype(jnp.bfloat16).reshape(seq_count, HALO + block_len, conv_width)
    gate_cols = jnp.concatenate([bf_dot(normed, g_left), bf_dot(normed, g_right)], axis=1)
    gate_cols = gate_cols.astype(jnp.bfloat16)
    lowrank = bf_dot(normed, w_low)
    gate_logit = (
        jnp.dot(lowrank, w_high, precision=highest, preferred_element_type=jnp.float32) + gate_bias
    )
    first = jnp.stack([block_start, lax.axis_index("seq") % GROUP]).astype(jnp.int32)
    starts = doc_start[:, :, None]
    logits = gate_logit.reshape(seq_count, block_len, key_width)
    gates = gate_cols.reshape(seq_count, block_len, value_width)
    gain_row = head_gain[None, :]
    local_out, reach, local_state, block_decay = mixer_forward(
        first, wide_mixed, conv_weight, logits, starts
    )
    incoming = carried_over(first, local_state, False)
    mixer_out, gated = mixer_output(first, local_out, reach, incoming, gates, gain_row)
    gated = gated.reshape(row_count, value_width)
    hidden_one = layer_in + jnp.concatenate(
        [bf_dot(gated, out_left), bf_dot(gated, out_right)], axis=1
    )
    out_rows_low = out_grad.reshape(row_count, model_width)
    (
        layer_out,
        hidden_grad,
        hidden_low,
        ffn_in,
        activation,
        gate_grad,
        up_grad,
        ffn_gain_row,
    ) = feed_forward(
        hidden_one, out_rows_low, ffn_gain[None, :], gate_full, up_full, down_left, down_right
    )
    ffn_gain_grad = ffn_gain_row[0]
    gate_up_terms = cores_summed(ffn_in, gate_grad, up_grad)
    down_terms = cores_summed(activation, out_rows_low[:, :half], out_rows_low[:, half:])
    out_terms = cores_summed(gated, hidden_low[:, :half], hidden_low[:, half:])
    gated_grad = nt_dot(hidden_low[:, :half], out_left) + nt_dot(hidden_low[:, half:], out_right)
    gated_grad = gated_grad.reshape(seq_count, block_len, value_width)
    mixer_grad, gate_vals_grad, state_term, head_gain_grad = mixer_output_back(
        first, mixer_out, reach, gated_grad, gates, gain_row, block_decay
    )
    gate_vals_grad = gate_vals_grad.reshape(row_count, value_width)
    head_gain_grad = jnp.sum(head_gain_grad, axis=(0, 1, 2))
    g_terms = cores_summed(normed, gate_vals_grad[:, :half], gate_vals_grad[:, half:])
    outgoing = carried_over(first, state_term, True)
    outgoing, gate_up_terms = together(outgoing, gate_up_terms)
    gate_up_terms = sides_summed([gate_up_terms])
    q_back, k_back, v_back, q_taps, k_taps, v_taps, logit_grad, gate_bias_grad = mixer_backward(
        first, wide_mixed, conv_weight, logits, starts, mixer_grad, incoming, outgoing
    )
    conv_weight_grad = jnp.sum(jnp.concatenate([q_taps, k_taps, v_taps], axis=-1), axis=0)
    padded_grad = jnp.concatenate([q_back, k_back, v_back], axis=-1)
    back_edge = shifted(padded_grad[:, :HALO].astype(jnp.bfloat16), -1).astype(jnp.float32)
    mixed_grad = padded_grad[:, HALO:] + jnp.pad(
        back_edge, ((0, 0), (block_len - HALO, 0), (0, 0))
    )
    mixed_grad = mixed_grad.reshape(row_count, conv_width).astype(jnp.bfloat16)
    qk_grad, v_grad = mixed_grad[:, : 2 * key_width], mixed_grad[:, 2 * key_width :]
    qk_grad, gate_up_terms, down_terms = together(qk_grad, gate_up_terms, down_terms)
    w_gate_up_grad = levels_summed(gate_up_terms)
    rest_terms = sides_summed([g_terms, out_terms, down_terms])
    qkv_terms = cores_summed(normed, qk_grad, v_grad)
    rest_terms, qkv_terms = together(rest_terms, qkv_terms)
    rest = levels_summed(rest_terms)
    qkv_grad = levels_summed(sides_summed([qkv_terms]))
    w_in_rows = w_in.shape[0]
    w_out_grad = rest[w_in_rows : 2 * w_in_rows]
    w_down_grad = rest[2 * w_in_rows :]
    w_in_grad = jnp.concatenate([qkv_grad, rest[:w_in_rows]], axis=1)
    logit_grad = logit_grad.reshape(row_count, key_width)
    gate_bias_grad = jnp.sum(gate_bias_grad, axis=0).reshape(-1)
    w_high_grad = jnp.dot(
        lowrank.T, logit_grad, precision=highest, preferred_element_type=jnp.float32
    )
    lowrank_grad = jnp.dot(
        logit_grad, w_high.T, precision=highest, preferred_element_type=jnp.float32
    ).astype(jnp.bfloat16)
    w_low_grad = jnp.dot(normed.T, lowrank_grad, preferred_element_type=jnp.float32)
    normed_grad = (
        bf_dot(qk_grad, qk_full.T)
        + bf_dot(v_grad, v_full.T)
        + nt_dot(gate_vals_grad[:, :half], g_left)
        + nt_dot(gate_vals_grad[:, half:], g_right)
        + bf_dot(lowrank_grad, w_low.T)
    )
    norm_gain_grad = jnp.sum(normed_grad * layer_in * inv_rms, axis=0)
    input_grad = hidden_grad + rms_back(normed_grad, layer_in, inv_rms, norm_gain)
    small = (
        norm_gain_grad,
        conv_weight_grad,
        w_low_grad,
        w_high_grad,
        gate_bias_grad,
        head_gain_grad,
        ffn_gain_grad,
    )
    summed = small_sum(jnp.concatenate([part.reshape(-1, 128) for part in small]))
    small_grads, start = [], 0
    for part in small:
        rows = part.size // 128
        small_grads.append(summed[start : start + rows].reshape(part.shape))
        start += rows
    return (
        layer_out.reshape(seq_count, block_len, model_width),
        input_grad.reshape(seq_count, block_len, model_width),
        small_grads[0],
        w_in_grad,
        small_grads[1],
        small_grads[2],
        small_grads[3],
        small_grads[4],
        small_grads[5],
        w_out_grad,
        small_grads[6],
        w_gate_up_grad,
        w_down_grad,
    )


def solution(mesh):
    placed = (
        P(None, "seq", None),
        P(None, "seq"),
        P(),
        P("seq", None),
        P(),
        P(),
        P(),
        P(),
        P(),
        P("seq", None),
        P(),
        P("seq", None),
        P("seq", None),
        P(None, "seq", None),
    )
    return jax.shard_map(
        local,
        mesh=mesh,
        in_specs=placed,
        out_specs=(
            P(None, "seq", None),
            P(None, "seq", None),
            P(),
            P("seq", None),
            P(),
            P(),
            P(),
            P(),
            P(),
            P("seq", None),
            P(),
            P("seq", None),
            P("seq", None),
        ),
        check_vma=False,
    )
```

time: 1120 us -> 632 us (0.56)
  starting transfers between devices: 359 us -> 104 us
  matrix products: 165 us -> 21 us
  Pallas kernels: 0 us -> 140 us
  local copies, waits for them, and re-layouts: 172 us -> 60.9 us
  other arithmetic: 148 us -> 50.7 us
    ppermute x102 -> x0, starting transfers between devices: 280 us -> none  [moved(): return lax.ppermute(array, 'seq', pairs)]
    pallas_call x0 -> x20, Pallas kernels: none -> 140 us  [the longest x4 48.2 us: launch(): pl.pallas_call(kernel, out_shape=[jax.ShapeDtypeStruct(shape, kind) for s...]
    ppermute x102 -> x0, waiting for transfers between devices: 116 us -> none  [moved(): return lax.ppermute(array, 'seq', pairs)]
    ppermute x79 -> x82, waiting for transfers between devices: 129 us -> 232 us  [swapped(): return lax.ppermute(array, 'seq', [(i, i ^ mask) for i in range(count)])]
    dot_general x66 -> x4, matrix products: 108 us -> 6.27 us  [nt_dot(): lax.dot_general(left, right, (NT, ((), ())), preferred_element_type=jnp.f...]
    dynamic_slice x50 -> x0, local copies, waits for them, and re-layouts: 41.9 us -> none  [the longest x14 21.6 us: pick(): return lax.dynamic_index_in_dim(block, index, at, False).astype(jnp.float32)]
    another operation x69 -> x22, other arithmetic: 49.1 us -> 7.6 us  [the longest x3 2.27 us: gather_all(): stacked = jnp.stack(pieces)]
    dot_general x18 -> x10, matrix products: 51.4 us -> 11.6 us  [bf_dot(): return jnp.dot(left, right, preferred_element_type=jnp.float32)]
  transfers between devices with their start and end apart: 185 -> 86, of which waited for: 71 -> 32; matrix products, arithmetic and copies ran while one was open for 24% -> 15% of each run, Pallas kernels for 0% -> 13%
where the time goes in v2:
time: 632 us; the launch traced here: 623 us
  waiting for transfers between devices  244 us (39%)
  Pallas kernels  140 us (22%)
  starting transfers between devices  104 us (16%)
  local copies, waits for them, and re-layouts  60.9 us (10%)
  other arithmetic  50.7 us (8%)
  matrix products  21 us (3%)
    ppermute x82, waiting for transfers between devices, swapped(): return lax.ppermute(array, 'seq', [(i, i ^ mask) for i in range(count)])  232 us
    ppermute x82, starting transfers between devices, swapped(): return lax.ppermute(array, 'seq', [(i, i ^ mask) for i in range(count)])  90.6 us
    pallas_call x4, Pallas kernels, launch(): pl.pallas_call(kernel, out_shape=[jax.ShapeDtypeStruct(shape, kind) for s...  48.2 us
    unnamed x213, local copies, waits for them, and re-layouts  38.5 us
    pallas_call x5, Pallas kernels, grad_products(): pl.pallas_call(kernel, out_shape=[shape for shape, _ in results], grid_sp...  33.1 us
    pallas_call x1, Pallas kernels, feed_forward(): pl.pallas_call(kernel, out_shape=[jax.ShapeDtypeStruct((tokens, width), j...  28.2 us
    pallas_call x6, Pallas kernels, placed_blocks(): pl.pallas_call(kernel, out_shape=[jax.ShapeDtypeStruct(sizes + (cut, colu...  22.4 us
    ppermute x4, starting transfers between devices, shifted(): return lax.ppermute(array, 'seq', pairs)  13.1 us
  transfers between devices with their start and end apart: 86, of which 32 were waited for; matrix products, arithmetic and copies ran while one was open for 15% of the time, Pallas kernels for 13%

profile of v2, /device:TPU:0, one launch (start us, length us, event | category | flops | bytes accessed | tf_op | source)
XLA Modules:
  0.0 623.3 jit_solution(11661635326556045593)
XLA Ops:
  1.6 3.1 collective-permute-start.1
  4.7 2.5 collective-permute-start.6
  9.1 5.3 collective-permute-done.6
  14.4 4.5 collective-permute-done.5
  22.2 4.4 collective-permute-done.9
  31.6 3.4 collective-permute-start.3
  35.0 4.7 collective-permute-start.4
  40.2 7.6 %collective-permute-done.2 = bf16[152,1024]{1,0:T(8,128)(2,1)} collective-permute-done((bf16[152,1024]{1,0:T(8,128)(2,1)S(1)}, bf16[152,1024]{1,0:T(8,128)(2,1)}, u32[]{:S(2)}, u32[]{:S(2)}) %collective-permute-start.2) | collective-permute-done | bytes 311328 | tf_op jit(solution)/shard_map/ppermute | solution.py:39
  47.8 8.9 %collective-permute-done.3 = bf16[152,1024]{1,0:T(8,128)(2,1)} collective-permute-done((bf16[152,1024]{1,0:T(8,128)(2,1)S(1)}, bf16[152,1024]{1,0:T(8,128)(2,1)}, u32[]{:S(2)}, u32[]{:S(2)}) %collective-permute-start.3) | collective-permute-done | bytes 311328 | tf_op jit(solution)/shard_map/ppermute | solution.py:39
  60.0 3.2 shard_map.237
  69.5 13.6 %shard_map.239 = (f32[2,256,1024]{2,1,0:T(8,128)S(1)}, f32[2,256,512]{2,1,0:T(8,128)S(1)}, bf16[8,144,256]{2,1,0:T(8,128)(2,1)S(1)}, f32[2,4,1,128]{3,2,1,0:T(1,128)S(1)}) custom-call(s32[2]{0:T(128)S(1)} %pad_add_fusion.first_ref.place_ref, bf16[2,264,2048]{2,1,0:T(8,128)(2,1)S(1)} %pad_maximum_fusion.2.q_ref.k_ref.v_ref, ...), custom_call_target="tpu_custom_call" | custom-call | flops 12999999488 | tf_op jit(solution)/shard_map/pallas_call | solution.py:437
  88.5 20.1 %collective-permute-done.16 = bf16[2,2,144,256]{3,2,1,0:T(8,128)(2,1)S(1)} collective-permute-done((bf16[2,2,144,256]{3,2,1,0:T(8,128)(2,1)S(1)}, bf16[2,2,144,256]{3,2,1,0:T(8,128)(2,1)S(1)}, u32[]{:S(2)}, u32[]{:S(2)}) %collective-permute-start.16) | collective-permute-done | bytes 294944 | tf_op jit(solution)/shard_map/ppermute | solution.py:39
  113.3 5.3 collective-permute-done.17
  121.5 9.1 %collective-permute-start.18 = (bf16[128,256]{1,0:T(8,128)(2,1)}, bf16[128,256]{1,0:T(8,128)(2,1)S(1)}, u32[]{:S(2)}, u32[]{:S(2)}) collective-permute-start(bf16[128,256]{1,0:T(8,128)(2,1)} %shard_map.240), channel_id=1, source_target_pairs={{0,8},{1,9},{2,10},{3,11},{4,12},{5,13},{6,14},{7,15},{8,16},{9,17... | collective-permute-start | bytes 196616 | tf_op jit(solution)/shard_map/ppermute | solution.py:45
  136.3 2.3 collective-permute-start.22
  141.1 13.8 %collective-permute-done.22 = bf16[32,5632]{1,0:T(8,128)(2,1)S(1)} collective-permute-done((bf16[32,5632]{1,0:T(8,128)(2,1)S(1)}, bf16[32,5632]{1,0:T(8,128)(2,1)S(1)}, u32[]{:S(2)}, u32[]{:S(2)}) %collective-permute-start.22) | collective-permute-done | bytes 360480 | tf_op jit(solution)/shard_map/ppermute | solution.py:39
  156.4 9.9 %collective-permute-done.23 = bf16[32,5632]{1,0:T(8,128)(2,1)S(1)} collective-permute-done((bf16[32,5632]{1,0:T(8,128)(2,1)S(1)}, bf16[32,5632]{1,0:T(8,128)(2,1)S(1)}, u32[]{:S(2)}, u32[]{:S(2)}) %collective-permute-start.23) | collective-permute-done | bytes 360480 | tf_op jit(solution)/shard_map/ppermute | solution.py:39
  173.8 15.4 %collective-permute-done.21 = bf16[2,2,128,256]{3,2,1,0:T(8,128)(2,1)S(1)} collective-permute-done((bf16[2,2,128,256]{3,2,1,0:T(8,128)(2,1)S(1)}, bf16[2,2,128,256]{3,2,1,0:T(8,128)(2,1)S(1)}, u32[]{:S(2)}, u32[]{:S(2)}) %collective-permute-start.21) | collective-permute-done | bytes 262176 | tf_op jit(solution)/shard_map/ppermute | solution.py:39
  192.4 4.4 shard_map.242
  202.6 4.1 shard_map.243
  207.5 16.0 %collective-permute-done.39.refs_2_ = bf16[2,4,32,2816]{3,2,1,0:T(8,128)(2,1)S(1)} collective-permute-done((bf16[2,4,32,2816]{3,2,1,0:T(8,128)(2,1)S(1)}, bf16[2,4,32,2816]{3,2,1,0:T(8,128)(2,1)S(1)}, u32[]{:S(2)}, u32[]{:S(2)}) %collective-permute-start.39) | collective-permute-done | bytes 1441824 | tf_op jit(solution)/shard_map/ppermute | solution.py:39
  223.8 4.1 shard_map.244
  232.6 4.0 shard_map.246
  236.6 2.5 copy-done.36
  239.1 5.2 shard_map.245
  244.3 2.5 copy-done.37
  246.9 28.2 %shard_map.247 = (f32[512,1024]{1,0:T(8,128)}, f32[512,1024]{1,0:T(8,128)}, bf16[512,1024]{1,0:T(8,128)(2,1)S(1)}, bf16[512,1024]{1,0:T(8,128)(2,1)}, bf16[512,2...) custom-call(f32[512,1024]{1,0:T(8,128)} %maximum_add_fusion.hid, ...), custom_call_target="tpu_custom_call" | custom-call | flops 28000000000 | tf_op jit(solution)/shard_map/pallas_call | solution.py:729
  276.3 13.6 %shard_map.251 = (bf16[2,2,4,32,2816]{4,3,2,1,0:T(8,128)(2,1)}, bf16[2,2,4,32,2816]{4,3,2,1,0:T(8,128)(2,1)}, bf16[2,2,4,32,2816]{4,3,2,1,0:T(8,128)(2,1)}, bf16[2,2,4,32,2816]{4,3,2,1,0:T(8,128)(2,1)}) custom-call(s32[4]{0:T(128)S(1)} %pad_add_fusion.1.me, bf16[512,1024]{1,0:T(8,128)(2,1)S(1)} %copy-done.56, bf16[512,2816]{1,0:T(8,128)(2,1)} %get-tuple-element.141.a_ref, ...), custom_call_target="tpu_custom_call" | custom-call | flops 14476128256 | tf_op jit(solution)/shard_map/pallas_call | solution.py:194
  293.0 5.3 shard_map.248
  299.8 8.3 %shard_map.253 = (bf16[2,2,4,88,512]{4,3,2,1,0:T(8,128)(2,1)}, bf16[2,2,4,88,512]{4,3,2,1,0:T(8,128)(2,1)S(1)}, bf16[2,2,4,88,512]{4,3,2,1,0:T(8,128)(2,1)}, bf16[2,2,4,88,512]{4,3,2,1,0:T(8,128)(2,1)}) custom-call(s32[4]{0:T(128)S(1)} %pad_add_fusion.1.me, bf16[512,2816]{1,0:T(8,128)(2,1)} %get-tuple-element.155.left_ref, ...), custom_call_target="tpu_custom_call" | custom-call | flops 7988064256 | tf_op jit(solution)/shard_map/pallas_call | solution.py:194
  309.8 2.7 shard_map.254
  316.4 2.7 shard_map.255
  321.5 2.7 collective-permute-done.42
  329.1 4.5 collective-permute-done.43
  340.1 9.5 %collective-permute-done.44.refs_0_ = bf16[128,256]{1,0:T(8,128)(2,1)S(1)} collective-permute-done((bf16[128,256]{1,0:T(8,128)(2,1)}, bf16[128,256]{1,0:T(8,128)(2,1)S(1)}, u32[]{:S(2)}, u32[]{:S(2)}) %collective-permute-start.44) | collective-permute-done | bytes 65568 | tf_op jit(solution)/shard_map/ppermute | solution.py:45
  358.1 2.3 convert_add_fusion.9
  360.5 4.3 collective-permute-done.46
  367.6 6.0 collective-permute-done.47
  373.8 25.2 %shard_map.252 = (f32[2,264,512]{2,1,0:T(8,128)S(1)}, f32[2,264,512]{2,1,0:T(8,128)S(1)}, f32[2,264,1024]{2,1,0:T(8,128)S(1)}, f32[2,4,512]{2,1,0:T(4,128)S(1)},...) custom-call(s32[2]{0:T(128)S(1)} %copy-done.46, ...), custom_call_target="tpu_custom_call" | custom-call | flops 24000000000 | tf_op jit(solution)/shard_map/pallas_call | solution.py:437
  402.5 2.5 convert_add_fusion
  410.0 2.5 convert_add_fusion.1
  423.3 2.7 fusion
  428.3 2.7 fusion.75
  431.0 11.0 %collective-permute-done.53 = bf16[2,4,32,2816]{3,2,1,0:T(8,128)(2,1)} collective-permute-done((bf16[2,4,32,2816]{3,2,1,0:T(8,128)(2,1)}, bf16[2,4,32,2816]{3,2,1,0:T(8,128)(2,1)}, u32[]{:S(2)}, u32[]{:S(2)}) %collective-permute-start.53) | collective-permute-done | bytes 1441824 | tf_op jit(solution)/shard_map/ppermute | solution.py:39
  443.8 2.4 collective-permute-start.54
  446.2 9.8 %collective-permute-done.51 = bf16[2,4,32,2816]{3,2,1,0:T(8,128)(2,1)} collective-permute-done((bf16[2,4,32,2816]{3,2,1,0:T(8,128)(2,1)}, bf16[2,4,32,2816]{3,2,1,0:T(8,128)(2,1)}, u32[]{:S(2)}, u32[]{:S(2)}) %collective-permute-start.51) | collective-permute-done | bytes 1441824 | tf_op jit(solution)/shard_map/ppermute | solution.py:39
  460.0 11.3 %collective-permute-done.54 = bf16[4,32,2816]{2,1,0:T(8,128)(2,1)S(1)} collective-permute-done((bf16[4,32,2816]{2,1,0:T(8,128)(2,1)S(1)}, bf16[4,32,2816]{2,1,0:T(8,128)(2,1)S(1)}, u32[]{:S(2)}, u32[]{:S(2)}) %collective-permute-start.54) | collective-permute-done | bytes 720928 | tf_op jit(solution)/shard_map/ppermute | solution.py:39
  471.4 4.7 collective-permute-done.52
  480.9 2.6 collective-permute-start.85
  483.6 5.9 shard_map.256
  494.0 2.7 fusion.12
  496.9 2.3 convert_add_fusion.2
  508.4 4.1 collective-permute-done.58
  513.0 4.9 collective-permute-done.59
  522.7 2.4 fusion.28
  525.1 6.7 %collective-permute-done.61 = f32[278,128]{1,0:T(8,128)S(1)} collective-permute-done((f32[278,128]{1,0:T(8,128)S(1)}, f32[278,128]{1,0:T(8,128)S(1)}, u32[]{:S(2)}, u32[]{:S(2)}) %collective-permute-start.61) | collective-permute-done | bytes 142368 | tf_op jit(solution)/shard_map/ppermute | solution.py:39
  533.9 12.0 %collective-permute-done.69 = bf16[2,4,152,512]{3,2,1,0:T(8,128)(2,1)S(1)} collective-permute-done((bf16[2,4,152,512]{3,2,1,0:T(8,128)(2,1)S(1)}, bf16[2,4,152,512]{3,2,1,0:T(8,128)(2,1)S(1)}, u32[]{:S(2)}, u32[]{:S(2)}) %collective-permute-start.69) | collective-permute-done | bytes 1245216 | tf_op jit(solution)/shard_map/ppermute | solution.py:39
  548.3 13.3 %collective-permute-done.65 = bf16[2,4,152,512]{3,2,1,0:T(8,128)(2,1)S(1)} collective-permute-done((bf16[2,4,152,512]{3,2,1,0:T(8,128)(2,1)S(1)}, bf16[2,4,152,512]{3,2,1,0:T(8,128)(2,1)S(1)}, u32[]{:S(2)}, u32[]{:S(2)}) %collective-permute-start.65) | collective-permute-done | bytes 1245216 | tf_op jit(solution)/shard_map/ppermute | solution.py:39
  570.6 8.3 %collective-permute-done.66 = bf16[4,152,512]{2,1,0:T(8,128)(2,1)} collective-permute-done((bf16[4,152,512]{2,1,0:T(8,128)(2,1)}, bf16[4,152,512]{2,1,0:T(8,128)(2,1)}, u32[]{:S(2)}, u32[]{:S(2)}) %collective-permute-start.66) | collective-permute-done | bytes 622624 | tf_op jit(solution)/shard_map/ppermute | solution.py:39
  587.9 2.5 collective-permute-start.81
  595.7 4.1 collective-permute-done.80
  599.9 6.5 %collective-permute-done.81 = bf16[152,1024]{1,0:T(8,128)(2,1)S(1)} collective-permute-done((bf16[152,1024]{1,0:T(8,128)(2,1)S(1)}, bf16[152,1024]{1,0:T(8,128)(2,1)S(1)}, u32[]{:S(2)}, u32[]{:S(2)}) %collective-permute-start.81) | collective-permute-done | bytes 311328 | tf_op jit(solution)/shard_map/ppermute | solution.py:39
  607.6 5.7 collective-permute-start.77
  616.4 5.6 collective-permute-done.78
  (483 shorter events, 185.5 us)
Async XLA Ops:
  4.7 9.7 %collective-permute-start.6 = (bf16[32,2048]{1,0:T(8,128)(2,1)S(1)}, bf16[32,2048]{1,0:T(8,128)(2,1)S(1)}, u32[]{:S(2)}, u32[]{:S(2)}) collective-permute-start(bf16[32,2048]{1,0:T(8,128)(2,1)S(1)} %get-tuple-element.264), channel_id=1, source_target_pairs={{0,24},{1,25},{2,26},{3,27},{4,28},{5,29},{6,30},{7,31},{8,16},{9,... | collective-permute-start | bytes 393224 | tf_op jit(solution)/shard_map/ppermute | solution.py:39
  7.2 11.8 %collective-permute-start.5 = (bf16[32,2048]{1,0:T(8,128)(2,1)S(1)}, bf16[32,2048]{1,0:T(8,128)(2,1)S(1)}, u32[]{:S(2)}, u32[]{:S(2)}) collective-permute-start(bf16[32,2048]{1,0:T(8,128)(2,1)S(1)} %get-tuple-element.264), channel_id=1, source_target_pairs={{0,16},{1,17},{2,18},{3,19},{4,20},{5,21},{6,22},{7,23},{8,24},{9,... | collective-permute-start | bytes 393224 | tf_op jit(solution)/shard_map/ppermute | solution.py:39
  26.7 30.0 %collective-permute-start.10 = (bf16[2,4,32,1024]{3,2,1,0:T(8,128)(2,1)S(1)}, bf16[2,4,32,1024]{3,2,1,0:T(8,128)(2,1)S(1)}, u32[]{:S(2)}, u32[]{:S(2)}) collective-permute-start(bf16[2,4,32,1024]{3,2,1,0:T(8,128)(2,1)S(1)} %pad_maximum_fusion.15.refs_0_), channel_id=1, source_target_pairs={{0,2},{1,3},{2,0},{3,1},{4,6},{5,7},{6,4},{7,5},{8,10},{9,11},{10,... | collective-permute-start | bytes 1572872 | tf_op jit(solution)/shard_map/ppermute | solution.py:39
  28.3 28.4 %collective-permute-start.8 = (bf16[2,4,32,1024]{3,2,1,0:T(8,128)(2,1)S(1)}, bf16[2,4,32,1024]{3,2,1,0:T(8,128)(2,1)}, u32[]{:S(2)}, u32[]{:S(2)}) collective-permute-start(bf16[2,4,32,1024]{3,2,1,0:T(8,128)(2,1)S(1)} %pad_maximum_fusion.14.refs_0_), channel_id=1, source_target_pairs={{0,4},{1,5},{2,6},{3,7},{4,0},{5,1},{6,2},{7,3},{8,12},{9,13},{10,... | collective-permute-start | bytes 1572872 | tf_op jit(solution)/shard_map/ppermute | solution.py:39
  31.3 16.5 %collective-permute-start.2 = (bf16[152,1024]{1,0:T(8,128)(2,1)S(1)}, bf16[152,1024]{1,0:T(8,128)(2,1)}, u32[]{:S(2)}, u32[]{:S(2)}) collective-permute-start(bf16[152,1024]{1,0:T(8,128)(2,1)S(1)} %pad_maximum_fusion.19), channel_id=1, source_target_pairs={{0,8},{1,9},{2,10},{3,11},{4,12},{5,13},{6,14},{7,15},{8,0},{9,1},... | collective-permute-start | bytes 933896 | tf_op jit(solution)/shard_map/ppermute | solution.py:39
  31.6 25.1 %collective-permute-start.3 = (bf16[152,1024]{1,0:T(8,128)(2,1)S(1)}, bf16[152,1024]{1,0:T(8,128)(2,1)}, u32[]{:S(2)}, u32[]{:S(2)}) collective-permute-start(bf16[152,1024]{1,0:T(8,128)(2,1)S(1)} %pad_maximum_fusion.19), channel_id=1, source_target_pairs={{0,16},{1,17},{2,18},{3,19},{4,20},{5,21},{6,22},{7,23},{8,24},{9,... | collective-permute-start | bytes 933896 | tf_op jit(solution)/shard_map/ppermute | solution.py:39
  35.0 21.7 %collective-permute-start.4 = (bf16[152,1024]{1,0:T(8,128)(2,1)S(1)}, bf16[152,1024]{1,0:T(8,128)(2,1)}, u32[]{:S(2)}, u32[]{:S(2)}) collective-permute-start(bf16[152,1024]{1,0:T(8,128)(2,1)S(1)} %pad_maximum_fusion.19), channel_id=1, source_target_pairs={{0,24},{1,25},{2,26},{3,27},{4,28},{5,29},{6,30},{7,31},{8,16},{9,... | collective-permute-start | bytes 933896 | tf_op jit(solution)/shard_map/ppermute | solution.py:39
  85.6 24.4 %collective-permute-start.27 = (bf16[4,152,512]{2,1,0:T(8,128)(2,1)S(1)}, bf16[4,152,512]{2,1,0:T(8,128)(2,1)S(1)}, u32[]{:S(2)}, u32[]{:S(2)}) collective-permute-start(bf16[4,152,512]{2,1,0:T(8,128)(2,1)S(1)} %get-tuple-element.222), channel_id=1, source_target_pairs={{0,4},{1,5},{2,6},{3,7},{4,0},{5,1},{6,2},{7,3},{8,12},{9,13},{10,... | collective-permute-start | bytes 1867784 | tf_op jit(solution)/shard_map/ppermute | solution.py:39
  86.4 24.6 %collective-permute-start.25 = (bf16[4,152,512]{2,1,0:T(8,128)(2,1)S(1)}, bf16[4,152,512]{2,1,0:T(8,128)(2,1)S(1)}, u32[]{:S(2)}, u32[]{:S(2)}) collective-permute-start(bf16[4,152,512]{2,1,0:T(8,128)(2,1)S(1)} %get-tuple-element.223), channel_id=1, source_target_pairs={{0,2},{1,3},{2,0},{3,1},{4,6},{5,7},{6,4},{7,5},{8,10},{9,11},{10,... | collective-permute-start | bytes 1867784 | tf_op jit(solution)/shard_map/ppermute | solution.py:39
  87.7 21.0 %collective-permute-start.16 = (bf16[2,2,144,256]{3,2,1,0:T(8,128)(2,1)S(1)}, bf16[2,2,144,256]{3,2,1,0:T(8,128)(2,1)S(1)}, u32[]{:S(2)}, u32[]{:S(2)}) collective-permute-start(bf16[2,2,144,256]{3,2,1,0:T(8,128)(2,1)S(1)} %get-tuple-element.241), channel_id=1, source_target_pairs={{0,2},{1,3},{2,0},{3,1},{4,6},{5,7},{6,4},{7,5},{8,10},{9,11},{10,... | collective-permute-start | bytes 884744 | tf_op jit(solution)/shard_map/ppermute | solution.py:39
  108.7 10.0 %collective-permute-start.17 = (bf16[2,2,144,256]{3,2,1,0:T(8,128)(2,1)S(1)}, bf16[2,2,144,256]{3,2,1,0:T(8,128)(2,1)S(1)}, u32[]{:S(2)}, u32[]{:S(2)}) collective-permute-start(bf16[2,2,144,256]{3,2,1,0:T(8,128)(2,1)S(1)} %get-tuple-element.239), channel_id=1, source_target_pairs={{0,4},{1,5},{2,6},{3,7},{4,0},{5,1},{6,2},{7,3},{8,12},{9,13},{10,... | collective-permute-start | bytes 884744 | tf_op jit(solution)/shard_map/ppermute | solution.py:39
  110.2 56.1 %collective-permute-start.28 = (bf16[2,4,152,512]{3,2,1,0:T(8,128)(2,1)S(1)}, bf16[2,4,152,512]{3,2,1,0:T(8,128)(2,1)}, u32[]{:S(2)}, u32[]{:S(2)}) collective-permute-start(bf16[2,4,152,512]{3,2,1,0:T(8,128)(2,1)S(1)} %pad_maximum_fusion.9.refs_0_), channel_id=1, source_target_pairs={{0,2},{1,3},{2,0},{3,1},{4,6},{5,7},{6,4},{7,5},{8,10},{9,11},{10,... | collective-permute-start | bytes 3735560 | tf_op jit(solution)/shard_map/ppermute | solution.py:39
  112.1 54.2 %collective-permute-start.26 = (bf16[2,4,152,512]{3,2,1,0:T(8,128)(2,1)}, bf16[2,4,152,512]{3,2,1,0:T(8,128)(2,1)}, u32[]{:S(2)}, u32[]{:S(2)}) collective-permute-start(bf16[2,4,152,512]{3,2,1,0:T(8,128)(2,1)} %pad_maximum_fusion.8.refs_0_), channel_id=1, source_target_pairs={{0,4},{1,5},{2,6},{3,7},{4,0},{5,1},{6,2},{7,3},{8,12},{9,13},{10,... | collective-permute-start | bytes 3735560 | tf_op jit(solution)/shard_map/ppermute | solution.py:39
  121.5 10.9 %collective-permute-start.18 = (bf16[128,256]{1,0:T(8,128)(2,1)}, bf16[128,256]{1,0:T(8,128)(2,1)S(1)}, u32[]{:S(2)}, u32[]{:S(2)}) collective-permute-start(bf16[128,256]{1,0:T(8,128)(2,1)} %shard_map.240), channel_id=1, source_target_pairs={{0,8},{1,9},{2,10},{3,11},{4,12},{5,13},{6,14},{7,15},{8,16},{9,17... | collective-permute-start | bytes 196616 | tf_op jit(solution)/shard_map/ppermute | solution.py:45
  136.3 18.6 %collective-permute-start.22 = (bf16[32,5632]{1,0:T(8,128)(2,1)S(1)}, bf16[32,5632]{1,0:T(8,128)(2,1)S(1)}, u32[]{:S(2)}, u32[]{:S(2)}) collective-permute-start(bf16[32,5632]{1,0:T(8,128)(2,1)S(1)} %copy-done.85), channel_id=1, source_target_pairs={{0,8},{1,9},{2,10},{3,11},{4,12},{5,13},{6,14},{7,15},{8,0},{9,1},... | collective-permute-start | bytes 1081352 | tf_op jit(solution)/shard_map/ppermute | solution.py:39
  138.6 27.7 %collective-permute-start.23 = (bf16[32,5632]{1,0:T(8,128)(2,1)S(1)}, bf16[32,5632]{1,0:T(8,128)(2,1)S(1)}, u32[]{:S(2)}, u32[]{:S(2)}) collective-permute-start(bf16[32,5632]{1,0:T(8,128)(2,1)S(1)} %copy-done.85), channel_id=1, source_target_pairs={{0,16},{1,17},{2,18},{3,19},{4,20},{5,21},{6,22},{7,23},{8,24},{9,... | collective-permute-start | bytes 1081352 | tf_op jit(solution)/shard_map/ppermute | solution.py:39
  139.7 26.6 %collective-permute-start.24 = (bf16[32,5632]{1,0:T(8,128)(2,1)S(1)}, bf16[32,5632]{1,0:T(8,128)(2,1)S(1)}, u32[]{:S(2)}, u32[]{:S(2)}) collective-permute-start(bf16[32,5632]{1,0:T(8,128)(2,1)S(1)} %copy-done.85), channel_id=1, source_target_pairs={{0,24},{1,25},{2,26},{3,27},{4,28},{5,29},{6,30},{7,31},{8,16},{9,... | collective-permute-start | bytes 1081352 | tf_op jit(solution)/shard_map/ppermute | solution.py:39
  154.9 14.2 %collective-permute-start.20 = (bf16[2,2,128,256]{3,2,1,0:T(8,128)(2,1)S(1)}, bf16[2,2,128,256]{3,2,1,0:T(8,128)(2,1)S(1)}, u32[]{:S(2)}, u32[]{:S(2)}) collective-permute-start(bf16[2,2,128,256]{3,2,1,0:T(8,128)(2,1)S(1)} %get-tuple-element.256), channel_id=1, source_target_pairs={{0,2},{1,3},{2,0},{3,1},{4,6},{5,7},{6,4},{7,5},{8,10},{9,11},{10,... | collective-permute-start | bytes 786440 | tf_op jit(solution)/shard_map/ppermute | solution.py:39
  166.8 22.4 %collective-permute-start.37 = (bf16[4,32,2816]{2,1,0:T(8,128)(2,1)S(1)}, bf16[4,32,2816]{2,1,0:T(8,128)(2,1)S(1)}, u32[]{:S(2)}, u32[]{:S(2)}) collective-permute-start(bf16[4,32,2816]{2,1,0:T(8,128)(2,1)S(1)} %get-tuple-element.215), channel_id=1, source_target_pairs={{0,4},{1,5},{2,6},{3,7},{4,0},{5,1},{6,2},{7,3},{8,12},{9,13},{10,... | collective-permute-start | bytes 2162696 | tf_op jit(solution)/shard_map/ppermute | solution.py:39
  168.5 23.1 %collective-permute-start.29 = (bf16[2,4,152,512]{3,2,1,0:T(8,128)(2,1)}, bf16[2,4,152,512]{3,2,1,0:T(8,128)(2,1)S(1)}, u32[]{:S(2)}, u32[]{:S(2)}) collective-permute-start(bf16[2,4,152,512]{3,2,1,0:T(8,128)(2,1)} %pad_maximum_fusion.8.refs_0_), channel_id=1, source_target_pairs={{0,1},{1,0},{2,3},{3,2},{4,5},{5,4},{6,7},{7,6},{8,9},{9,8},{10,11... | collective-permute-start | bytes 3735560 | tf_op jit(solution)/shard_map/ppermute | solution.py:39
  168.6 23.1 %collective-permute-start.30 = (bf16[2,4,152,512]{3,2,1,0:T(8,128)(2,1)}, bf16[2,4,152,512]{3,2,1,0:T(8,128)(2,1)S(1)}, u32[]{:S(2)}, u32[]{:S(2)}) collective-permute-start(bf16[2,4,152,512]{3,2,1,0:T(8,128)(2,1)} %collective-permute-done.26.refs_2_), channel_id=1, source_target_pairs={{0,1},{1,0},{2,3},{3,2},{4,5},{5,4},{6,7},{7,6},{8,9},{9,8},{10,11... | collective-permute-start | bytes 3735560 | tf_op jit(solution)/shard_map/ppermute | solution.py:39
  169.2 20.0 %collective-permute-start.21 = (bf16[2,2,128,256]{3,2,1,0:T(8,128)(2,1)S(1)}, bf16[2,2,128,256]{3,2,1,0:T(8,128)(2,1)S(1)}, u32[]{:S(2)}, u32[]{:S(2)}) collective-permute-start(bf16[2,2,128,256]{3,2,1,0:T(8,128)(2,1)S(1)} %get-tuple-element.254), channel_id=1, source_target_pairs={{0,4},{1,5},{2,6},{3,7},{4,0},{5,1},{6,2},{7,3},{8,12},{9,13},{10,... | collective-permute-start | bytes 786440 | tf_op jit(solution)/shard_map/ppermute | solution.py:39
  171.8 18.1 %collective-permute-start.33 = (bf16[4,32,2816]{2,1,0:T(8,128)(2,1)S(1)}, bf16[4,32,2816]{2,1,0:T(8,128)(2,1)S(1)}, u32[]{:S(2)}, u32[]{:S(2)}) collective-permute-start(bf16[4,32,2816]{2,1,0:T(8,128)(2,1)S(1)} %get-tuple-element.216), channel_id=1, source_target_pairs={{0,2},{1,3},{2,0},{3,1},{4,6},{5,7},{6,4},{7,5},{8,10},{9,11},{10,... | collective-permute-start | bytes 2162696 | tf_op jit(solution)/shard_map/ppermute | solution.py:39
  189.3 9.7 %collective-permute-start.32 = (bf16[2,4,152,512]{3,2,1,0:T(8,128)(2,1)}, bf16[2,4,152,512]{3,2,1,0:T(8,128)(2,1)S(1)}, u32[]{:S(2)}, u32[]{:S(2)}) collective-permute-start(bf16[2,4,152,512]{3,2,1,0:T(8,128)(2,1)} %collective-permute-done.28.refs_2_), channel_id=1, source_target_pairs={{0,1},{1,0},{2,3},{3,2},{4,5},{5,4},{6,7},{7,6},{8,9},{9,8},{10,11... | collective-permute-start | bytes 3735560 | tf_op jit(solution)/shard_map/ppermute | solution.py:39
  190.0 33.6 %collective-permute-start.39 = (bf16[2,4,32,2816]{3,2,1,0:T(8,128)(2,1)S(1)}, bf16[2,4,32,2816]{3,2,1,0:T(8,128)(2,1)S(1)}, u32[]{:S(2)}, u32[]{:S(2)}) collective-permute-start(bf16[2,4,32,2816]{3,2,1,0:T(8,128)(2,1)S(1)} %pad_maximum_fusion.5.refs_0_), channel_id=1, source_target_pairs={{0,2},{1,3},{2,0},{3,1},{4,6},{5,7},{6,4},{7,5},{8,10},{9,11},{10,... | collective-permute-start | bytes 4325384 | tf_op jit(solution)/shard_map/ppermute | solution.py:39
  191.7 40.9 %collective-permute-start.38 = (bf16[2,4,32,2816]{3,2,1,0:T(8,128)(2,1)S(1)}, bf16[2,4,32,2816]{3,2,1,0:T(8,128)(2,1)}, u32[]{:S(2)}, u32[]{:S(2)}) collective-permute-start(bf16[2,4,32,2816]{3,2,1,0:T(8,128)(2,1)S(1)} %pad_maximum_fusion.5.refs_0_), channel_id=1, source_target_pairs={{0,1},{1,0},{2,3},{3,2},{4,5},{5,4},{6,7},{7,6},{8,9},{9,8},{10,11... | collective-permute-start | bytes 4325384 | tf_op jit(solution)/shard_map/ppermute | solution.py:39
  191.8 36.2 %collective-permute-start.35 = (bf16[2,4,32,2816]{3,2,1,0:T(8,128)(2,1)S(1)}, bf16[2,4,32,2816]{3,2,1,0:T(8,128)(2,1)}, u32[]{:S(2)}, u32[]{:S(2)}) collective-permute-start(bf16[2,4,32,2816]{3,2,1,0:T(8,128)(2,1)S(1)} %pad_maximum_fusion.4.refs_0_), channel_id=1, source_target_pairs={{0,4},{1,5},{2,6},{3,7},{4,0},{5,1},{6,2},{7,3},{8,12},{9,13},{10,... | collective-permute-start | bytes 4325384 | tf_op jit(solution)/shard_map/ppermute | solution.py:39
  198.8 40.3 %collective-permute-start.34 = (bf16[2,4,32,2816]{3,2,1,0:T(8,128)(2,1)S(1)}, bf16[2,4,32,2816]{3,2,1,0:T(8,128)(2,1)}, u32[]{:S(2)}, u32[]{:S(2)}) collective-permute-start(bf16[2,4,32,2816]{3,2,1,0:T(8,128)(2,1)S(1)} %pad_maximum_fusion.4.refs_0_), channel_id=1, source_target_pairs={{0,1},{1,0},{2,3},{3,2},{4,5},{5,4},{6,7},{7,6},{8,9},{9,8},{10,11... | collective-permute-start | bytes 4325384 | tf_op jit(solution)/shard_map/ppermute | solution.py:39
  223.6 9.0 %collective-permute-start.40 = (bf16[2,4,32,2816]{3,2,1,0:T(8,128)(2,1)S(1)}, bf16[2,4,32,2816]{3,2,1,0:T(8,128)(2,1)S(1)}, u32[]{:S(2)}, u32[]{:S(2)}) collective-permute-start(bf16[2,4,32,2816]{3,2,1,0:T(8,128)(2,1)S(1)} %collective-permute-done.39.refs_2_), channel_id=1, source_target_pairs={{0,1},{1,0},{2,3},{3,2},{4,5},{5,4},{6,7},{7,6},{8,9},{9,8},{10,11... | collective-permute-start | bytes 4325384 | tf_op jit(solution)/shard_map/ppermute | solution.py:39
  227.9 11.1 %collective-permute-start.36 = (bf16[2,4,32,2816]{3,2,1,0:T(8,128)(2,1)}, bf16[2,4,32,2816]{3,2,1,0:T(8,128)(2,1)S(1)}, u32[]{:S(2)}, u32[]{:S(2)}) collective-permute-start(bf16[2,4,32,2816]{3,2,1,0:T(8,128)(2,1)} %collective-permute-done.35.refs_2_), channel_id=1, source_target_pairs={{0,1},{1,0},{2,3},{3,2},{4,5},{5,4},{6,7},{7,6},{8,9},{9,8},{10,11... | collective-permute-start | bytes 4325384 | tf_op jit(solution)/shard_map/ppermute | solution.py:39
  289.9 83.8 %collective-permute-start.48 = (bf16[2,2,4,32,2816]{4,3,2,1,0:T(8,128)(2,1)}, bf16[2,2,4,32,2816]{4,3,2,1,0:T(8,128)(2,1)}, u32[]{:S(2)}, u32[]{:S(2)}) collective-permute-start(bf16[2,2,4,32,2816]{4,3,2,1,0:T(8,128)(2,1)} %get-tuple-element.144), channel_id=1, source_target_pairs={{0,1},{1,0},{2,3},{3,2},{4,5},{5,4},{6,7},{7,6},{8,9},{9,8},{10,11... | collective-permute-start | bytes 8650760 | tf_op jit(solution)/shard_map/ppermute | solution.py:39
  289.9 83.8 %collective-permute-start.49 = (bf16[2,2,4,32,2816]{4,3,2,1,0:T(8,128)(2,1)}, bf16[2,2,4,32,2816]{4,3,2,1,0:T(8,128)(2,1)}, u32[]{:S(2)}, u32[]{:S(2)}) collective-permute-start(bf16[2,2,4,32,2816]{4,3,2,1,0:T(8,128)(2,1)} %get-tuple-element.146), channel_id=1, source_target_pairs={{0,1},{1,0},{2,3},{3,2},{4,5},{5,4},{6,7},{7,6},{8,9},{9,8},{10,11... | collective-permute-start | bytes 8650760 | tf_op jit(solution)/shard_map/ppermute | solution.py:39
  299.7 14.4 %collective-permute-start.41 = (bf16[2,2,144,256]{3,2,0,1:T(8,128)(2,1)S(1)}, bf16[2,2,144,256]{3,2,0,1:T(8,128)(2,1)S(1)}, u32[]{:S(2)}, u32[]{:S(2)}) collective-permute-start(bf16[2,2,144,256]{3,2,0,1:T(8,128)(2,1)S(1)} %bitcast.369), channel_id=1, source_target_pairs={{0,1},{1,0},{2,3},{3,2},{4,5},{5,4},{6,7},{7,6},{8,9},{9,8},{10,11... | collective-permute-start | bytes 884744 | tf_op jit(solution)/shard_map/ppermute | solution.py:39
  309.2 167.0 %collective-permute-start.55 = (bf16[2,2,4,88,512]{4,3,2,1,0:T(8,128)(2,1)}, bf16[2,2,4,88,512]{4,3,2,1,0:T(8,128)(2,1)}, u32[]{:S(2)}, u32[]{:S(2)}) collective-permute-start(bf16[2,2,4,88,512]{4,3,2,1,0:T(8,128)(2,1)} %get-tuple-element.157), channel_id=1, source_target_pairs={{0,1},{1,0},{2,3},{3,2},{4,5},{5,4},{6,7},{7,6},{8,9},{9,8},{10,11... | collective-permute-start | bytes 4325384 | tf_op jit(solution)/shard_map/ppermute | solution.py:39
  313.2 23.2 %collective-permute-start.67 = (bf16[2,2,4,32,512]{4,3,2,1,0:T(8,128)(2,1)}, bf16[2,2,4,32,512]{4,3,2,1,0:T(8,128)(2,1)}, u32[]{:S(2)}, u32[]{:S(2)}) collective-permute-start(bf16[2,2,4,32,512]{4,3,2,1,0:T(8,128)(2,1)} %get-tuple-element.176), channel_id=1, source_target_pairs={{0,1},{1,0},{2,3},{3,2},{4,5},{5,4},{6,7},{7,6},{8,9},{9,8},{10,11... | collective-permute-start | bytes 1572872 | tf_op jit(solution)/shard_map/ppermute | solution.py:39
  314.9 9.3 %collective-permute-start.42 = (bf16[2,2,144,256]{3,2,1,0:T(8,128)(2,1)}, bf16[2,2,144,256]{3,2,1,0:T(8,128)(2,1)}, u32[]{:S(2)}, u32[]{:S(2)}) collective-permute-start(bf16[2,2,144,256]{3,2,1,0:T(8,128)(2,1)} %get-tuple-element.235), channel_id=1, source_target_pairs={{0,2},{1,3},{2,0},{3,1},{4,6},{5,7},{6,4},{7,5},{8,10},{9,11},{10,... | collective-permute-start | bytes 884744 | tf_op jit(solution)/shard_map/ppermute | solution.py:39
  333.6 20.0 %collective-permute-start.68 = (bf16[2,2,4,32,512]{4,3,2,1,0:T(8,128)(2,1)}, bf16[2,2,4,32,512]{4,3,2,1,0:T(8,128)(2,1)}, u32[]{:S(2)}, u32[]{:S(2)}) collective-permute-start(bf16[2,2,4,32,512]{4,3,2,1,0:T(8,128)(2,1)} %get-tuple-element.178), channel_id=1, source_target_pairs={{0,1},{1,0},{2,3},{3,2},{4,5},{5,4},{6,7},{7,6},{8,9},{9,8},{10,11... | collective-permute-start | bytes 1572872 | tf_op jit(solution)/shard_map/ppermute | solution.py:39
  336.5 13.2 %collective-permute-start.44 = (bf16[128,256]{1,0:T(8,128)(2,1)}, bf16[128,256]{1,0:T(8,128)(2,1)S(1)}, u32[]{:S(2)}, u32[]{:S(2)}) collective-permute-start(bf16[128,256]{1,0:T(8,128)(2,1)} %shard_map.249), channel_id=1, source_target_pairs={{8,0},{9,1},{10,2},{11,3},{12,4},{13,5},{14,6},{15,7},{16,8},{17,9... | collective-permute-start | bytes 196616 | tf_op jit(solution)/shard_map/ppermute | solution.py:45
  355.9 8.9 %collective-permute-start.64 = (bf16[2,2,4,32,512]{4,3,2,1,0:T(8,128)(2,1)S(1)}, bf16[2,2,4,32,512]{4,3,2,1,0:T(8,128)(2,1)S(1)}, u32[]{:S(2)}, u32[]{:S(2)}) collective-permute-start(bf16[2,2,4,32,512]{4,3,2,1,0:T(8,128)(2,1)S(1)} %copy-done.32), channel_id=1, source_target_pairs={{0,1},{1,0},{2,3},{3,2},{4,5},{5,4},{6,7},{7,6},{8,9},{9,8},{10,11... | collective-permute-start | bytes 1572872 | tf_op jit(solution)/shard_map/ppermute | solution.py:39
  364.8 111.5 %collective-permute-start.56 = (bf16[2,2,4,88,512]{4,3,2,1,0:T(8,128)(2,1)}, bf16[2,2,4,88,512]{4,3,2,1,0:T(8,128)(2,1)}, u32[]{:S(2)}, u32[]{:S(2)}) collective-permute-start(bf16[2,2,4,88,512]{4,3,2,1,0:T(8,128)(2,1)} %get-tuple-element.159), channel_id=1, source_target_pairs={{0,1},{1,0},{2,3},{3,2},{4,5},{5,4},{6,7},{7,6},{8,9},{9,8},{10,11... | collective-permute-start | bytes 4325384 | tf_op jit(solution)/shard_map/ppermute | solution.py:39
  408.5 33.5 %collective-permute-start.53 = (bf16[2,4,32,2816]{3,2,1,0:T(8,128)(2,1)}, bf16[2,4,32,2816]{3,2,1,0:T(8,128)(2,1)}, u32[]{:S(2)}, u32[]{:S(2)}) collective-permute-start(bf16[2,4,32,2816]{3,2,1,0:T(8,128)(2,1)} %fusion.14), channel_id=1, source_target_pairs={{0,4},{1,5},{2,6},{3,7},{4,0},{5,1},{6,2},{7,3},{8,12},{9,13},{10,... | collective-permute-start | bytes 4325384 | tf_op jit(solution)/shard_map/ppermute | solution.py:39
  421.3 34.7 %collective-permute-start.51 = (bf16[2,4,32,2816]{3,2,1,0:T(8,128)(2,1)}, bf16[2,4,32,2816]{3,2,1,0:T(8,128)(2,1)}, u32[]{:S(2)}, u32[]{:S(2)}) collective-permute-start(bf16[2,4,32,2816]{3,2,1,0:T(8,128)(2,1)} %fusion.13), channel_id=1, source_target_pairs={{0,2},{1,3},{2,0},{3,1},{4,6},{5,7},{6,4},{7,5},{8,10},{9,11},{10,... | collective-permute-start | bytes 4325384 | tf_op jit(solution)/shard_map/ppermute | solution.py:39
  443.8 27.5 %collective-permute-start.54 = (bf16[4,32,2816]{2,1,0:T(8,128)(2,1)S(1)}, bf16[4,32,2816]{2,1,0:T(8,128)(2,1)S(1)}, u32[]{:S(2)}, u32[]{:S(2)}) collective-permute-start(bf16[4,32,2816]{2,1,0:T(8,128)(2,1)S(1)} %fusion.25), channel_id=1, source_target_pairs={{0,2},{1,3},{2,0},{3,1},{4,6},{5,7},{6,4},{7,5},{8,10},{9,11},{10,... | collective-permute-start | bytes 2162696 | tf_op jit(solution)/shard_map/ppermute | solution.py:39
  457.7 18.4 %collective-permute-start.52 = (bf16[4,32,2816]{2,1,0:T(8,128)(2,1)S(1)}, bf16[4,32,2816]{2,1,0:T(8,128)(2,1)S(1)}, u32[]{:S(2)}, u32[]{:S(2)}) collective-permute-start(bf16[4,32,2816]{2,1,0:T(8,128)(2,1)S(1)} %fusion.24), channel_id=1, source_target_pairs={{0,4},{1,5},{2,6},{3,7},{4,0},{5,1},{6,2},{7,3},{8,12},{9,13},{10,... | collective-permute-start | bytes 2162696 | tf_op jit(solution)/shard_map/ppermute | solution.py:39
  479.2 39.0 %collective-permute-start.83 = (bf16[32,5632]{1,0:T(8,128)(2,1)}, bf16[32,5632]{1,0:T(8,128)(2,1)}, u32[]{:S(2)}, u32[]{:S(2)}) collective-permute-start(bf16[32,5632]{1,0:T(8,128)(2,1)} %get-tuple-element.210), channel_id=1, source_target_pairs={{0,8},{1,9},{2,10},{3,11},{4,12},{5,13},{6,14},{7,15},{8,0},{9,1},... | collective-permute-start | bytes 1081352 | tf_op jit(solution)/shard_map/ppermute | solution.py:39
  480.3 38.9 %collective-permute-start.84 = (bf16[32,5632]{1,0:T(8,128)(2,1)}, bf16[32,5632]{1,0:T(8,128)(2,1)}, u32[]{:S(2)}, u32[]{:S(2)}) collective-permute-start(bf16[32,5632]{1,0:T(8,128)(2,1)} %get-tuple-element.212), channel_id=1, source_target_pairs={{0,16},{1,17},{2,18},{3,19},{4,20},{5,21},{6,22},{7,23},{8,24},{9,... | collective-permute-start | bytes 1081352 | tf_op jit(solution)/shard_map/ppermute | solution.py:39
  480.9 39.9 %collective-permute-start.85 = (bf16[32,5632]{1,0:T(8,128)(2,1)}, bf16[32,5632]{1,0:T(8,128)(2,1)}, u32[]{:S(2)}, u32[]{:S(2)}) collective-permute-start(bf16[32,5632]{1,0:T(8,128)(2,1)} %get-tuple-element.211), channel_id=1, source_target_pairs={{0,24},{1,25},{2,26},{3,27},{4,28},{5,29},{6,30},{7,31},{8,16},{9,... | collective-permute-start | bytes 1081352 | tf_op jit(solution)/shard_map/ppermute | solution.py:39
  489.5 90.8 %collective-permute-start.71 = (bf16[2,2,4,32,1024]{4,3,2,1,0:T(8,128)(2,1)}, bf16[2,2,4,32,1024]{4,3,2,1,0:T(8,128)(2,1)}, u32[]{:S(2)}, u32[]{:S(2)}) collective-permute-start(bf16[2,2,4,32,1024]{4,3,2,1,0:T(8,128)(2,1)} %get-tuple-element.182), channel_id=1, source_target_pairs={{0,1},{1,0},{2,3},{3,2},{4,5},{5,4},{6,7},{7,6},{8,9},{9,8},{10,11... | collective-permute-start | bytes 3145736 | tf_op jit(solution)/shard_map/ppermute | solution.py:39
  496.8 9.4 %collective-permute-start.57 = (f32[278,128]{1,0:T(8,128)S(1)}, f32[278,128]{1,0:T(8,128)S(1)}, u32[]{:S(2)}, u32[]{:S(2)}) collective-permute-start(f32[278,128]{1,0:T(8,128)S(1)} %concatenate.58), channel_id=1, source_target_pairs={{0,1},{1,0},{2,3},{3,2},{4,5},{5,4},{6,7},{7,6},{8,9},{9,8},{10,11... | collective-permute-start | bytes 427016 | tf_op jit(solution)/shard_map/ppermute | solution.py:39
  517.9 28.1 %collective-permute-start.69 = (bf16[2,4,152,512]{3,2,1,0:T(8,128)(2,1)S(1)}, bf16[2,4,152,512]{3,2,1,0:T(8,128)(2,1)S(1)}, u32[]{:S(2)}, u32[]{:S(2)}) collective-permute-start(bf16[2,4,152,512]{3,2,1,0:T(8,128)(2,1)S(1)} %fusion.18), channel_id=1, source_target_pairs={{0,4},{1,5},{2,6},{3,7},{4,0},{5,1},{6,2},{7,3},{8,12},{9,13},{10,... | collective-permute-start | bytes 3735560 | tf_op jit(solution)/shard_map/ppermute | solution.py:39
  519.2 12.7 %collective-permute-start.61 = (f32[278,128]{1,0:T(8,128)S(1)}, f32[278,128]{1,0:T(8,128)S(1)}, u32[]{:S(2)}, u32[]{:S(2)}) collective-permute-start(f32[278,128]{1,0:T(8,128)S(1)} %add.246), channel_id=1, source_target_pairs={{0,16},{1,17},{2,18},{3,19},{4,20},{5,21},{6,22},{7,23},{8,24},{9,... | collective-permute-start | bytes 427016 | tf_op jit(solution)/shard_map/ppermute | solution.py:39
  520.8 12.5 %collective-permute-start.62 = (f32[278,128]{1,0:T(8,128)S(1)}, f32[278,128]{1,0:T(8,128)S(1)}, u32[]{:S(2)}, u32[]{:S(2)}) collective-permute-start(f32[278,128]{1,0:T(8,128)S(1)} %add.246), channel_id=1, source_target_pairs={{0,24},{1,25},{2,26},{3,27},{4,28},{5,29},{6,30},{7,31},{8,16},{9,... | collective-permute-start | bytes 427016 | tf_op jit(solution)/shard_map/ppermute | solution.py:39
  525.1 55.2 %collective-permute-start.72 = (bf16[2,2,4,32,1024]{4,3,2,1,0:T(8,128)(2,1)S(1)}, bf16[2,2,4,32,1024]{4,3,2,1,0:T(8,128)(2,1)}, u32[]{:S(2)}, u32[]{:S(2)}) collective-permute-start(bf16[2,2,4,32,1024]{4,3,2,1,0:T(8,128)(2,1)S(1)} %copy-done.28), channel_id=1, source_target_pairs={{0,1},{1,0},{2,3},{3,2},{4,5},{5,4},{6,7},{7,6},{8,9},{9,8},{10,11... | collective-permute-start | bytes 3145736 | tf_op jit(solution)/shard_map/ppermute | solution.py:39
  531.8 29.7 %collective-permute-start.65 = (bf16[2,4,152,512]{3,2,1,0:T(8,128)(2,1)S(1)}, bf16[2,4,152,512]{3,2,1,0:T(8,128)(2,1)S(1)}, u32[]{:S(2)}, u32[]{:S(2)}) collective-permute-start(bf16[2,4,152,512]{3,2,1,0:T(8,128)(2,1)S(1)} %fusion.17), channel_id=1, source_target_pairs={{0,2},{1,3},{2,0},{3,1},{4,6},{5,7},{6,4},{7,5},{8,10},{9,11},{10,... | collective-permute-start | bytes 3735560 | tf_op jit(solution)/shard_map/ppermute | solution.py:39
  547.4 21.4 %collective-permute-start.70 = (bf16[4,152,512]{2,1,0:T(8,128)(2,1)}, bf16[4,152,512]{2,1,0:T(8,128)(2,1)}, u32[]{:S(2)}, u32[]{:S(2)}) collective-permute-start(bf16[4,152,512]{2,1,0:T(8,128)(2,1)} %fusion.30), channel_id=1, source_target_pairs={{0,2},{1,3},{2,0},{3,1},{4,6},{5,7},{6,4},{7,5},{8,10},{9,11},{10,... | collective-permute-start | bytes 1867784 | tf_op jit(solution)/shard_map/ppermute | solution.py:39
  563.7 15.2 %collective-permute-start.66 = (bf16[4,152,512]{2,1,0:T(8,128)(2,1)}, bf16[4,152,512]{2,1,0:T(8,128)(2,1)}, u32[]{:S(2)}, u32[]{:S(2)}) collective-permute-start(bf16[4,152,512]{2,1,0:T(8,128)(2,1)} %fusion.29), channel_id=1, source_target_pairs={{0,4},{1,5},{2,6},{3,7},{4,0},{5,1},{6,2},{7,3},{8,12},{9,13},{10,... | collective-permute-start | bytes 1867784 | tf_op jit(solution)/shard_map/ppermute | solution.py:39
  582.0 10.8 %collective-permute-start.75 = (bf16[2,4,32,1024]{3,2,1,0:T(8,128)(2,1)S(1)}, bf16[2,4,32,1024]{3,2,1,0:T(8,128)(2,1)S(1)}, u32[]{:S(2)}, u32[]{:S(2)}) collective-permute-start(bf16[2,4,32,1024]{3,2,1,0:T(8,128)(2,1)S(1)} %fusion.35), channel_id=1, source_target_pairs={{0,4},{1,5},{2,6},{3,7},{4,0},{5,1},{6,2},{7,3},{8,12},{9,13},{10,... | collective-permute-start | bytes 1572872 | tf_op jit(solution)/shard_map/ppermute | solution.py:39
  585.3 9.2 %collective-permute-start.73 = (bf16[2,4,32,1024]{3,2,1,0:T(8,128)(2,1)S(1)}, bf16[2,4,32,1024]{3,2,1,0:T(8,128)(2,1)S(1)}, u32[]{:S(2)}, u32[]{:S(2)}) collective-permute-start(bf16[2,4,32,1024]{3,2,1,0:T(8,128)(2,1)S(1)} %fusion.34), channel_id=1, source_target_pairs={{0,2},{1,3},{2,0},{3,1},{4,6},{5,7},{6,4},{7,5},{8,10},{9,11},{10,... | collective-permute-start | bytes 1572872 | tf_op jit(solution)/shard_map/ppermute | solution.py:39
  587.9 12.0 %collective-permute-start.80 = (bf16[152,1024]{1,0:T(8,128)(2,1)S(1)}, bf16[152,1024]{1,0:T(8,128)(2,1)S(1)}, u32[]{:S(2)}, u32[]{:S(2)}) collective-permute-start(bf16[152,1024]{1,0:T(8,128)(2,1)S(1)} %get-tuple-element.217), channel_id=1, source_target_pairs={{0,8},{1,9},{2,10},{3,11},{4,12},{5,13},{6,14},{7,15},{8,0},{9,1},... | collective-permute-start | bytes 933896 | tf_op jit(solution)/shard_map/ppermute | solution.py:39
  587.9 18.5 %collective-permute-start.81 = (bf16[152,1024]{1,0:T(8,128)(2,1)S(1)}, bf16[152,1024]{1,0:T(8,128)(2,1)S(1)}, u32[]{:S(2)}, u32[]{:S(2)}) collective-permute-start(bf16[152,1024]{1,0:T(8,128)(2,1)S(1)} %get-tuple-element.219), channel_id=1, source_target_pairs={{0,16},{1,17},{2,18},{3,19},{4,20},{5,21},{6,22},{7,23},{8,24},{9,... | collective-permute-start | bytes 933896 | tf_op jit(solution)/shard_map/ppermute | solution.py:39
  590.4 16.0 %collective-permute-start.82 = (bf16[152,1024]{1,0:T(8,128)(2,1)S(1)}, bf16[152,1024]{1,0:T(8,128)(2,1)S(1)}, u32[]{:S(2)}, u32[]{:S(2)}) collective-permute-start(bf16[152,1024]{1,0:T(8,128)(2,1)S(1)} %get-tuple-element.218), channel_id=1, source_target_pairs={{0,24},{1,25},{2,26},{3,27},{4,28},{5,29},{6,30},{7,31},{8,16},{9,... | collective-permute-start | bytes 933896 | tf_op jit(solution)/shard_map/ppermute | solution.py:39
  592.9 14.4 %collective-permute-start.76 = (bf16[4,32,1024]{2,1,0:T(8,128)(2,1)S(1)}, bf16[4,32,1024]{2,1,0:T(8,128)(2,1)S(1)}, u32[]{:S(2)}, u32[]{:S(2)}) collective-permute-start(bf16[4,32,1024]{2,1,0:T(8,128)(2,1)S(1)} %fusion.55), channel_id=1, source_target_pairs={{0,2},{1,3},{2,0},{3,1},{4,6},{5,7},{6,4},{7,5},{8,10},{9,11},{10,... | collective-permute-start | bytes 786440 | tf_op jit(solution)/shard_map/ppermute | solution.py:39
  594.8 12.7 %collective-permute-start.74 = (bf16[4,32,1024]{2,1,0:T(8,128)(2,1)S(1)}, bf16[4,32,1024]{2,1,0:T(8,128)(2,1)S(1)}, u32[]{:S(2)}, u32[]{:S(2)}) collective-permute-start(bf16[4,32,1024]{2,1,0:T(8,128)(2,1)S(1)} %fusion.54), channel_id=1, source_target_pairs={{0,4},{1,5},{2,6},{3,7},{4,0},{5,1},{6,2},{7,3},{8,12},{9,13},{10,... | collective-permute-start | bytes 786440 | tf_op jit(solution)/shard_map/ppermute | solution.py:39
  607.6 8.8 %collective-permute-start.77 = (bf16[32,2048]{1,0:T(8,128)(2,1)S(1)}, bf16[32,2048]{1,0:T(8,128)(2,1)S(1)}, u32[]{:S(2)}, u32[]{:S(2)}) collective-permute-start(bf16[32,2048]{1,0:T(8,128)(2,1)S(1)} %get-tuple-element.244), channel_id=1, source_target_pairs={{0,8},{1,9},{2,10},{3,11},{4,12},{5,13},{6,14},{7,15},{8,0},{9,1},... | collective-permute-start | bytes 393224 | tf_op jit(solution)/shard_map/ppermute | solution.py:39
  (123 other events, 964.1 us)

commit v3 on v2

--- a/solution.py
+++ b/solution.py
@@ -21,6 +21,8 @@
 GROUP = 8
 HALO = 8
 EXTRA = 16
+SMALL = 40
+PER_HEAD = 2 * DK + DV
 
 
 def chip_axes():
@@ -59,54 +61,63 @@
     return jnp.stack([(mine // stride) % size for size, stride in chip_axes()]).astype(jnp.int32)
 
 
-def placed_blocks(pieces, one, two, cuts):
+def placed_blocks(sources, one, two, cuts):
     axes = chip_axes()
     sizes = tuple(size for size, _ in axes)
-    depth, sides, mine = sizes[0], sizes[one], coordinates()
-    rows, columns = pieces[0].shape[2:]
-
-    def target(step, side, me):
+    depth, mine = sizes[0], coordinates()
+    (rows, columns), kind = sources[0][0].shape[3:], sources[0][0].dtype
+
+    def target(core, second, first, me):
         spot = [0, 0, 0, 0]
-        spot[one] = jnp.bitwise_xor(side, me[one])
-        spot[two] = jnp.bitwise_xor(step // sizes[3], me[two])
-        spot[3] = jnp.bitwise_xor(step % sizes[3], me[3])
+        spot[one] = jnp.bitwise_xor(first, me[one])
+        spot[two] = jnp.bitwise_xor(second, me[two])
+        spot[3] = jnp.bitwise_xor(core, me[3])
         return tuple(spot) + (0, 0)
 
-    def source(which):
-        def index(step, side, me):
-            before = jnp.where(step < which, 0, sides - 1)
-            return (jnp.where(step == which, side, before), 0, 0, 0)
+    def source(mine_core, base, extent):
+        def index(core, second, first, me):
+            step = core * sizes[two] + second - mine_core * sizes[two] - base
+            early, late = step < 0, step >= extent
+            held = jnp.where(early, 0, jnp.where(late, extent - 1, step))
+            return (
+                held,
+                jnp.where(early, 0, jnp.where(late, sizes[one] - 1, first)),
+                0,
+                0,
+                0,
+            )
 
         return index
 
     def kernel(me, *refs):
-        sources, outs = refs[: len(pieces)], refs[len(pieces) :]
-        step = pl.program_id(0)
-        for which, piece in enumerate(sources):
-
-            @pl.when(step == which)
+        pieces, outs = refs[: len(sources)], refs[len(sources) :]
+        step = pl.program_id(0) * sizes[two] + pl.program_id(1)
+        for piece, (array, core, base) in zip(pieces, sources):
+            begin = core * sizes[two] + base
+
+            @pl.when((step >= begin) & (step < begin + array.shape[0]))
             def _():
                 for level in range(depth):
-                    block, start = piece[0, level], 0
+                    block, start = piece[0, 0, level], 0
                     for out, cut in zip(outs, cuts):
                         out[jnp.bitwise_xor(me[0], level), 0, 0, 0] = block[start : start + cut]
                         start += cut
 
     found = pl.pallas_call(
         kernel,
-        out_shape=[jax.ShapeDtypeStruct(sizes + (cut, columns), pieces[0].dtype) for cut in cuts],
+        out_shape=[jax.ShapeDtypeStruct(sizes + (cut, columns), kind) for cut in cuts],
         grid_spec=pltpu.PrefetchScalarGridSpec(
             num_scalar_prefetch=1,
-            grid=(len(pieces), sides),
+            grid=(2, sizes[two], sizes[one]),
             in_specs=[
-                pl.BlockSpec((1, depth, rows, columns), source(which))
-                for which in range(len(pieces))
+                pl.BlockSpec((1, 1, depth, rows, columns), source(core, base, array.shape[0]))
+                for array, core, base in sources
             ],
             out_specs=[pl.BlockSpec((depth, 1, 1, 1, cut, columns), target) for cut in cuts],
         ),
         compiler_params=pltpu.CompilerParams(vmem_limit_bytes=40 * 2**20),
         cost_estimate=takes(1.0 + rows * columns * 5e-5),
-    )(mine, *pieces)
+    )(mine, *[array for array, _, _ in sources])
     return [array.reshape(-1, columns) for array in found]
 
 
@@ -114,41 +125,117 @@
     return lax.optimization_barrier(values)
 
 
-def gather_all(groups):
-    axis_z, axis_y, axis_x, axis_c = chip_axes()
-    near = []
-    for shards in groups:
-        shard = jnp.concatenate(shards, axis=0) if len(shards) > 1 else shards[0]
-        if near:
-            shard, near[-1][1] = together(shard, near[-1][1])
-        near.append(spread(shard, axis_z))
-    crossed, gathered = None, []
-    for pieces in near:
-        if crossed is not None:
-            pieces, crossed = together(pieces, crossed)
-            gathered.append(crossed)
-        half = pieces[0].shape[1] // 2
-        stacked = jnp.stack(pieces)
-        sides = [
-            jnp.stack(spread(stacked[..., :half], axis_x)),
-            jnp.stack(spread(stacked[..., half:], axis_y)),
-        ]
-        crossed = [spread(sides[0], axis_y), spread(sides[1], axis_x)]
-    gathered.append(crossed)
-    full = []
-    for shards, crossed in zip(groups, gathered):
-        cuts, halves = [shard.shape[0] for shard in shards], []
-        for pieces, one, two in zip(crossed, (2, 1), (1, 2)):
-            pieces = [copy for piece in pieces for copy in spread(piece, axis_c)]
-            halves.append(placed_blocks(pieces, one, two, cuts))
-        full.extend(zip(*halves))
-    return full
-
-
-def grad_products(left, right_a, right_b):
+def gather_levels(shard):
+    return spread(shard, chip_axes()[0])
+
+
+def gather_first(levels):
+    half = levels[0].shape[1] // 2
+    stacked = jnp.stack(levels)
+    axes = chip_axes()
+    return [spread(stacked[..., :half], axes[2]), spread(stacked[..., half:], axes[1])]
+
+
+def gather_second(sides):
+    axes = chip_axes()
+    return [spread(jnp.stack(sides[0]), axes[1]), spread(jnp.stack(sides[1]), axes[2])]
+
+
+def gather_cores(crossed):
+    found = []
+    for pieces in crossed:
+        own = jnp.stack(pieces)
+        found.append([own, swapped(own, 1)])
+    return found
+
+
+def gather_done(pairs, cuts):
+    halves = [
+        placed_blocks([(own, 0, 0), (other, 1, 0)], one, two, cuts)
+        for (own, other), one, two in zip(pairs, (2, 1), (1, 2))
+    ]
+    return list(zip(*halves))
+
+
+def core_sources(crossed, early):
+    halves = []
+    for pieces, before in zip(crossed, early):
+        sources = []
+        for step, piece in enumerate(pieces):
+            other = before if step == 0 else swapped(piece, 1)
+            sources.extend([(piece[None], 0, step), (other[None], 1, step)])
+        halves.append(sources)
+    return halves
+
+
+def assemble(held, refs, sources, me, one, two):
+    for ref, (array, core, base) in zip(refs, sources):
+        for second in range(array.shape[0]):
+            for first in range(array.shape[1]):
+                for level in range(array.shape[2]):
+                    spot = [jnp.bitwise_xor(me[0], level), 0, 0, jnp.bitwise_xor(me[3], core)]
+                    spot[one] = jnp.bitwise_xor(me[one], first)
+                    spot[two] = jnp.bitwise_xor(me[two], base + second)
+                    held[tuple(spot)] = ref[second, first, level]
+    return held[...].reshape(-1, held.shape[-1])
+
+
+def tile_spec(array, tile, index):
+    return pl.BlockSpec(array.shape[:4] + (tile,), index)
+
+
+def projected(rows, sources_a, sources_b):
+    sizes, mine = tuple(size for size, _ in chip_axes()), coordinates()
+    tokens, width = rows.shape
+    block_rows, half = sources_a[0][0].shape[3:]
+    tile = 256
+    tiles = half // tile
+
+    def kernel(me, row_ref, *refs):
+        refs_a = refs[: len(sources_a)]
+        refs_b = refs[len(sources_a) : -2]
+        out, held = refs[-2:]
+
+        @pl.when(pl.program_id(0) == 0)
+        def _():
+            assemble(held, refs_a, sources_a, me, 2, 1)
+
+        @pl.when(pl.program_id(0) == 1)
+        def _():
+            assemble(held, refs_b, sources_b, me, 1, 2)
+
+        full = held[...].reshape(width, tile)
+        out[...] = bf_dot(row_ref[...], full).astype(jnp.bfloat16)
+
+    def at_a(part, i, me):
+        return (0, 0, 0, 0, jnp.where(part == 0, i, tiles - 1))
+
+    def at_b(part, i, me):
+        return (0, 0, 0, 0, jnp.where(part == 0, 0, i))
+
+    return pl.pallas_call(
+        kernel,
+        out_shape=jax.ShapeDtypeStruct((tokens, 2 * half), jnp.bfloat16),
+        grid_spec=pltpu.PrefetchScalarGridSpec(
+            num_scalar_prefetch=1,
+            grid=(2, tiles),
+            in_specs=[pl.BlockSpec((tokens, width), lambda part, i, me: (0, 0))]
+            + [tile_spec(array, tile, at_a) for array, _, _ in sources_a]
+            + [tile_spec(array, tile, at_b) for array, _, _ in sources_b],
+            out_specs=pl.BlockSpec((tokens, tile), lambda part, i, me: (0, part * tiles + i)),
+            scratch_shapes=[pltpu.VMEM(sizes + (block_rows, tile), jnp.bfloat16)],
+        ),
+        compiler_params=pltpu.CompilerParams(vmem_limit_bytes=40 * 2**20),
+        cost_estimate=takes(6),
+    )(mine, rows, *[array for array, _, _ in sources_a + sources_b])
+
+
+def grad_products(left, right_a, right_b=None):
     sizes = tuple(size for size, _ in chip_axes())
     strides = tuple(stride for _, stride in chip_axes())
     (tokens, features), columns = left.shape, right_a.shape[1]
+    if right_b is None:
+        columns = columns // 2
     count, mine = lax.axis_size("seq"), coordinates()
     rows = features // count
     tile = 512 if columns % 512 == 0 and features <= 1024 else 256
@@ -160,27 +247,33 @@
         def _():
             flipped[...] = left_ref[...].T
 
-        even = me[3] == 0
-        for right, away, keep, order in (
-            (a_ref, away_a, keep_a, (2, 1, 0)),
-            (b_ref, away_b, keep_b, (1, 2, 0)),
-        ):
-            for part in range(chunks):
-                full = jnp.dot(
-                    flipped[part * chunk : (part + 1) * chunk],
-                    right[...],
-                    preferred_element_type=jnp.float32,
-                )
-                for start in range(0, chunk, 2 * rows):
-                    device = (part * chunk + start) // rows
-                    spot = tuple(
-                        jnp.bitwise_xor(device // strides[axis] % sizes[axis], me[axis])
-                        for axis in order
+        def products(odd):
+            for right, away, keep, order in (
+                (a_ref, away_a, keep_a, (2, 1, 0)),
+                (b_ref, away_b, keep_b, (1, 2, 0)),
+            ):
+                for part in range(chunks):
+                    full = jnp.dot(
+                        flipped[part * chunk : (part + 1) * chunk],
+                        right[...],
+                        preferred_element_type=jnp.float32,
                     )
-                    low = full[start : start + rows]
-                    high = full[start + rows : start + 2 * rows]
-                    away[spot] = jnp.where(even, high, low).astype(jnp.bfloat16)
-                    keep[spot] = jnp.where(even, low, high).astype(jnp.bfloat16)
+                    for start in range(0, chunk, rows):
+                        device = (part * chunk + start) // rows
+                        spot = tuple(
+                            jnp.bitwise_xor(device // strides[axis] % sizes[axis], me[axis])
+                            for axis in order
+                        )
+                        target = keep if device % 2 == odd else away
+                        target[spot] = full[start : start + rows].astype(jnp.bfloat16)
+
+        @pl.when(me[3] == 0)
+        def _():
+            products(0)
+
+        @pl.when(me[3] == 1)
+        def _():
+            products(1)
 
     def result(one, two):
         shape = (sizes[one], sizes[two], sizes[0], rows)
@@ -190,7 +283,8 @@
         )
 
     results = [result(2, 1), result(2, 1), result(1, 2), result(1, 2)]
-    right_spec = pl.BlockSpec((tokens, tile), lambda i, me: (0, i))
+    skip = columns // tile if right_b is None else 0
+    right_b = right_a if right_b is None else right_b
     return pl.pallas_call(
         kernel,
         out_shape=[shape for shape, _ in results],
@@ -199,8 +293,8 @@
             grid=(columns // tile,),
             in_specs=[
                 pl.BlockSpec((tokens, features), lambda i, me: (0, 0)),
-                right_spec,
-                right_spec,
+                pl.BlockSpec((tokens, tile), lambda i, me: (0, i)),
+                pl.BlockSpec((tokens, tile), lambda i, me: (0, i + skip)),
             ],
             out_specs=[spec for _, spec in results],
             scratch_shapes=[pltpu.VMEM((features, tokens), jnp.bfloat16)],
@@ -210,46 +304,239 @@
     )(mine, left, right_a, right_b)
 
 
-def fold(block, axis):
-    total = block[0].astype(jnp.float32)
-    for step in range(1, axis[0]):
-        part = swapped(block[step].astype(jnp.bfloat16), step * axis[1])
-        total = total + part.astype(jnp.float32)
-    return total
-
-
-def cores_summed(left, right_a, right_b):
-    away_a, keep_a, away_b, keep_b = grad_products(left, right_a, right_b)
-    return [keep_a, swapped(away_a, 1), keep_b, swapped(away_b, 1)]
-
-
-def sides_summed(products):
+def total_of(groups):
+    parts = []
+    for refs, lead in groups:
+        rows = [ref[(0,) * lead].astype(jnp.float32) for ref in refs]
+        parts.append(jnp.concatenate(rows, axis=0) if len(rows) > 1 else rows[0])
+    return sum(parts[1:], parts[0])
+
+
+def flat_terms(terms):
+    return [(since, arrays) for since, group in enumerate(terms) for arrays in group]
+
+
+def regrouped(refs, flat):
+    groups, at = [], 0
+    for since, arrays in flat:
+        groups.append((refs[at : at + len(arrays)], since))
+        at += len(arrays)
+    return groups, at
+
+
+def phase_sums(pair, phase, step):
+    flats = [flat_terms(terms) for terms in pair]
+    depth = chip_axes()[0][0]
+    second = chip_axes()[1][0] if phase == 0 else 1
+    rows = sum(array.shape[-2] for array in flats[0][0][1])
+    columns = flats[0][0][1][0].shape[-1]
+    lead = 2 - phase
+
+    def index(since):
+        def found(i, j):
+            spot = [0 if dim < phase else step if dim == phase else (i, j)[dim - 1] for dim in range(3)]
+            return tuple(spot[since:]) + (0, 0)
+
+        return found
+
+    def kernel(*refs):
+        ins, outs = refs[:-2], refs[-2:]
+        at = 0
+        for flat, out in zip(flats, outs):
+            groups, used = regrouped(ins[at:], flat)
+            at += used
+            total = total_of([(part, 3 - since) for part, since in groups])
+            out[(0,) * lead] = total.astype(jnp.bfloat16)
+
+    arrays = [(array, since) for flat in flats for since, group in flat for array in group]
+    shape = ((second, depth) if phase == 0 else (depth,)) + (rows, columns)
+    out_spec = pl.BlockSpec(
+        (1,) * lead + (rows, columns), lambda i, j: ((i, j) if phase == 0 else (j,)) + (0, 0)
+    )
+    return pl.pallas_call(
+        kernel,
+        out_shape=[jax.ShapeDtypeStruct(shape, jnp.bfloat16)] * 2,
+        grid=(second, depth),
+        in_specs=[
+            pl.BlockSpec((1,) * (3 - since) + array.shape[-2:], index(since))
+            for array, since in arrays
+        ],
+        out_specs=[out_spec] * 2,
+        compiler_params=pltpu.CompilerParams(vmem_limit_bytes=32 * 2**20),
+        cost_estimate=takes(3),
+    )(*[array for array, _ in arrays])
+
+
+def level_sums(pair):
+    flats = [flat_terms(terms) for terms in pair]
+    depth = chip_axes()[0][0]
+    rows = sum(array.shape[-2] for array in flats[0][0][1])
+    columns = flats[0][0][1][0].shape[-1]
+
+    def kernel(*refs):
+        ins, outs = refs[:-depth], refs[-depth:]
+        at = 0
+        for side, flat in enumerate(flats):
+            groups, used = regrouped(ins[at:], flat)
+            at += used
+            cut = slice(side * columns, (side + 1) * columns)
+            for level in range(depth):
+                parts = []
+                for part, since in groups:
+                    spot = (0,) * (2 - since) + (level,)
+                    values = [ref[spot].astype(jnp.float32) for ref in part]
+                    parts.append(
+                        jnp.concatenate(values, axis=0) if len(values) > 1 else values[0]
+                    )
+                total = sum(parts[1:], parts[0])
+                outs[level][:, cut] = total.astype(outs[level].dtype)
+
+    arrays = [(array, since) for flat in flats for since, group in flat for array in group]
+
+    def spec(array, since):
+        lead = (1,) * (2 - since) + (depth,)
+        return pl.BlockSpec(lead + array.shape[-2:], lambda i: (0,) * (len(lead) + 2))
+
+    shape = (rows, 2 * columns)
+    return pl.pallas_call(
+        kernel,
+        out_shape=[jax.ShapeDtypeStruct(shape, jnp.float32)]
+        + [jax.ShapeDtypeStruct(shape, jnp.bfloat16)] * (depth - 1),
+        grid=(1,),
+        in_specs=[spec(array, since) for array, since in arrays],
+        out_specs=[pl.BlockSpec(shape, lambda i: (0, 0))] * depth,
+        compiler_params=pltpu.CompilerParams(vmem_limit_bytes=40 * 2**20),
+        cost_estimate=takes(3),
+    )(*[array for array, _ in arrays])
+
+
+def cores_send(products):
+    found = []
+    for keep, which in ((1, 0), (3, 2)):
+        aways = [part[which] for part in products]
+        away = jnp.concatenate(aways, axis=3) if len(aways) > 1 else aways[0]
+        found.append([[[part[keep] for part in products], [swapped(away, 1)]]])
+    return found
+
+
+def phase_send(pair, phase):
     axes = chip_axes()
-    products = [[piece.astype(jnp.float32) for piece in pieces] for pieces in products]
-    end_a = jnp.concatenate([pieces[0] + pieces[1] for pieces in products], axis=3)
-    end_b = jnp.concatenate([pieces[2] + pieces[3] for pieces in products], axis=3)
-    ends = [fold(end_a, axes[2]), fold(end_b, axes[1])]
-    return [fold(ends[0], axes[1]), fold(ends[1], axes[2])]
-
-
-def levels_summed(ends):
-    return fold(jnp.concatenate(ends, axis=-1), chip_axes()[0])
-
-
-def small_sum(value):
-    for axis in chip_axes()[::-1]:
-        value = sum(spread(value, axis))
-    return value
-
-
-def exchanged(pieces):
-    shape = pieces.shape
+    size = axes[2][0]
+    received = [[], []]
+    for step in range(1, size):
+        for side, part in enumerate(phase_sums(pair, phase, step)):
+            stride = axes[((2, 1), (1, 2))[side][phase]][1]
+            received[side].append([swapped(part, step * stride)])
+    return [terms + [parts] for terms, parts in zip(pair, received)]
+
+
+def levels_send(pair):
+    own, *parts = level_sums(pair)
+    stride = chip_axes()[0][1]
+    return own, [swapped(part, (step + 1) * stride) for step, part in enumerate(parts)]
+
+
+def reduced(own, found):
+    return sum((part.astype(jnp.float32) for part in found), own)
+
+
+def small_packed(logit_grad, lowrank, w_high, normed, tap_grads, bias, head_gain, ffn_gain):
+    tokens, keys = logit_grad.shape
+    width, rank = normed.shape[1], w_high.shape[0]
+
+    def kernel(grad_ref, low_ref, high_ref, normed_ref, taps, bias_ref, head, ffn, out, low_grad):
+        grad = grad_ref[...]
+        back = split_dot(grad, high_ref[...], NT).astype(jnp.bfloat16)
+        low_grad[...] = back
+        out[:rank] = lax.dot_general(
+            back, normed_ref[...], (TN, ((), ())), preferred_element_type=jnp.float32
+        )
+        tap = jnp.sum(taps[...], axis=0)
+        out[rank : rank + CONV] = tap[:, :width]
+        out[rank + CONV : rank + 2 * CONV] = tap[:, width:]
+        high = split_dot(low_ref[...], grad, TN)
+        out[24:32, :keys] = high[:8]
+        out[24:32, keys:] = high[8:]
+        out[32:40] = jnp.zeros((8, width), jnp.float32)
+        out[32:33, :keys] = jnp.sum(bias_ref[...], axis=0, keepdims=True)
+        gains = [jnp.sum(head[:, h, 0], axis=0, keepdims=True) for h in range(HEADS)]
+        out[32:33, keys : keys + DV] = sum(gains)
+        out[33:34] = ffn[...]
+
+    return pl.pallas_call(
+        kernel,
+        out_shape=[
+            jax.ShapeDtypeStruct((SMALL, width), jnp.float32),
+            jax.ShapeDtypeStruct((tokens, rank), jnp.bfloat16),
+        ],
+        compiler_params=pltpu.CompilerParams(vmem_limit_bytes=32 * 2**20),
+        cost_estimate=takes(4),
+    )(logit_grad, lowrank, w_high, normed, tap_grads, bias, head_gain, ffn_gain)
+
+
+def small_unpacked(parts, keys, rank):
+    width = parts[0].shape[1]
+
+    def kernel(*refs):
+        ins, (norm, conv, low, high, bias, head, ffn) = refs[: len(parts)], refs[len(parts) :]
+        total = sum(ref[...] for ref in ins)
+        low[...] = total[:rank]
+        for h in range(HEADS):
+            side, at = divmod(h * PER_HEAD, width)
+            block = total[rank + side * CONV : rank + (side + 1) * CONV]
+            conv[:, h * DK : (h + 1) * DK] = block[:, at : at + DK]
+            conv[:, keys + h * DK : keys + (h + 1) * DK] = block[:, at + DK : at + 2 * DK]
+            conv[:, 2 * keys + h * DV : 2 * keys + (h + 1) * DV] = block[
+                :, at + 2 * DK : at + PER_HEAD
+            ]
+        high[:8] = total[24:32, :keys]
+        high[8:] = total[24:32, keys:]
+        bias[...] = total[32:33, :keys]
+        head[...] = total[32:33, keys : keys + DV]
+        ffn[...] = total[33:34]
+        norm[...] = total[34:35]
+
+    shapes = ((1, width), (CONV, 2 * width), (rank, width), (rank, keys))
+    shapes += ((1, keys), (1, DV), (1, width))
+    return pl.pallas_call(
+        kernel,
+        out_shape=[jax.ShapeDtypeStruct(shape, jnp.float32) for shape in shapes],
+        cost_estimate=takes(2),
+    )(*parts)
+
+
+def by_head(array):
+    lead, (keys, values) = array.shape[:-1], (HEADS * DK, HEADS * DV)
+    parts = [
+        part.reshape(lead + (HEADS, -1))
+        for part in (array[..., :keys], array[..., keys : 2 * keys], array[..., 2 * keys :])
+    ]
+    return jnp.concatenate(parts, axis=-1).reshape(lead + (2 * keys + values,))
+
+
+def by_kind(array):
+    lead = array.shape[:-1]
+    array = array.reshape(lead + (HEADS, -1))
+    parts = (array[..., :DK], array[..., DK : 2 * DK], array[..., 2 * DK :])
+    return jnp.concatenate([part.reshape(lead + (-1,)) for part in parts], axis=-1)
+
+
+def exchange_step(pieces, at, mask):
+    kept = lax.index_in_dim(pieces, 0, at, False)
+    return [kept, swapped(lax.index_in_dim(pieces, 1, at, False), mask)]
+
+
+def exchanged(pieces, fillers=((), (), ())):
+    shape, filled = pieces.shape, []
     pieces = pieces.reshape((2, 2, 2) + shape[1:])
-    kept, sent = pieces[:, :, 0], pieces[:, :, 1]
-    pieces = jnp.stack([kept, swapped(sent, 1)], axis=2)
-    kept, sent = pieces[:, 0], pieces[:, 1]
-    pieces = jnp.stack([kept, swapped(sent, 2)], axis=1)
-    return jnp.stack([pieces[0], swapped(pieces[1], 4)]).reshape(shape)
+    for at, mask, filler in zip((2, 1, 0), (1, 2, 4), fillers):
+        pair = exchange_step(pieces, at, mask)
+        if filler:
+            values = filler[0](*filled[-1:])
+            pair, values = together(pair, values)
+            filled.append(values)
+        pieces = jnp.stack(pair, axis=at)
+    return pieces.reshape(shape), filled
 
 
 def column(row):
@@ -296,13 +583,6 @@
     )(place, got, *extra)
 
 
-def carried_over(place, pieces, backward):
-    got = exchanged(pieces)
-    total = composed(place, got, backward)
-    beyond = shifted(total, -GROUP if backward else GROUP)
-    return exchanged(composed(place, got, backward, beyond))
-
-
 def split_dot(left, right, dims):
     dims = (dims, ((), ()))
     left_high, right_high = left.astype(jnp.bfloat16), right.astype(jnp.bfloat16)
@@ -330,13 +610,17 @@
 NN, NT, TN = ((1,), (0,)), ((1,), (1,)), ((0,), (0,))
 
 
-def conv_in(piece, taps, pos, starts, block_len):
-    wide = piece[0].astype(jnp.float32)
+def activations(block, taps, starts, first, block_len):
+    pos = first + lax.broadcasted_iota(jnp.int32, (block_len, 1), 0)
+    wide = block[0].astype(jnp.float32)
     total = taps[0:1, :] * wide[HALO:]
     for tap in range(1, CONV):
         usable = (pos - tap >= starts).astype(jnp.float32)
         total = total + taps[tap : tap + 1, :] * wide[HALO - tap : HALO - tap + block_len] * usable
-    return wide, total
+    sig = jax.nn.sigmoid(total)
+    active = total * sig
+    query, key, value = active[:, :DK], active[:, DK : 2 * DK], active[:, 2 * DK :]
+    return pos, (wide, total, sig), query * DK ** (-0.5), key, value
 
 
 def decays(logit):
@@ -392,25 +676,10 @@
     )
 
 
-def activations(refs, starts, first, block_len):
-    pos = first + lax.broadcasted_iota(jnp.int32, (block_len, 1), 0)
-    found = []
-    for piece, taps in refs:
-        wide, total = conv_in(piece, taps, pos, starts, block_len)
-        sig = jax.nn.sigmoid(total)
-        found.append((wide, total, sig))
-    return pos, found
-
-
 def mixer_specs(block_len):
-    wide = HALO + block_len
     return [
-        pl.BlockSpec((1, wide, DK), lambda s, h, first: (s, 0, h)),
-        pl.BlockSpec((1, wide, DK), lambda s, h, first: (s, 0, HEADS + h)),
-        pl.BlockSpec((1, wide, DV), lambda s, h, first: (s, 0, HEADS + h)),
-        pl.BlockSpec((CONV, DK), lambda s, h, first: (0, h)),
-        pl.BlockSpec((CONV, DK), lambda s, h, first: (0, HEADS + h)),
-        pl.BlockSpec((CONV, DV), lambda s, h, first: (0, HEADS + h)),
+        pl.BlockSpec((1, HALO + block_len, PER_HEAD), lambda s, h, first: (s, 0, h)),
+        pl.BlockSpec((CONV, PER_HEAD), lambda s, h, first: (0, h)),
         pl.BlockSpec((1, block_len, DK), lambda s, h, first: (s, 0, h)),
         pl.BlockSpec((1, block_len, 1), lambda s, h, first: (s, 0, 0)),
     ]
@@ -451,15 +720,9 @@
 def mixer_forward(first, wide_mixed, conv_weight, logits, starts):
     seq_count, block_len = starts.shape[:2]
 
-    def kernel(
-        first_ref, q_ref, k_ref, v_ref, tq, tk, tv, logit_ref, start_ref, out, reach, state, decay
-    ):
+    def kernel(first_ref, block, taps, logit_ref, start_ref, out, reach, state, decay):
         first, starts = first_ref[0], start_ref[0]
-        pos, found = activations(
-            ((q_ref, tq), (k_ref, tk), (v_ref, tv)), starts, first, block_len
-        )
-        query, key, value = [total * sig for _, total, sig in found]
-        query = query * DK ** (-0.5)
+        pos, _, query, key, value = activations(block, taps, starts, first, block_len)
         log_decay = decays(logit_ref[0])
         running = None
         before = jnp.zeros((1, DK), jnp.float32)
@@ -479,8 +742,7 @@
 
     return launch(
         kernel,
-        (first, wide_mixed, wide_mixed, wide_mixed)
-        + (conv_weight, conv_weight, conv_weight, logits, starts),
+        (first, wide_mixed, conv_weight, logits, starts),
         mixer_specs(block_len),
         (
             ((seq_count, block_len, HEADS * DV), jnp.float32),
@@ -589,18 +851,11 @@
 
 def mixer_backward(first, wide_mixed, conv_weight, logits, starts, out_grad, incoming, outgoing):
     seq_count, block_len = starts.shape[:2]
-    conv_width = wide_mixed.shape[2]
-    wide_len = HALO + block_len
-
-    def kernel(first_ref, q_ref, k_ref, v_ref, tq, tk, tv, logit_ref, start_ref, *refs):
-        grad_ref, in_ref, end_ref, dq, dk, dv, wq, wk, wv, dlogit, bias = refs
+
+    def kernel(first_ref, block, taps, logit_ref, start_ref, *refs):
+        grad_ref, in_ref, end_ref, main, edge, tail, tap_grad, dlogit, bias = refs
         first, starts = first_ref[0], start_ref[0]
-        taps = (tq, tk, tv)
-        pos, found = activations(
-            tuple(zip((q_ref, k_ref, v_ref), taps)), starts, first, block_len
-        )
-        query, key, value = [total * sig for _, total, sig in found]
-        query = query * DK ** (-0.5)
+        pos, found, query, key, value = activations(block, taps, starts, first, block_len)
         logit = logit_ref[0]
         log_decay = decays(logit)
         count = block_len // WIDE
@@ -635,39 +890,34 @@
         grads = [
             jnp.concatenate(parts[::-1], axis=0) for parts in (query_grads, key_grads, value_grads)
         ]
-        grads[0] = grads[0] * DK ** (-0.5)
-        for grad, piece, tap, out, tap_grad in zip(
-            grads, found, taps, (dq, dk, dv), (wq, wk, wv)
-        ):
-            out[0], tap_grad[0] = conv_back(grad, piece, tap, pos, starts, block_len)
+        grads = jnp.concatenate([grads[0] * DK ** (-0.5)] + grads[1:], axis=1)
+        wide_grad, tap_grad[0] = conv_back(grads, found, taps, pos, starts, block_len)
+        edge[0] = wide_grad[:HALO]
+        main[0] = wide_grad[HALO:].astype(jnp.bfloat16)
+        tail[0] = wide_grad[block_len:]
         decay_grad = jnp.concatenate(decay_grads[::-1], axis=0)
         decay_grad = jnp.where(starts < pos, decay_grad, 0.0)
         logit_grad = decay_grad / gate_scale * jax.nn.sigmoid(-logit)
         dlogit[0] = logit_grad
         bias[0, 0] = jnp.sum(logit_grad, axis=0, keepdims=True)
 
-    wide_keys = pl.BlockSpec((1, wide_len, DK), lambda s, h, first: (s, 0, h))
-    wide_values = pl.BlockSpec((1, wide_len, DV), lambda s, h, first: (s, 0, h))
-    tap_keys = pl.BlockSpec((1, CONV, DK), lambda s, h, first: (s, 0, h))
-    tap_values = pl.BlockSpec((1, CONV, DV), lambda s, h, first: (s, 0, h))
-    keys, values = HEADS * DK, HEADS * DV
+    def heads_spec(rows):
+        return pl.BlockSpec((1, rows, PER_HEAD), lambda s, h, first: (s, 0, h))
+
+    width = HEADS * PER_HEAD
     return launch(
         kernel,
-        (first, wide_mixed, wide_mixed, wide_mixed)
-        + (conv_weight, conv_weight, conv_weight, logits, starts)
-        + (out_grad, incoming, outgoing),
+        (first, wide_mixed, conv_weight, logits, starts, out_grad, incoming, outgoing),
         mixer_specs(block_len) + [value_spec(block_len), pair_spec(DK), pair_spec(DK)],
         (
-            ((seq_count, wide_len, keys), jnp.float32),
-            ((seq_count, wide_len, keys), jnp.float32),
-            ((seq_count, wide_len, values), jnp.float32),
-            ((seq_count, CONV, keys), jnp.float32),
-            ((seq_count, CONV, keys), jnp.float32),
-            ((seq_count, CONV, values), jnp.float32),
-            ((seq_count, block_len, keys), jnp.float32),
+            ((seq_count, block_len, width), jnp.bfloat16),
+            ((seq_count, HALO, width), jnp.float32),
+            ((seq_count, HALO, width), jnp.float32),
+            ((seq_count, CONV, width), jnp.float32),
+            ((seq_count, block_len, HEADS * DK), jnp.float32),
             ((seq_count, HEADS, 1, DK), jnp.float32),
         ),
-        [wide_keys, wide_keys, wide_values, tap_keys, tap_keys, tap_values]
+        [heads_spec(block_len), heads_spec(HALO), heads_spec(HALO), heads_spec(CONV)]
         + [key_spec(block_len), decay_spec],
         seq_count,
         24,
@@ -678,15 +928,21 @@
     return jnp.dot(left, right, preferred_element_type=jnp.float32)
 
 
-def feed_forward(hidden, out_grad, gain, w_gate, w_up, down_left, down_right):
+def feed_forward(hidden, out_grad, gain, gate_sources, up_sources, down_left, down_right):
     tokens, width = hidden.shape
-    inner, tile = w_gate.shape[1], 256
+    sizes, mine = tuple(size for size, _ in chip_axes()), coordinates()
+    block_rows, inner = gate_sources[0][0].shape[3:]
+    count, tile = len(gate_sources), 256
     half = width // 2
     steps = inner // tile
 
-    def kernel(hid, grad, gain_ref, wg, wu, wl, wr, *refs):
-        out, back, back_low, normed, act, gate_back, up_back, gain_back, total, turned = refs
+    def kernel(me, hid, grad, gain_ref, wl, wr, *refs):
+        gate_refs, up_refs, refs = refs[:count], refs[count : 2 * count], refs[2 * count :]
+        out, back, back_low, normed, act, gate_back, up_back, gain_back = refs[:8]
+        total, turned, gate_held, up_held = refs[8:]
         step = pl.program_id(0)
+        w_gate = assemble(gate_held, gate_refs, gate_sources, me, 2, 1)
+        w_up = assemble(up_held, up_refs, up_sources, me, 1, 2)
 
         @pl.when(step == 0)
         def _():
@@ -697,7 +953,7 @@
             turned[...] = jnp.zeros_like(turned)
 
         source, low = normed[...], grad[...]
-        gate, up = bf_dot(source, wg[...]), bf_dot(source, wu[...])
+        gate, up = bf_dot(source, w_gate), bf_dot(source, w_up)
         inner_grad = nt_dot(low[:, :half], wl[...]) + nt_dot(low[:, half:], wr[...])
         sig = jax.nn.sigmoid(gate)
         silu = gate * sig
@@ -707,7 +963,7 @@
         act[...], gate_back[...], up_back[...] = active, gate_grad, up_grad
         total[:, :half] += bf_dot(active, wl[...])
         total[:, half:] += bf_dot(active, wr[...])
-        turned[...] += nt_dot(gate_grad, wg[...]) + nt_dot(up_grad, wu[...])
+        turned[...] += nt_dot(gate_grad, w_gate) + nt_dot(up_grad, w_up)
 
         @pl.when(step == steps - 1)
         def _():
@@ -720,12 +976,13 @@
             back_low[...] = result.astype(jnp.bfloat16)
 
     def whole(rows, columns):
-        return pl.BlockSpec((rows, columns), lambda i: (0, 0))
-
-    across = pl.BlockSpec((width, tile), lambda i: (0, i))
-    along = pl.BlockSpec((tile, half), lambda i: (i, 0))
-    inner_spec = pl.BlockSpec((tokens, tile), lambda i: (0, i))
+        return pl.BlockSpec((rows, columns), lambda i, me: (0, 0))
+
+    along = pl.BlockSpec((tile, half), lambda i, me: (i, 0))
+    inner_spec = pl.BlockSpec((tokens, tile), lambda i, me: (0, i))
     inner_shape = jax.ShapeDtypeStruct((tokens, inner), jnp.bfloat16)
+    arrays = [array for array, _, _ in gate_sources + up_sources]
+    held = pltpu.VMEM(sizes + (block_rows, tile), jnp.bfloat16)
     return pl.pallas_call(
         kernel,
         out_shape=[
@@ -738,17 +995,22 @@
             inner_shape,
             jax.ShapeDtypeStruct((1, width), jnp.float32),
         ],
-        grid=(steps,),
-        in_specs=[whole(tokens, width), whole(tokens, width), whole(1, width)]
-        + [across, across, along, along],
-        out_specs=[whole(tokens, width)] * 4 + [inner_spec] * 3 + [whole(1, width)],
-        scratch_shapes=[
-            pltpu.VMEM((tokens, width), jnp.float32),
-            pltpu.VMEM((tokens, width), jnp.float32),
-        ],
-        compiler_params=pltpu.CompilerParams(vmem_limit_bytes=52 * 2**20),
+        grid_spec=pltpu.PrefetchScalarGridSpec(
+            num_scalar_prefetch=1,
+            grid=(steps,),
+            in_specs=[whole(tokens, width), whole(tokens, width), whole(1, width), along, along]
+            + [tile_spec(array, tile, lambda i, me: (0, 0, 0, 0, i)) for array in arrays],
+            out_specs=[whole(tokens, width)] * 4 + [inner_spec] * 3 + [whole(1, width)],
+            scratch_shapes=[
+                pltpu.VMEM((tokens, width), jnp.float32),
+                pltpu.VMEM((tokens, width), jnp.float32),
+                held,
+                held,
+            ],
+        ),
+        compiler_params=pltpu.CompilerParams(vmem_limit_bytes=58 * 2**20),
         cost_estimate=takes(28),
-    )(hidden, out_grad, gain, w_gate, w_up, down_left, down_right)
+    )(mine, hidden, out_grad, gain, down_left, down_right, *arrays)
 
 
 def nt_dot(left, right):
@@ -785,43 +1047,69 @@
     conv_width = 2 * key_width + value_width
     block_start = lax.axis_index("seq") * block_len
     half = model_width // 2
-    (
-        (qk_full, v_full),
-        (g_left, g_right),
-        (out_left, out_right),
-        (down_left, down_right),
-        (gate_full, up_full),
-    ) = gather_all([[w_in[:, :conv_width]], [w_in[:, conv_width:], w_out, w_down], [w_gate_up]])
+    first_shard = by_head(w_in[:, :conv_width])
+    taps = by_head(conv_weight)
+    rest_shard = jnp.concatenate([w_in[:, conv_width:], w_out, w_down], axis=0)
+    rest_cuts = [w_in.shape[0], w_out.shape[0], w_down.shape[0]]
+    place = jnp.stack([block_start, lax.axis_index("seq") % GROUP]).astype(jnp.int32)
+    starts = doc_start[:, :, None]
+    gain_row = head_gain[None, :]
+    axes = chip_axes()
+
+    fast = gather_levels(first_shard)
     edge = shifted(inputs[:, block_len - HALO :, :], 1)
     wide = jnp.concatenate([edge, inputs], axis=1).astype(jnp.float32)
     wide_rms = lax.rsqrt(jnp.mean(wide * wide, axis=-1, keepdims=True) + epsilon)
     wide_normed = (wide * wide_rms * norm_gain).astype(jnp.bfloat16)
     layer_in = wide[:, HALO:].reshape(row_count, model_width)
     inv_rms = wide_rms[:, HALO:].reshape(row_count, 1)
+    fast, wide_normed, rest_shard = together(fast, wide_normed, rest_shard)
+    rest = gather_levels(rest_shard)
+    fast = gather_first(fast)
     normed = wide_normed[:, HALO:].reshape(row_count, model_width)
     wide_rows = wide_normed.reshape(-1, model_width)
-    wide_mixed = jnp.concatenate([bf_dot(wide_rows, qk_full), bf_dot(wide_rows, v_full)], axis=1)
-    wide_mixed = wide_mixed.astype(jnp.bfloat16).reshape(seq_count, HALO + block_len, conv_width)
-    gate_cols = jnp.concatenate([bf_dot(normed, g_left), bf_dot(normed, g_right)], axis=1)
-    gate_cols = gate_cols.astype(jnp.bfloat16)
     lowrank = bf_dot(normed, w_low)
     gate_logit = (
         jnp.dot(lowrank, w_high, precision=highest, preferred_element_type=jnp.float32) + gate_bias
     )
-    first = jnp.stack([block_start, lax.axis_index("seq") % GROUP]).astype(jnp.int32)
-    starts = doc_start[:, :, None]
+    fast, gate_logit, rest[1] = together(fast, gate_logit, rest[1])
+    fast = gather_second(fast)
+    fast, rest[2], wide_shard = together(fast, rest[2], w_gate_up)
+    fast = gather_cores(fast)
+    wide_pieces = gather_levels(wide_shard)
+    wide_mixed = projected(wide_rows, *[[(own, 0, 0), (other, 1, 0)] for own, other in fast])
+    wide_mixed = wide_mixed.reshape(seq_count, HALO + block_len, conv_width)
+    wide_mixed, rest = together(wide_mixed, rest)
+    rest = gather_first(rest)
     logits = gate_logit.reshape(seq_count, block_len, key_width)
-    gates = gate_cols.reshape(seq_count, block_len, value_width)
-    gain_row = head_gain[None, :]
     local_out, reach, local_state, block_decay = mixer_forward(
-        first, wide_mixed, conv_weight, logits, starts
-    )
-    incoming = carried_over(first, local_state, False)
-    mixer_out, gated = mixer_output(first, local_out, reach, incoming, gates, gain_row)
+        place, wide_mixed, taps, logits, starts
+    )
+    local_state, rest, wide_pieces[1] = together(local_state, rest, wide_pieces[1])
+    got, _ = exchanged(local_state)
+    got, rest = together(got, rest)
+    rest = gather_second(rest)
+    beyond = shifted(composed(place, got, False), GROUP)
+    incoming = composed(place, got, False, beyond)
+    incoming, rest, wide_pieces = together(incoming, rest, wide_pieces)
+    wide_pieces = gather_first(wide_pieces)
+    rest = gather_cores(rest)
+    incoming, _ = exchanged(incoming)
+    incoming, rest, wide_pieces = together(incoming, rest, wide_pieces)
+    crossed = gather_second(wide_pieces)
+    early = [swapped(pieces[0], 1) for pieces in crossed]
+    incoming, fast = together(incoming, fast)
+    [(left_full, right_full)] = gather_done(fast, [first_shard.shape[0]])
+    (g_left, g_right), (out_left, out_right), (down_left, down_right) = gather_done(rest, rest_cuts)
+    gate_cols = jnp.concatenate([bf_dot(normed, g_left), bf_dot(normed, g_right)], axis=1)
+    gates = gate_cols.astype(jnp.bfloat16).reshape(seq_count, block_len, value_width)
+    mixer_out, gated = mixer_output(place, local_out, reach, incoming, gates, gain_row)
     gated = gated.reshape(row_count, value_width)
     hidden_one = layer_in + jnp.concatenate(
         [bf_dot(gated, out_left), bf_dot(gated, out_right)], axis=1
     )
+    hidden_one, crossed, early = together(hidden_one, crossed, early)
+    gate_sources, up_sources = core_sources(crossed, early)
     out_rows_low = out_grad.reshape(row_count, model_width)
     (
         layer_out,
@@ -833,90 +1121,111 @@
         up_grad,
         ffn_gain_row,
     ) = feed_forward(
-        hidden_one, out_rows_low, ffn_gain[None, :], gate_full, up_full, down_left, down_right
-    )
-    ffn_gain_grad = ffn_gain_row[0]
-    gate_up_terms = cores_summed(ffn_in, gate_grad, up_grad)
-    down_terms = cores_summed(activation, out_rows_low[:, :half], out_rows_low[:, half:])
-    out_terms = cores_summed(gated, hidden_low[:, :half], hidden_low[:, half:])
+        hidden_one, out_rows_low, ffn_gain[None, :], gate_sources, up_sources, down_left, down_right
+    )
     gated_grad = nt_dot(hidden_low[:, :half], out_left) + nt_dot(hidden_low[:, half:], out_right)
     gated_grad = gated_grad.reshape(seq_count, block_len, value_width)
     mixer_grad, gate_vals_grad, state_term, head_gain_grad = mixer_output_back(
-        first, mixer_out, reach, gated_grad, gates, gain_row, block_decay
+        place, mixer_out, reach, gated_grad, gates, gain_row, block_decay
     )
     gate_vals_grad = gate_vals_grad.reshape(row_count, value_width)
-    head_gain_grad = jnp.sum(head_gain_grad, axis=(0, 1, 2))
-    g_terms = cores_summed(normed, gate_vals_grad[:, :half], gate_vals_grad[:, half:])
-    outgoing = carried_over(first, state_term, True)
-    outgoing, gate_up_terms = together(outgoing, gate_up_terms)
-    gate_up_terms = sides_summed([gate_up_terms])
-    q_back, k_back, v_back, q_taps, k_taps, v_taps, logit_grad, gate_bias_grad = mixer_backward(
-        first, wide_mixed, conv_weight, logits, starts, mixer_grad, incoming, outgoing
-    )
-    conv_weight_grad = jnp.sum(jnp.concatenate([q_taps, k_taps, v_taps], axis=-1), axis=0)
-    padded_grad = jnp.concatenate([q_back, k_back, v_back], axis=-1)
-    back_edge = shifted(padded_grad[:, :HALO].astype(jnp.bfloat16), -1).astype(jnp.float32)
-    mixed_grad = padded_grad[:, HALO:] + jnp.pad(
-        back_edge, ((0, 0), (block_len - HALO, 0), (0, 0))
-    )
-    mixed_grad = mixed_grad.reshape(row_count, conv_width).astype(jnp.bfloat16)
-    qk_grad, v_grad = mixed_grad[:, : 2 * key_width], mixed_grad[:, 2 * key_width :]
-    qk_grad, gate_up_terms, down_terms = together(qk_grad, gate_up_terms, down_terms)
-    w_gate_up_grad = levels_summed(gate_up_terms)
-    rest_terms = sides_summed([g_terms, out_terms, down_terms])
-    qkv_terms = cores_summed(normed, qk_grad, v_grad)
-    rest_terms, qkv_terms = together(rest_terms, qkv_terms)
-    rest = levels_summed(rest_terms)
-    qkv_grad = levels_summed(sides_summed([qkv_terms]))
-    w_in_rows = w_in.shape[0]
-    w_out_grad = rest[w_in_rows : 2 * w_in_rows]
-    w_down_grad = rest[2 * w_in_rows :]
-    w_in_grad = jnp.concatenate([qkv_grad, rest[:w_in_rows]], axis=1)
-    logit_grad = logit_grad.reshape(row_count, key_width)
-    gate_bias_grad = jnp.sum(gate_bias_grad, axis=0).reshape(-1)
-    w_high_grad = jnp.dot(
-        lowrank.T, logit_grad, precision=highest, preferred_element_type=jnp.float32
-    )
-    lowrank_grad = jnp.dot(
-        logit_grad, w_high.T, precision=highest, preferred_element_type=jnp.float32
-    ).astype(jnp.bfloat16)
-    w_low_grad = jnp.dot(normed.T, lowrank_grad, preferred_element_type=jnp.float32)
+
+    state_term, gated, ffn_in, activation = together(state_term, gated, ffn_in, activation)
+    got, (out_terms, wide_terms, down_terms) = exchanged(
+        state_term,
+        (
+            (lambda: grad_products(gated, hidden_low),),
+            (lambda _: grad_products(ffn_in, gate_grad, up_grad),),
+            (lambda _: grad_products(activation, out_rows_low),),
+        ),
+    )
+    wide_terms = cores_send([wide_terms])
+    beyond = shifted(composed(place, got, True), -GROUP)
+    g_terms = grad_products(normed, gate_vals_grad)
+    beyond, g_terms = together(beyond, g_terms)
+    outgoing = composed(place, got, True, beyond)
+    outgoing, wide_terms = together(outgoing, wide_terms)
+    wide_terms = phase_send(wide_terms, 0)
+    rest_terms = cores_send([g_terms, out_terms, down_terms])
+    outgoing, _ = exchanged(outgoing)
+    outgoing, wide_terms, rest_terms = together(outgoing, wide_terms, rest_terms)
+    wide_terms = phase_send(wide_terms, 1)
+    rest_terms = phase_send(rest_terms, 0)
+    backs = mixer_backward(
+        place, wide_mixed, taps, logits, starts, mixer_grad, incoming, outgoing
+    )
+    backs, wide_terms = together(backs, wide_terms)
+    wide_own, wide_last = levels_send(wide_terms)
+    mixed_grad, back_edge, back_tail, tap_grads, logit_grad, gate_bias_grad = backs
+    back_edge = shifted(back_edge.astype(jnp.bfloat16), -1).astype(jnp.float32)
+    mixed_grad = lax.dynamic_update_slice(
+        mixed_grad, (back_tail + back_edge).astype(jnp.bfloat16), (0, block_len - HALO, 0)
+    )
+    mixed_grad = mixed_grad.reshape(row_count, conv_width)
+    mixed_grad, rest_terms = together(mixed_grad, rest_terms)
+    rest_terms = phase_send(rest_terms, 1)
+    fast_terms = grad_products(normed, mixed_grad)
+    fast_terms, wide_last[0] = together(fast_terms, wide_last[0])
+    fast_terms = cores_send([fast_terms])
+    small_rows, lowrank_grad = small_packed(
+        logit_grad.reshape(row_count, key_width),
+        lowrank,
+        w_high,
+        normed,
+        tap_grads,
+        gate_bias_grad.reshape(seq_count, key_width),
+        head_gain_grad,
+        ffn_gain_row,
+    )
     normed_grad = (
-        bf_dot(qk_grad, qk_full.T)
-        + bf_dot(v_grad, v_full.T)
+        nt_dot(mixed_grad[:, : conv_width // 2], left_full)
+        + nt_dot(mixed_grad[:, conv_width // 2 :], right_full)
         + nt_dot(gate_vals_grad[:, :half], g_left)
         + nt_dot(gate_vals_grad[:, half:], g_right)
-        + bf_dot(lowrank_grad, w_low.T)
+        + nt_dot(lowrank_grad, w_low)
     )
     norm_gain_grad = jnp.sum(normed_grad * layer_in * inv_rms, axis=0)
     input_grad = hidden_grad + rms_back(normed_grad, layer_in, inv_rms, norm_gain)
-    small = (
-        norm_gain_grad,
+    small_rows = lax.dynamic_update_slice(small_rows, norm_gain_grad[None, :], (34, 0))
+    small_rows, rest_terms, fast_terms, input_grad, wide_last[1] = together(
+        small_rows, rest_terms, fast_terms, input_grad, wide_last[1]
+    )
+    fast_terms = phase_send(fast_terms, 0)
+    rest_own, rest_last = levels_send(rest_terms)
+    small_rows = spread(small_rows, axes[3])
+    fast_terms, small_rows, wide_last[2], rest_last[0] = together(
+        fast_terms, small_rows, wide_last[2], rest_last[0]
+    )
+    fast_terms = phase_send(fast_terms, 1)
+    small_rows = spread(sum(small_rows), axes[2])
+    fast_terms, small_rows, rest_last[1] = together(fast_terms, small_rows, rest_last[1])
+    fast_own, fast_last = levels_send(fast_terms)
+    small_rows = spread(sum(small_rows), axes[1])
+    small_rows, fast_last[0], rest_last[2] = together(small_rows, fast_last[0], rest_last[2])
+    small_parts = spread(sum(small_rows), axes[0])
+    norm_gain_grad, conv_weight_grad, w_low_grad, w_high_grad, *rows_found = small_unpacked(
+        small_parts, key_width, w_high.shape[0]
+    )
+    gate_bias_grad, head_gain_grad, ffn_gain_grad = [row[0] for row in rows_found]
+    rest_grad = reduced(rest_own, rest_last)
+    w_gate_up_grad = reduced(wide_own, wide_last)
+    fast_grad = by_kind(reduced(fast_own, fast_last))
+    ends = [rest_cuts[0], rest_cuts[0] + rest_cuts[1]]
+    w_in_grad = jnp.concatenate([fast_grad, rest_grad[: ends[0]]], axis=1)
+    w_out_grad = rest_grad[ends[0] : ends[1]]
+    w_down_grad = rest_grad[ends[1] :]
+    return (
+        layer_out.reshape(seq_count, block_len, model_width),
+        input_grad.reshape(seq_count, block_len, model_width),
+        norm_gain_grad[0],
+        w_in_grad,
         conv_weight_grad,
-        w_low_grad,
+        w_low_grad.T,
         w_high_grad,
         gate_bias_grad,
         head_gain_grad,
+        w_out_grad,
         ffn_gain_grad,
-    )
-    summed = small_sum(jnp.concatenate([part.reshape(-1, 128) for part in small]))
-    small_grads, start = [], 0
-    for part in small:
-        rows = part.size // 128
-        small_grads.append(summed[start : start + rows].reshape(part.shape))
-        start += rows
-    return (
-        layer_out.reshape(seq_count, block_len, model_width),
-        input_grad.reshape(seq_count, block_len, model_width),
-        small_grads[0],
-        w_in_grad,
-        small_grads[1],
-        small_grads[2],
-        small_grads[3],
-        small_grads[4],
-        small_grads[5],
-        w_out_grad,
-        small_grads[6],
         w_gate_up_grad,
         w_down_grad,
     )

time: 632 us -> 544 us (0.86)
  waiting for transfers between devices: 244 us -> 184 us
  Pallas kernels: 140 us -> 177 us
  local copies, waits for them, and re-layouts: 60.9 us -> 36.4 us
  other arithmetic: 50.7 us -> 29 us
  starting transfers between devices: 104 us -> 83.9 us
    ppermute x82 -> x74, waiting for transfers between devices: 232 us -> 164 us  [swapped(): return lax.ppermute(array, 'seq', [(i, i ^ mask) for i in range(count)])]
    pallas_call x0 -> x12, Pallas kernels: none -> 43.1 us  [the longest x6 25.6 us: phase_sums(): pl.pallas_call(kernel, out_shape=[jax.ShapeDtypeStruct(shape, jnp.bfloat1...]
    add x29 -> x6, other arithmetic: 31.2 us -> 2.25 us  [the longest x3 2.19 us: reduced(): return sum((part.astype(jnp.float32) for part in found), own)]
    ppermute x82 -> x74, starting transfers between devices: 90.6 us -> 78 us  [swapped(): return lax.ppermute(array, 'seq', [(i, i ^ mask) for i in range(count)])]
    dot_general x4 -> x7, matrix products: 6.27 us -> 18.4 us  [nt_dot(): lax.dot_general(left, right, (NT, ((), ())), preferred_element_type=jnp.f...]
    unnamed x213 -> x249, local copies, waits for them, and re-layouts: 38.5 us -> 28.7 us
    ppermute x4, waiting for transfers between devices: 11.2 us -> 20 us  [shifted(): return lax.ppermute(array, 'seq', pairs)]
    dot_general x10 -> x5, matrix products: 11.6 us -> 3.22 us  [bf_dot(): return jnp.dot(left, right, preferred_element_type=jnp.float32)]
  transfers between devices with their start and end apart: 86 -> 78, of which waited for: 32 -> 30; matrix products, arithmetic and copies ran while one was open for 15% -> 9% of each run, Pallas kernels for 13% -> 25%
where the time goes in v3:
time: 544 us; the launch traced here: 536 us
  waiting for transfers between devices  184 us (34%)
  Pallas kernels  177 us (33%)
  starting transfers between devices  83.9 us (15%)
  local copies, waits for them, and re-layouts  36.4 us (7%)
  other arithmetic  29 us (5%)
  matrix products  22.7 us (4%)
    ppermute x74, waiting for transfers between devices, swapped(): return lax.ppermute(array, 'seq', [(i, i ^ mask) for i in range(count)])  164 us
    ppermute x74, starting transfers between devices, swapped(): return lax.ppermute(array, 'seq', [(i, i ^ mask) for i in range(count)])  78 us
    pallas_call x4, Pallas kernels, launch(): pl.pallas_call(kernel, out_shape=[jax.ShapeDtypeStruct(shape, kind) for s...  47.4 us
    pallas_call x5, Pallas kernels, grad_products(): pl.pallas_call(kernel, out_shape=[shape for shape, _ in results], grid_sp...  33.1 us
    pallas_call x1, Pallas kernels, feed_forward(): pl.pallas_call(kernel, out_shape=[jax.ShapeDtypeStruct((tokens, width), j...  30.7 us
    unnamed x249, local copies, waits for them, and re-layouts  28.7 us
    pallas_call x6, Pallas kernels, phase_sums(): pl.pallas_call(kernel, out_shape=[jax.ShapeDtypeStruct(shape, jnp.bfloat1...  25.6 us
    ppermute x4, waiting for transfers between devices, shifted(): return lax.ppermute(array, 'seq', pairs)  20 us
  transfers between devices with their start and end apart: 78, of which 30 were waited for; matrix products, arithmetic and copies ran while one was open for 9% of the time, Pallas kernels for 25%

profile of v3, /device:TPU:0, one launch (start us, length us, event | category | flops | bytes accessed | tf_op | source)
XLA Modules:
  0.0 535.6 jit_solution(6362518153627775160)
XLA Ops:
  2.6 3.1 collective-permute-start.1
  5.7 2.6 collective-permute-start.2
  12.0 6.7 %collective-permute-done.2 = bf16[32,2048]{1,0:T(8,128)(2,1)S(1)} collective-permute-done((bf16[32,2048]{1,0:T(8,128)(2,1)S(1)}, bf16[32,2048]{1,0:T(8,128)(2,1)S(1)}, u32[]{:S(2)}, u32[]{:S(2)}) %collective-permute-start.2) | collective-permute-done | bytes 131104 | tf_op jit(solution)/shard_map/ppermute | solution.py:41
  21.9 2.0 collective-permute-start.6
  26.7 3.6 collective-permute-done.6
  31.9 4.0 collective-permute-start.9
  35.9 10.4 %collective-permute-done.9 = bf16[152,1024]{1,0:T(8,128)(2,1)S(1)} collective-permute-done((bf16[152,1024]{1,0:T(8,128)(2,1)S(1)}, bf16[152,1024]{1,0:T(8,128)(2,1)S(1)}, u32[]{:S(2)}, u32[]{:S(2)}) %collective-permute-start.9) | collective-permute-done | bytes 311328 | tf_op jit(solution)/shard_map/ppermute | solution.py:41
  52.6 7.7 %shard_map.237 = bf16[528,2048]{1,0:T(8,128)(2,1)S(1)} custom-call(s32[4]{0:T(128)S(1)} %pad_add_fusion.me, bf16[528,1024]{1,0:T(8,128)(2,1)S(1)} %bitcast.208, bf16[2,2,4,32,1024]{4,3,2,1,0:T(8,128)(2,1)} %pad_maximum_fusion.10.refs_0_, bf16[2,2,4,32,1024]{4,3,2,1,0:T(8,128)(2,1)} %collective-permute-done.10.refs_1_, ...), custom_call_target="tpu_custom_call" | custom-call | flops 6000000000 | tf_op jit(solution)/shard_map/pallas_call | solution.py:216
  60.3 2.2 collective-permute-done.12
  66.2 13.2 %shard_map.238 = (f32[2,256,1024]{2,1,0:T(8,128)S(1)}, f32[2,256,512]{2,1,0:T(8,128)S(1)}, bf16[8,144,256]{2,1,0:T(8,128)(2,1)S(1)}, f32[2,4,1,128]{3,2,1,0:T(1,128)S(1)}) custom-call(s32[2]{0:T(128)S(1)} %pad_add_fusion.1.first_ref.place_ref, bf16[2,264,2048]{2,1,0:T(8,128)(2,1)S(1)} %bitcast.245, f32[4,2048]{1,0:T(4,128)S(1)} %bitcast.234, ...), custom_call_target="tpu_custom_call" | custom-call | flops 12999999488 | tf_op jit(solution)/shard_map/pallas_call | solution.py:706
  81.6 8.8 %collective-permute-done.17 = bf16[2,2,144,256]{3,2,1,0:T(8,128)(2,1)S(1)} collective-permute-done((bf16[2,2,144,256]{3,2,1,0:T(8,128)(2,1)S(1)}, bf16[2,2,144,256]{3,2,1,0:T(8,128)(2,1)S(1)}, u32[]{:S(2)}, u32[]{:S(2)}) %collective-permute-start.17) | collective-permute-done | bytes 294944 | tf_op jit(solution)/shard_map/ppermute | solution.py:41
  91.1 7.7 %collective-permute-done.18 = bf16[2,2,144,256]{3,2,1,0:T(8,128)(2,1)S(1)} collective-permute-done((bf16[2,2,144,256]{3,2,1,0:T(8,128)(2,1)S(1)}, bf16[2,2,144,256]{3,2,1,0:T(8,128)(2,1)S(1)}, u32[]{:S(2)}, u32[]{:S(2)}) %collective-permute-start.18) | collective-permute-done | bytes 294944 | tf_op jit(solution)/shard_map/ppermute | solution.py:41
  101.8 4.4 collective-permute-start.22
  111.2 10.2 %collective-permute-done.19.refs_0_ = bf16[128,256]{1,0:T(8,128)(2,1)S(1)} collective-permute-done((bf16[128,256]{1,0:T(8,128)(2,1)}, bf16[128,256]{1,0:T(8,128)(2,1)S(1)}, u32[]{:S(2)}, u32[]{:S(2)}) %collective-permute-start.19) | collective-permute-done | bytes 65568 | tf_op jit(solution)/shard_map/ppermute | solution.py:47
  122.0 2.1 shard_map.240
  124.1 5.4 %collective-permute-done.22 = bf16[32,5632]{1,0:T(8,128)(2,1)} collective-permute-done((bf16[32,5632]{1,0:T(8,128)(2,1)}, bf16[32,5632]{1,0:T(8,128)(2,1)}, u32[]{:S(2)}, u32[]{:S(2)}) %collective-permute-start.22) | collective-permute-done | bytes 360480 | tf_op jit(solution)/shard_map/ppermute | solution.py:41
  135.2 4.6 collective-permute-done.24
  142.6 6.5 %collective-permute-done.25 = bf16[2,2,128,256]{3,2,1,0:T(8,128)(2,1)S(1)} collective-permute-done((bf16[2,2,128,256]{3,2,1,0:T(8,128)(2,1)S(1)}, bf16[2,2,128,256]{3,2,1,0:T(8,128)(2,1)S(1)}, u32[]{:S(2)}, u32[]{:S(2)}) %collective-permute-start.25) | collective-permute-done | bytes 262176 | tf_op jit(solution)/shard_map/ppermute | solution.py:41
  151.5 13.9 %collective-permute-done.26 = bf16[2,2,128,256]{3,2,1,0:T(8,128)(2,1)S(1)} collective-permute-done((bf16[2,2,128,256]{3,2,1,0:T(8,128)(2,1)S(1)}, bf16[2,2,128,256]{3,2,1,0:T(8,128)(2,1)S(1)}, u32[]{:S(2)}, u32[]{:S(2)}) %collective-permute-start.26) | collective-permute-done | bytes 262176 | tf_op jit(solution)/shard_map/ppermute | solution.py:41
  180.6 4.1 shard_map.243
  189.2 10.1 %collective-permute-done.32 = bf16[2,4,32,2816]{3,2,1,0:T(8,128)(2,1)} collective-permute-done((bf16[2,4,32,2816]{3,2,1,0:T(8,128)(2,1)}, bf16[2,4,32,2816]{3,2,1,0:T(8,128)(2,1)}, u32[]{:S(2)}, u32[]{:S(2)}) %collective-permute-start.32) | collective-permute-done | bytes 1441824 | tf_op jit(solution)/shard_map/ppermute | solution.py:41
  199.2 4.6 collective-permute-done.31
  204.4 3.1 collective-permute-done.35
  207.5 2.1 collective-permute-done.36
  209.5 30.7 %shard_map.244 = (f32[512,1024]{1,0:T(8,128)}, f32[512,1024]{1,0:T(8,128)}, bf16[512,1024]{1,0:T(8,128)(2,1)}, bf16[512,1024]{1,0:T(8,128)(2,1)}, bf16[512,2816]...) custom-call(s32[4]{0:T(128)} %copy-done.52, ...), custom_call_target="tpu_custom_call" | custom-call | flops 28000000000 | tf_op jit(solution)/shard_map/pallas_call | solution.py:986
  243.9 5.3 shard_map.245
  252.2 2.3 shard_map.246
  256.7 14.5 %shard_map.247 = (bf16[2,2,4,32,2816]{4,3,2,1,0:T(8,128)(2,1)}, bf16[2,2,4,32,2816]{4,3,2,1,0:T(8,128)(2,1)}, bf16[2,2,4,32,2816]{4,3,2,1,0:T(8,128)(2,1)}, bf16[2,2,4,32,2816]{4,3,2,1,0:T(8,128)(2,1)}) custom-call(s32[4]{0:T(128)S(1)} %copy-done.53, bf16[512,1024]{1,0:T(8,128)(2,1)S(1)} %copy-done.82, bf16[512,2816]{1,0:T(8,128)(2,1)} %get-tuple-element.368.a_ref, ...), custom_call_target="tpu_custom_call" | custom-call | flops 14476128256 | tf_op jit(solution)/shard_map/pallas_call | solution.py:288
  272.4 8.0 %shard_map.248 = (bf16[2,2,4,88,512]{4,3,2,1,0:T(8,128)(2,1)S(1)}, bf16[2,2,4,88,512]{4,3,2,1,0:T(8,128)(2,1)S(1)}, bf16[2,2,4,88,512]{4,3,2,1,0:T(8,128)(2,1)S(1)}, bf16[2,2,4,88,512]{4,3,2,1,0:T(8,128)(2,1)}) custom-call(s32[4]{0:T(128)S(1)} %copy-done.53, bf16[512,2816]{1,0:T(8,128)(2,1)} %get-tuple-element.376.left_ref, bf16[512,1024]{1,0:T(8,128)(2,1)S(1)} %bitcast.239, ...), custom_call_target="tpu_custom_call" | custom-call | flops 7988064256 | tf_op jit(solution)/shard_map/pallas_call | solution.py:288
  287.9 2.4 shard_map.250
  290.3 9.9 %collective-permute-done.40.refs_0_ = bf16[128,256]{1,0:T(8,128)(2,1)S(1)} collective-permute-done((bf16[128,256]{1,0:T(8,128)(2,1)}, bf16[128,256]{1,0:T(8,128)(2,1)S(1)}, u32[]{:S(2)}, u32[]{:S(2)}) %collective-permute-start.40) | collective-permute-done | bytes 65568 | tf_op jit(solution)/shard_map/ppermute | solution.py:47
  305.7 2.3 shard_map.251
  309.8 4.8 shard_map.252
  317.9 5.0 shard_map.258
  322.9 5.8 %shard_map.257 = bf16[4,2,2,2,32,1024]{5,4,3,2,1,0:T(8,128)(2,1)S(1)} custom-call(s32[4]{0:T(128)S(1)} %copy-done.53, bf16[2,2,4,32,1024]{4,3,2,1,0:T(8,128)(2,1)} %pad_maximum_fusion.10.refs_0_, bf16[2,2,4,32,1024]{4,3,2,1,0:T(8,128)(2,1)} %collective-permute-done.10.refs_1_), custom_call_target="tpu_custom_call" | custom-call | flops 2638400000 | tf_op jit(solution)/shard_map/pallas_call | solution.py:106
  329.2 2.1 fusion.13
  331.3 22.9 %collective-permute-done.44 = bf16[2,2,128,256]{3,2,1,0:T(8,128)(2,1)S(1)} collective-permute-done((bf16[2,2,128,256]{3,2,1,0:T(8,128)(2,1)S(1)}, bf16[2,2,128,256]{3,2,1,0:T(8,128)(2,1)S(1)}, u32[]{:S(2)}, u32[]{:S(2)}) %collective-permute-start.44) | collective-permute-done | bytes 262176 | tf_op jit(solution)/shard_map/ppermute | solution.py:41
  355.9 2.1 fusion.11
  358.0 4.3 collective-permute-done.45
  362.4 6.2 %shard_map.256 = (bf16[2,4,152,512]{3,2,1,0:T(8,128)(2,1)}, bf16[2,4,152,512]{3,2,1,0:T(8,128)(2,1)}) custom-call(bf16[2,2,4,32,512]{4,3,2,1,0:T(8,128)(2,1)S(1)} %copy-done.17, bf16[2,2,4,32,512]{4,3,2,1,0:T(8,128)(2,1)S(1)} %get-tuple-element.493.refs_1_, bf16[2,2,4,88,512]{4,3,2,1,0:T(8,128)(2,1)S(1)} %copy-done.5, ...), custom_call_target="tpu_custom_call" | custom-call | flops 3000000000 | tf_op jit(solution)/shard_map/pallas_call | solution.py:356
  371.8 3.7 shard_map.254
  379.6 24.8 %shard_map.253 = (bf16[2,256,2048]{2,1,0:T(8,128)(2,1)}, f32[2,8,2048]{2,1,0:T(8,128)S(1)}, f32[2,8,2048]{2,1,0:T(8,128)S(1)}, f32[2,4,2048]{2,1,0:T(4,128)S(1)}...) custom-call(s32[2]{0:T(128)S(1)} %copy-done.68, bf16[2,264,2048]{2,1,0:T(8,128)(2,1)S(1)} %bitcast.246, ...), custom_call_target="tpu_custom_call" | custom-call | flops 24000000000 | tf_op jit(solution)/shard_map/pallas_call | solution.py:706
  404.5 9.3 %collective-permute-done.50.refs_3_ = bf16[4,32,2816]{2,1,0:T(8,128)(2,1)S(1)} collective-permute-done((bf16[4,32,2816]{2,1,0:T(8,128)(2,1)}, bf16[4,32,2816]{2,1,0:T(8,128)(2,1)S(1)}, u32[]{:S(2)}, u32[]{:S(2)}) %collective-permute-start.50) | collective-permute-done | bytes 720928 | tf_op jit(solution)/shard_map/ppermute | solution.py:41
  419.5 2.9 shard_map.261
  424.0 3.0 collective-permute-start.57
  429.2 5.9 %shard_map.260 = (bf16[2,2,4,32,1024]{4,3,2,1,0:T(8,128)(2,1)}, bf16[2,2,4,32,1024]{4,3,2,1,0:T(8,128)(2,1)S(1)}, bf16[2,2,4,32,1024]{4,3,2,1,0:T(8,128)(2,1)}, bf16[2,2,4,32,1024]{4,3,2,1,0:T(8,128)(2,1)S(1)}) custom-call(s32[4]{0:T(128)S(1)} %copy-done.53, bf16[512,1024]{1,0:T(8,128)(2,1)S(1)} %bitcast.212, bf16[512,2048]{1,0:T(8,128)(2,1)} %bitcast.110.a_ref.b_ref, ...), custom_call_target="tpu_custom_call" | custom-call | flops 6218592256 | tf_op jit(solution)/shard_map/pallas_call | solution.py:288
  435.1 4.6 fusion.8
  439.8 4.0 collective-permute-done.57
  444.4 5.1 shard_map.259
  451.5 5.1 fusion.7
  457.0 4.9 fusion.6
  463.0 2.8 collective-permute-done.55.refs_5_
  467.1 4.0 shard_map.262
  473.1 2.2 shard_map.263
  475.5 3.4 collective-permute-start.69
  478.9 7.4 %collective-permute-done.65 = bf16[152,1024]{1,0:T(8,128)(2,1)S(1)} collective-permute-done((bf16[152,1024]{1,0:T(8,128)(2,1)S(1)}, bf16[152,1024]{1,0:T(8,128)(2,1)S(1)}, u32[]{:S(2)}, u32[]{:S(2)}) %collective-permute-start.65) | collective-permute-done | bytes 311328 | tf_op jit(solution)/shard_map/ppermute | solution.py:41
  491.8 2.2 collective-permute-start.72
  494.0 3.2 collective-permute-done.69
  499.5 3.6 collective-permute-start.70
  503.1 2.6 collective-permute-start.76
  508.5 7.1 %collective-permute-done.76 = bf16[32,2048]{1,0:T(8,128)(2,1)S(1)} collective-permute-done((bf16[32,2048]{1,0:T(8,128)(2,1)S(1)}, bf16[32,2048]{1,0:T(8,128)(2,1)S(1)}, u32[]{:S(2)}, u32[]{:S(2)}) %collective-permute-start.76) | collective-permute-done | bytes 131104 | tf_op jit(solution)/shard_map/ppermute | solution.py:41
  515.9 2.5 collective-permute-start.73
  518.7 2.2 collective-permute-start.75
  524.3 7.6 %collective-permute-done.74.refs_2_ = f32[40,1024]{1,0:T(8,128)S(1)} collective-permute-done((f32[40,1024]{1,0:T(8,128)S(1)}, f32[40,1024]{1,0:T(8,128)S(1)}, u32[]{:S(2)}, u32[]{:S(2)}) %collective-permute-start.74) | collective-permute-done | bytes 163872 | tf_op jit(solution)/shard_map/ppermute | solution.py:41
  (463 shorter events, 137.8 us)
Async XLA Ops:
  2.6 9.4 %collective-permute-start.1 = (bf16[32,2048]{1,0:T(8,128)(2,1)S(1)}, bf16[32,2048]{1,0:T(8,128)(2,1)S(1)}, u32[]{:S(2)}, u32[]{:S(2)}) collective-permute-start(bf16[32,2048]{1,0:T(8,128)(2,1)S(1)} %bitcast.281), channel_id=1, source_target_pairs={{0,8},{1,9},{2,10},{3,11},{4,12},{5,13},{6,14},{7,15},{8,0},{9,1},... | collective-permute-start | bytes 393224 | tf_op jit(solution)/shard_map/ppermute | solution.py:41
  5.7 12.9 %collective-permute-start.2 = (bf16[32,2048]{1,0:T(8,128)(2,1)S(1)}, bf16[32,2048]{1,0:T(8,128)(2,1)S(1)}, u32[]{:S(2)}, u32[]{:S(2)}) collective-permute-start(bf16[32,2048]{1,0:T(8,128)(2,1)S(1)} %bitcast.282), channel_id=1, source_target_pairs={{0,16},{1,17},{2,18},{3,19},{4,20},{5,21},{6,22},{7,23},{8,24},{9,... | collective-permute-start | bytes 393224 | tf_op jit(solution)/shard_map/ppermute | solution.py:41
  8.3 10.3 %collective-permute-start.3 = (bf16[32,2048]{1,0:T(8,128)(2,1)S(1)}, bf16[32,2048]{1,0:T(8,128)(2,1)S(1)}, u32[]{:S(2)}, u32[]{:S(2)}) collective-permute-start(bf16[32,2048]{1,0:T(8,128)(2,1)S(1)} %bitcast.283), channel_id=1, source_target_pairs={{0,24},{1,25},{2,26},{3,27},{4,28},{5,29},{6,30},{7,31},{8,16},{9,... | collective-permute-start | bytes 393224 | tf_op jit(solution)/shard_map/ppermute | solution.py:41
  21.9 8.3 %collective-permute-start.6 = (bf16[152,1024]{1,0:T(8,128)(2,1)S(1)}, bf16[152,1024]{1,0:T(8,128)(2,1)S(1)}, u32[]{:S(2)}, u32[]{:S(2)}) collective-permute-start(bf16[152,1024]{1,0:T(8,128)(2,1)S(1)} %pad_maximum_fusion.21), channel_id=1, source_target_pairs={{0,8},{1,9},{2,10},{3,11},{4,12},{5,13},{6,14},{7,15},{8,0},{9,1},... | collective-permute-start | bytes 933896 | tf_op jit(solution)/shard_map/ppermute | solution.py:41
  31.1 15.2 %collective-permute-start.8 = (bf16[2,4,32,1024]{3,2,1,0:T(8,128)(2,1)S(1)}, bf16[2,4,32,1024]{3,2,1,0:T(8,128)(2,1)S(1)}, u32[]{:S(2)}, u32[]{:S(2)}) collective-permute-start(bf16[2,4,32,1024]{3,2,1,0:T(8,128)(2,1)S(1)} %pad_maximum_fusion.17), channel_id=1, source_target_pairs={{0,2},{1,3},{2,0},{3,1},{4,6},{5,7},{6,4},{7,5},{8,10},{9,11},{10,... | collective-permute-start | bytes 1572872 | tf_op jit(solution)/shard_map/ppermute | solution.py:41
  31.5 14.7 %collective-permute-start.7 = (bf16[2,4,32,1024]{3,2,1,0:T(8,128)(2,1)S(1)}, bf16[2,4,32,1024]{3,2,1,0:T(8,128)(2,1)S(1)}, u32[]{:S(2)}, u32[]{:S(2)}) collective-permute-start(bf16[2,4,32,1024]{3,2,1,0:T(8,128)(2,1)S(1)} %pad_maximum_fusion.16), channel_id=1, source_target_pairs={{0,4},{1,5},{2,6},{3,7},{4,0},{5,1},{6,2},{7,3},{8,12},{9,13},{10,... | collective-permute-start | bytes 1572872 | tf_op jit(solution)/shard_map/ppermute | solution.py:41
  31.9 14.4 %collective-permute-start.9 = (bf16[152,1024]{1,0:T(8,128)(2,1)S(1)}, bf16[152,1024]{1,0:T(8,128)(2,1)S(1)}, u32[]{:S(2)}, u32[]{:S(2)}) collective-permute-start(bf16[152,1024]{1,0:T(8,128)(2,1)S(1)} %pad_maximum_fusion.21), channel_id=1, source_target_pairs={{0,16},{1,17},{2,18},{3,19},{4,20},{5,21},{6,22},{7,23},{8,24},{9,... | collective-permute-start | bytes 933896 | tf_op jit(solution)/shard_map/ppermute | solution.py:41
  50.2 12.3 %collective-permute-start.12 = (bf16[152,1024]{1,0:T(8,128)(2,1)}, bf16[152,1024]{1,0:T(8,128)(2,1)S(1)}, u32[]{:S(2)}, u32[]{:S(2)}) collective-permute-start(bf16[152,1024]{1,0:T(8,128)(2,1)} %copy-done.91), channel_id=1, source_target_pairs={{0,24},{1,25},{2,26},{3,27},{4,28},{5,29},{6,30},{7,31},{8,16},{9,... | collective-permute-start | bytes 933896 | tf_op jit(solution)/shard_map/ppermute | solution.py:41
  51.5 27.9 %collective-permute-start.15 = (bf16[32,5632]{1,0:T(8,128)(2,1)}, bf16[32,5632]{1,0:T(8,128)(2,1)S(1)}, u32[]{:S(2)}, u32[]{:S(2)}) collective-permute-start(bf16[32,5632]{1,0:T(8,128)(2,1)} %param.25), channel_id=1, source_target_pairs={{0,8},{1,9},{2,10},{3,11},{4,12},{5,13},{6,14},{7,15},{8,0},{9,1},... | collective-permute-start | bytes 1081352 | tf_op jit(solution)/shard_map/ppermute | solution.py:41
  62.7 16.7 %collective-permute-start.13 = (bf16[4,152,512]{2,1,0:T(8,128)(2,1)S(1)}, bf16[4,152,512]{2,1,0:T(8,128)(2,1)S(1)}, u32[]{:S(2)}, u32[]{:S(2)}) collective-permute-start(bf16[4,152,512]{2,1,0:T(8,128)(2,1)S(1)} %get-tuple-element.313), channel_id=1, source_target_pairs={{0,2},{1,3},{2,0},{3,1},{4,6},{5,7},{6,4},{7,5},{8,10},{9,11},{10,... | collective-permute-start | bytes 1867784 | tf_op jit(solution)/shard_map/ppermute | solution.py:41
  64.5 14.9 %collective-permute-start.14 = (bf16[4,152,512]{2,1,0:T(8,128)(2,1)S(1)}, bf16[4,152,512]{2,1,0:T(8,128)(2,1)S(1)}, u32[]{:S(2)}, u32[]{:S(2)}) collective-permute-start(bf16[4,152,512]{2,1,0:T(8,128)(2,1)S(1)} %get-tuple-element.315), channel_id=1, source_target_pairs={{0,4},{1,5},{2,6},{3,7},{4,0},{5,1},{6,2},{7,3},{8,12},{9,13},{10,... | collective-permute-start | bytes 1867784 | tf_op jit(solution)/shard_map/ppermute | solution.py:41
  81.2 9.1 %collective-permute-start.17 = (bf16[2,2,144,256]{3,2,1,0:T(8,128)(2,1)S(1)}, bf16[2,2,144,256]{3,2,1,0:T(8,128)(2,1)S(1)}, u32[]{:S(2)}, u32[]{:S(2)}) collective-permute-start(bf16[2,2,144,256]{3,2,1,0:T(8,128)(2,1)S(1)} %get-tuple-element.566), channel_id=1, source_target_pairs={{0,2},{1,3},{2,0},{3,1},{4,6},{5,7},{6,4},{7,5},{8,10},{9,11},{10,... | collective-permute-start | bytes 884744 | tf_op jit(solution)/shard_map/ppermute | solution.py:41
  99.7 29.8 %collective-permute-start.21 = (bf16[2,4,152,512]{3,2,1,0:T(8,128)(2,1)S(1)}, bf16[2,4,152,512]{3,2,1,0:T(8,128)(2,1)}, u32[]{:S(2)}, u32[]{:S(2)}) collective-permute-start(bf16[2,4,152,512]{3,2,1,0:T(8,128)(2,1)S(1)} %pad_maximum_fusion.9), channel_id=1, source_target_pairs={{0,2},{1,3},{2,0},{3,1},{4,6},{5,7},{6,4},{7,5},{8,10},{9,11},{10,... | collective-permute-start | bytes 3735560 | tf_op jit(solution)/shard_map/ppermute | solution.py:41
  101.2 28.3 %collective-permute-start.20 = (bf16[2,4,152,512]{3,2,1,0:T(8,128)(2,1)}, bf16[2,4,152,512]{3,2,1,0:T(8,128)(2,1)}, u32[]{:S(2)}, u32[]{:S(2)}) collective-permute-start(bf16[2,4,152,512]{3,2,1,0:T(8,128)(2,1)} %pad_maximum_fusion.8), channel_id=1, source_target_pairs={{0,4},{1,5},{2,6},{3,7},{4,0},{5,1},{6,2},{7,3},{8,12},{9,13},{10,... | collective-permute-start | bytes 3735560 | tf_op jit(solution)/shard_map/ppermute | solution.py:41
  101.8 27.7 %collective-permute-start.22 = (bf16[32,5632]{1,0:T(8,128)(2,1)}, bf16[32,5632]{1,0:T(8,128)(2,1)}, u32[]{:S(2)}, u32[]{:S(2)}) collective-permute-start(bf16[32,5632]{1,0:T(8,128)(2,1)} %param.25), channel_id=1, source_target_pairs={{0,16},{1,17},{2,18},{3,19},{4,20},{5,21},{6,22},{7,23},{8,24},{9,... | collective-permute-start | bytes 1081352 | tf_op jit(solution)/shard_map/ppermute | solution.py:41
  106.2 23.3 %collective-permute-start.23 = (bf16[32,5632]{1,0:T(8,128)(2,1)}, bf16[32,5632]{1,0:T(8,128)(2,1)}, u32[]{:S(2)}, u32[]{:S(2)}) collective-permute-start(bf16[32,5632]{1,0:T(8,128)(2,1)} %param.25), channel_id=1, source_target_pairs={{0,24},{1,25},{2,26},{3,27},{4,28},{5,29},{6,30},{7,31},{8,16},{9,... | collective-permute-start | bytes 1081352 | tf_op jit(solution)/shard_map/ppermute | solution.py:41
  109.4 12.0 %collective-permute-start.19 = (bf16[128,256]{1,0:T(8,128)(2,1)}, bf16[128,256]{1,0:T(8,128)(2,1)S(1)}, u32[]{:S(2)}, u32[]{:S(2)}) collective-permute-start(bf16[128,256]{1,0:T(8,128)(2,1)} %shard_map.239), channel_id=1, source_target_pairs={{0,8},{1,9},{2,10},{3,11},{4,12},{5,13},{6,14},{7,15},{8,16},{9,17... | collective-permute-start | bytes 196616 | tf_op jit(solution)/shard_map/ppermute | solution.py:47
  131.1 34.4 %collective-permute-start.28 = (bf16[2,2,4,152,512]{4,3,2,1,0:T(8,128)(2,1)S(1)}, bf16[2,2,4,152,512]{4,3,2,1,0:T(8,128)(2,1)S(1)}, u32[]{:S(2)}, u32[]{:S(2)}) collective-permute-start(bf16[2,2,4,152,512]{4,3,2,1,0:T(8,128)(2,1)S(1)} %pad_maximum_fusion.1.refs_0_), channel_id=1, source_target_pairs={{0,1},{1,0},{2,3},{3,2},{4,5},{5,4},{6,7},{7,6},{8,9},{9,8},{10,11... | collective-permute-start | bytes 7471112 | tf_op jit(solution)/shard_map/ppermute | solution.py:41
  133.1 32.3 %collective-permute-start.27 = (bf16[2,2,4,152,512]{4,3,2,1,0:T(8,128)(2,1)S(1)}, bf16[2,2,4,152,512]{4,3,2,1,0:T(8,128)(2,1)S(1)}, u32[]{:S(2)}, u32[]{:S(2)}) collective-permute-start(bf16[2,2,4,152,512]{4,3,2,1,0:T(8,128)(2,1)S(1)} %pad_maximum_fusion.refs_0_), channel_id=1, source_target_pairs={{0,1},{1,0},{2,3},{3,2},{4,5},{5,4},{6,7},{7,6},{8,9},{9,8},{10,11... | collective-permute-start | bytes 7471112 | tf_op jit(solution)/shard_map/ppermute | solution.py:41
  139.8 9.2 %collective-permute-start.25 = (bf16[2,2,128,256]{3,2,1,0:T(8,128)(2,1)S(1)}, bf16[2,2,128,256]{3,2,1,0:T(8,128)(2,1)S(1)}, u32[]{:S(2)}, u32[]{:S(2)}) collective-permute-start(bf16[2,2,128,256]{3,2,1,0:T(8,128)(2,1)S(1)} %get-tuple-element.578), channel_id=1, source_target_pairs={{0,2},{1,3},{2,0},{3,1},{4,6},{5,7},{6,4},{7,5},{8,10},{9,11},{10,... | collective-permute-start | bytes 786440 | tf_op jit(solution)/shard_map/ppermute | solution.py:41
  141.6 23.8 %collective-permute-start.29 = (bf16[4,32,2816]{2,1,0:T(8,128)(2,1)S(1)}, bf16[4,32,2816]{2,1,0:T(8,128)(2,1)S(1)}, u32[]{:S(2)}, u32[]{:S(2)}) collective-permute-start(bf16[4,32,2816]{2,1,0:T(8,128)(2,1)S(1)} %get-tuple-element.338), channel_id=1, source_target_pairs={{0,2},{1,3},{2,0},{3,1},{4,6},{5,7},{6,4},{7,5},{8,10},{9,11},{10,... | collective-permute-start | bytes 2162696 | tf_op jit(solution)/shard_map/ppermute | solution.py:41
  142.1 23.3 %collective-permute-start.30 = (bf16[4,32,2816]{2,1,0:T(8,128)(2,1)S(1)}, bf16[4,32,2816]{2,1,0:T(8,128)(2,1)S(1)}, u32[]{:S(2)}, u32[]{:S(2)}) collective-permute-start(bf16[4,32,2816]{2,1,0:T(8,128)(2,1)S(1)} %get-tuple-element.340), channel_id=1, source_target_pairs={{0,4},{1,5},{2,6},{3,7},{4,0},{5,1},{6,2},{7,3},{8,12},{9,13},{10,... | collective-permute-start | bytes 2162696 | tf_op jit(solution)/shard_map/ppermute | solution.py:41
  149.1 16.3 %collective-permute-start.26 = (bf16[2,2,128,256]{3,2,1,0:T(8,128)(2,1)S(1)}, bf16[2,2,128,256]{3,2,1,0:T(8,128)(2,1)S(1)}, u32[]{:S(2)}, u32[]{:S(2)}) collective-permute-start(bf16[2,2,128,256]{3,2,1,0:T(8,128)(2,1)S(1)} %get-tuple-element.576), channel_id=1, source_target_pairs={{0,4},{1,5},{2,6},{3,7},{4,0},{5,1},{6,2},{7,3},{8,12},{9,13},{10,... | collective-permute-start | bytes 786440 | tf_op jit(solution)/shard_map/ppermute | solution.py:41
  166.7 32.5 %collective-permute-start.32 = (bf16[2,4,32,2816]{3,2,1,0:T(8,128)(2,1)}, bf16[2,4,32,2816]{3,2,1,0:T(8,128)(2,1)}, u32[]{:S(2)}, u32[]{:S(2)}) collective-permute-start(bf16[2,4,32,2816]{3,2,1,0:T(8,128)(2,1)} %pad_maximum_fusion.6), channel_id=1, source_target_pairs={{0,2},{1,3},{2,0},{3,1},{4,6},{5,7},{6,4},{7,5},{8,10},{9,11},{10,... | collective-permute-start | bytes 4325384 | tf_op jit(solution)/shard_map/ppermute | solution.py:41
  168.4 30.9 %collective-permute-start.34 = (bf16[2,4,32,2816]{3,2,1,0:T(8,128)(2,1)}, bf16[2,4,32,2816]{3,2,1,0:T(8,128)(2,1)}, u32[]{:S(2)}, u32[]{:S(2)}) collective-permute-start(bf16[2,4,32,2816]{3,2,1,0:T(8,128)(2,1)} %pad_maximum_fusion.6), channel_id=1, source_target_pairs={{0,1},{1,0},{2,3},{3,2},{4,5},{5,4},{6,7},{7,6},{8,9},{9,8},{10,11... | collective-permute-start | bytes 4325384 | tf_op jit(solution)/shard_map/ppermute | solution.py:41
  169.6 34.3 %collective-permute-start.31 = (bf16[2,4,32,2816]{3,2,1,0:T(8,128)(2,1)}, bf16[2,4,32,2816]{3,2,1,0:T(8,128)(2,1)}, u32[]{:S(2)}, u32[]{:S(2)}) collective-permute-start(bf16[2,4,32,2816]{3,2,1,0:T(8,128)(2,1)} %pad_maximum_fusion.5), channel_id=1, source_target_pairs={{0,4},{1,5},{2,6},{3,7},{4,0},{5,1},{6,2},{7,3},{8,12},{9,13},{10,... | collective-permute-start | bytes 4325384 | tf_op jit(solution)/shard_map/ppermute | solution.py:41
  170.1 33.8 %collective-permute-start.33 = (bf16[2,4,32,2816]{3,2,1,0:T(8,128)(2,1)}, bf16[2,4,32,2816]{3,2,1,0:T(8,128)(2,1)}, u32[]{:S(2)}, u32[]{:S(2)}) collective-permute-start(bf16[2,4,32,2816]{3,2,1,0:T(8,128)(2,1)} %pad_maximum_fusion.5), channel_id=1, source_target_pairs={{0,1},{1,0},{2,3},{3,2},{4,5},{5,4},{6,7},{7,6},{8,9},{9,8},{10,11... | collective-permute-start | bytes 4325384 | tf_op jit(solution)/shard_map/ppermute | solution.py:41
  256.2 15.0 %collective-permute-start.38 = (bf16[2,2,144,256]{3,2,1,0:T(8,128)(2,1)S(1)}, bf16[2,2,144,256]{3,2,1,0:T(8,128)(2,1)S(1)}, u32[]{:S(2)}, u32[]{:S(2)}) collective-permute-start(bf16[2,2,144,256]{3,2,1,0:T(8,128)(2,1)S(1)} %get-tuple-element.559), channel_id=1, source_target_pairs={{0,2},{1,3},{2,0},{3,1},{4,6},{5,7},{6,4},{7,5},{8,10},{9,11},{10,... | collective-permute-start | bytes 884744 | tf_op jit(solution)/shard_map/ppermute | solution.py:41
  271.2 36.7 %collective-permute-start.41 = (bf16[2,2,4,32,2816]{4,3,2,1,0:T(8,128)(2,1)}, bf16[2,2,4,32,2816]{4,3,2,1,0:T(8,128)(2,1)}, u32[]{:S(2)}, u32[]{:S(2)}) collective-permute-start(bf16[2,2,4,32,2816]{4,3,2,1,0:T(8,128)(2,1)} %get-tuple-element.390), channel_id=1, source_target_pairs={{0,1},{1,0},{2,3},{3,2},{4,5},{5,4},{6,7},{7,6},{8,9},{9,8},{10,11... | collective-permute-start | bytes 8650760 | tf_op jit(solution)/shard_map/ppermute | solution.py:41
  271.3 36.7 %collective-permute-start.42 = (bf16[2,2,4,32,2816]{4,3,2,1,0:T(8,128)(2,1)}, bf16[2,2,4,32,2816]{4,3,2,1,0:T(8,128)(2,1)}, u32[]{:S(2)}, u32[]{:S(2)}) collective-permute-start(bf16[2,2,4,32,2816]{4,3,2,1,0:T(8,128)(2,1)} %get-tuple-element.392), channel_id=1, source_target_pairs={{0,1},{1,0},{2,3},{3,2},{4,5},{5,4},{6,7},{7,6},{8,9},{9,8},{10,11... | collective-permute-start | bytes 8650760 | tf_op jit(solution)/shard_map/ppermute | solution.py:41
  271.8 11.9 %collective-permute-start.39 = (bf16[2,2,144,256]{3,2,1,0:T(8,128)(2,1)S(1)}, bf16[2,2,144,256]{3,2,1,0:T(8,128)(2,1)S(1)}, u32[]{:S(2)}, u32[]{:S(2)}) collective-permute-start(bf16[2,2,144,256]{3,2,1,0:T(8,128)(2,1)S(1)} %get-tuple-element.557), channel_id=1, source_target_pairs={{0,4},{1,5},{2,6},{3,7},{4,0},{5,1},{6,2},{7,3},{8,12},{9,13},{10,... | collective-permute-start | bytes 884744 | tf_op jit(solution)/shard_map/ppermute | solution.py:41
  286.5 13.6 %collective-permute-start.40 = (bf16[128,256]{1,0:T(8,128)(2,1)}, bf16[128,256]{1,0:T(8,128)(2,1)S(1)}, u32[]{:S(2)}, u32[]{:S(2)}) collective-permute-start(bf16[128,256]{1,0:T(8,128)(2,1)} %shard_map.249), channel_id=1, source_target_pairs={{8,0},{9,1},{10,2},{11,3},{12,4},{13,5},{14,6},{15,7},{16,8},{17,9... | collective-permute-start | bytes 196616 | tf_op jit(solution)/shard_map/ppermute | solution.py:47
  302.4 60.0 %collective-permute-start.49 = (bf16[2,2,4,152,512]{4,3,2,1,0:T(8,128)(2,1)}, bf16[2,2,4,152,512]{4,3,2,1,0:T(8,128)(2,1)}, u32[]{:S(2)}, u32[]{:S(2)}) collective-permute-start(bf16[2,2,4,152,512]{4,3,2,1,0:T(8,128)(2,1)} %pad_maximum_fusion.3), channel_id=1, source_target_pairs={{0,1},{1,0},{2,3},{3,2},{4,5},{5,4},{6,7},{7,6},{8,9},{9,8},{10,11... | collective-permute-start | bytes 7471112 | tf_op jit(solution)/shard_map/ppermute | solution.py:41
  304.7 57.6 %collective-permute-start.48 = (bf16[2,2,4,152,512]{4,3,2,1,0:T(8,128)(2,1)}, bf16[2,2,4,152,512]{4,3,2,1,0:T(8,128)(2,1)}, u32[]{:S(2)}, u32[]{:S(2)}) collective-permute-start(bf16[2,2,4,152,512]{4,3,2,1,0:T(8,128)(2,1)} %pad_maximum_fusion.2), channel_id=1, source_target_pairs={{0,1},{1,0},{2,3},{3,2},{4,5},{5,4},{6,7},{7,6},{8,9},{9,8},{10,11... | collective-permute-start | bytes 7471112 | tf_op jit(solution)/shard_map/ppermute | solution.py:41
  314.5 47.8 %collective-permute-start.46 = (bf16[2,4,32,2816]{3,2,1,0:T(8,128)(2,1)S(1)}, bf16[2,4,32,2816]{3,2,1,0:T(8,128)(2,1)S(1)}, u32[]{:S(2)}, u32[]{:S(2)}) collective-permute-start(bf16[2,4,32,2816]{3,2,1,0:T(8,128)(2,1)S(1)} %get-tuple-element.398), channel_id=1, source_target_pairs={{0,2},{1,3},{2,0},{3,1},{4,6},{5,7},{6,4},{7,5},{8,10},{9,11},{10,... | collective-permute-start | bytes 4325384 | tf_op jit(solution)/shard_map/ppermute | solution.py:41
  316.2 46.1 %collective-permute-start.47 = (bf16[2,4,32,2816]{3,2,1,0:T(8,128)(2,1)S(1)}, bf16[2,4,32,2816]{3,2,1,0:T(8,128)(2,1)S(1)}, u32[]{:S(2)}, u32[]{:S(2)}) collective-permute-start(bf16[2,4,32,2816]{3,2,1,0:T(8,128)(2,1)S(1)} %get-tuple-element.399), channel_id=1, source_target_pairs={{0,4},{1,5},{2,6},{3,7},{4,0},{5,1},{6,2},{7,3},{8,12},{9,13},{10,... | collective-permute-start | bytes 4325384 | tf_op jit(solution)/shard_map/ppermute | solution.py:41
  317.8 10.9 %collective-permute-start.43 = (bf16[2,2,128,256]{3,2,0,1:T(8,128)(2,1)S(1)}, bf16[2,2,128,256]{3,2,0,1:T(8,128)(2,1)S(1)}, u32[]{:S(2)}, u32[]{:S(2)}) collective-permute-start(bf16[2,2,128,256]{3,2,0,1:T(8,128)(2,1)S(1)} %bitcast.297), channel_id=1, source_target_pairs={{0,1},{1,0},{2,3},{3,2},{4,5},{5,4},{6,7},{7,6},{8,9},{9,8},{10,11... | collective-permute-start | bytes 786440 | tf_op jit(solution)/shard_map/ppermute | solution.py:41
  328.7 25.5 %collective-permute-start.44 = (bf16[2,2,128,256]{3,2,1,0:T(8,128)(2,1)S(1)}, bf16[2,2,128,256]{3,2,1,0:T(8,128)(2,1)S(1)}, u32[]{:S(2)}, u32[]{:S(2)}) collective-permute-start(bf16[2,2,128,256]{3,2,1,0:T(8,128)(2,1)S(1)} %get-tuple-element.572), channel_id=1, source_target_pairs={{0,2},{1,3},{2,0},{3,1},{4,6},{5,7},{6,4},{7,5},{8,10},{9,11},{10,... | collective-permute-start | bytes 786440 | tf_op jit(solution)/shard_map/ppermute | solution.py:41
  368.6 60.6 %collective-permute-start.53 = (bf16[2,4,152,512]{3,2,1,0:T(8,128)(2,1)}, bf16[2,4,152,512]{3,2,1,0:T(8,128)(2,1)}, u32[]{:S(2)}, u32[]{:S(2)}) collective-permute-start(bf16[2,4,152,512]{3,2,1,0:T(8,128)(2,1)} %get-tuple-element.444), channel_id=1, source_target_pairs={{0,2},{1,3},{2,0},{3,1},{4,6},{5,7},{6,4},{7,5},{8,10},{9,11},{10,... | collective-permute-start | bytes 3735560 | tf_op jit(solution)/shard_map/ppermute | solution.py:41
  370.3 59.0 %collective-permute-start.54 = (bf16[2,4,152,512]{3,2,1,0:T(8,128)(2,1)}, bf16[2,4,152,512]{3,2,1,0:T(8,128)(2,1)}, u32[]{:S(2)}, u32[]{:S(2)}) collective-permute-start(bf16[2,4,152,512]{3,2,1,0:T(8,128)(2,1)} %get-tuple-element.445), channel_id=1, source_target_pairs={{0,4},{1,5},{2,6},{3,7},{4,0},{5,1},{6,2},{7,3},{8,12},{9,13},{10,... | collective-permute-start | bytes 3735560 | tf_op jit(solution)/shard_map/ppermute | solution.py:41
  375.5 38.3 %collective-permute-start.50 = (bf16[4,32,2816]{2,1,0:T(8,128)(2,1)}, bf16[4,32,2816]{2,1,0:T(8,128)(2,1)S(1)}, u32[]{:S(2)}, u32[]{:S(2)}) collective-permute-start(bf16[4,32,2816]{2,1,0:T(8,128)(2,1)} %get-tuple-element.425), channel_id=1, source_target_pairs={{0,4},{1,5},{2,6},{3,7},{4,0},{5,1},{6,2},{7,3},{8,12},{9,13},{10,... | collective-permute-start | bytes 2162696 | tf_op jit(solution)/shard_map/ppermute | solution.py:41
  376.0 37.8 %collective-permute-start.51 = (bf16[4,32,2816]{2,1,0:T(8,128)(2,1)}, bf16[4,32,2816]{2,1,0:T(8,128)(2,1)S(1)}, u32[]{:S(2)}, u32[]{:S(2)}) collective-permute-start(bf16[4,32,2816]{2,1,0:T(8,128)(2,1)} %get-tuple-element.426), channel_id=1, source_target_pairs={{0,2},{1,3},{2,0},{3,1},{4,6},{5,7},{6,4},{7,5},{8,10},{9,11},{10,... | collective-permute-start | bytes 2162696 | tf_op jit(solution)/shard_map/ppermute | solution.py:41
  413.8 14.7 %collective-permute-start.52 = (bf16[2,8,2048]{2,1,0:T(8,128)(2,1)S(1)}, bf16[2,8,2048]{2,1,0:T(8,128)(2,1)S(1)}, u32[]{:S(2)}, u32[]{:S(2)}) collective-permute-start(bf16[2,8,2048]{2,1,0:T(8,128)(2,1)S(1)} %convert_element_type.46), channel_id=1, source_target_pairs={{1,0},{2,1},{3,2},{4,3},{5,4},{6,5},{7,6},{8,7},{9,8},{10,9},{11,1... | collective-permute-start | bytes 196616 | tf_op jit(solution)/shard_map/ppermute | solution.py:47
  424.0 19.8 %collective-permute-start.57 = (bf16[32,5632]{1,0:T(8,128)(2,1)S(1)}, bf16[32,5632]{1,0:T(8,128)(2,1)S(1)}, u32[]{:S(2)}, u32[]{:S(2)}) collective-permute-start(bf16[32,5632]{1,0:T(8,128)(2,1)S(1)} %get-tuple-element.476), channel_id=1, source_target_pairs={{0,8},{1,9},{2,10},{3,11},{4,12},{5,13},{6,14},{7,15},{8,0},{9,1},... | collective-permute-start | bytes 1081352 | tf_op jit(solution)/shard_map/ppermute | solution.py:41
  427.0 34.9 %collective-permute-start.60 = (bf16[32,5632]{1,0:T(8,128)(2,1)}, bf16[32,5632]{1,0:T(8,128)(2,1)S(1)}, u32[]{:S(2)}, u32[]{:S(2)}) collective-permute-start(bf16[32,5632]{1,0:T(8,128)(2,1)} %get-tuple-element.482), channel_id=1, source_target_pairs={{0,16},{1,17},{2,18},{3,19},{4,20},{5,21},{6,22},{7,23},{8,24},{9,... | collective-permute-start | bytes 1081352 | tf_op jit(solution)/shard_map/ppermute | solution.py:41
  443.8 23.2 %collective-permute-start.58 = (bf16[2,2,4,32,1024]{4,3,2,1,0:T(8,128)(2,1)}, bf16[2,2,4,32,1024]{4,3,2,1,0:T(8,128)(2,1)}, u32[]{:S(2)}, u32[]{:S(2)}) collective-permute-start(bf16[2,2,4,32,1024]{4,3,2,1,0:T(8,128)(2,1)} %get-tuple-element.478), channel_id=1, source_target_pairs={{0,1},{1,0},{2,3},{3,2},{4,5},{5,4},{6,7},{7,6},{8,9},{9,8},{10,11... | collective-permute-start | bytes 3145736 | tf_op jit(solution)/shard_map/ppermute | solution.py:41
  443.9 23.2 %collective-permute-start.59 = (bf16[2,2,4,32,1024]{4,3,2,1,0:T(8,128)(2,1)}, bf16[2,2,4,32,1024]{4,3,2,1,0:T(8,128)(2,1)}, u32[]{:S(2)}, u32[]{:S(2)}) collective-permute-start(bf16[2,2,4,32,1024]{4,3,2,1,0:T(8,128)(2,1)} %get-tuple-element.480), channel_id=1, source_target_pairs={{0,1},{1,0},{2,3},{3,2},{4,5},{5,4},{6,7},{7,6},{8,9},{9,8},{10,11... | collective-permute-start | bytes 3145736 | tf_op jit(solution)/shard_map/ppermute | solution.py:41
  449.4 16.4 %collective-permute-start.55 = (bf16[4,152,512]{2,1,0:T(8,128)(2,1)}, bf16[4,152,512]{2,1,0:T(8,128)(2,1)S(1)}, u32[]{:S(2)}, u32[]{:S(2)}) collective-permute-start(bf16[4,152,512]{2,1,0:T(8,128)(2,1)} %get-tuple-element.462), channel_id=1, source_target_pairs={{0,4},{1,5},{2,6},{3,7},{4,0},{5,1},{6,2},{7,3},{8,12},{9,13},{10,... | collective-permute-start | bytes 1867784 | tf_op jit(solution)/shard_map/ppermute | solution.py:41
  451.0 16.0 %collective-permute-start.56 = (bf16[4,152,512]{2,1,0:T(8,128)(2,1)}, bf16[4,152,512]{2,1,0:T(8,128)(2,1)S(1)}, u32[]{:S(2)}, u32[]{:S(2)}) collective-permute-start(bf16[4,152,512]{2,1,0:T(8,128)(2,1)} %get-tuple-element.463), channel_id=1, source_target_pairs={{0,2},{1,3},{2,0},{3,1},{4,6},{5,7},{6,4},{7,5},{8,10},{9,11},{10,... | collective-permute-start | bytes 1867784 | tf_op jit(solution)/shard_map/ppermute | solution.py:41
  461.9 13.6 %collective-permute-start.64 = (bf16[32,5632]{1,0:T(8,128)(2,1)S(1)}, bf16[32,5632]{1,0:T(8,128)(2,1)S(1)}, u32[]{:S(2)}, u32[]{:S(2)}) collective-permute-start(bf16[32,5632]{1,0:T(8,128)(2,1)S(1)} %copy-done.56), channel_id=1, source_target_pairs={{0,24},{1,25},{2,26},{3,27},{4,28},{5,29},{6,30},{7,31},{8,16},{9,... | collective-permute-start | bytes 1081352 | tf_op jit(solution)/shard_map/ppermute | solution.py:41
  471.1 15.2 %collective-permute-start.61 = (bf16[2,4,32,1024]{3,2,1,0:T(8,128)(2,1)S(1)}, bf16[2,4,32,1024]{3,2,1,0:T(8,128)(2,1)S(1)}, u32[]{:S(2)}, u32[]{:S(2)}) collective-permute-start(bf16[2,4,32,1024]{3,2,1,0:T(8,128)(2,1)S(1)} %get-tuple-element.488), channel_id=1, source_target_pairs={{0,2},{1,3},{2,0},{3,1},{4,6},{5,7},{6,4},{7,5},{8,10},{9,11},{10,... | collective-permute-start | bytes 1572872 | tf_op jit(solution)/shard_map/ppermute | solution.py:41
  471.6 14.7 %collective-permute-start.62 = (bf16[2,4,32,1024]{3,2,1,0:T(8,128)(2,1)S(1)}, bf16[2,4,32,1024]{3,2,1,0:T(8,128)(2,1)S(1)}, u32[]{:S(2)}, u32[]{:S(2)}) collective-permute-start(bf16[2,4,32,1024]{3,2,1,0:T(8,128)(2,1)S(1)} %get-tuple-element.489), channel_id=1, source_target_pairs={{0,4},{1,5},{2,6},{3,7},{4,0},{5,1},{6,2},{7,3},{8,12},{9,13},{10,... | collective-permute-start | bytes 1572872 | tf_op jit(solution)/shard_map/ppermute | solution.py:41
  475.4 10.9 %collective-permute-start.65 = (bf16[152,1024]{1,0:T(8,128)(2,1)S(1)}, bf16[152,1024]{1,0:T(8,128)(2,1)S(1)}, u32[]{:S(2)}, u32[]{:S(2)}) collective-permute-start(bf16[152,1024]{1,0:T(8,128)(2,1)S(1)} %get-tuple-element.504), channel_id=1, source_target_pairs={{0,8},{1,9},{2,10},{3,11},{4,12},{5,13},{6,14},{7,15},{8,0},{9,1},... | collective-permute-start | bytes 933896 | tf_op jit(solution)/shard_map/ppermute | solution.py:41
  475.5 21.6 %collective-permute-start.69 = (bf16[152,1024]{1,0:T(8,128)(2,1)S(1)}, bf16[152,1024]{1,0:T(8,128)(2,1)S(1)}, u32[]{:S(2)}, u32[]{:S(2)}) collective-permute-start(bf16[152,1024]{1,0:T(8,128)(2,1)S(1)} %get-tuple-element.515), channel_id=1, source_target_pairs={{0,16},{1,17},{2,18},{3,19},{4,20},{5,21},{6,22},{7,23},{8,24},{9,... | collective-permute-start | bytes 933896 | tf_op jit(solution)/shard_map/ppermute | solution.py:41
  488.3 9.8 %collective-permute-start.66 = (bf16[4,32,1024]{2,1,0:T(8,128)(2,1)S(1)}, bf16[4,32,1024]{2,1,0:T(8,128)(2,1)S(1)}, u32[]{:S(2)}, u32[]{:S(2)}) collective-permute-start(bf16[4,32,1024]{2,1,0:T(8,128)(2,1)S(1)} %get-tuple-element.511), channel_id=1, source_target_pairs={{0,4},{1,5},{2,6},{3,7},{4,0},{5,1},{6,2},{7,3},{8,12},{9,13},{10,... | collective-permute-start | bytes 786440 | tf_op jit(solution)/shard_map/ppermute | solution.py:41
  489.7 8.4 %collective-permute-start.67 = (bf16[4,32,1024]{2,1,0:T(8,128)(2,1)S(1)}, bf16[4,32,1024]{2,1,0:T(8,128)(2,1)S(1)}, u32[]{:S(2)}, u32[]{:S(2)}) collective-permute-start(bf16[4,32,1024]{2,1,0:T(8,128)(2,1)S(1)} %get-tuple-element.512), channel_id=1, source_target_pairs={{0,2},{1,3},{2,0},{3,1},{4,6},{5,7},{6,4},{7,5},{8,10},{9,11},{10,... | collective-permute-start | bytes 786440 | tf_op jit(solution)/shard_map/ppermute | solution.py:41
  491.8 16.7 %collective-permute-start.72 = (bf16[152,1024]{1,0:T(8,128)(2,1)S(1)}, bf16[152,1024]{1,0:T(8,128)(2,1)S(1)}, u32[]{:S(2)}, u32[]{:S(2)}) collective-permute-start(bf16[152,1024]{1,0:T(8,128)(2,1)S(1)} %get-tuple-element.527), channel_id=1, source_target_pairs={{0,24},{1,25},{2,26},{3,27},{4,28},{5,29},{6,30},{7,31},{8,16},{9,... | collective-permute-start | bytes 933896 | tf_op jit(solution)/shard_map/ppermute | solution.py:41
  499.4 9.1 %collective-permute-start.71 = (bf16[32,2048]{1,0:T(8,128)(2,1)S(1)}, bf16[32,2048]{1,0:T(8,128)(2,1)S(1)}, u32[]{:S(2)}, u32[]{:S(2)}) collective-permute-start(bf16[32,2048]{1,0:T(8,128)(2,1)S(1)} %get-tuple-element.526), channel_id=1, source_target_pairs={{0,8},{1,9},{2,10},{3,11},{4,12},{5,13},{6,14},{7,15},{8,0},{9,1},... | collective-permute-start | bytes 393224 | tf_op jit(solution)/shard_map/ppermute | solution.py:41
  499.5 9.0 %collective-permute-start.70 = (f32[40,1024]{1,0:T(8,128)S(1)}, f32[40,1024]{1,0:T(8,128)S(1)}, u32[]{:S(2)}, u32[]{:S(2)}) collective-permute-start(f32[40,1024]{1,0:T(8,128)S(1)} %add.162), channel_id=1, source_target_pairs={{0,4},{1,5},{2,6},{3,7},{4,0},{5,1},{6,2},{7,3},{8,12},{9,13},{10,... | collective-permute-start | bytes 491528 | tf_op jit(solution)/shard_map/ppermute | solution.py:41
  503.1 12.5 %collective-permute-start.76 = (bf16[32,2048]{1,0:T(8,128)(2,1)S(1)}, bf16[32,2048]{1,0:T(8,128)(2,1)S(1)}, u32[]{:S(2)}, u32[]{:S(2)}) collective-permute-start(bf16[32,2048]{1,0:T(8,128)(2,1)S(1)} %get-tuple-element.533), channel_id=1, source_target_pairs={{0,16},{1,17},{2,18},{3,19},{4,20},{5,21},{6,22},{7,23},{8,24},{9,... | collective-permute-start | bytes 393224 | tf_op jit(solution)/shard_map/ppermute | solution.py:41
  505.7 9.9 %collective-permute-start.77 = (bf16[32,2048]{1,0:T(8,128)(2,1)S(1)}, bf16[32,2048]{1,0:T(8,128)(2,1)S(1)}, u32[]{:S(2)}, u32[]{:S(2)}) collective-permute-start(bf16[32,2048]{1,0:T(8,128)(2,1)S(1)} %get-tuple-element.534), channel_id=1, source_target_pairs={{0,24},{1,25},{2,26},{3,27},{4,28},{5,29},{6,30},{7,31},{8,16},{9,... | collective-permute-start | bytes 393224 | tf_op jit(solution)/shard_map/ppermute | solution.py:41
  515.9 8.4 %collective-permute-start.73 = (f32[40,1024]{1,0:T(8,128)S(1)}, f32[40,1024]{1,0:T(8,128)S(1)}, u32[]{:S(2)}, u32[]{:S(2)}) collective-permute-start(f32[40,1024]{1,0:T(8,128)S(1)} %add.163.refs_0_), channel_id=1, source_target_pairs={{0,8},{1,9},{2,10},{3,11},{4,12},{5,13},{6,14},{7,15},{8,0},{9,1},... | collective-permute-start | bytes 491528 | tf_op jit(solution)/shard_map/ppermute | solution.py:41
  518.5 13.5 %collective-permute-start.74 = (f32[40,1024]{1,0:T(8,128)S(1)}, f32[40,1024]{1,0:T(8,128)S(1)}, u32[]{:S(2)}, u32[]{:S(2)}) collective-permute-start(f32[40,1024]{1,0:T(8,128)S(1)} %add.163.refs_0_), channel_id=1, source_target_pairs={{0,16},{1,17},{2,18},{3,19},{4,20},{5,21},{6,22},{7,23},{8,24},{9,... | collective-permute-start | bytes 491528 | tf_op jit(solution)/shard_map/ppermute | solution.py:41
  518.7 13.2 %collective-permute-start.75 = (f32[40,1024]{1,0:T(8,128)S(1)}, f32[40,1024]{1,0:T(8,128)S(1)}, u32[]{:S(2)}, u32[]{:S(2)}) collective-permute-start(f32[40,1024]{1,0:T(8,128)S(1)} %add.163.refs_0_), channel_id=1, source_target_pairs={{0,24},{1,25},{2,26},{3,27},{4,28},{5,29},{6,30},{7,31},{8,16},{9,... | collective-permute-start | bytes 491528 | tf_op jit(solution)/shard_map/ppermute | solution.py:41
  (134 other events, 1443.2 us)

commit v4 on v3

--- a/solution.py
+++ b/solution.py
@@ -130,8 +130,8 @@
 
 
 def gather_first(levels):
-    half = levels[0].shape[1] // 2
-    stacked = jnp.stack(levels)
+    stacked = levels if isinstance(levels, jax.Array) else jnp.stack(levels)
+    half = stacked.shape[2] // 2
     axes = chip_axes()
     return [spread(stacked[..., :half], axes[2]), spread(stacked[..., half:], axes[1])]
 
@@ -419,19 +419,25 @@
     return found
 
 
+def phase_parts(pair, phase):
+    return [phase_sums(pair, phase, step) for step in range(1, chip_axes()[2][0])]
+
+
+def phase_swap(pair, phase, parts):
+    axes, received = chip_axes(), [[], []]
+    for step, sides in enumerate(parts):
+        for side, part in enumerate(sides):
+            stride = axes[((2, 1), (1, 2))[side][phase]][1]
+            received[side].append([swapped(part, (step + 1) * stride)])
+    return [terms + [parts] for terms, parts in zip(pair, received)]
+
+
 def phase_send(pair, phase):
-    axes = chip_axes()
-    size = axes[2][0]
-    received = [[], []]
-    for step in range(1, size):
-        for side, part in enumerate(phase_sums(pair, phase, step)):
-            stride = axes[((2, 1), (1, 2))[side][phase]][1]
-            received[side].append([swapped(part, step * stride)])
-    return [terms + [parts] for terms, parts in zip(pair, received)]
-
-
-def levels_send(pair):
-    own, *parts = level_sums(pair)
+    return phase_swap(pair, phase, phase_parts(pair, phase))
+
+
+def levels_send(sums):
+    own, *parts = sums
     stride = chip_axes()[0][1]
     return own, [swapped(part, (step + 1) * stride) for step, part in enumerate(parts)]
 
@@ -479,7 +485,7 @@
 
     def kernel(*refs):
         ins, (norm, conv, low, high, bias, head, ffn) = refs[: len(parts)], refs[len(parts) :]
-        total = sum(ref[...] for ref in ins)
+        total = sum((ref[...].astype(jnp.float32) for ref in ins[1:]), ins[0][...])
         low[...] = total[:rank]
         for h in range(HEADS):
             side, at = divmod(h * PER_HEAD, width)
@@ -1140,33 +1146,37 @@
         ),
     )
     wide_terms = cores_send([wide_terms])
-    beyond = shifted(composed(place, got, True), -GROUP)
+    total = composed(place, got, True)
+    total, parts, wide_terms = together(total, phase_parts(wide_terms, 0), wide_terms)
+    wide_terms = phase_swap(wide_terms, 0, parts)
+    beyond = shifted(total, -GROUP)
     g_terms = grad_products(normed, gate_vals_grad)
-    beyond, g_terms = together(beyond, g_terms)
+    beyond, g_terms, out_terms, down_terms = together(beyond, g_terms, out_terms, down_terms)
+    rest_terms = cores_send([g_terms, out_terms, down_terms])
     outgoing = composed(place, got, True, beyond)
-    outgoing, wide_terms = together(outgoing, wide_terms)
-    wide_terms = phase_send(wide_terms, 0)
-    rest_terms = cores_send([g_terms, out_terms, down_terms])
-    outgoing, _ = exchanged(outgoing)
+    shape = outgoing.shape
+    outgoing = outgoing.reshape((2, 2, 2) + shape[1:])
+    outgoing = jnp.stack(exchange_step(outgoing, 2, 1), axis=2)
+    outgoing = jnp.stack(exchange_step(outgoing, 1, 2), axis=1)
     outgoing, wide_terms, rest_terms = together(outgoing, wide_terms, rest_terms)
     wide_terms = phase_send(wide_terms, 1)
+    outgoing = jnp.stack(exchange_step(outgoing, 0, 4)).reshape(shape)
+    outgoing, wide_terms = together(outgoing, wide_terms)
+    wide_sums = level_sums(wide_terms)
+    outgoing, wide_sums, rest_terms = together(outgoing, wide_sums, rest_terms)
+    wide_own, wide_last = levels_send(wide_sums)
     rest_terms = phase_send(rest_terms, 0)
     backs = mixer_backward(
         place, wide_mixed, taps, logits, starts, mixer_grad, incoming, outgoing
     )
-    backs, wide_terms = together(backs, wide_terms)
-    wide_own, wide_last = levels_send(wide_terms)
+    backs, rest_terms, wide_last[0] = together(backs, rest_terms, wide_last[0])
+    rest_terms = phase_send(rest_terms, 1)
     mixed_grad, back_edge, back_tail, tap_grads, logit_grad, gate_bias_grad = backs
     back_edge = shifted(back_edge.astype(jnp.bfloat16), -1).astype(jnp.float32)
     mixed_grad = lax.dynamic_update_slice(
         mixed_grad, (back_tail + back_edge).astype(jnp.bfloat16), (0, block_len - HALO, 0)
     )
     mixed_grad = mixed_grad.reshape(row_count, conv_width)
-    mixed_grad, rest_terms = together(mixed_grad, rest_terms)
-    rest_terms = phase_send(rest_terms, 1)
-    fast_terms = grad_products(normed, mixed_grad)
-    fast_terms, wide_last[0] = together(fast_terms, wide_last[0])
-    fast_terms = cores_send([fast_terms])
     small_rows, lowrank_grad = small_packed(
         logit_grad.reshape(row_count, key_width),
         lowrank,
@@ -1187,22 +1197,28 @@
     norm_gain_grad = jnp.sum(normed_grad * layer_in * inv_rms, axis=0)
     input_grad = hidden_grad + rms_back(normed_grad, layer_in, inv_rms, norm_gain)
     small_rows = lax.dynamic_update_slice(small_rows, norm_gain_grad[None, :], (34, 0))
-    small_rows, rest_terms, fast_terms, input_grad, wide_last[1] = together(
-        small_rows, rest_terms, fast_terms, input_grad, wide_last[1]
-    )
+    mixed_grad, small_rows, rest_terms, input_grad, wide_last[1] = together(
+        mixed_grad, small_rows, rest_terms, input_grad, wide_last[1]
+    )
+    rest_sums = level_sums(rest_terms)
+    small_rows = spread(small_rows, axes[3])
+    mixed_grad, rest_sums, small_rows = together(mixed_grad, rest_sums, small_rows)
+    rest_own, rest_last = levels_send(rest_sums)
+    fast_terms = grad_products(normed, mixed_grad)
+    small_rows = spread(sum(small_rows), axes[2])
+    fast_terms, small_rows, wide_last[2] = together(fast_terms, small_rows, wide_last[2])
+    fast_terms = cores_send([fast_terms])
+    small_rows = spread(sum(small_rows), axes[1])
+    fast_terms, small_rows = together(fast_terms, small_rows)
     fast_terms = phase_send(fast_terms, 0)
-    rest_own, rest_last = levels_send(rest_terms)
-    small_rows = spread(small_rows, axes[3])
-    fast_terms, small_rows, wide_last[2], rest_last[0] = together(
-        fast_terms, small_rows, wide_last[2], rest_last[0]
-    )
+    small_rows = sum(small_rows)
+    fast_terms, small_rows, rest_last[0] = together(fast_terms, small_rows, rest_last[0])
     fast_terms = phase_send(fast_terms, 1)
-    small_rows = spread(sum(small_rows), axes[2])
-    fast_terms, small_rows, rest_last[1] = together(fast_terms, small_rows, rest_last[1])
-    fast_own, fast_last = levels_send(fast_terms)
-    small_rows = spread(sum(small_rows), axes[1])
-    small_rows, fast_last[0], rest_last[2] = together(small_rows, fast_last[0], rest_last[2])
-    small_parts = spread(sum(small_rows), axes[0])
+    fast_terms, rest_last[1] = together(fast_terms, rest_last[1])
+    fast_own, fast_last = levels_send(level_sums(fast_terms))
+    small_rows = [small_rows]
+    small_own = sum(small_rows)
+    small_parts = [small_own] + spread(small_own.astype(jnp.bfloat16), axes[0])[1:]
     norm_gain_grad, conv_weight_grad, w_low_grad, w_high_grad, *rows_found = small_unpacked(
         small_parts, key_width, w_high.shape[0]
     )

time: 544 us -> 522 us (0.960)
  waiting for transfers between devices: 184 us -> 175 us
  Pallas kernels: 177 us -> 170 us
  matrix products: 22.7 us -> 15.8 us
    ppermute x74, waiting for transfers between devices: 164 us -> 155 us  [swapped(): return lax.ppermute(array, 'seq', [(i, i ^ mask) for i in range(count)])]
    dot_general x7, matrix products: 18.4 us -> 11.5 us  [nt_dot(): lax.dot_general(left, right, (NT, ((), ())), preferred_element_type=jnp.f...]
    unnamed x249 -> x255, local copies, waits for them, and re-layouts: 28.7 us -> 31.5 us
  transfers between devices with their start and end apart: 78 -> 78, of which waited for: 30 -> 28; matrix products, arithmetic and copies ran while one was open for 9% -> 8% of each run, Pallas kernels for 25% -> 22%
where the time goes in v4:
time: 522 us; the launch traced here: 513 us
  waiting for transfers between devices  175 us (34%)
  Pallas kernels  170 us (33%)
  starting transfers between devices  80.2 us (15%)
  local copies, waits for them, and re-layouts  39.6 us (8%)
  other arithmetic  29.3 us (6%)
  matrix products  15.8 us (3%)
    ppermute x74, waiting for transfers between devices, swapped(): return lax.ppermute(array, 'seq', [(i, i ^ mask) for i in range(count)])  155 us
    ppermute x74, starting transfers between devices, swapped(): return lax.ppermute(array, 'seq', [(i, i ^ mask) for i in range(count)])  75.1 us
    pallas_call x4, Pallas kernels, launch(): pl.pallas_call(kernel, out_shape=[jax.ShapeDtypeStruct(shape, kind) for s...  47 us
    pallas_call x5, Pallas kernels, grad_products(): pl.pallas_call(kernel, out_shape=[shape for shape, _ in results], grid_sp...  32 us
    unnamed x255, local copies, waits for them, and re-layouts  31.5 us
    pallas_call x1, Pallas kernels, feed_forward(): pl.pallas_call(kernel, out_shape=[jax.ShapeDtypeStruct((tokens, width), j...  30.7 us
    pallas_call x6, Pallas kernels, phase_sums(): pl.pallas_call(kernel, out_shape=[jax.ShapeDtypeStruct(shape, jnp.bfloat1...  20.5 us
    ppermute x4, waiting for transfers between devices, shifted(): return lax.ppermute(array, 'seq', pairs)  20.4 us
  transfers between devices with their start and end apart: 78, of which 28 were waited for; matrix products, arithmetic and copies ran while one was open for 8% of the time, Pallas kernels for 22%

profile of v4, /device:TPU:0, one launch (start us, length us, event | category | flops | bytes accessed | tf_op | source)
XLA Modules:
  0.0 513.1 jit_solution(8038151066668227624)
XLA Ops:
  2.6 3.1 collective-permute-start.1
  5.7 2.6 collective-permute-start.2
  12.0 6.7 %collective-permute-done.2 = bf16[32,2048]{1,0:T(8,128)(2,1)S(1)} collective-permute-done((bf16[32,2048]{1,0:T(8,128)(2,1)S(1)}, bf16[32,2048]{1,0:T(8,128)(2,1)S(1)}, u32[]{:S(2)}, u32[]{:S(2)}) %collective-permute-start.2) | collective-permute-done | bytes 131104 | tf_op jit(solution)/shard_map/ppermute | solution.py:41
  21.9 2.0 collective-permute-start.6
  26.7 3.6 collective-permute-done.6
  31.9 4.0 collective-permute-start.9
  35.9 10.4 %collective-permute-done.9 = bf16[152,1024]{1,0:T(8,128)(2,1)S(1)} collective-permute-done((bf16[152,1024]{1,0:T(8,128)(2,1)S(1)}, bf16[152,1024]{1,0:T(8,128)(2,1)S(1)}, u32[]{:S(2)}, u32[]{:S(2)}) %collective-permute-start.9) | collective-permute-done | bytes 311328 | tf_op jit(solution)/shard_map/ppermute | solution.py:41
  51.7 7.5 %shard_map.237 = bf16[528,2048]{1,0:T(8,128)(2,1)S(1)} custom-call(s32[4]{0:T(128)S(1)} %pad_add_fusion.me, bf16[528,1024]{1,0:T(8,128)(2,1)S(1)} %bitcast.208, bf16[2,2,4,32,1024]{4,3,2,1,0:T(8,128)(2,1)} %pad_maximum_fusion.10.refs_0_, bf16[2,2,4,32,1024]{4,3,2,1,0:T(8,128)(2,1)} %collective-permute-done.10.refs_1_, ...), custom_call_target="tpu_custom_call" | custom-call | flops 6000000000 | tf_op jit(solution)/shard_map/pallas_call | solution.py:216
  59.2 2.3 collective-permute-done.12
  65.3 13.2 %shard_map.238 = (f32[2,256,1024]{2,1,0:T(8,128)S(1)}, f32[2,256,512]{2,1,0:T(8,128)S(1)}, bf16[8,144,256]{2,1,0:T(8,128)(2,1)S(1)}, f32[2,4,1,128]{3,2,1,0:T(1,128)S(1)}) custom-call(s32[2]{0:T(128)S(1)} %pad_add_fusion.1.first_ref.place_ref, bf16[2,264,2048]{2,1,0:T(8,128)(2,1)S(1)} %bitcast.248, f32[4,2048]{1,0:T(4,128)S(1)} %bitcast.233, ...), custom_call_target="tpu_custom_call" | custom-call | flops 12999999488 | tf_op jit(solution)/shard_map/pallas_call | solution.py:712
  80.7 8.7 %collective-permute-done.17 = bf16[2,2,144,256]{3,2,1,0:T(8,128)(2,1)S(1)} collective-permute-done((bf16[2,2,144,256]{3,2,1,0:T(8,128)(2,1)S(1)}, bf16[2,2,144,256]{3,2,1,0:T(8,128)(2,1)S(1)}, u32[]{:S(2)}, u32[]{:S(2)}) %collective-permute-start.17) | collective-permute-done | bytes 294944 | tf_op jit(solution)/shard_map/ppermute | solution.py:41
  90.5 7.4 %collective-permute-done.18 = bf16[2,2,144,256]{3,2,1,0:T(8,128)(2,1)S(1)} collective-permute-done((bf16[2,2,144,256]{3,2,1,0:T(8,128)(2,1)S(1)}, bf16[2,2,144,256]{3,2,1,0:T(8,128)(2,1)S(1)}, u32[]{:S(2)}, u32[]{:S(2)}) %collective-permute-start.18) | collective-permute-done | bytes 294944 | tf_op jit(solution)/shard_map/ppermute | solution.py:41
  102.2 4.4 collective-permute-start.22
  107.9 1.9 shard_map.239
  111.1 10.5 %collective-permute-done.19.refs_0_ = bf16[128,256]{1,0:T(8,128)(2,1)S(1)} collective-permute-done((bf16[128,256]{1,0:T(8,128)(2,1)}, bf16[128,256]{1,0:T(8,128)(2,1)S(1)}, u32[]{:S(2)}, u32[]{:S(2)}) %collective-permute-start.19) | collective-permute-done | bytes 65568 | tf_op jit(solution)/shard_map/ppermute | solution.py:47
  122.2 2.1 shard_map.240
  124.3 5.3 %collective-permute-done.22 = bf16[32,5632]{1,0:T(8,128)(2,1)S(1)} collective-permute-done((bf16[32,5632]{1,0:T(8,128)(2,1)S(1)}, bf16[32,5632]{1,0:T(8,128)(2,1)S(1)}, u32[]{:S(2)}, u32[]{:S(2)}) %collective-permute-start.22) | collective-permute-done | bytes 360480 | tf_op jit(solution)/shard_map/ppermute | solution.py:41
  129.6 2.0 pad_maximum_fusion.1.refs_0_
  131.8 2.0 pad_maximum_fusion.refs_0_
  135.7 4.7 collective-permute-done.24
  143.1 6.6 %collective-permute-done.25 = bf16[2,2,128,256]{3,2,1,0:T(8,128)(2,1)S(1)} collective-permute-done((bf16[2,2,128,256]{3,2,1,0:T(8,128)(2,1)S(1)}, bf16[2,2,128,256]{3,2,1,0:T(8,128)(2,1)S(1)}, u32[]{:S(2)}, u32[]{:S(2)}) %collective-permute-start.25) | collective-permute-done | bytes 262176 | tf_op jit(solution)/shard_map/ppermute | solution.py:41
  150.7 15.3 %collective-permute-done.26 = bf16[2,2,128,256]{3,2,1,0:T(8,128)(2,1)S(1)} collective-permute-done((bf16[2,2,128,256]{3,2,1,0:T(8,128)(2,1)S(1)}, bf16[2,2,128,256]{3,2,1,0:T(8,128)(2,1)S(1)}, u32[]{:S(2)}, u32[]{:S(2)}) %collective-permute-start.26) | collective-permute-done | bytes 262176 | tf_op jit(solution)/shard_map/ppermute | solution.py:41
  168.7 2.2 shard_map.241
  179.2 4.1 shard_map.243
  185.1 1.8 maximum_add_fusion.hid
  186.9 11.7 %collective-permute-done.32 = bf16[2,4,32,2816]{3,2,1,0:T(8,128)(2,1)} collective-permute-done((bf16[2,4,32,2816]{3,2,1,0:T(8,128)(2,1)S(1)}, bf16[2,4,32,2816]{3,2,1,0:T(8,128)(2,1)}, u32[]{:S(2)}, u32[]{:S(2)}) %collective-permute-start.32) | collective-permute-done | bytes 1441824 | tf_op jit(solution)/shard_map/ppermute | solution.py:41
  198.6 3.6 collective-permute-done.31
  202.7 4.9 collective-permute-done.35
  208.8 30.7 %shard_map.244 = (f32[512,1024]{1,0:T(8,128)}, f32[512,1024]{1,0:T(8,128)}, bf16[512,1024]{1,0:T(8,128)(2,1)}, bf16[512,1024]{1,0:T(8,128)(2,1)}, bf16[512,2816]...) custom-call(s32[4]{0:T(128)} %copy-done.53, ...), custom_call_target="tpu_custom_call" | custom-call | flops 28000000000 | tf_op jit(solution)/shard_map/pallas_call | solution.py:992
  239.5 1.9 fusion.16
  243.0 5.3 %shard_map.245 = (f32[2,256,1024]{2,1,0:T(8,128)S(1)}, bf16[2,256,1024]{2,1,0:T(8,128)(2,1)S(1)}, bf16[8,144,256]{2,1,0:T(8,128)(2,1)S(1)}, f32[2,4,1,256]{3,2,1,0:T(1,128)S(1)}) custom-call(s32[2]{0:T(128)S(1)} %copy-done.69, f32[2,256,1024]{2,1,0:T(8,128)S(1)} %copy-done.78, f32[2,256,512]{2,1,0:T(8,128)S(1)} %get-tuple-element.328.reach_ref, ...), custom_call_target="tpu_custom_call" | custom-call | flops 5000000000 | tf_op jit(solution)/shard_map/pallas_call | solution.py:712
  251.2 2.1 shard_map.246
  256.3 14.6 %shard_map.247 = (bf16[2,2,4,32,2816]{4,3,2,1,0:T(8,128)(2,1)}, bf16[2,2,4,32,2816]{4,3,2,1,0:T(8,128)(2,1)}, bf16[2,2,4,32,2816]{4,3,2,1,0:T(8,128)(2,1)}, bf16[2,2,4,32,2816]{4,3,2,1,0:T(8,128)(2,1)}) custom-call(s32[4]{0:T(128)S(1)} %copy-done.54, bf16[512,1024]{1,0:T(8,128)(2,1)S(1)} %copy-done.81, bf16[512,2816]{1,0:T(8,128)(2,1)} %get-tuple-element.396.a_ref, ...), custom_call_target="tpu_custom_call" | custom-call | flops 14476128256 | tf_op jit(solution)/shard_map/pallas_call | solution.py:288
  272.0 8.1 %shard_map.248 = (bf16[2,2,4,88,512]{4,3,2,1,0:T(8,128)(2,1)S(1)}, bf16[2,2,4,88,512]{4,3,2,1,0:T(8,128)(2,1)S(1)}, bf16[2,2,4,88,512]{4,3,2,1,0:T(8,128)(2,1)S(1)}, bf16[2,2,4,88,512]{4,3,2,1,0:T(8,128)(2,1)}) custom-call(s32[4]{0:T(128)S(1)} %copy-done.54, bf16[512,2816]{1,0:T(8,128)(2,1)} %get-tuple-element.404.left_ref, bf16[512,1024]{1,0:T(8,128)(2,1)S(1)} %bitcast.242, ...), custom_call_target="tpu_custom_call" | custom-call | flops 7988064256 | tf_op jit(solution)/shard_map/pallas_call | solution.py:288
  284.4 2.1 shard_map.249
  286.5 1.8 copy-done.2
  288.3 6.4 %shard_map.250 = (bf16[2,4,32,2816]{3,2,1,0:T(8,128)(2,1)}, bf16[2,4,32,2816]{3,2,1,0:T(8,128)(2,1)}) custom-call(bf16[2,2,4,32,2816]{4,3,2,1,0:T(8,128)(2,1)S(1)} %copy-done.1, bf16[2,2,4,32,2816]{4,3,2,1,0:T(8,128)(2,1)} %collective-permute-done.40.refs_1_, bf16[2,2,4,32,2816]{4,3,2,1,0:T(8,128)(2,1)S(1)} %copy-done.2, ...), custom_call_target="tpu_custom_call" | custom-call | flops 3000000000 | tf_op jit(solution)/shard_map/pallas_call | solution.py:356
  296.0 2.2 shard_map.251
  298.2 9.9 %collective-permute-done.42.refs_0_ = bf16[128,256]{1,0:T(8,128)(2,1)S(1)} collective-permute-done((bf16[128,256]{1,0:T(8,128)(2,1)S(1)}, bf16[128,256]{1,0:T(8,128)(2,1)S(1)}, u32[]{:S(2)}, u32[]{:S(2)}) %collective-permute-start.42) | collective-permute-done | bytes 65568 | tf_op jit(solution)/shard_map/ppermute | solution.py:47
  315.4 2.2 shard_map.252
  324.8 4.2 shard_map.259
  330.3 5.2 %shard_map.258 = bf16[4,2,2,2,32,1024]{5,4,3,2,1,0:T(8,128)(2,1)S(1)} custom-call(s32[4]{0:T(128)S(1)} %copy-done.54, bf16[2,2,4,32,1024]{4,3,2,1,0:T(8,128)(2,1)} %pad_maximum_fusion.10.refs_0_, bf16[2,2,4,32,1024]{4,3,2,1,0:T(8,128)(2,1)} %collective-permute-done.10.refs_1_), custom_call_target="tpu_custom_call" | custom-call | flops 2638400000 | tf_op jit(solution)/shard_map/pallas_call | solution.py:106
  335.6 16.4 %collective-permute-done.44 = bf16[2,2,128,256]{3,2,1,0:T(8,128)(2,1)S(1)} collective-permute-done((bf16[2,2,128,256]{3,2,1,0:T(8,128)(2,1)S(1)}, bf16[2,2,128,256]{3,2,1,0:T(8,128)(2,1)S(1)}, u32[]{:S(2)}, u32[]{:S(2)}) %collective-permute-start.44) | collective-permute-done | bytes 262176 | tf_op jit(solution)/shard_map/ppermute | solution.py:41
  352.1 3.0 shard_map.253
  358.5 2.1 fusion.14
  361.0 2.1 fusion.12
  363.1 15.4 %collective-permute-done.49 = bf16[2,2,128,256]{3,2,1,0:T(8,128)(2,1)S(1)} collective-permute-done((bf16[2,2,128,256]{3,2,1,0:T(8,128)(2,1)S(1)}, bf16[2,2,128,256]{3,2,1,0:T(8,128)(2,1)S(1)}, u32[]{:S(2)}, u32[]{:S(2)}) %collective-permute-start.49) | collective-permute-done | bytes 262176 | tf_op jit(solution)/shard_map/ppermute | solution.py:41
  378.6 3.4 shard_map.254
  383.0 5.5 %shard_map.256 = (bf16[2,4,152,512]{3,2,1,0:T(8,128)(2,1)S(1)}, bf16[2,4,152,512]{3,2,1,0:T(8,128)(2,1)S(1)}) custom-call(bf16[2,2,4,32,512]{4,3,2,1,0:T(8,128)(2,1)S(1)} %copy-done.17, bf16[2,2,4,32,512]{4,3,2,1,0:T(8,128)(2,1)S(1)} %get-tuple-element.529.refs_1_, bf16[2,2,4,88,512]{4,3,2,1,0:T(8,128)(2,1)S(1)} %copy-done.5, ...), custom_call_target="tpu_custom_call" | custom-call | flops 3000000000 | tf_op jit(solution)/shard_map/pallas_call | solution.py:356
  391.8 2.4 collective-permute-start.54
  394.2 2.0 collective-permute-start.58
  397.2 24.3 %shard_map.255 = (bf16[2,256,2048]{2,1,0:T(8,128)(2,1)S(1)}, f32[2,8,2048]{2,1,0:T(8,128)S(1)}, f32[2,8,2048]{2,1,0:T(8,128)S(1)}, f32[2,4,2048]{2,1,0:T(4,128)S...) custom-call(s32[2]{0:T(128)S(1)} %copy-done.70, bf16[2,264,2048]{2,1,0:T(8,128)(2,1)S(1)} %bitcast.249, ...), custom_call_target="tpu_custom_call" | custom-call | flops 24000000000 | tf_op jit(solution)/shard_map/pallas_call | solution.py:712
  422.9 3.7 shard_map.260
  434.9 2.2 fusion.7
  437.5 4.9 fusion.6
  444.1 2.7 shard_map.261
  448.2 5.0 shard_map.262
  456.6 4.4 collective-permute-done.64
  464.5 2.9 collective-permute-start.73
  467.4 11.1 %collective-permute-done.67 = bf16[152,1024]{1,0:T(8,128)(2,1)S(1)} collective-permute-done((bf16[152,1024]{1,0:T(8,128)(2,1)S(1)}, bf16[152,1024]{1,0:T(8,128)(2,1)S(1)}, u32[]{:S(2)}, u32[]{:S(2)}) %collective-permute-start.67) | collective-permute-done | bytes 311328 | tf_op jit(solution)/shard_map/ppermute | solution.py:41
  481.1 2.7 collective-permute-start.70
  486.6 2.1 convert_add_fusion
  496.1 3.2 collective-permute-start.75
  503.2 8.3 %collective-permute-done.75 = bf16[32,2048]{1,0:T(8,128)(2,1)S(1)} collective-permute-done((bf16[32,2048]{1,0:T(8,128)(2,1)S(1)}, bf16[32,2048]{1,0:T(8,128)(2,1)S(1)}, u32[]{:S(2)}, u32[]{:S(2)}) %collective-permute-start.75) | collective-permute-done | bytes 131104 | tf_op jit(solution)/shard_map/ppermute | solution.py:41
  (471 shorter events, 129.1 us)
Async XLA Ops:
  2.6 9.4 %collective-permute-start.1 = (bf16[32,2048]{1,0:T(8,128)(2,1)S(1)}, bf16[32,2048]{1,0:T(8,128)(2,1)S(1)}, u32[]{:S(2)}, u32[]{:S(2)}) collective-permute-start(bf16[32,2048]{1,0:T(8,128)(2,1)S(1)} %bitcast.286), channel_id=1, source_target_pairs={{0,8},{1,9},{2,10},{3,11},{4,12},{5,13},{6,14},{7,15},{8,0},{9,1},... | collective-permute-start | bytes 393224 | tf_op jit(solution)/shard_map/ppermute | solution.py:41
  5.7 12.9 %collective-permute-start.2 = (bf16[32,2048]{1,0:T(8,128)(2,1)S(1)}, bf16[32,2048]{1,0:T(8,128)(2,1)S(1)}, u32[]{:S(2)}, u32[]{:S(2)}) collective-permute-start(bf16[32,2048]{1,0:T(8,128)(2,1)S(1)} %bitcast.287), channel_id=1, source_target_pairs={{0,16},{1,17},{2,18},{3,19},{4,20},{5,21},{6,22},{7,23},{8,24},{9,... | collective-permute-start | bytes 393224 | tf_op jit(solution)/shard_map/ppermute | solution.py:41
  8.3 10.3 %collective-permute-start.3 = (bf16[32,2048]{1,0:T(8,128)(2,1)S(1)}, bf16[32,2048]{1,0:T(8,128)(2,1)S(1)}, u32[]{:S(2)}, u32[]{:S(2)}) collective-permute-start(bf16[32,2048]{1,0:T(8,128)(2,1)S(1)} %bitcast.288), channel_id=1, source_target_pairs={{0,24},{1,25},{2,26},{3,27},{4,28},{5,29},{6,30},{7,31},{8,16},{9,... | collective-permute-start | bytes 393224 | tf_op jit(solution)/shard_map/ppermute | solution.py:41
  21.9 8.3 %collective-permute-start.6 = (bf16[152,1024]{1,0:T(8,128)(2,1)S(1)}, bf16[152,1024]{1,0:T(8,128)(2,1)S(1)}, u32[]{:S(2)}, u32[]{:S(2)}) collective-permute-start(bf16[152,1024]{1,0:T(8,128)(2,1)S(1)} %pad_maximum_fusion.22), channel_id=1, source_target_pairs={{0,8},{1,9},{2,10},{3,11},{4,12},{5,13},{6,14},{7,15},{8,0},{9,1},... | collective-permute-start | bytes 933896 | tf_op jit(solution)/shard_map/ppermute | solution.py:41
  31.1 15.2 %collective-permute-start.8 = (bf16[2,4,32,1024]{3,2,1,0:T(8,128)(2,1)S(1)}, bf16[2,4,32,1024]{3,2,1,0:T(8,128)(2,1)S(1)}, u32[]{:S(2)}, u32[]{:S(2)}) collective-permute-start(bf16[2,4,32,1024]{3,2,1,0:T(8,128)(2,1)S(1)} %pad_maximum_fusion.17), channel_id=1, source_target_pairs={{0,2},{1,3},{2,0},{3,1},{4,6},{5,7},{6,4},{7,5},{8,10},{9,11},{10,... | collective-permute-start | bytes 1572872 | tf_op jit(solution)/shard_map/ppermute | solution.py:41
  31.5 14.7 %collective-permute-start.7 = (bf16[2,4,32,1024]{3,2,1,0:T(8,128)(2,1)S(1)}, bf16[2,4,32,1024]{3,2,1,0:T(8,128)(2,1)S(1)}, u32[]{:S(2)}, u32[]{:S(2)}) collective-permute-start(bf16[2,4,32,1024]{3,2,1,0:T(8,128)(2,1)S(1)} %pad_maximum_fusion.16), channel_id=1, source_target_pairs={{0,4},{1,5},{2,6},{3,7},{4,0},{5,1},{6,2},{7,3},{8,12},{9,13},{10,... | collective-permute-start | bytes 1572872 | tf_op jit(solution)/shard_map/ppermute | solution.py:41
  31.9 14.4 %collective-permute-start.9 = (bf16[152,1024]{1,0:T(8,128)(2,1)S(1)}, bf16[152,1024]{1,0:T(8,128)(2,1)S(1)}, u32[]{:S(2)}, u32[]{:S(2)}) collective-permute-start(bf16[152,1024]{1,0:T(8,128)(2,1)S(1)} %pad_maximum_fusion.22), channel_id=1, source_target_pairs={{0,16},{1,17},{2,18},{3,19},{4,20},{5,21},{6,22},{7,23},{8,24},{9,... | collective-permute-start | bytes 933896 | tf_op jit(solution)/shard_map/ppermute | solution.py:41
  49.3 12.3 %collective-permute-start.12 = (bf16[152,1024]{1,0:T(8,128)(2,1)}, bf16[152,1024]{1,0:T(8,128)(2,1)S(1)}, u32[]{:S(2)}, u32[]{:S(2)}) collective-permute-start(bf16[152,1024]{1,0:T(8,128)(2,1)} %copy-done.91), channel_id=1, source_target_pairs={{0,24},{1,25},{2,26},{3,27},{4,28},{5,29},{6,30},{7,31},{8,16},{9,... | collective-permute-start | bytes 933896 | tf_op jit(solution)/shard_map/ppermute | solution.py:41
  50.6 28.0 %collective-permute-start.15 = (bf16[32,5632]{1,0:T(8,128)(2,1)}, bf16[32,5632]{1,0:T(8,128)(2,1)S(1)}, u32[]{:S(2)}, u32[]{:S(2)}) collective-permute-start(bf16[32,5632]{1,0:T(8,128)(2,1)} %param.25), channel_id=1, source_target_pairs={{0,8},{1,9},{2,10},{3,11},{4,12},{5,13},{6,14},{7,15},{8,0},{9,1},... | collective-permute-start | bytes 1081352 | tf_op jit(solution)/shard_map/ppermute | solution.py:41
  61.8 16.7 %collective-permute-start.13 = (bf16[4,152,512]{2,1,0:T(8,128)(2,1)S(1)}, bf16[4,152,512]{2,1,0:T(8,128)(2,1)S(1)}, u32[]{:S(2)}, u32[]{:S(2)}) collective-permute-start(bf16[4,152,512]{2,1,0:T(8,128)(2,1)S(1)} %get-tuple-element.341), channel_id=1, source_target_pairs={{0,2},{1,3},{2,0},{3,1},{4,6},{5,7},{6,4},{7,5},{8,10},{9,11},{10,... | collective-permute-start | bytes 1867784 | tf_op jit(solution)/shard_map/ppermute | solution.py:41
  63.6 15.0 %collective-permute-start.14 = (bf16[4,152,512]{2,1,0:T(8,128)(2,1)S(1)}, bf16[4,152,512]{2,1,0:T(8,128)(2,1)S(1)}, u32[]{:S(2)}, u32[]{:S(2)}) collective-permute-start(bf16[4,152,512]{2,1,0:T(8,128)(2,1)S(1)} %get-tuple-element.343), channel_id=1, source_target_pairs={{0,4},{1,5},{2,6},{3,7},{4,0},{5,1},{6,2},{7,3},{8,12},{9,13},{10,... | collective-permute-start | bytes 1867784 | tf_op jit(solution)/shard_map/ppermute | solution.py:41
  80.4 9.1 %collective-permute-start.17 = (bf16[2,2,144,256]{3,2,1,0:T(8,128)(2,1)S(1)}, bf16[2,2,144,256]{3,2,1,0:T(8,128)(2,1)S(1)}, u32[]{:S(2)}, u32[]{:S(2)}) collective-permute-start(bf16[2,2,144,256]{3,2,1,0:T(8,128)(2,1)S(1)} %get-tuple-element.622), channel_id=1, source_target_pairs={{0,2},{1,3},{2,0},{3,1},{4,6},{5,7},{6,4},{7,5},{8,10},{9,11},{10,... | collective-permute-start | bytes 884744 | tf_op jit(solution)/shard_map/ppermute | solution.py:41
  89.5 8.3 %collective-permute-start.18 = (bf16[2,2,144,256]{3,2,1,0:T(8,128)(2,1)S(1)}, bf16[2,2,144,256]{3,2,1,0:T(8,128)(2,1)S(1)}, u32[]{:S(2)}, u32[]{:S(2)}) collective-permute-start(bf16[2,2,144,256]{3,2,1,0:T(8,128)(2,1)S(1)} %get-tuple-element.620), channel_id=1, source_target_pairs={{0,4},{1,5},{2,6},{3,7},{4,0},{5,1},{6,2},{7,3},{8,12},{9,13},{10,... | collective-permute-start | bytes 884744 | tf_op jit(solution)/shard_map/ppermute | solution.py:41
  99.8 29.8 %collective-permute-start.21 = (bf16[2,4,152,512]{3,2,1,0:T(8,128)(2,1)}, bf16[2,4,152,512]{3,2,1,0:T(8,128)(2,1)}, u32[]{:S(2)}, u32[]{:S(2)}) collective-permute-start(bf16[2,4,152,512]{3,2,1,0:T(8,128)(2,1)} %pad_maximum_fusion.9), channel_id=1, source_target_pairs={{0,2},{1,3},{2,0},{3,1},{4,6},{5,7},{6,4},{7,5},{8,10},{9,11},{10,... | collective-permute-start | bytes 3735560 | tf_op jit(solution)/shard_map/ppermute | solution.py:41
  101.3 28.3 %collective-permute-start.20 = (bf16[2,4,152,512]{3,2,1,0:T(8,128)(2,1)}, bf16[2,4,152,512]{3,2,1,0:T(8,128)(2,1)}, u32[]{:S(2)}, u32[]{:S(2)}) collective-permute-start(bf16[2,4,152,512]{3,2,1,0:T(8,128)(2,1)} %pad_maximum_fusion.8), channel_id=1, source_target_pairs={{0,4},{1,5},{2,6},{3,7},{4,0},{5,1},{6,2},{7,3},{8,12},{9,13},{10,... | collective-permute-start | bytes 3735560 | tf_op jit(solution)/shard_map/ppermute | solution.py:41
  102.2 27.4 %collective-permute-start.22 = (bf16[32,5632]{1,0:T(8,128)(2,1)S(1)}, bf16[32,5632]{1,0:T(8,128)(2,1)S(1)}, u32[]{:S(2)}, u32[]{:S(2)}) collective-permute-start(bf16[32,5632]{1,0:T(8,128)(2,1)S(1)} %copy-done.97), channel_id=1, source_target_pairs={{0,16},{1,17},{2,18},{3,19},{4,20},{5,21},{6,22},{7,23},{8,24},{9,... | collective-permute-start | bytes 1081352 | tf_op jit(solution)/shard_map/ppermute | solution.py:41
  106.6 23.0 %collective-permute-start.23 = (bf16[32,5632]{1,0:T(8,128)(2,1)S(1)}, bf16[32,5632]{1,0:T(8,128)(2,1)}, u32[]{:S(2)}, u32[]{:S(2)}) collective-permute-start(bf16[32,5632]{1,0:T(8,128)(2,1)S(1)} %copy-done.97), channel_id=1, source_target_pairs={{0,24},{1,25},{2,26},{3,27},{4,28},{5,29},{6,30},{7,31},{8,16},{9,... | collective-permute-start | bytes 1081352 | tf_op jit(solution)/shard_map/ppermute | solution.py:41
  109.8 11.8 %collective-permute-start.19 = (bf16[128,256]{1,0:T(8,128)(2,1)}, bf16[128,256]{1,0:T(8,128)(2,1)S(1)}, u32[]{:S(2)}, u32[]{:S(2)}) collective-permute-start(bf16[128,256]{1,0:T(8,128)(2,1)} %shard_map.239), channel_id=1, source_target_pairs={{0,8},{1,9},{2,10},{3,11},{4,12},{5,13},{6,14},{7,15},{8,16},{9,17... | collective-permute-start | bytes 196616 | tf_op jit(solution)/shard_map/ppermute | solution.py:47
  131.7 34.4 %collective-permute-start.28 = (bf16[2,2,4,152,512]{4,3,2,1,0:T(8,128)(2,1)S(1)}, bf16[2,2,4,152,512]{4,3,2,1,0:T(8,128)(2,1)S(1)}, u32[]{:S(2)}, u32[]{:S(2)}) collective-permute-start(bf16[2,2,4,152,512]{4,3,2,1,0:T(8,128)(2,1)S(1)} %pad_maximum_fusion.1.refs_0_), channel_id=1, source_target_pairs={{0,1},{1,0},{2,3},{3,2},{4,5},{5,4},{6,7},{7,6},{8,9},{9,8},{10,11... | collective-permute-start | bytes 7471112 | tf_op jit(solution)/shard_map/ppermute | solution.py:41
  133.8 32.3 %collective-permute-start.27 = (bf16[2,2,4,152,512]{4,3,2,1,0:T(8,128)(2,1)S(1)}, bf16[2,2,4,152,512]{4,3,2,1,0:T(8,128)(2,1)S(1)}, u32[]{:S(2)}, u32[]{:S(2)}) collective-permute-start(bf16[2,2,4,152,512]{4,3,2,1,0:T(8,128)(2,1)S(1)} %pad_maximum_fusion.refs_0_), channel_id=1, source_target_pairs={{0,1},{1,0},{2,3},{3,2},{4,5},{5,4},{6,7},{7,6},{8,9},{9,8},{10,11... | collective-permute-start | bytes 7471112 | tf_op jit(solution)/shard_map/ppermute | solution.py:41
  140.4 9.2 %collective-permute-start.25 = (bf16[2,2,128,256]{3,2,1,0:T(8,128)(2,1)S(1)}, bf16[2,2,128,256]{3,2,1,0:T(8,128)(2,1)S(1)}, u32[]{:S(2)}, u32[]{:S(2)}) collective-permute-start(bf16[2,2,128,256]{3,2,1,0:T(8,128)(2,1)S(1)} %get-tuple-element.634), channel_id=1, source_target_pairs={{0,2},{1,3},{2,0},{3,1},{4,6},{5,7},{6,4},{7,5},{8,10},{9,11},{10,... | collective-permute-start | bytes 786440 | tf_op jit(solution)/shard_map/ppermute | solution.py:41
  142.3 23.8 %collective-permute-start.29 = (bf16[4,32,2816]{2,1,0:T(8,128)(2,1)S(1)}, bf16[4,32,2816]{2,1,0:T(8,128)(2,1)S(1)}, u32[]{:S(2)}, u32[]{:S(2)}) collective-permute-start(bf16[4,32,2816]{2,1,0:T(8,128)(2,1)S(1)} %get-tuple-element.366), channel_id=1, source_target_pairs={{0,2},{1,3},{2,0},{3,1},{4,6},{5,7},{6,4},{7,5},{8,10},{9,11},{10,... | collective-permute-start | bytes 2162696 | tf_op jit(solution)/shard_map/ppermute | solution.py:41
  142.7 23.3 %collective-permute-start.30 = (bf16[4,32,2816]{2,1,0:T(8,128)(2,1)S(1)}, bf16[4,32,2816]{2,1,0:T(8,128)(2,1)S(1)}, u32[]{:S(2)}, u32[]{:S(2)}) collective-permute-start(bf16[4,32,2816]{2,1,0:T(8,128)(2,1)S(1)} %get-tuple-element.368), channel_id=1, source_target_pairs={{0,4},{1,5},{2,6},{3,7},{4,0},{5,1},{6,2},{7,3},{8,12},{9,13},{10,... | collective-permute-start | bytes 2162696 | tf_op jit(solution)/shard_map/ppermute | solution.py:41
  149.7 16.3 %collective-permute-start.26 = (bf16[2,2,128,256]{3,2,1,0:T(8,128)(2,1)S(1)}, bf16[2,2,128,256]{3,2,1,0:T(8,128)(2,1)S(1)}, u32[]{:S(2)}, u32[]{:S(2)}) collective-permute-start(bf16[2,2,128,256]{3,2,1,0:T(8,128)(2,1)S(1)} %get-tuple-element.632), channel_id=1, source_target_pairs={{0,4},{1,5},{2,6},{3,7},{4,0},{5,1},{6,2},{7,3},{8,12},{9,13},{10,... | collective-permute-start | bytes 786440 | tf_op jit(solution)/shard_map/ppermute | solution.py:41
  166.2 32.4 %collective-permute-start.32 = (bf16[2,4,32,2816]{3,2,1,0:T(8,128)(2,1)S(1)}, bf16[2,4,32,2816]{3,2,1,0:T(8,128)(2,1)}, u32[]{:S(2)}, u32[]{:S(2)}) collective-permute-start(bf16[2,4,32,2816]{3,2,1,0:T(8,128)(2,1)S(1)} %pad_maximum_fusion.6), channel_id=1, source_target_pairs={{0,2},{1,3},{2,0},{3,1},{4,6},{5,7},{6,4},{7,5},{8,10},{9,11},{10,... | collective-permute-start | bytes 4325384 | tf_op jit(solution)/shard_map/ppermute | solution.py:41
  167.9 30.7 %collective-permute-start.34 = (bf16[2,4,32,2816]{3,2,1,0:T(8,128)(2,1)S(1)}, bf16[2,4,32,2816]{3,2,1,0:T(8,128)(2,1)}, u32[]{:S(2)}, u32[]{:S(2)}) collective-permute-start(bf16[2,4,32,2816]{3,2,1,0:T(8,128)(2,1)S(1)} %pad_maximum_fusion.6), channel_id=1, source_target_pairs={{0,1},{1,0},{2,3},{3,2},{4,5},{5,4},{6,7},{7,6},{8,9},{9,8},{10,11... | collective-permute-start | bytes 4325384 | tf_op jit(solution)/shard_map/ppermute | solution.py:41
  168.1 34.2 %collective-permute-start.31 = (bf16[2,4,32,2816]{3,2,1,0:T(8,128)(2,1)S(1)}, bf16[2,4,32,2816]{3,2,1,0:T(8,128)(2,1)}, u32[]{:S(2)}, u32[]{:S(2)}) collective-permute-start(bf16[2,4,32,2816]{3,2,1,0:T(8,128)(2,1)S(1)} %pad_maximum_fusion.5), channel_id=1, source_target_pairs={{0,4},{1,5},{2,6},{3,7},{4,0},{5,1},{6,2},{7,3},{8,12},{9,13},{10,... | collective-permute-start | bytes 4325384 | tf_op jit(solution)/shard_map/ppermute | solution.py:41
  168.5 33.7 %collective-permute-start.33 = (bf16[2,4,32,2816]{3,2,1,0:T(8,128)(2,1)S(1)}, bf16[2,4,32,2816]{3,2,1,0:T(8,128)(2,1)}, u32[]{:S(2)}, u32[]{:S(2)}) collective-permute-start(bf16[2,4,32,2816]{3,2,1,0:T(8,128)(2,1)S(1)} %pad_maximum_fusion.5), channel_id=1, source_target_pairs={{0,1},{1,0},{2,3},{3,2},{4,5},{5,4},{6,7},{7,6},{8,9},{9,8},{10,11... | collective-permute-start | bytes 4325384 | tf_op jit(solution)/shard_map/ppermute | solution.py:41
  255.8 15.1 %collective-permute-start.38 = (bf16[2,2,144,256]{3,2,1,0:T(8,128)(2,1)S(1)}, bf16[2,2,144,256]{3,2,1,0:T(8,128)(2,1)S(1)}, u32[]{:S(2)}, u32[]{:S(2)}) collective-permute-start(bf16[2,2,144,256]{3,2,1,0:T(8,128)(2,1)S(1)} %get-tuple-element.615), channel_id=1, source_target_pairs={{0,2},{1,3},{2,0},{3,1},{4,6},{5,7},{6,4},{7,5},{8,10},{9,11},{10,... | collective-permute-start | bytes 884744 | tf_op jit(solution)/shard_map/ppermute | solution.py:41
  271.0 15.5 %collective-permute-start.40 = (bf16[2,2,4,32,2816]{4,3,2,1,0:T(8,128)(2,1)}, bf16[2,2,4,32,2816]{4,3,2,1,0:T(8,128)(2,1)}, u32[]{:S(2)}, u32[]{:S(2)}) collective-permute-start(bf16[2,2,4,32,2816]{4,3,2,1,0:T(8,128)(2,1)} %get-tuple-element.412), channel_id=1, source_target_pairs={{0,1},{1,0},{2,3},{3,2},{4,5},{5,4},{6,7},{7,6},{8,9},{9,8},{10,11... | collective-permute-start | bytes 8650760 | tf_op jit(solution)/shard_map/ppermute | solution.py:41
  271.0 15.4 %collective-permute-start.41 = (bf16[2,2,4,32,2816]{4,3,2,1,0:T(8,128)(2,1)}, bf16[2,2,4,32,2816]{4,3,2,1,0:T(8,128)(2,1)}, u32[]{:S(2)}, u32[]{:S(2)}) collective-permute-start(bf16[2,2,4,32,2816]{4,3,2,1,0:T(8,128)(2,1)} %get-tuple-element.414), channel_id=1, source_target_pairs={{0,1},{1,0},{2,3},{3,2},{4,5},{5,4},{6,7},{7,6},{8,9},{9,8},{10,11... | collective-permute-start | bytes 8650760 | tf_op jit(solution)/shard_map/ppermute | solution.py:41
  271.6 11.9 %collective-permute-start.39 = (bf16[2,2,144,256]{3,2,1,0:T(8,128)(2,1)S(1)}, bf16[2,2,144,256]{3,2,1,0:T(8,128)(2,1)S(1)}, u32[]{:S(2)}, u32[]{:S(2)}) collective-permute-start(bf16[2,2,144,256]{3,2,1,0:T(8,128)(2,1)S(1)} %get-tuple-element.613), channel_id=1, source_target_pairs={{0,4},{1,5},{2,6},{3,7},{4,0},{5,1},{6,2},{7,3},{8,12},{9,13},{10,... | collective-permute-start | bytes 884744 | tf_op jit(solution)/shard_map/ppermute | solution.py:41
  294.7 13.4 %collective-permute-start.42 = (bf16[128,256]{1,0:T(8,128)(2,1)S(1)}, bf16[128,256]{1,0:T(8,128)(2,1)S(1)}, u32[]{:S(2)}, u32[]{:S(2)}) collective-permute-start(bf16[128,256]{1,0:T(8,128)(2,1)S(1)} %copy-done.120), channel_id=1, source_target_pairs={{8,0},{9,1},{10,2},{11,3},{12,4},{13,5},{14,6},{15,7},{16,8},{17,9... | collective-permute-start | bytes 196616 | tf_op jit(solution)/shard_map/ppermute | solution.py:47
  309.9 42.1 %collective-permute-start.48 = (bf16[2,2,4,152,512]{4,3,2,1,0:T(8,128)(2,1)}, bf16[2,2,4,152,512]{4,3,2,1,0:T(8,128)(2,1)}, u32[]{:S(2)}, u32[]{:S(2)}) collective-permute-start(bf16[2,2,4,152,512]{4,3,2,1,0:T(8,128)(2,1)} %pad_maximum_fusion.3), channel_id=1, source_target_pairs={{0,1},{1,0},{2,3},{3,2},{4,5},{5,4},{6,7},{7,6},{8,9},{9,8},{10,11... | collective-permute-start | bytes 7471112 | tf_op jit(solution)/shard_map/ppermute | solution.py:41
  312.1 39.9 %collective-permute-start.47 = (bf16[2,2,4,152,512]{4,3,2,1,0:T(8,128)(2,1)}, bf16[2,2,4,152,512]{4,3,2,1,0:T(8,128)(2,1)}, u32[]{:S(2)}, u32[]{:S(2)}) collective-permute-start(bf16[2,2,4,152,512]{4,3,2,1,0:T(8,128)(2,1)} %pad_maximum_fusion.2), channel_id=1, source_target_pairs={{0,1},{1,0},{2,3},{3,2},{4,5},{5,4},{6,7},{7,6},{8,9},{9,8},{10,11... | collective-permute-start | bytes 7471112 | tf_op jit(solution)/shard_map/ppermute | solution.py:41
  312.2 39.8 %collective-permute-start.45 = (bf16[2,4,32,2816]{3,2,1,0:T(8,128)(2,1)}, bf16[2,4,32,2816]{3,2,1,0:T(8,128)(2,1)}, u32[]{:S(2)}, u32[]{:S(2)}) collective-permute-start(bf16[2,4,32,2816]{3,2,1,0:T(8,128)(2,1)} %get-tuple-element.434), channel_id=1, source_target_pairs={{0,2},{1,3},{2,0},{3,1},{4,6},{5,7},{6,4},{7,5},{8,10},{9,11},{10,... | collective-permute-start | bytes 4325384 | tf_op jit(solution)/shard_map/ppermute | solution.py:41
  313.8 38.2 %collective-permute-start.46 = (bf16[2,4,32,2816]{3,2,1,0:T(8,128)(2,1)}, bf16[2,4,32,2816]{3,2,1,0:T(8,128)(2,1)}, u32[]{:S(2)}, u32[]{:S(2)}) collective-permute-start(bf16[2,4,32,2816]{3,2,1,0:T(8,128)(2,1)} %get-tuple-element.437), channel_id=1, source_target_pairs={{0,4},{1,5},{2,6},{3,7},{4,0},{5,1},{6,2},{7,3},{8,12},{9,13},{10,... | collective-permute-start | bytes 4325384 | tf_op jit(solution)/shard_map/ppermute | solution.py:41
  323.1 28.8 %collective-permute-start.44 = (bf16[2,2,128,256]{3,2,1,0:T(8,128)(2,1)S(1)}, bf16[2,2,128,256]{3,2,1,0:T(8,128)(2,1)S(1)}, u32[]{:S(2)}, u32[]{:S(2)}) collective-permute-start(bf16[2,2,128,256]{3,2,1,0:T(8,128)(2,1)S(1)} %get-tuple-element.628), channel_id=1, source_target_pairs={{0,2},{1,3},{2,0},{3,1},{4,6},{5,7},{6,4},{7,5},{8,10},{9,11},{10,... | collective-permute-start | bytes 786440 | tf_op jit(solution)/shard_map/ppermute | solution.py:41
  355.1 23.4 %collective-permute-start.50 = (bf16[4,32,2816]{2,1,0:T(8,128)(2,1)S(1)}, bf16[4,32,2816]{2,1,0:T(8,128)(2,1)S(1)}, u32[]{:S(2)}, u32[]{:S(2)}) collective-permute-start(bf16[4,32,2816]{2,1,0:T(8,128)(2,1)S(1)} %get-tuple-element.457), channel_id=1, source_target_pairs={{0,4},{1,5},{2,6},{3,7},{4,0},{5,1},{6,2},{7,3},{8,12},{9,13},{10,... | collective-permute-start | bytes 2162696 | tf_op jit(solution)/shard_map/ppermute | solution.py:41
  356.8 21.7 %collective-permute-start.51 = (bf16[4,32,2816]{2,1,0:T(8,128)(2,1)S(1)}, bf16[4,32,2816]{2,1,0:T(8,128)(2,1)S(1)}, u32[]{:S(2)}, u32[]{:S(2)}) collective-permute-start(bf16[4,32,2816]{2,1,0:T(8,128)(2,1)S(1)} %get-tuple-element.458), channel_id=1, source_target_pairs={{0,2},{1,3},{2,0},{3,1},{4,6},{5,7},{6,4},{7,5},{8,10},{9,11},{10,... | collective-permute-start | bytes 2162696 | tf_op jit(solution)/shard_map/ppermute | solution.py:41
  360.6 17.9 %collective-permute-start.49 = (bf16[2,2,128,256]{3,2,1,0:T(8,128)(2,1)S(1)}, bf16[2,2,128,256]{3,2,1,0:T(8,128)(2,1)S(1)}, u32[]{:S(2)}, u32[]{:S(2)}) collective-permute-start(bf16[2,2,128,256]{3,2,1,0:T(8,128)(2,1)S(1)} %get-tuple-element.626), channel_id=1, source_target_pairs={{0,4},{1,5},{2,6},{3,7},{4,0},{5,1},{6,2},{7,3},{8,12},{9,13},{10,... | collective-permute-start | bytes 786440 | tf_op jit(solution)/shard_map/ppermute | solution.py:41
  388.5 33.0 %collective-permute-start.52 = (bf16[2,4,152,512]{3,2,1,0:T(8,128)(2,1)S(1)}, bf16[2,4,152,512]{3,2,1,0:T(8,128)(2,1)S(1)}, u32[]{:S(2)}, u32[]{:S(2)}) collective-permute-start(bf16[2,4,152,512]{3,2,1,0:T(8,128)(2,1)S(1)} %get-tuple-element.495), channel_id=1, source_target_pairs={{0,2},{1,3},{2,0},{3,1},{4,6},{5,7},{6,4},{7,5},{8,10},{9,11},{10,... | collective-permute-start | bytes 3735560 | tf_op jit(solution)/shard_map/ppermute | solution.py:41
  390.2 31.4 %collective-permute-start.53 = (bf16[2,4,152,512]{3,2,1,0:T(8,128)(2,1)S(1)}, bf16[2,4,152,512]{3,2,1,0:T(8,128)(2,1)S(1)}, u32[]{:S(2)}, u32[]{:S(2)}) collective-permute-start(bf16[2,4,152,512]{3,2,1,0:T(8,128)(2,1)S(1)} %get-tuple-element.496), channel_id=1, source_target_pairs={{0,4},{1,5},{2,6},{3,7},{4,0},{5,1},{6,2},{7,3},{8,12},{9,13},{10,... | collective-permute-start | bytes 3735560 | tf_op jit(solution)/shard_map/ppermute | solution.py:41
  391.8 29.7 %collective-permute-start.54 = (bf16[32,5632]{1,0:T(8,128)(2,1)S(1)}, bf16[32,5632]{1,0:T(8,128)(2,1)S(1)}, u32[]{:S(2)}, u32[]{:S(2)}) collective-permute-start(bf16[32,5632]{1,0:T(8,128)(2,1)S(1)} %get-tuple-element.497), channel_id=1, source_target_pairs={{0,8},{1,9},{2,10},{3,11},{4,12},{5,13},{6,14},{7,15},{8,0},{9,1},... | collective-permute-start | bytes 1081352 | tf_op jit(solution)/shard_map/ppermute | solution.py:41
  394.2 48.2 %collective-permute-start.58 = (bf16[32,5632]{1,0:T(8,128)(2,1)}, bf16[32,5632]{1,0:T(8,128)(2,1)}, u32[]{:S(2)}, u32[]{:S(2)}) collective-permute-start(bf16[32,5632]{1,0:T(8,128)(2,1)} %get-tuple-element.525), channel_id=1, source_target_pairs={{0,16},{1,17},{2,18},{3,19},{4,20},{5,21},{6,22},{7,23},{8,24},{9,... | collective-permute-start | bytes 1081352 | tf_op jit(solution)/shard_map/ppermute | solution.py:41
  396.2 57.0 %collective-permute-start.61 = (bf16[32,5632]{1,0:T(8,128)(2,1)}, bf16[32,5632]{1,0:T(8,128)(2,1)}, u32[]{:S(2)}, u32[]{:S(2)}) collective-permute-start(bf16[32,5632]{1,0:T(8,128)(2,1)} %get-tuple-element.552), channel_id=1, source_target_pairs={{0,24},{1,25},{2,26},{3,27},{4,28},{5,29},{6,30},{7,31},{8,16},{9,... | collective-permute-start | bytes 1081352 | tf_op jit(solution)/shard_map/ppermute | solution.py:41
  421.5 8.1 %collective-permute-start.55 = (bf16[2,8,2048]{2,1,0:T(8,128)(2,1)S(1)}, bf16[2,8,2048]{2,1,0:T(8,128)(2,1)S(1)}, u32[]{:S(2)}, u32[]{:S(2)}) collective-permute-start(bf16[2,8,2048]{2,1,0:T(8,128)(2,1)S(1)} %convert_element_type.49), channel_id=1, source_target_pairs={{1,0},{2,1},{3,2},{4,3},{5,4},{6,5},{7,6},{8,7},{9,8},{10,9},{11,1... | collective-permute-start | bytes 196616 | tf_op jit(solution)/shard_map/ppermute | solution.py:47
  426.6 17.1 %collective-permute-start.56 = (bf16[4,152,512]{2,1,0:T(8,128)(2,1)}, bf16[4,152,512]{2,1,0:T(8,128)(2,1)}, u32[]{:S(2)}, u32[]{:S(2)}) collective-permute-start(bf16[4,152,512]{2,1,0:T(8,128)(2,1)} %get-tuple-element.522), channel_id=1, source_target_pairs={{0,4},{1,5},{2,6},{3,7},{4,0},{5,1},{6,2},{7,3},{8,12},{9,13},{10,... | collective-permute-start | bytes 1867784 | tf_op jit(solution)/shard_map/ppermute | solution.py:41
  427.6 16.5 %collective-permute-start.57 = (bf16[4,152,512]{2,1,0:T(8,128)(2,1)}, bf16[4,152,512]{2,1,0:T(8,128)(2,1)}, u32[]{:S(2)}, u32[]{:S(2)}) collective-permute-start(bf16[4,152,512]{2,1,0:T(8,128)(2,1)} %get-tuple-element.523), channel_id=1, source_target_pairs={{0,2},{1,3},{2,0},{3,1},{4,6},{5,7},{6,4},{7,5},{8,10},{9,11},{10,... | collective-permute-start | bytes 1867784 | tf_op jit(solution)/shard_map/ppermute | solution.py:41
  447.7 6.7 %collective-permute-start.60 = (f32[40,1024]{1,0:T(8,128)S(1)}, f32[40,1024]{1,0:T(8,128)S(1)}, u32[]{:S(2)}, u32[]{:S(2)}) collective-permute-start(f32[40,1024]{1,0:T(8,128)S(1)} %add.161), channel_id=1, source_target_pairs={{0,2},{1,3},{2,0},{3,1},{4,6},{5,7},{6,4},{7,5},{8,10},{9,11},{10,... | collective-permute-start | bytes 491528 | tf_op jit(solution)/shard_map/ppermute | solution.py:41
  454.3 6.7 %collective-permute-start.62 = (bf16[2,2,4,32,1024]{4,3,2,1,0:T(8,128)(2,1)S(1)}, bf16[2,2,4,32,1024]{4,3,2,1,0:T(8,128)(2,1)S(1)}, u32[]{:S(2)}, u32[]{:S(2)}) collective-permute-start(bf16[2,2,4,32,1024]{4,3,2,1,0:T(8,128)(2,1)S(1)} %get-tuple-element.554), channel_id=1, source_target_pairs={{0,1},{1,0},{2,3},{3,2},{4,5},{5,4},{6,7},{7,6},{8,9},{9,8},{10,11... | collective-permute-start | bytes 3145736 | tf_op jit(solution)/shard_map/ppermute | solution.py:41
  454.4 6.7 %collective-permute-start.63 = (bf16[2,2,4,32,1024]{4,3,2,1,0:T(8,128)(2,1)S(1)}, bf16[2,2,4,32,1024]{4,3,2,1,0:T(8,128)(2,1)S(1)}, u32[]{:S(2)}, u32[]{:S(2)}) collective-permute-start(bf16[2,2,4,32,1024]{4,3,2,1,0:T(8,128)(2,1)S(1)} %get-tuple-element.556), channel_id=1, source_target_pairs={{0,1},{1,0},{2,3},{3,2},{4,5},{5,4},{6,7},{7,6},{8,9},{9,8},{10,11... | collective-permute-start | bytes 3145736 | tf_op jit(solution)/shard_map/ppermute | solution.py:41
  461.4 17.1 %collective-permute-start.65 = (bf16[2,4,32,1024]{3,2,1,0:T(8,128)(2,1)S(1)}, bf16[2,4,32,1024]{3,2,1,0:T(8,128)(2,1)S(1)}, u32[]{:S(2)}, u32[]{:S(2)}) collective-permute-start(bf16[2,4,32,1024]{3,2,1,0:T(8,128)(2,1)S(1)} %get-tuple-element.563), channel_id=1, source_target_pairs={{0,2},{1,3},{2,0},{3,1},{4,6},{5,7},{6,4},{7,5},{8,10},{9,11},{10,... | collective-permute-start | bytes 1572872 | tf_op jit(solution)/shard_map/ppermute | solution.py:41
  462.2 16.3 %collective-permute-start.66 = (bf16[2,4,32,1024]{3,2,1,0:T(8,128)(2,1)S(1)}, bf16[2,4,32,1024]{3,2,1,0:T(8,128)(2,1)S(1)}, u32[]{:S(2)}, u32[]{:S(2)}) collective-permute-start(bf16[2,4,32,1024]{3,2,1,0:T(8,128)(2,1)S(1)} %get-tuple-element.564), channel_id=1, source_target_pairs={{0,4},{1,5},{2,6},{3,7},{4,0},{5,1},{6,2},{7,3},{8,12},{9,13},{10,... | collective-permute-start | bytes 1572872 | tf_op jit(solution)/shard_map/ppermute | solution.py:41
  463.9 14.6 %collective-permute-start.67 = (bf16[152,1024]{1,0:T(8,128)(2,1)S(1)}, bf16[152,1024]{1,0:T(8,128)(2,1)S(1)}, u32[]{:S(2)}, u32[]{:S(2)}) collective-permute-start(bf16[152,1024]{1,0:T(8,128)(2,1)S(1)} %get-tuple-element.567), channel_id=1, source_target_pairs={{0,8},{1,9},{2,10},{3,11},{4,12},{5,13},{6,14},{7,15},{8,0},{9,1},... | collective-permute-start | bytes 933896 | tf_op jit(solution)/shard_map/ppermute | solution.py:41
  464.5 27.8 %collective-permute-start.73 = (bf16[152,1024]{1,0:T(8,128)(2,1)}, bf16[152,1024]{1,0:T(8,128)(2,1)}, u32[]{:S(2)}, u32[]{:S(2)}) collective-permute-start(bf16[152,1024]{1,0:T(8,128)(2,1)} %get-tuple-element.578), channel_id=1, source_target_pairs={{0,16},{1,17},{2,18},{3,19},{4,20},{5,21},{6,22},{7,23},{8,24},{9,... | collective-permute-start | bytes 933896 | tf_op jit(solution)/shard_map/ppermute | solution.py:41
  479.4 9.3 %collective-permute-start.69 = (bf16[40,1024]{1,0:T(8,128)(2,1)S(1)}, bf16[40,1024]{1,0:T(8,128)(2,1)S(1)}, u32[]{:S(2)}, u32[]{:S(2)}) collective-permute-start(bf16[40,1024]{1,0:T(8,128)(2,1)S(1)} %convert_element_type.52), channel_id=1, source_target_pairs={{0,16},{1,17},{2,18},{3,19},{4,20},{5,21},{6,22},{7,23},{8,24},{9,... | collective-permute-start | bytes 245768 | tf_op jit(solution)/shard_map/ppermute | solution.py:41
  481.1 9.4 %collective-permute-start.70 = (bf16[40,1024]{1,0:T(8,128)(2,1)S(1)}, bf16[40,1024]{1,0:T(8,128)(2,1)}, u32[]{:S(2)}, u32[]{:S(2)}) collective-permute-start(bf16[40,1024]{1,0:T(8,128)(2,1)S(1)} %convert_element_type.52), channel_id=1, source_target_pairs={{0,24},{1,25},{2,26},{3,27},{4,28},{5,29},{6,30},{7,31},{8,16},{9,... | collective-permute-start | bytes 245768 | tf_op jit(solution)/shard_map/ppermute | solution.py:41
  485.2 7.0 %collective-permute-start.71 = (bf16[4,32,1024]{2,1,0:T(8,128)(2,1)}, bf16[4,32,1024]{2,1,0:T(8,128)(2,1)S(1)}, u32[]{:S(2)}, u32[]{:S(2)}) collective-permute-start(bf16[4,32,1024]{2,1,0:T(8,128)(2,1)} %get-tuple-element.576), channel_id=1, source_target_pairs={{0,4},{1,5},{2,6},{3,7},{4,0},{5,1},{6,2},{7,3},{8,12},{9,13},{10,... | collective-permute-start | bytes 786440 | tf_op jit(solution)/shard_map/ppermute | solution.py:41
  485.6 6.7 %collective-permute-start.72 = (bf16[4,32,1024]{2,1,0:T(8,128)(2,1)}, bf16[4,32,1024]{2,1,0:T(8,128)(2,1)}, u32[]{:S(2)}, u32[]{:S(2)}) collective-permute-start(bf16[4,32,1024]{2,1,0:T(8,128)(2,1)} %get-tuple-element.577), channel_id=1, source_target_pairs={{0,2},{1,3},{2,0},{3,1},{4,6},{5,7},{6,4},{7,5},{8,10},{9,11},{10,... | collective-permute-start | bytes 786440 | tf_op jit(solution)/shard_map/ppermute | solution.py:41
  489.3 11.2 %collective-permute-start.77 = (bf16[152,1024]{1,0:T(8,128)(2,1)}, bf16[152,1024]{1,0:T(8,128)(2,1)}, u32[]{:S(2)}, u32[]{:S(2)}) collective-permute-start(bf16[152,1024]{1,0:T(8,128)(2,1)} %get-tuple-element.594), channel_id=1, source_target_pairs={{0,24},{1,25},{2,26},{3,27},{4,28},{5,29},{6,30},{7,31},{8,16},{9,... | collective-permute-start | bytes 933896 | tf_op jit(solution)/shard_map/ppermute | solution.py:41
  496.0 7.1 %collective-permute-start.74 = (bf16[32,2048]{1,0:T(8,128)(2,1)S(1)}, bf16[32,2048]{1,0:T(8,128)(2,1)S(1)}, u32[]{:S(2)}, u32[]{:S(2)}) collective-permute-start(bf16[32,2048]{1,0:T(8,128)(2,1)S(1)} %get-tuple-element.588), channel_id=1, source_target_pairs={{0,8},{1,9},{2,10},{3,11},{4,12},{5,13},{6,14},{7,15},{8,0},{9,1},... | collective-permute-start | bytes 393224 | tf_op jit(solution)/shard_map/ppermute | solution.py:41
  496.1 15.4 %collective-permute-start.75 = (bf16[32,2048]{1,0:T(8,128)(2,1)S(1)}, bf16[32,2048]{1,0:T(8,128)(2,1)S(1)}, u32[]{:S(2)}, u32[]{:S(2)}) collective-permute-start(bf16[32,2048]{1,0:T(8,128)(2,1)S(1)} %get-tuple-element.589), channel_id=1, source_target_pairs={{0,16},{1,17},{2,18},{3,19},{4,20},{5,21},{6,22},{7,23},{8,24},{9,... | collective-permute-start | bytes 393224 | tf_op jit(solution)/shard_map/ppermute | solution.py:41
  499.3 12.2 %collective-permute-start.76 = (bf16[32,2048]{1,0:T(8,128)(2,1)S(1)}, bf16[32,2048]{1,0:T(8,128)(2,1)S(1)}, u32[]{:S(2)}, u32[]{:S(2)}) collective-permute-start(bf16[32,2048]{1,0:T(8,128)(2,1)S(1)} %get-tuple-element.590), channel_id=1, source_target_pairs={{0,24},{1,25},{2,26},{3,27},{4,28},{5,29},{6,30},{7,31},{8,16},{9,... | collective-permute-start | bytes 393224 | tf_op jit(solution)/shard_map/ppermute | solution.py:41
  (137 other events, 1043.5 us)

commit v5 on v4

--- a/solution.py
+++ b/solution.py
@@ -188,7 +188,7 @@
     sizes, mine = tuple(size for size, _ in chip_axes()), coordinates()
     tokens, width = rows.shape
     block_rows, half = sources_a[0][0].shape[3:]
-    tile = 256
+    tile = 512
     tiles = half // tile
 
     def kernel(me, row_ref, *refs):
@@ -238,7 +238,7 @@
         columns = columns // 2
     count, mine = lax.axis_size("seq"), coordinates()
     rows = features // count
-    tile = 512 if columns % 512 == 0 and features <= 1024 else 256
+    tile = next(t for t in (512, 1408, 256) if columns % t == 0)
     chunks = next(c for c in (4, 2, 1) if features // c % 128 == 0)
     chunk = features // chunks
 

time: 522 us -> 520 us (level)
  no operation moved by 1% of the time
where the time goes in v5:
time: 520 us; the launch traced here: 511 us
  waiting for transfers between devices  178 us (34%)
  Pallas kernels  165 us (32%)
  starting transfers between devices  80.5 us (15%)
  local copies, waits for them, and re-layouts  39.3 us (8%)
  other arithmetic  29.3 us (6%)
  matrix products  15.7 us (3%)
    ppermute x74, waiting for transfers between devices, swapped(): return lax.ppermute(array, 'seq', [(i, i ^ mask) for i in range(count)])  157 us
    ppermute x74, starting transfers between devices, swapped(): return lax.ppermute(array, 'seq', [(i, i ^ mask) for i in range(count)])  75.1 us
    pallas_call x4, Pallas kernels, launch(): pl.pallas_call(kernel, out_shape=[jax.ShapeDtypeStruct(shape, kind) for s...  47 us
    unnamed x255, local copies, waits for them, and re-layouts  31.5 us
    pallas_call x1, Pallas kernels, feed_forward(): pl.pallas_call(kernel, out_shape=[jax.ShapeDtypeStruct((tokens, width), j...  30.7 us
    pallas_call x5, Pallas kernels, grad_products(): pl.pallas_call(kernel, out_shape=[shape for shape, _ in results], grid_sp...  29.4 us
    pallas_call x6, Pallas kernels, phase_sums(): pl.pallas_call(kernel, out_shape=[jax.ShapeDtypeStruct(shape, jnp.bfloat1...  20.5 us
    ppermute x4, waiting for transfers between devices, shifted(): return lax.ppermute(array, 'seq', pairs)  20.4 us
  transfers between devices with their start and end apart: 78, of which 28 were waited for; matrix products, arithmetic and copies ran while one was open for 8% of the time, Pallas kernels for 22%

profile of v5, /device:TPU:0, one launch (start us, length us, event | category | flops | bytes accessed | tf_op | source)
XLA Modules:
  0.0 510.7 jit_solution(14412092791082297556)
XLA Ops:
  2.6 3.1 collective-permute-start.1
  5.7 2.6 collective-permute-start.2
  12.0 6.7 %collective-permute-done.2 = bf16[32,2048]{1,0:T(8,128)(2,1)S(1)} collective-permute-done((bf16[32,2048]{1,0:T(8,128)(2,1)S(1)}, bf16[32,2048]{1,0:T(8,128)(2,1)S(1)}, u32[]{:S(2)}, u32[]{:S(2)}) %collective-permute-start.2) | collective-permute-done | bytes 131104 | tf_op jit(solution)/shard_map/ppermute | solution.py:41
  21.9 2.0 collective-permute-start.6
  26.7 3.6 collective-permute-done.6
  31.9 4.0 collective-permute-start.9
  35.9 10.4 %collective-permute-done.9 = bf16[152,1024]{1,0:T(8,128)(2,1)S(1)} collective-permute-done((bf16[152,1024]{1,0:T(8,128)(2,1)S(1)}, bf16[152,1024]{1,0:T(8,128)(2,1)S(1)}, u32[]{:S(2)}, u32[]{:S(2)}) %collective-permute-start.9) | collective-permute-done | bytes 311328 | tf_op jit(solution)/shard_map/ppermute | solution.py:41
  51.7 5.6 %shard_map.237 = bf16[528,2048]{1,0:T(8,128)(2,1)S(1)} custom-call(s32[4]{0:T(128)S(1)} %pad_add_fusion.me, bf16[528,1024]{1,0:T(8,128)(2,1)S(1)} %bitcast.208, bf16[2,2,4,32,1024]{4,3,2,1,0:T(8,128)(2,1)} %pad_maximum_fusion.10.refs_0_, bf16[2,2,4,32,1024]{4,3,2,1,0:T(8,128)(2,1)} %collective-permute-done.10.refs_1_, ...), custom_call_target="tpu_custom_call" | custom-call | flops 6000000000 | tf_op jit(solution)/shard_map/pallas_call | solution.py:216
  57.3 4.2 collective-permute-done.12
  65.3 13.2 %shard_map.238 = (f32[2,256,1024]{2,1,0:T(8,128)S(1)}, f32[2,256,512]{2,1,0:T(8,128)S(1)}, bf16[8,144,256]{2,1,0:T(8,128)(2,1)S(1)}, f32[2,4,1,128]{3,2,1,0:T(1,128)S(1)}) custom-call(s32[2]{0:T(128)S(1)} %pad_add_fusion.1.first_ref.place_ref, bf16[2,264,2048]{2,1,0:T(8,128)(2,1)S(1)} %bitcast.248, f32[4,2048]{1,0:T(4,128)S(1)} %bitcast.233, ...), custom_call_target="tpu_custom_call" | custom-call | flops 12999999488 | tf_op jit(solution)/shard_map/pallas_call | solution.py:712
  80.7 8.7 %collective-permute-done.17 = bf16[2,2,144,256]{3,2,1,0:T(8,128)(2,1)S(1)} collective-permute-done((bf16[2,2,144,256]{3,2,1,0:T(8,128)(2,1)S(1)}, bf16[2,2,144,256]{3,2,1,0:T(8,128)(2,1)S(1)}, u32[]{:S(2)}, u32[]{:S(2)}) %collective-permute-start.17) | collective-permute-done | bytes 294944 | tf_op jit(solution)/shard_map/ppermute | solution.py:41
  90.5 7.4 %collective-permute-done.18 = bf16[2,2,144,256]{3,2,1,0:T(8,128)(2,1)S(1)} collective-permute-done((bf16[2,2,144,256]{3,2,1,0:T(8,128)(2,1)S(1)}, bf16[2,2,144,256]{3,2,1,0:T(8,128)(2,1)S(1)}, u32[]{:S(2)}, u32[]{:S(2)}) %collective-permute-start.18) | collective-permute-done | bytes 294944 | tf_op jit(solution)/shard_map/ppermute | solution.py:41
  102.2 4.4 collective-permute-start.22
  107.9 1.9 shard_map.239
  111.1 10.5 %collective-permute-done.19.refs_0_ = bf16[128,256]{1,0:T(8,128)(2,1)S(1)} collective-permute-done((bf16[128,256]{1,0:T(8,128)(2,1)}, bf16[128,256]{1,0:T(8,128)(2,1)S(1)}, u32[]{:S(2)}, u32[]{:S(2)}) %collective-permute-start.19) | collective-permute-done | bytes 65568 | tf_op jit(solution)/shard_map/ppermute | solution.py:47
  122.2 2.1 shard_map.240
  124.3 5.3 %collective-permute-done.22 = bf16[32,5632]{1,0:T(8,128)(2,1)S(1)} collective-permute-done((bf16[32,5632]{1,0:T(8,128)(2,1)S(1)}, bf16[32,5632]{1,0:T(8,128)(2,1)S(1)}, u32[]{:S(2)}, u32[]{:S(2)}) %collective-permute-start.22) | collective-permute-done | bytes 360480 | tf_op jit(solution)/shard_map/ppermute | solution.py:41
  129.6 2.0 pad_maximum_fusion.1.refs_0_
  131.8 2.0 pad_maximum_fusion.refs_0_
  135.7 4.7 collective-permute-done.24
  143.1 6.6 %collective-permute-done.25 = bf16[2,2,128,256]{3,2,1,0:T(8,128)(2,1)S(1)} collective-permute-done((bf16[2,2,128,256]{3,2,1,0:T(8,128)(2,1)S(1)}, bf16[2,2,128,256]{3,2,1,0:T(8,128)(2,1)S(1)}, u32[]{:S(2)}, u32[]{:S(2)}) %collective-permute-start.25) | collective-permute-done | bytes 262176 | tf_op jit(solution)/shard_map/ppermute | solution.py:41
  150.7 15.3 %collective-permute-done.26 = bf16[2,2,128,256]{3,2,1,0:T(8,128)(2,1)S(1)} collective-permute-done((bf16[2,2,128,256]{3,2,1,0:T(8,128)(2,1)S(1)}, bf16[2,2,128,256]{3,2,1,0:T(8,128)(2,1)S(1)}, u32[]{:S(2)}, u32[]{:S(2)}) %collective-permute-start.26) | collective-permute-done | bytes 262176 | tf_op jit(solution)/shard_map/ppermute | solution.py:41
  168.7 2.2 shard_map.241
  179.2 4.1 shard_map.243
  185.1 1.8 maximum_add_fusion.hid
  186.9 11.7 %collective-permute-done.32 = bf16[2,4,32,2816]{3,2,1,0:T(8,128)(2,1)} collective-permute-done((bf16[2,4,32,2816]{3,2,1,0:T(8,128)(2,1)S(1)}, bf16[2,4,32,2816]{3,2,1,0:T(8,128)(2,1)}, u32[]{:S(2)}, u32[]{:S(2)}) %collective-permute-start.32) | collective-permute-done | bytes 1441824 | tf_op jit(solution)/shard_map/ppermute | solution.py:41
  198.6 3.6 collective-permute-done.31
  202.7 4.9 collective-permute-done.35
  208.8 30.7 %shard_map.244 = (f32[512,1024]{1,0:T(8,128)}, f32[512,1024]{1,0:T(8,128)}, bf16[512,1024]{1,0:T(8,128)(2,1)}, bf16[512,1024]{1,0:T(8,128)(2,1)}, bf16[512,2816]...) custom-call(s32[4]{0:T(128)} %copy-done.53, ...), custom_call_target="tpu_custom_call" | custom-call | flops 28000000000 | tf_op jit(solution)/shard_map/pallas_call | solution.py:992
  239.5 1.9 fusion.16
  243.0 5.3 %shard_map.245 = (f32[2,256,1024]{2,1,0:T(8,128)S(1)}, bf16[2,256,1024]{2,1,0:T(8,128)(2,1)S(1)}, bf16[8,144,256]{2,1,0:T(8,128)(2,1)S(1)}, f32[2,4,1,256]{3,2,1,0:T(1,128)S(1)}) custom-call(s32[2]{0:T(128)S(1)} %copy-done.69, f32[2,256,1024]{2,1,0:T(8,128)S(1)} %copy-done.78, f32[2,256,512]{2,1,0:T(8,128)S(1)} %get-tuple-element.328.reach_ref, ...), custom_call_target="tpu_custom_call" | custom-call | flops 5000000000 | tf_op jit(solution)/shard_map/pallas_call | solution.py:712
  251.2 2.1 shard_map.246
  256.3 12.4 %shard_map.247 = (bf16[2,2,4,32,2816]{4,3,2,1,0:T(8,128)(2,1)}, bf16[2,2,4,32,2816]{4,3,2,1,0:T(8,128)(2,1)}, bf16[2,2,4,32,2816]{4,3,2,1,0:T(8,128)(2,1)}, bf16[2,2,4,32,2816]{4,3,2,1,0:T(8,128)(2,1)}) custom-call(s32[4]{0:T(128)S(1)} %copy-done.54, bf16[512,1024]{1,0:T(8,128)(2,1)S(1)} %copy-done.81, bf16[512,2816]{1,0:T(8,128)(2,1)} %get-tuple-element.396.a_ref, ...), custom_call_target="tpu_custom_call" | custom-call | flops 14476128256 | tf_op jit(solution)/shard_map/pallas_call | solution.py:288
  269.8 7.6 %shard_map.248 = (bf16[2,2,4,88,512]{4,3,2,1,0:T(8,128)(2,1)S(1)}, bf16[2,2,4,88,512]{4,3,2,1,0:T(8,128)(2,1)S(1)}, bf16[2,2,4,88,512]{4,3,2,1,0:T(8,128)(2,1)S(1)}, bf16[2,2,4,88,512]{4,3,2,1,0:T(8,128)(2,1)}) custom-call(s32[4]{0:T(128)S(1)} %copy-done.54, bf16[512,2816]{1,0:T(8,128)(2,1)} %get-tuple-element.404.left_ref, bf16[512,1024]{1,0:T(8,128)(2,1)S(1)} %bitcast.242, ...), custom_call_target="tpu_custom_call" | custom-call | flops 7988064256 | tf_op jit(solution)/shard_map/pallas_call | solution.py:288
  281.7 2.1 shard_map.249
  283.8 1.8 copy-done.2
  285.6 6.4 %shard_map.250 = (bf16[2,4,32,2816]{3,2,1,0:T(8,128)(2,1)}, bf16[2,4,32,2816]{3,2,1,0:T(8,128)(2,1)}) custom-call(bf16[2,2,4,32,2816]{4,3,2,1,0:T(8,128)(2,1)S(1)} %copy-done.1, bf16[2,2,4,32,2816]{4,3,2,1,0:T(8,128)(2,1)} %collective-permute-done.40.refs_1_, bf16[2,2,4,32,2816]{4,3,2,1,0:T(8,128)(2,1)S(1)} %copy-done.2, ...), custom_call_target="tpu_custom_call" | custom-call | flops 3000000000 | tf_op jit(solution)/shard_map/pallas_call | solution.py:356
  293.3 2.2 shard_map.251
  295.5 9.9 %collective-permute-done.42.refs_0_ = bf16[128,256]{1,0:T(8,128)(2,1)S(1)} collective-permute-done((bf16[128,256]{1,0:T(8,128)(2,1)S(1)}, bf16[128,256]{1,0:T(8,128)(2,1)S(1)}, u32[]{:S(2)}, u32[]{:S(2)}) %collective-permute-start.42) | collective-permute-done | bytes 65568 | tf_op jit(solution)/shard_map/ppermute | solution.py:47
  312.8 2.2 shard_map.252
  322.2 3.9 shard_map.259
  327.4 5.2 %shard_map.258 = bf16[4,2,2,2,32,1024]{5,4,3,2,1,0:T(8,128)(2,1)S(1)} custom-call(s32[4]{0:T(128)S(1)} %copy-done.54, bf16[2,2,4,32,1024]{4,3,2,1,0:T(8,128)(2,1)} %pad_maximum_fusion.10.refs_0_, bf16[2,2,4,32,1024]{4,3,2,1,0:T(8,128)(2,1)} %collective-permute-done.10.refs_1_), custom_call_target="tpu_custom_call" | custom-call | flops 2638400000 | tf_op jit(solution)/shard_map/pallas_call | solution.py:106
  332.7 16.6 %collective-permute-done.44 = bf16[2,2,128,256]{3,2,1,0:T(8,128)(2,1)S(1)} collective-permute-done((bf16[2,2,128,256]{3,2,1,0:T(8,128)(2,1)S(1)}, bf16[2,2,128,256]{3,2,1,0:T(8,128)(2,1)S(1)}, u32[]{:S(2)}, u32[]{:S(2)}) %collective-permute-start.44) | collective-permute-done | bytes 262176 | tf_op jit(solution)/shard_map/ppermute | solution.py:41
  349.4 3.0 shard_map.253
  355.8 2.1 fusion.14
  358.3 2.1 fusion.12
  360.4 15.4 %collective-permute-done.49 = bf16[2,2,128,256]{3,2,1,0:T(8,128)(2,1)S(1)} collective-permute-done((bf16[2,2,128,256]{3,2,1,0:T(8,128)(2,1)S(1)}, bf16[2,2,128,256]{3,2,1,0:T(8,128)(2,1)S(1)}, u32[]{:S(2)}, u32[]{:S(2)}) %collective-permute-start.49) | collective-permute-done | bytes 262176 | tf_op jit(solution)/shard_map/ppermute | solution.py:41
  375.9 3.4 shard_map.254
  380.3 5.5 %shard_map.256 = (bf16[2,4,152,512]{3,2,1,0:T(8,128)(2,1)S(1)}, bf16[2,4,152,512]{3,2,1,0:T(8,128)(2,1)S(1)}) custom-call(bf16[2,2,4,32,512]{4,3,2,1,0:T(8,128)(2,1)S(1)} %copy-done.17, bf16[2,2,4,32,512]{4,3,2,1,0:T(8,128)(2,1)S(1)} %get-tuple-element.529.refs_1_, bf16[2,2,4,88,512]{4,3,2,1,0:T(8,128)(2,1)S(1)} %copy-done.5, ...), custom_call_target="tpu_custom_call" | custom-call | flops 3000000000 | tf_op jit(solution)/shard_map/pallas_call | solution.py:356
  389.2 2.4 collective-permute-start.54
  391.5 2.0 collective-permute-start.58
  394.5 24.3 %shard_map.255 = (bf16[2,256,2048]{2,1,0:T(8,128)(2,1)S(1)}, f32[2,8,2048]{2,1,0:T(8,128)S(1)}, f32[2,8,2048]{2,1,0:T(8,128)S(1)}, f32[2,4,2048]{2,1,0:T(4,128)S...) custom-call(s32[2]{0:T(128)S(1)} %copy-done.70, bf16[2,264,2048]{2,1,0:T(8,128)(2,1)S(1)} %bitcast.249, ...), custom_call_target="tpu_custom_call" | custom-call | flops 24000000000 | tf_op jit(solution)/shard_map/pallas_call | solution.py:712
  420.5 3.7 shard_map.260
  432.5 2.2 fusion.7
  434.8 4.9 fusion.6
  441.7 2.7 shard_map.261
  445.8 5.0 shard_map.262
  454.2 4.4 collective-permute-done.64
  462.1 2.9 collective-permute-start.73
  465.0 11.1 %collective-permute-done.67 = bf16[152,1024]{1,0:T(8,128)(2,1)S(1)} collective-permute-done((bf16[152,1024]{1,0:T(8,128)(2,1)S(1)}, bf16[152,1024]{1,0:T(8,128)(2,1)S(1)}, u32[]{:S(2)}, u32[]{:S(2)}) %collective-permute-start.67) | collective-permute-done | bytes 311328 | tf_op jit(solution)/shard_map/ppermute | solution.py:41
  478.7 2.7 collective-permute-start.70
  484.2 2.1 convert_add_fusion
  493.7 3.2 collective-permute-start.75
  500.8 8.3 %collective-permute-done.75 = bf16[32,2048]{1,0:T(8,128)(2,1)S(1)} collective-permute-done((bf16[32,2048]{1,0:T(8,128)(2,1)S(1)}, bf16[32,2048]{1,0:T(8,128)(2,1)S(1)}, u32[]{:S(2)}, u32[]{:S(2)}) %collective-permute-start.75) | collective-permute-done | bytes 131104 | tf_op jit(solution)/shard_map/ppermute | solution.py:41
  (471 shorter events, 129.3 us)
Async XLA Ops:
  2.6 9.4 %collective-permute-start.1 = (bf16[32,2048]{1,0:T(8,128)(2,1)S(1)}, bf16[32,2048]{1,0:T(8,128)(2,1)S(1)}, u32[]{:S(2)}, u32[]{:S(2)}) collective-permute-start(bf16[32,2048]{1,0:T(8,128)(2,1)S(1)} %bitcast.286), channel_id=1, source_target_pairs={{0,8},{1,9},{2,10},{3,11},{4,12},{5,13},{6,14},{7,15},{8,0},{9,1},... | collective-permute-start | bytes 393224 | tf_op jit(solution)/shard_map/ppermute | solution.py:41
  5.7 12.9 %collective-permute-start.2 = (bf16[32,2048]{1,0:T(8,128)(2,1)S(1)}, bf16[32,2048]{1,0:T(8,128)(2,1)S(1)}, u32[]{:S(2)}, u32[]{:S(2)}) collective-permute-start(bf16[32,2048]{1,0:T(8,128)(2,1)S(1)} %bitcast.287), channel_id=1, source_target_pairs={{0,16},{1,17},{2,18},{3,19},{4,20},{5,21},{6,22},{7,23},{8,24},{9,... | collective-permute-start | bytes 393224 | tf_op jit(solution)/shard_map/ppermute | solution.py:41
  8.3 10.3 %collective-permute-start.3 = (bf16[32,2048]{1,0:T(8,128)(2,1)S(1)}, bf16[32,2048]{1,0:T(8,128)(2,1)S(1)}, u32[]{:S(2)}, u32[]{:S(2)}) collective-permute-start(bf16[32,2048]{1,0:T(8,128)(2,1)S(1)} %bitcast.288), channel_id=1, source_target_pairs={{0,24},{1,25},{2,26},{3,27},{4,28},{5,29},{6,30},{7,31},{8,16},{9,... | collective-permute-start | bytes 393224 | tf_op jit(solution)/shard_map/ppermute | solution.py:41
  21.9 8.3 %collective-permute-start.6 = (bf16[152,1024]{1,0:T(8,128)(2,1)S(1)}, bf16[152,1024]{1,0:T(8,128)(2,1)S(1)}, u32[]{:S(2)}, u32[]{:S(2)}) collective-permute-start(bf16[152,1024]{1,0:T(8,128)(2,1)S(1)} %pad_maximum_fusion.22), channel_id=1, source_target_pairs={{0,8},{1,9},{2,10},{3,11},{4,12},{5,13},{6,14},{7,15},{8,0},{9,1},... | collective-permute-start | bytes 933896 | tf_op jit(solution)/shard_map/ppermute | solution.py:41
  31.1 15.2 %collective-permute-start.8 = (bf16[2,4,32,1024]{3,2,1,0:T(8,128)(2,1)S(1)}, bf16[2,4,32,1024]{3,2,1,0:T(8,128)(2,1)S(1)}, u32[]{:S(2)}, u32[]{:S(2)}) collective-permute-start(bf16[2,4,32,1024]{3,2,1,0:T(8,128)(2,1)S(1)} %pad_maximum_fusion.17), channel_id=1, source_target_pairs={{0,2},{1,3},{2,0},{3,1},{4,6},{5,7},{6,4},{7,5},{8,10},{9,11},{10,... | collective-permute-start | bytes 1572872 | tf_op jit(solution)/shard_map/ppermute | solution.py:41
  31.5 14.7 %collective-permute-start.7 = (bf16[2,4,32,1024]{3,2,1,0:T(8,128)(2,1)S(1)}, bf16[2,4,32,1024]{3,2,1,0:T(8,128)(2,1)S(1)}, u32[]{:S(2)}, u32[]{:S(2)}) collective-permute-start(bf16[2,4,32,1024]{3,2,1,0:T(8,128)(2,1)S(1)} %pad_maximum_fusion.16), channel_id=1, source_target_pairs={{0,4},{1,5},{2,6},{3,7},{4,0},{5,1},{6,2},{7,3},{8,12},{9,13},{10,... | collective-permute-start | bytes 1572872 | tf_op jit(solution)/shard_map/ppermute | solution.py:41
  31.9 14.4 %collective-permute-start.9 = (bf16[152,1024]{1,0:T(8,128)(2,1)S(1)}, bf16[152,1024]{1,0:T(8,128)(2,1)S(1)}, u32[]{:S(2)}, u32[]{:S(2)}) collective-permute-start(bf16[152,1024]{1,0:T(8,128)(2,1)S(1)} %pad_maximum_fusion.22), channel_id=1, source_target_pairs={{0,16},{1,17},{2,18},{3,19},{4,20},{5,21},{6,22},{7,23},{8,24},{9,... | collective-permute-start | bytes 933896 | tf_op jit(solution)/shard_map/ppermute | solution.py:41
  49.3 12.3 %collective-permute-start.12 = (bf16[152,1024]{1,0:T(8,128)(2,1)}, bf16[152,1024]{1,0:T(8,128)(2,1)S(1)}, u32[]{:S(2)}, u32[]{:S(2)}) collective-permute-start(bf16[152,1024]{1,0:T(8,128)(2,1)} %copy-done.91), channel_id=1, source_target_pairs={{0,24},{1,25},{2,26},{3,27},{4,28},{5,29},{6,30},{7,31},{8,16},{9,... | collective-permute-start | bytes 933896 | tf_op jit(solution)/shard_map/ppermute | solution.py:41
  50.6 28.0 %collective-permute-start.15 = (bf16[32,5632]{1,0:T(8,128)(2,1)}, bf16[32,5632]{1,0:T(8,128)(2,1)S(1)}, u32[]{:S(2)}, u32[]{:S(2)}) collective-permute-start(bf16[32,5632]{1,0:T(8,128)(2,1)} %param.25), channel_id=1, source_target_pairs={{0,8},{1,9},{2,10},{3,11},{4,12},{5,13},{6,14},{7,15},{8,0},{9,1},... | collective-permute-start | bytes 1081352 | tf_op jit(solution)/shard_map/ppermute | solution.py:41
  61.8 16.7 %collective-permute-start.13 = (bf16[4,152,512]{2,1,0:T(8,128)(2,1)S(1)}, bf16[4,152,512]{2,1,0:T(8,128)(2,1)S(1)}, u32[]{:S(2)}, u32[]{:S(2)}) collective-permute-start(bf16[4,152,512]{2,1,0:T(8,128)(2,1)S(1)} %get-tuple-element.341), channel_id=1, source_target_pairs={{0,2},{1,3},{2,0},{3,1},{4,6},{5,7},{6,4},{7,5},{8,10},{9,11},{10,... | collective-permute-start | bytes 1867784 | tf_op jit(solution)/shard_map/ppermute | solution.py:41
  63.6 15.0 %collective-permute-start.14 = (bf16[4,152,512]{2,1,0:T(8,128)(2,1)S(1)}, bf16[4,152,512]{2,1,0:T(8,128)(2,1)S(1)}, u32[]{:S(2)}, u32[]{:S(2)}) collective-permute-start(bf16[4,152,512]{2,1,0:T(8,128)(2,1)S(1)} %get-tuple-element.343), channel_id=1, source_target_pairs={{0,4},{1,5},{2,6},{3,7},{4,0},{5,1},{6,2},{7,3},{8,12},{9,13},{10,... | collective-permute-start | bytes 1867784 | tf_op jit(solution)/shard_map/ppermute | solution.py:41
  80.4 9.1 %collective-permute-start.17 = (bf16[2,2,144,256]{3,2,1,0:T(8,128)(2,1)S(1)}, bf16[2,2,144,256]{3,2,1,0:T(8,128)(2,1)S(1)}, u32[]{:S(2)}, u32[]{:S(2)}) collective-permute-start(bf16[2,2,144,256]{3,2,1,0:T(8,128)(2,1)S(1)} %get-tuple-element.622), channel_id=1, source_target_pairs={{0,2},{1,3},{2,0},{3,1},{4,6},{5,7},{6,4},{7,5},{8,10},{9,11},{10,... | collective-permute-start | bytes 884744 | tf_op jit(solution)/shard_map/ppermute | solution.py:41
  89.5 8.3 %collective-permute-start.18 = (bf16[2,2,144,256]{3,2,1,0:T(8,128)(2,1)S(1)}, bf16[2,2,144,256]{3,2,1,0:T(8,128)(2,1)S(1)}, u32[]{:S(2)}, u32[]{:S(2)}) collective-permute-start(bf16[2,2,144,256]{3,2,1,0:T(8,128)(2,1)S(1)} %get-tuple-element.620), channel_id=1, source_target_pairs={{0,4},{1,5},{2,6},{3,7},{4,0},{5,1},{6,2},{7,3},{8,12},{9,13},{10,... | collective-permute-start | bytes 884744 | tf_op jit(solution)/shard_map/ppermute | solution.py:41
  99.8 29.8 %collective-permute-start.21 = (bf16[2,4,152,512]{3,2,1,0:T(8,128)(2,1)}, bf16[2,4,152,512]{3,2,1,0:T(8,128)(2,1)}, u32[]{:S(2)}, u32[]{:S(2)}) collective-permute-start(bf16[2,4,152,512]{3,2,1,0:T(8,128)(2,1)} %pad_maximum_fusion.9), channel_id=1, source_target_pairs={{0,2},{1,3},{2,0},{3,1},{4,6},{5,7},{6,4},{7,5},{8,10},{9,11},{10,... | collective-permute-start | bytes 3735560 | tf_op jit(solution)/shard_map/ppermute | solution.py:41
  101.3 28.3 %collective-permute-start.20 = (bf16[2,4,152,512]{3,2,1,0:T(8,128)(2,1)}, bf16[2,4,152,512]{3,2,1,0:T(8,128)(2,1)}, u32[]{:S(2)}, u32[]{:S(2)}) collective-permute-start(bf16[2,4,152,512]{3,2,1,0:T(8,128)(2,1)} %pad_maximum_fusion.8), channel_id=1, source_target_pairs={{0,4},{1,5},{2,6},{3,7},{4,0},{5,1},{6,2},{7,3},{8,12},{9,13},{10,... | collective-permute-start | bytes 3735560 | tf_op jit(solution)/shard_map/ppermute | solution.py:41
  102.2 27.4 %collective-permute-start.22 = (bf16[32,5632]{1,0:T(8,128)(2,1)S(1)}, bf16[32,5632]{1,0:T(8,128)(2,1)S(1)}, u32[]{:S(2)}, u32[]{:S(2)}) collective-permute-start(bf16[32,5632]{1,0:T(8,128)(2,1)S(1)} %copy-done.97), channel_id=1, source_target_pairs={{0,16},{1,17},{2,18},{3,19},{4,20},{5,21},{6,22},{7,23},{8,24},{9,... | collective-permute-start | bytes 1081352 | tf_op jit(solution)/shard_map/ppermute | solution.py:41
  106.6 23.0 %collective-permute-start.23 = (bf16[32,5632]{1,0:T(8,128)(2,1)S(1)}, bf16[32,5632]{1,0:T(8,128)(2,1)}, u32[]{:S(2)}, u32[]{:S(2)}) collective-permute-start(bf16[32,5632]{1,0:T(8,128)(2,1)S(1)} %copy-done.97), channel_id=1, source_target_pairs={{0,24},{1,25},{2,26},{3,27},{4,28},{5,29},{6,30},{7,31},{8,16},{9,... | collective-permute-start | bytes 1081352 | tf_op jit(solution)/shard_map/ppermute | solution.py:41
  109.8 11.8 %collective-permute-start.19 = (bf16[128,256]{1,0:T(8,128)(2,1)}, bf16[128,256]{1,0:T(8,128)(2,1)S(1)}, u32[]{:S(2)}, u32[]{:S(2)}) collective-permute-start(bf16[128,256]{1,0:T(8,128)(2,1)} %shard_map.239), channel_id=1, source_target_pairs={{0,8},{1,9},{2,10},{3,11},{4,12},{5,13},{6,14},{7,15},{8,16},{9,17... | collective-permute-start | bytes 196616 | tf_op jit(solution)/shard_map/ppermute | solution.py:47
  131.7 34.4 %collective-permute-start.28 = (bf16[2,2,4,152,512]{4,3,2,1,0:T(8,128)(2,1)S(1)}, bf16[2,2,4,152,512]{4,3,2,1,0:T(8,128)(2,1)S(1)}, u32[]{:S(2)}, u32[]{:S(2)}) collective-permute-start(bf16[2,2,4,152,512]{4,3,2,1,0:T(8,128)(2,1)S(1)} %pad_maximum_fusion.1.refs_0_), channel_id=1, source_target_pairs={{0,1},{1,0},{2,3},{3,2},{4,5},{5,4},{6,7},{7,6},{8,9},{9,8},{10,11... | collective-permute-start | bytes 7471112 | tf_op jit(solution)/shard_map/ppermute | solution.py:41
  133.8 32.3 %collective-permute-start.27 = (bf16[2,2,4,152,512]{4,3,2,1,0:T(8,128)(2,1)S(1)}, bf16[2,2,4,152,512]{4,3,2,1,0:T(8,128)(2,1)S(1)}, u32[]{:S(2)}, u32[]{:S(2)}) collective-permute-start(bf16[2,2,4,152,512]{4,3,2,1,0:T(8,128)(2,1)S(1)} %pad_maximum_fusion.refs_0_), channel_id=1, source_target_pairs={{0,1},{1,0},{2,3},{3,2},{4,5},{5,4},{6,7},{7,6},{8,9},{9,8},{10,11... | collective-permute-start | bytes 7471112 | tf_op jit(solution)/shard_map/ppermute | solution.py:41
  140.4 9.2 %collective-permute-start.25 = (bf16[2,2,128,256]{3,2,1,0:T(8,128)(2,1)S(1)}, bf16[2,2,128,256]{3,2,1,0:T(8,128)(2,1)S(1)}, u32[]{:S(2)}, u32[]{:S(2)}) collective-permute-start(bf16[2,2,128,256]{3,2,1,0:T(8,128)(2,1)S(1)} %get-tuple-element.634), channel_id=1, source_target_pairs={{0,2},{1,3},{2,0},{3,1},{4,6},{5,7},{6,4},{7,5},{8,10},{9,11},{10,... | collective-permute-start | bytes 786440 | tf_op jit(solution)/shard_map/ppermute | solution.py:41
  142.3 23.8 %collective-permute-start.29 = (bf16[4,32,2816]{2,1,0:T(8,128)(2,1)S(1)}, bf16[4,32,2816]{2,1,0:T(8,128)(2,1)S(1)}, u32[]{:S(2)}, u32[]{:S(2)}) collective-permute-start(bf16[4,32,2816]{2,1,0:T(8,128)(2,1)S(1)} %get-tuple-element.366), channel_id=1, source_target_pairs={{0,2},{1,3},{2,0},{3,1},{4,6},{5,7},{6,4},{7,5},{8,10},{9,11},{10,... | collective-permute-start | bytes 2162696 | tf_op jit(solution)/shard_map/ppermute | solution.py:41
  142.7 23.3 %collective-permute-start.30 = (bf16[4,32,2816]{2,1,0:T(8,128)(2,1)S(1)}, bf16[4,32,2816]{2,1,0:T(8,128)(2,1)S(1)}, u32[]{:S(2)}, u32[]{:S(2)}) collective-permute-start(bf16[4,32,2816]{2,1,0:T(8,128)(2,1)S(1)} %get-tuple-element.368), channel_id=1, source_target_pairs={{0,4},{1,5},{2,6},{3,7},{4,0},{5,1},{6,2},{7,3},{8,12},{9,13},{10,... | collective-permute-start | bytes 2162696 | tf_op jit(solution)/shard_map/ppermute | solution.py:41
  149.7 16.3 %collective-permute-start.26 = (bf16[2,2,128,256]{3,2,1,0:T(8,128)(2,1)S(1)}, bf16[2,2,128,256]{3,2,1,0:T(8,128)(2,1)S(1)}, u32[]{:S(2)}, u32[]{:S(2)}) collective-permute-start(bf16[2,2,128,256]{3,2,1,0:T(8,128)(2,1)S(1)} %get-tuple-element.632), channel_id=1, source_target_pairs={{0,4},{1,5},{2,6},{3,7},{4,0},{5,1},{6,2},{7,3},{8,12},{9,13},{10,... | collective-permute-start | bytes 786440 | tf_op jit(solution)/shard_map/ppermute | solution.py:41
  166.2 32.4 %collective-permute-start.32 = (bf16[2,4,32,2816]{3,2,1,0:T(8,128)(2,1)S(1)}, bf16[2,4,32,2816]{3,2,1,0:T(8,128)(2,1)}, u32[]{:S(2)}, u32[]{:S(2)}) collective-permute-start(bf16[2,4,32,2816]{3,2,1,0:T(8,128)(2,1)S(1)} %pad_maximum_fusion.6), channel_id=1, source_target_pairs={{0,2},{1,3},{2,0},{3,1},{4,6},{5,7},{6,4},{7,5},{8,10},{9,11},{10,... | collective-permute-start | bytes 4325384 | tf_op jit(solution)/shard_map/ppermute | solution.py:41
  167.9 30.7 %collective-permute-start.34 = (bf16[2,4,32,2816]{3,2,1,0:T(8,128)(2,1)S(1)}, bf16[2,4,32,2816]{3,2,1,0:T(8,128)(2,1)}, u32[]{:S(2)}, u32[]{:S(2)}) collective-permute-start(bf16[2,4,32,2816]{3,2,1,0:T(8,128)(2,1)S(1)} %pad_maximum_fusion.6), channel_id=1, source_target_pairs={{0,1},{1,0},{2,3},{3,2},{4,5},{5,4},{6,7},{7,6},{8,9},{9,8},{10,11... | collective-permute-start | bytes 4325384 | tf_op jit(solution)/shard_map/ppermute | solution.py:41
  168.1 34.2 %collective-permute-start.31 = (bf16[2,4,32,2816]{3,2,1,0:T(8,128)(2,1)S(1)}, bf16[2,4,32,2816]{3,2,1,0:T(8,128)(2,1)}, u32[]{:S(2)}, u32[]{:S(2)}) collective-permute-start(bf16[2,4,32,2816]{3,2,1,0:T(8,128)(2,1)S(1)} %pad_maximum_fusion.5), channel_id=1, source_target_pairs={{0,4},{1,5},{2,6},{3,7},{4,0},{5,1},{6,2},{7,3},{8,12},{9,13},{10,... | collective-permute-start | bytes 4325384 | tf_op jit(solution)/shard_map/ppermute | solution.py:41
  168.5 33.7 %collective-permute-start.33 = (bf16[2,4,32,2816]{3,2,1,0:T(8,128)(2,1)S(1)}, bf16[2,4,32,2816]{3,2,1,0:T(8,128)(2,1)}, u32[]{:S(2)}, u32[]{:S(2)}) collective-permute-start(bf16[2,4,32,2816]{3,2,1,0:T(8,128)(2,1)S(1)} %pad_maximum_fusion.5), channel_id=1, source_target_pairs={{0,1},{1,0},{2,3},{3,2},{4,5},{5,4},{6,7},{7,6},{8,9},{9,8},{10,11... | collective-permute-start | bytes 4325384 | tf_op jit(solution)/shard_map/ppermute | solution.py:41
  255.8 12.9 %collective-permute-start.38 = (bf16[2,2,144,256]{3,2,1,0:T(8,128)(2,1)S(1)}, bf16[2,2,144,256]{3,2,1,0:T(8,128)(2,1)S(1)}, u32[]{:S(2)}, u32[]{:S(2)}) collective-permute-start(bf16[2,2,144,256]{3,2,1,0:T(8,128)(2,1)S(1)} %get-tuple-element.615), channel_id=1, source_target_pairs={{0,2},{1,3},{2,0},{3,1},{4,6},{5,7},{6,4},{7,5},{8,10},{9,11},{10,... | collective-permute-start | bytes 884744 | tf_op jit(solution)/shard_map/ppermute | solution.py:41
  268.7 15.0 %collective-permute-start.40 = (bf16[2,2,4,32,2816]{4,3,2,1,0:T(8,128)(2,1)}, bf16[2,2,4,32,2816]{4,3,2,1,0:T(8,128)(2,1)}, u32[]{:S(2)}, u32[]{:S(2)}) collective-permute-start(bf16[2,2,4,32,2816]{4,3,2,1,0:T(8,128)(2,1)} %get-tuple-element.412), channel_id=1, source_target_pairs={{0,1},{1,0},{2,3},{3,2},{4,5},{5,4},{6,7},{7,6},{8,9},{9,8},{10,11... | collective-permute-start | bytes 8650760 | tf_op jit(solution)/shard_map/ppermute | solution.py:41
  268.8 15.0 %collective-permute-start.41 = (bf16[2,2,4,32,2816]{4,3,2,1,0:T(8,128)(2,1)}, bf16[2,2,4,32,2816]{4,3,2,1,0:T(8,128)(2,1)}, u32[]{:S(2)}, u32[]{:S(2)}) collective-permute-start(bf16[2,2,4,32,2816]{4,3,2,1,0:T(8,128)(2,1)} %get-tuple-element.414), channel_id=1, source_target_pairs={{0,1},{1,0},{2,3},{3,2},{4,5},{5,4},{6,7},{7,6},{8,9},{9,8},{10,11... | collective-permute-start | bytes 8650760 | tf_op jit(solution)/shard_map/ppermute | solution.py:41
  269.4 11.5 %collective-permute-start.39 = (bf16[2,2,144,256]{3,2,1,0:T(8,128)(2,1)S(1)}, bf16[2,2,144,256]{3,2,1,0:T(8,128)(2,1)S(1)}, u32[]{:S(2)}, u32[]{:S(2)}) collective-permute-start(bf16[2,2,144,256]{3,2,1,0:T(8,128)(2,1)S(1)} %get-tuple-element.613), channel_id=1, source_target_pairs={{0,4},{1,5},{2,6},{3,7},{4,0},{5,1},{6,2},{7,3},{8,12},{9,13},{10,... | collective-permute-start | bytes 884744 | tf_op jit(solution)/shard_map/ppermute | solution.py:41
  292.0 13.4 %collective-permute-start.42 = (bf16[128,256]{1,0:T(8,128)(2,1)S(1)}, bf16[128,256]{1,0:T(8,128)(2,1)S(1)}, u32[]{:S(2)}, u32[]{:S(2)}) collective-permute-start(bf16[128,256]{1,0:T(8,128)(2,1)S(1)} %copy-done.120), channel_id=1, source_target_pairs={{8,0},{9,1},{10,2},{11,3},{12,4},{13,5},{14,6},{15,7},{16,8},{17,9... | collective-permute-start | bytes 196616 | tf_op jit(solution)/shard_map/ppermute | solution.py:47
  307.2 42.1 %collective-permute-start.48 = (bf16[2,2,4,152,512]{4,3,2,1,0:T(8,128)(2,1)}, bf16[2,2,4,152,512]{4,3,2,1,0:T(8,128)(2,1)}, u32[]{:S(2)}, u32[]{:S(2)}) collective-permute-start(bf16[2,2,4,152,512]{4,3,2,1,0:T(8,128)(2,1)} %pad_maximum_fusion.3), channel_id=1, source_target_pairs={{0,1},{1,0},{2,3},{3,2},{4,5},{5,4},{6,7},{7,6},{8,9},{9,8},{10,11... | collective-permute-start | bytes 7471112 | tf_op jit(solution)/shard_map/ppermute | solution.py:41
  309.4 39.9 %collective-permute-start.47 = (bf16[2,2,4,152,512]{4,3,2,1,0:T(8,128)(2,1)}, bf16[2,2,4,152,512]{4,3,2,1,0:T(8,128)(2,1)}, u32[]{:S(2)}, u32[]{:S(2)}) collective-permute-start(bf16[2,2,4,152,512]{4,3,2,1,0:T(8,128)(2,1)} %pad_maximum_fusion.2), channel_id=1, source_target_pairs={{0,1},{1,0},{2,3},{3,2},{4,5},{5,4},{6,7},{7,6},{8,9},{9,8},{10,11... | collective-permute-start | bytes 7471112 | tf_op jit(solution)/shard_map/ppermute | solution.py:41
  309.5 39.8 %collective-permute-start.45 = (bf16[2,4,32,2816]{3,2,1,0:T(8,128)(2,1)}, bf16[2,4,32,2816]{3,2,1,0:T(8,128)(2,1)}, u32[]{:S(2)}, u32[]{:S(2)}) collective-permute-start(bf16[2,4,32,2816]{3,2,1,0:T(8,128)(2,1)} %get-tuple-element.434), channel_id=1, source_target_pairs={{0,2},{1,3},{2,0},{3,1},{4,6},{5,7},{6,4},{7,5},{8,10},{9,11},{10,... | collective-permute-start | bytes 4325384 | tf_op jit(solution)/shard_map/ppermute | solution.py:41
  311.1 38.2 %collective-permute-start.46 = (bf16[2,4,32,2816]{3,2,1,0:T(8,128)(2,1)}, bf16[2,4,32,2816]{3,2,1,0:T(8,128)(2,1)}, u32[]{:S(2)}, u32[]{:S(2)}) collective-permute-start(bf16[2,4,32,2816]{3,2,1,0:T(8,128)(2,1)} %get-tuple-element.437), channel_id=1, source_target_pairs={{0,4},{1,5},{2,6},{3,7},{4,0},{5,1},{6,2},{7,3},{8,12},{9,13},{10,... | collective-permute-start | bytes 4325384 | tf_op jit(solution)/shard_map/ppermute | solution.py:41
  320.5 28.8 %collective-permute-start.44 = (bf16[2,2,128,256]{3,2,1,0:T(8,128)(2,1)S(1)}, bf16[2,2,128,256]{3,2,1,0:T(8,128)(2,1)S(1)}, u32[]{:S(2)}, u32[]{:S(2)}) collective-permute-start(bf16[2,2,128,256]{3,2,1,0:T(8,128)(2,1)S(1)} %get-tuple-element.628), channel_id=1, source_target_pairs={{0,2},{1,3},{2,0},{3,1},{4,6},{5,7},{6,4},{7,5},{8,10},{9,11},{10,... | collective-permute-start | bytes 786440 | tf_op jit(solution)/shard_map/ppermute | solution.py:41
  352.4 23.4 %collective-permute-start.50 = (bf16[4,32,2816]{2,1,0:T(8,128)(2,1)S(1)}, bf16[4,32,2816]{2,1,0:T(8,128)(2,1)S(1)}, u32[]{:S(2)}, u32[]{:S(2)}) collective-permute-start(bf16[4,32,2816]{2,1,0:T(8,128)(2,1)S(1)} %get-tuple-element.457), channel_id=1, source_target_pairs={{0,4},{1,5},{2,6},{3,7},{4,0},{5,1},{6,2},{7,3},{8,12},{9,13},{10,... | collective-permute-start | bytes 2162696 | tf_op jit(solution)/shard_map/ppermute | solution.py:41
  354.2 21.7 %collective-permute-start.51 = (bf16[4,32,2816]{2,1,0:T(8,128)(2,1)S(1)}, bf16[4,32,2816]{2,1,0:T(8,128)(2,1)S(1)}, u32[]{:S(2)}, u32[]{:S(2)}) collective-permute-start(bf16[4,32,2816]{2,1,0:T(8,128)(2,1)S(1)} %get-tuple-element.458), channel_id=1, source_target_pairs={{0,2},{1,3},{2,0},{3,1},{4,6},{5,7},{6,4},{7,5},{8,10},{9,11},{10,... | collective-permute-start | bytes 2162696 | tf_op jit(solution)/shard_map/ppermute | solution.py:41
  357.9 17.9 %collective-permute-start.49 = (bf16[2,2,128,256]{3,2,1,0:T(8,128)(2,1)S(1)}, bf16[2,2,128,256]{3,2,1,0:T(8,128)(2,1)S(1)}, u32[]{:S(2)}, u32[]{:S(2)}) collective-permute-start(bf16[2,2,128,256]{3,2,1,0:T(8,128)(2,1)S(1)} %get-tuple-element.626), channel_id=1, source_target_pairs={{0,4},{1,5},{2,6},{3,7},{4,0},{5,1},{6,2},{7,3},{8,12},{9,13},{10,... | collective-permute-start | bytes 786440 | tf_op jit(solution)/shard_map/ppermute | solution.py:41
  385.8 33.0 %collective-permute-start.52 = (bf16[2,4,152,512]{3,2,1,0:T(8,128)(2,1)S(1)}, bf16[2,4,152,512]{3,2,1,0:T(8,128)(2,1)S(1)}, u32[]{:S(2)}, u32[]{:S(2)}) collective-permute-start(bf16[2,4,152,512]{3,2,1,0:T(8,128)(2,1)S(1)} %get-tuple-element.495), channel_id=1, source_target_pairs={{0,2},{1,3},{2,0},{3,1},{4,6},{5,7},{6,4},{7,5},{8,10},{9,11},{10,... | collective-permute-start | bytes 3735560 | tf_op jit(solution)/shard_map/ppermute | solution.py:41
  387.5 31.4 %collective-permute-start.53 = (bf16[2,4,152,512]{3,2,1,0:T(8,128)(2,1)S(1)}, bf16[2,4,152,512]{3,2,1,0:T(8,128)(2,1)S(1)}, u32[]{:S(2)}, u32[]{:S(2)}) collective-permute-start(bf16[2,4,152,512]{3,2,1,0:T(8,128)(2,1)S(1)} %get-tuple-element.496), channel_id=1, source_target_pairs={{0,4},{1,5},{2,6},{3,7},{4,0},{5,1},{6,2},{7,3},{8,12},{9,13},{10,... | collective-permute-start | bytes 3735560 | tf_op jit(solution)/shard_map/ppermute | solution.py:41
  389.2 29.7 %collective-permute-start.54 = (bf16[32,5632]{1,0:T(8,128)(2,1)S(1)}, bf16[32,5632]{1,0:T(8,128)(2,1)S(1)}, u32[]{:S(2)}, u32[]{:S(2)}) collective-permute-start(bf16[32,5632]{1,0:T(8,128)(2,1)S(1)} %get-tuple-element.497), channel_id=1, source_target_pairs={{0,8},{1,9},{2,10},{3,11},{4,12},{5,13},{6,14},{7,15},{8,0},{9,1},... | collective-permute-start | bytes 1081352 | tf_op jit(solution)/shard_map/ppermute | solution.py:41
  391.5 48.2 %collective-permute-start.58 = (bf16[32,5632]{1,0:T(8,128)(2,1)}, bf16[32,5632]{1,0:T(8,128)(2,1)}, u32[]{:S(2)}, u32[]{:S(2)}) collective-permute-start(bf16[32,5632]{1,0:T(8,128)(2,1)} %get-tuple-element.525), channel_id=1, source_target_pairs={{0,16},{1,17},{2,18},{3,19},{4,20},{5,21},{6,22},{7,23},{8,24},{9,... | collective-permute-start | bytes 1081352 | tf_op jit(solution)/shard_map/ppermute | solution.py:41
  393.5 57.2 %collective-permute-start.61 = (bf16[32,5632]{1,0:T(8,128)(2,1)}, bf16[32,5632]{1,0:T(8,128)(2,1)}, u32[]{:S(2)}, u32[]{:S(2)}) collective-permute-start(bf16[32,5632]{1,0:T(8,128)(2,1)} %get-tuple-element.552), channel_id=1, source_target_pairs={{0,24},{1,25},{2,26},{3,27},{4,28},{5,29},{6,30},{7,31},{8,16},{9,... | collective-permute-start | bytes 1081352 | tf_op jit(solution)/shard_map/ppermute | solution.py:41
  418.9 8.4 %collective-permute-start.55 = (bf16[2,8,2048]{2,1,0:T(8,128)(2,1)S(1)}, bf16[2,8,2048]{2,1,0:T(8,128)(2,1)S(1)}, u32[]{:S(2)}, u32[]{:S(2)}) collective-permute-start(bf16[2,8,2048]{2,1,0:T(8,128)(2,1)S(1)} %convert_element_type.49), channel_id=1, source_target_pairs={{1,0},{2,1},{3,2},{4,3},{5,4},{6,5},{7,6},{8,7},{9,8},{10,9},{11,1... | collective-permute-start | bytes 196616 | tf_op jit(solution)/shard_map/ppermute | solution.py:47
  424.2 17.1 %collective-permute-start.56 = (bf16[4,152,512]{2,1,0:T(8,128)(2,1)}, bf16[4,152,512]{2,1,0:T(8,128)(2,1)}, u32[]{:S(2)}, u32[]{:S(2)}) collective-permute-start(bf16[4,152,512]{2,1,0:T(8,128)(2,1)} %get-tuple-element.522), channel_id=1, source_target_pairs={{0,4},{1,5},{2,6},{3,7},{4,0},{5,1},{6,2},{7,3},{8,12},{9,13},{10,... | collective-permute-start | bytes 1867784 | tf_op jit(solution)/shard_map/ppermute | solution.py:41
  425.2 16.5 %collective-permute-start.57 = (bf16[4,152,512]{2,1,0:T(8,128)(2,1)}, bf16[4,152,512]{2,1,0:T(8,128)(2,1)}, u32[]{:S(2)}, u32[]{:S(2)}) collective-permute-start(bf16[4,152,512]{2,1,0:T(8,128)(2,1)} %get-tuple-element.523), channel_id=1, source_target_pairs={{0,2},{1,3},{2,0},{3,1},{4,6},{5,7},{6,4},{7,5},{8,10},{9,11},{10,... | collective-permute-start | bytes 1867784 | tf_op jit(solution)/shard_map/ppermute | solution.py:41
  445.3 6.7 %collective-permute-start.60 = (f32[40,1024]{1,0:T(8,128)S(1)}, f32[40,1024]{1,0:T(8,128)S(1)}, u32[]{:S(2)}, u32[]{:S(2)}) collective-permute-start(f32[40,1024]{1,0:T(8,128)S(1)} %add.161), channel_id=1, source_target_pairs={{0,2},{1,3},{2,0},{3,1},{4,6},{5,7},{6,4},{7,5},{8,10},{9,11},{10,... | collective-permute-start | bytes 491528 | tf_op jit(solution)/shard_map/ppermute | solution.py:41
  451.9 6.7 %collective-permute-start.62 = (bf16[2,2,4,32,1024]{4,3,2,1,0:T(8,128)(2,1)S(1)}, bf16[2,2,4,32,1024]{4,3,2,1,0:T(8,128)(2,1)S(1)}, u32[]{:S(2)}, u32[]{:S(2)}) collective-permute-start(bf16[2,2,4,32,1024]{4,3,2,1,0:T(8,128)(2,1)S(1)} %get-tuple-element.554), channel_id=1, source_target_pairs={{0,1},{1,0},{2,3},{3,2},{4,5},{5,4},{6,7},{7,6},{8,9},{9,8},{10,11... | collective-permute-start | bytes 3145736 | tf_op jit(solution)/shard_map/ppermute | solution.py:41
  451.9 6.7 %collective-permute-start.63 = (bf16[2,2,4,32,1024]{4,3,2,1,0:T(8,128)(2,1)S(1)}, bf16[2,2,4,32,1024]{4,3,2,1,0:T(8,128)(2,1)S(1)}, u32[]{:S(2)}, u32[]{:S(2)}) collective-permute-start(bf16[2,2,4,32,1024]{4,3,2,1,0:T(8,128)(2,1)S(1)} %get-tuple-element.556), channel_id=1, source_target_pairs={{0,1},{1,0},{2,3},{3,2},{4,5},{5,4},{6,7},{7,6},{8,9},{9,8},{10,11... | collective-permute-start | bytes 3145736 | tf_op jit(solution)/shard_map/ppermute | solution.py:41
  459.0 17.1 %collective-permute-start.65 = (bf16[2,4,32,1024]{3,2,1,0:T(8,128)(2,1)S(1)}, bf16[2,4,32,1024]{3,2,1,0:T(8,128)(2,1)S(1)}, u32[]{:S(2)}, u32[]{:S(2)}) collective-permute-start(bf16[2,4,32,1024]{3,2,1,0:T(8,128)(2,1)S(1)} %get-tuple-element.563), channel_id=1, source_target_pairs={{0,2},{1,3},{2,0},{3,1},{4,6},{5,7},{6,4},{7,5},{8,10},{9,11},{10,... | collective-permute-start | bytes 1572872 | tf_op jit(solution)/shard_map/ppermute | solution.py:41
  459.8 16.3 %collective-permute-start.66 = (bf16[2,4,32,1024]{3,2,1,0:T(8,128)(2,1)S(1)}, bf16[2,4,32,1024]{3,2,1,0:T(8,128)(2,1)S(1)}, u32[]{:S(2)}, u32[]{:S(2)}) collective-permute-start(bf16[2,4,32,1024]{3,2,1,0:T(8,128)(2,1)S(1)} %get-tuple-element.564), channel_id=1, source_target_pairs={{0,4},{1,5},{2,6},{3,7},{4,0},{5,1},{6,2},{7,3},{8,12},{9,13},{10,... | collective-permute-start | bytes 1572872 | tf_op jit(solution)/shard_map/ppermute | solution.py:41
  461.5 14.6 %collective-permute-start.67 = (bf16[152,1024]{1,0:T(8,128)(2,1)S(1)}, bf16[152,1024]{1,0:T(8,128)(2,1)S(1)}, u32[]{:S(2)}, u32[]{:S(2)}) collective-permute-start(bf16[152,1024]{1,0:T(8,128)(2,1)S(1)} %get-tuple-element.567), channel_id=1, source_target_pairs={{0,8},{1,9},{2,10},{3,11},{4,12},{5,13},{6,14},{7,15},{8,0},{9,1},... | collective-permute-start | bytes 933896 | tf_op jit(solution)/shard_map/ppermute | solution.py:41
  462.1 27.7 %collective-permute-start.73 = (bf16[152,1024]{1,0:T(8,128)(2,1)}, bf16[152,1024]{1,0:T(8,128)(2,1)}, u32[]{:S(2)}, u32[]{:S(2)}) collective-permute-start(bf16[152,1024]{1,0:T(8,128)(2,1)} %get-tuple-element.578), channel_id=1, source_target_pairs={{0,16},{1,17},{2,18},{3,19},{4,20},{5,21},{6,22},{7,23},{8,24},{9,... | collective-permute-start | bytes 933896 | tf_op jit(solution)/shard_map/ppermute | solution.py:41
  477.0 9.3 %collective-permute-start.69 = (bf16[40,1024]{1,0:T(8,128)(2,1)S(1)}, bf16[40,1024]{1,0:T(8,128)(2,1)S(1)}, u32[]{:S(2)}, u32[]{:S(2)}) collective-permute-start(bf16[40,1024]{1,0:T(8,128)(2,1)S(1)} %convert_element_type.52), channel_id=1, source_target_pairs={{0,16},{1,17},{2,18},{3,19},{4,20},{5,21},{6,22},{7,23},{8,24},{9,... | collective-permute-start | bytes 245768 | tf_op jit(solution)/shard_map/ppermute | solution.py:41
  478.7 9.4 %collective-permute-start.70 = (bf16[40,1024]{1,0:T(8,128)(2,1)S(1)}, bf16[40,1024]{1,0:T(8,128)(2,1)}, u32[]{:S(2)}, u32[]{:S(2)}) collective-permute-start(bf16[40,1024]{1,0:T(8,128)(2,1)S(1)} %convert_element_type.52), channel_id=1, source_target_pairs={{0,24},{1,25},{2,26},{3,27},{4,28},{5,29},{6,30},{7,31},{8,16},{9,... | collective-permute-start | bytes 245768 | tf_op jit(solution)/shard_map/ppermute | solution.py:41
  482.8 7.0 %collective-permute-start.71 = (bf16[4,32,1024]{2,1,0:T(8,128)(2,1)}, bf16[4,32,1024]{2,1,0:T(8,128)(2,1)S(1)}, u32[]{:S(2)}, u32[]{:S(2)}) collective-permute-start(bf16[4,32,1024]{2,1,0:T(8,128)(2,1)} %get-tuple-element.576), channel_id=1, source_target_pairs={{0,4},{1,5},{2,6},{3,7},{4,0},{5,1},{6,2},{7,3},{8,12},{9,13},{10,... | collective-permute-start | bytes 786440 | tf_op jit(solution)/shard_map/ppermute | solution.py:41
  483.2 6.7 %collective-permute-start.72 = (bf16[4,32,1024]{2,1,0:T(8,128)(2,1)}, bf16[4,32,1024]{2,1,0:T(8,128)(2,1)}, u32[]{:S(2)}, u32[]{:S(2)}) collective-permute-start(bf16[4,32,1024]{2,1,0:T(8,128)(2,1)} %get-tuple-element.577), channel_id=1, source_target_pairs={{0,2},{1,3},{2,0},{3,1},{4,6},{5,7},{6,4},{7,5},{8,10},{9,11},{10,... | collective-permute-start | bytes 786440 | tf_op jit(solution)/shard_map/ppermute | solution.py:41
  486.9 11.2 %collective-permute-start.77 = (bf16[152,1024]{1,0:T(8,128)(2,1)}, bf16[152,1024]{1,0:T(8,128)(2,1)}, u32[]{:S(2)}, u32[]{:S(2)}) collective-permute-start(bf16[152,1024]{1,0:T(8,128)(2,1)} %get-tuple-element.594), channel_id=1, source_target_pairs={{0,24},{1,25},{2,26},{3,27},{4,28},{5,29},{6,30},{7,31},{8,16},{9,... | collective-permute-start | bytes 933896 | tf_op jit(solution)/shard_map/ppermute | solution.py:41
  493.6 7.1 %collective-permute-start.74 = (bf16[32,2048]{1,0:T(8,128)(2,1)S(1)}, bf16[32,2048]{1,0:T(8,128)(2,1)S(1)}, u32[]{:S(2)}, u32[]{:S(2)}) collective-permute-start(bf16[32,2048]{1,0:T(8,128)(2,1)S(1)} %get-tuple-element.588), channel_id=1, source_target_pairs={{0,8},{1,9},{2,10},{3,11},{4,12},{5,13},{6,14},{7,15},{8,0},{9,1},... | collective-permute-start | bytes 393224 | tf_op jit(solution)/shard_map/ppermute | solution.py:41
  493.7 15.4 %collective-permute-start.75 = (bf16[32,2048]{1,0:T(8,128)(2,1)S(1)}, bf16[32,2048]{1,0:T(8,128)(2,1)S(1)}, u32[]{:S(2)}, u32[]{:S(2)}) collective-permute-start(bf16[32,2048]{1,0:T(8,128)(2,1)S(1)} %get-tuple-element.589), channel_id=1, source_target_pairs={{0,16},{1,17},{2,18},{3,19},{4,20},{5,21},{6,22},{7,23},{8,24},{9,... | collective-permute-start | bytes 393224 | tf_op jit(solution)/shard_map/ppermute | solution.py:41
  496.9 12.2 %collective-permute-start.76 = (bf16[32,2048]{1,0:T(8,128)(2,1)S(1)}, bf16[32,2048]{1,0:T(8,128)(2,1)S(1)}, u32[]{:S(2)}, u32[]{:S(2)}) collective-permute-start(bf16[32,2048]{1,0:T(8,128)(2,1)S(1)} %get-tuple-element.590), channel_id=1, source_target_pairs={{0,24},{1,25},{2,26},{3,27},{4,28},{5,29},{6,30},{7,31},{8,16},{9,... | collective-permute-start | bytes 393224 | tf_op jit(solution)/shard_map/ppermute | solution.py:41
  (137 other events, 1043.5 us)

commit v6 on v5

--- a/solution.py
+++ b/solution.py
@@ -485,7 +485,10 @@
 
     def kernel(*refs):
         ins, (norm, conv, low, high, bias, head, ffn) = refs[: len(parts)], refs[len(parts) :]
-        total = sum((ref[...].astype(jnp.float32) for ref in ins[1:]), ins[0][...])
+        values = [ref[...].astype(jnp.float32) for ref in ins]
+        while len(values) > 1:
+            values = [sum(values[at : at + 2]) for at in range(0, len(values), 2)]
+        total = values[0]
         low[...] = total[:rank]
         for h in range(HEADS):
             side, at = divmod(h * PER_HEAD, width)
@@ -1218,7 +1221,7 @@
     fast_own, fast_last = levels_send(level_sums(fast_terms))
     small_rows = [small_rows]
     small_own = sum(small_rows)
-    small_parts = [small_own] + spread(small_own.astype(jnp.bfloat16), axes[0])[1:]
+    small_parts = spread(small_own.astype(jnp.bfloat16), axes[0])
     norm_gain_grad, conv_weight_grad, w_low_grad, w_high_grad, *rows_found = small_unpacked(
         small_parts, key_width, w_high.shape[0]
     )

time: 520 us -> 519 us (level)
  transfers between devices with their start and end apart: 78 -> 78, of which waited for: 28 -> 29; matrix products, arithmetic and copies ran while one was open for 8% -> 8% of each run, Pallas kernels for 22% -> 22%
where the time goes in v6:
time: 519 us; the launch traced here: 510 us
  waiting for transfers between devices  178 us (34%)
  Pallas kernels  165 us (32%)
  starting transfers between devices  81 us (16%)
  local copies, waits for them, and re-layouts  38 us (7%)
  other arithmetic  29.3 us (6%)
  matrix products  15.7 us (3%)
    ppermute x74, waiting for transfers between devices, swapped(): return lax.ppermute(array, 'seq', [(i, i ^ mask) for i in range(count)])  158 us
    ppermute x74, starting transfers between devices, swapped(): return lax.ppermute(array, 'seq', [(i, i ^ mask) for i in range(count)])  75.6 us
    pallas_call x4, Pallas kernels, launch(): pl.pallas_call(kernel, out_shape=[jax.ShapeDtypeStruct(shape, kind) for s...  47 us
    pallas_call x1, Pallas kernels, feed_forward(): pl.pallas_call(kernel, out_shape=[jax.ShapeDtypeStruct((tokens, width), j...  30.7 us
    unnamed x255, local copies, waits for them, and re-layouts  30.2 us
    pallas_call x5, Pallas kernels, grad_products(): pl.pallas_call(kernel, out_shape=[shape for shape, _ in results], grid_sp...  29.4 us
    pallas_call x6, Pallas kernels, phase_sums(): pl.pallas_call(kernel, out_shape=[jax.ShapeDtypeStruct(shape, jnp.bfloat1...  20.5 us
    ppermute x4, waiting for transfers between devices, shifted(): return lax.ppermute(array, 'seq', pairs)  20.4 us
  transfers between devices with their start and end apart: 78, of which 29 were waited for; matrix products, arithmetic and copies ran while one was open for 8% of the time, Pallas kernels for 22%

profile of v6, /device:TPU:0, one launch (start us, length us, event | category | flops | bytes accessed | tf_op | source)
XLA Modules:
  0.0 510.2 jit_solution(17152514660126655766)
XLA Ops:
  2.6 3.1 collective-permute-start.1
  5.7 2.6 collective-permute-start.2
  12.0 6.7 %collective-permute-done.2 = bf16[32,2048]{1,0:T(8,128)(2,1)S(1)} collective-permute-done((bf16[32,2048]{1,0:T(8,128)(2,1)S(1)}, bf16[32,2048]{1,0:T(8,128)(2,1)S(1)}, u32[]{:S(2)}, u32[]{:S(2)}) %collective-permute-start.2) | collective-permute-done | bytes 131104 | tf_op jit(solution)/shard_map/ppermute | solution.py:41
  21.9 2.0 collective-permute-start.6
  26.7 3.6 collective-permute-done.6
  31.9 4.0 collective-permute-start.9
  35.9 10.4 %collective-permute-done.9 = bf16[152,1024]{1,0:T(8,128)(2,1)S(1)} collective-permute-done((bf16[152,1024]{1,0:T(8,128)(2,1)S(1)}, bf16[152,1024]{1,0:T(8,128)(2,1)S(1)}, u32[]{:S(2)}, u32[]{:S(2)}) %collective-permute-start.9) | collective-permute-done | bytes 311328 | tf_op jit(solution)/shard_map/ppermute | solution.py:41
  51.7 5.6 %shard_map.237 = bf16[528,2048]{1,0:T(8,128)(2,1)S(1)} custom-call(s32[4]{0:T(128)S(1)} %pad_add_fusion.me, bf16[528,1024]{1,0:T(8,128)(2,1)S(1)} %bitcast.208, bf16[2,2,4,32,1024]{4,3,2,1,0:T(8,128)(2,1)} %pad_maximum_fusion.10.refs_0_, bf16[2,2,4,32,1024]{4,3,2,1,0:T(8,128)(2,1)} %collective-permute-done.10.refs_1_, ...), custom_call_target="tpu_custom_call" | custom-call | flops 6000000000 | tf_op jit(solution)/shard_map/pallas_call | solution.py:216
  57.3 4.2 collective-permute-done.12
  65.3 13.2 %shard_map.238 = (f32[2,256,1024]{2,1,0:T(8,128)S(1)}, f32[2,256,512]{2,1,0:T(8,128)S(1)}, bf16[8,144,256]{2,1,0:T(8,128)(2,1)S(1)}, f32[2,4,1,128]{3,2,1,0:T(1,128)S(1)}) custom-call(s32[2]{0:T(128)S(1)} %pad_add_fusion.1.first_ref.place_ref, bf16[2,264,2048]{2,1,0:T(8,128)(2,1)S(1)} %bitcast.248, f32[4,2048]{1,0:T(4,128)S(1)} %bitcast.233, ...), custom_call_target="tpu_custom_call" | custom-call | flops 12999999488 | tf_op jit(solution)/shard_map/pallas_call | solution.py:715
  80.7 8.7 %collective-permute-done.17 = bf16[2,2,144,256]{3,2,1,0:T(8,128)(2,1)S(1)} collective-permute-done((bf16[2,2,144,256]{3,2,1,0:T(8,128)(2,1)S(1)}, bf16[2,2,144,256]{3,2,1,0:T(8,128)(2,1)S(1)}, u32[]{:S(2)}, u32[]{:S(2)}) %collective-permute-start.17) | collective-permute-done | bytes 294944 | tf_op jit(solution)/shard_map/ppermute | solution.py:41
  90.5 7.4 %collective-permute-done.18 = bf16[2,2,144,256]{3,2,1,0:T(8,128)(2,1)S(1)} collective-permute-done((bf16[2,2,144,256]{3,2,1,0:T(8,128)(2,1)S(1)}, bf16[2,2,144,256]{3,2,1,0:T(8,128)(2,1)S(1)}, u32[]{:S(2)}, u32[]{:S(2)}) %collective-permute-start.18) | collective-permute-done | bytes 294944 | tf_op jit(solution)/shard_map/ppermute | solution.py:41
  102.2 4.4 collective-permute-start.22
  107.9 1.9 shard_map.239
  111.1 10.5 %collective-permute-done.19.refs_0_ = bf16[128,256]{1,0:T(8,128)(2,1)S(1)} collective-permute-done((bf16[128,256]{1,0:T(8,128)(2,1)}, bf16[128,256]{1,0:T(8,128)(2,1)S(1)}, u32[]{:S(2)}, u32[]{:S(2)}) %collective-permute-start.19) | collective-permute-done | bytes 65568 | tf_op jit(solution)/shard_map/ppermute | solution.py:47
  122.2 2.1 shard_map.240
  124.3 5.3 %collective-permute-done.22 = bf16[32,5632]{1,0:T(8,128)(2,1)S(1)} collective-permute-done((bf16[32,5632]{1,0:T(8,128)(2,1)S(1)}, bf16[32,5632]{1,0:T(8,128)(2,1)S(1)}, u32[]{:S(2)}, u32[]{:S(2)}) %collective-permute-start.22) | collective-permute-done | bytes 360480 | tf_op jit(solution)/shard_map/ppermute | solution.py:41
  129.6 2.0 pad_maximum_fusion.1.refs_0_
  131.8 2.0 pad_maximum_fusion.refs_0_
  135.7 4.7 collective-permute-done.24
  143.1 6.6 %collective-permute-done.25 = bf16[2,2,128,256]{3,2,1,0:T(8,128)(2,1)S(1)} collective-permute-done((bf16[2,2,128,256]{3,2,1,0:T(8,128)(2,1)S(1)}, bf16[2,2,128,256]{3,2,1,0:T(8,128)(2,1)S(1)}, u32[]{:S(2)}, u32[]{:S(2)}) %collective-permute-start.25) | collective-permute-done | bytes 262176 | tf_op jit(solution)/shard_map/ppermute | solution.py:41
  150.7 15.3 %collective-permute-done.26 = bf16[2,2,128,256]{3,2,1,0:T(8,128)(2,1)S(1)} collective-permute-done((bf16[2,2,128,256]{3,2,1,0:T(8,128)(2,1)S(1)}, bf16[2,2,128,256]{3,2,1,0:T(8,128)(2,1)S(1)}, u32[]{:S(2)}, u32[]{:S(2)}) %collective-permute-start.26) | collective-permute-done | bytes 262176 | tf_op jit(solution)/shard_map/ppermute | solution.py:41
  168.7 2.2 shard_map.241
  179.2 4.1 shard_map.243
  185.1 1.8 maximum_add_fusion.hid
  186.9 11.7 %collective-permute-done.32 = bf16[2,4,32,2816]{3,2,1,0:T(8,128)(2,1)} collective-permute-done((bf16[2,4,32,2816]{3,2,1,0:T(8,128)(2,1)S(1)}, bf16[2,4,32,2816]{3,2,1,0:T(8,128)(2,1)}, u32[]{:S(2)}, u32[]{:S(2)}) %collective-permute-start.32) | collective-permute-done | bytes 1441824 | tf_op jit(solution)/shard_map/ppermute | solution.py:41
  198.6 3.6 collective-permute-done.31
  202.7 4.9 collective-permute-done.35
  208.8 30.7 %shard_map.244 = (f32[512,1024]{1,0:T(8,128)}, f32[512,1024]{1,0:T(8,128)}, bf16[512,1024]{1,0:T(8,128)(2,1)}, bf16[512,1024]{1,0:T(8,128)(2,1)}, bf16[512,2816]...) custom-call(s32[4]{0:T(128)} %copy-done.53, ...), custom_call_target="tpu_custom_call" | custom-call | flops 28000000000 | tf_op jit(solution)/shard_map/pallas_call | solution.py:995
  239.5 1.9 fusion.16
  243.0 5.3 %shard_map.245 = (f32[2,256,1024]{2,1,0:T(8,128)S(1)}, bf16[2,256,1024]{2,1,0:T(8,128)(2,1)S(1)}, bf16[8,144,256]{2,1,0:T(8,128)(2,1)S(1)}, f32[2,4,1,256]{3,2,1,0:T(1,128)S(1)}) custom-call(s32[2]{0:T(128)S(1)} %copy-done.69, f32[2,256,1024]{2,1,0:T(8,128)S(1)} %copy-done.78, f32[2,256,512]{2,1,0:T(8,128)S(1)} %get-tuple-element.328.reach_ref, ...), custom_call_target="tpu_custom_call" | custom-call | flops 5000000000 | tf_op jit(solution)/shard_map/pallas_call | solution.py:715
  251.2 2.1 shard_map.246
  256.3 12.4 %shard_map.247 = (bf16[2,2,4,32,2816]{4,3,2,1,0:T(8,128)(2,1)}, bf16[2,2,4,32,2816]{4,3,2,1,0:T(8,128)(2,1)}, bf16[2,2,4,32,2816]{4,3,2,1,0:T(8,128)(2,1)}, bf16[2,2,4,32,2816]{4,3,2,1,0:T(8,128)(2,1)}) custom-call(s32[4]{0:T(128)S(1)} %copy-done.54, bf16[512,1024]{1,0:T(8,128)(2,1)S(1)} %copy-done.81, bf16[512,2816]{1,0:T(8,128)(2,1)} %get-tuple-element.396.a_ref, ...), custom_call_target="tpu_custom_call" | custom-call | flops 14476128256 | tf_op jit(solution)/shard_map/pallas_call | solution.py:288
  269.8 7.6 %shard_map.248 = (bf16[2,2,4,88,512]{4,3,2,1,0:T(8,128)(2,1)S(1)}, bf16[2,2,4,88,512]{4,3,2,1,0:T(8,128)(2,1)S(1)}, bf16[2,2,4,88,512]{4,3,2,1,0:T(8,128)(2,1)S(1)}, bf16[2,2,4,88,512]{4,3,2,1,0:T(8,128)(2,1)}) custom-call(s32[4]{0:T(128)S(1)} %copy-done.54, bf16[512,2816]{1,0:T(8,128)(2,1)} %get-tuple-element.404.left_ref, bf16[512,1024]{1,0:T(8,128)(2,1)S(1)} %bitcast.242, ...), custom_call_target="tpu_custom_call" | custom-call | flops 7988064256 | tf_op jit(solution)/shard_map/pallas_call | solution.py:288
  281.7 2.1 shard_map.249
  283.8 1.8 copy-done.2
  285.6 6.4 %shard_map.250 = (bf16[2,4,32,2816]{3,2,1,0:T(8,128)(2,1)}, bf16[2,4,32,2816]{3,2,1,0:T(8,128)(2,1)}) custom-call(bf16[2,2,4,32,2816]{4,3,2,1,0:T(8,128)(2,1)S(1)} %copy-done.1, bf16[2,2,4,32,2816]{4,3,2,1,0:T(8,128)(2,1)} %collective-permute-done.40.refs_1_, bf16[2,2,4,32,2816]{4,3,2,1,0:T(8,128)(2,1)S(1)} %copy-done.2, ...), custom_call_target="tpu_custom_call" | custom-call | flops 3000000000 | tf_op jit(solution)/shard_map/pallas_call | solution.py:356
  293.3 2.2 shard_map.251
  295.5 9.9 %collective-permute-done.42.refs_0_ = bf16[128,256]{1,0:T(8,128)(2,1)S(1)} collective-permute-done((bf16[128,256]{1,0:T(8,128)(2,1)S(1)}, bf16[128,256]{1,0:T(8,128)(2,1)S(1)}, u32[]{:S(2)}, u32[]{:S(2)}) %collective-permute-start.42) | collective-permute-done | bytes 65568 | tf_op jit(solution)/shard_map/ppermute | solution.py:47
  312.8 2.2 shard_map.252
  322.2 3.9 shard_map.259
  327.4 5.2 %shard_map.258 = bf16[4,2,2,2,32,1024]{5,4,3,2,1,0:T(8,128)(2,1)S(1)} custom-call(s32[4]{0:T(128)S(1)} %copy-done.54, bf16[2,2,4,32,1024]{4,3,2,1,0:T(8,128)(2,1)} %pad_maximum_fusion.10.refs_0_, bf16[2,2,4,32,1024]{4,3,2,1,0:T(8,128)(2,1)} %collective-permute-done.10.refs_1_), custom_call_target="tpu_custom_call" | custom-call | flops 2638400000 | tf_op jit(solution)/shard_map/pallas_call | solution.py:106
  332.7 16.6 %collective-permute-done.44 = bf16[2,2,128,256]{3,2,1,0:T(8,128)(2,1)S(1)} collective-permute-done((bf16[2,2,128,256]{3,2,1,0:T(8,128)(2,1)S(1)}, bf16[2,2,128,256]{3,2,1,0:T(8,128)(2,1)S(1)}, u32[]{:S(2)}, u32[]{:S(2)}) %collective-permute-start.44) | collective-permute-done | bytes 262176 | tf_op jit(solution)/shard_map/ppermute | solution.py:41
  349.4 3.0 shard_map.253
  355.8 2.1 fusion.14
  358.3 2.1 fusion.12
  360.4 15.4 %collective-permute-done.49 = bf16[2,2,128,256]{3,2,1,0:T(8,128)(2,1)S(1)} collective-permute-done((bf16[2,2,128,256]{3,2,1,0:T(8,128)(2,1)S(1)}, bf16[2,2,128,256]{3,2,1,0:T(8,128)(2,1)S(1)}, u32[]{:S(2)}, u32[]{:S(2)}) %collective-permute-start.49) | collective-permute-done | bytes 262176 | tf_op jit(solution)/shard_map/ppermute | solution.py:41
  375.9 3.4 shard_map.254
  380.3 5.5 %shard_map.256 = (bf16[2,4,152,512]{3,2,1,0:T(8,128)(2,1)S(1)}, bf16[2,4,152,512]{3,2,1,0:T(8,128)(2,1)S(1)}) custom-call(bf16[2,2,4,32,512]{4,3,2,1,0:T(8,128)(2,1)S(1)} %copy-done.17, bf16[2,2,4,32,512]{4,3,2,1,0:T(8,128)(2,1)S(1)} %get-tuple-element.529.refs_1_, bf16[2,2,4,88,512]{4,3,2,1,0:T(8,128)(2,1)S(1)} %copy-done.5, ...), custom_call_target="tpu_custom_call" | custom-call | flops 3000000000 | tf_op jit(solution)/shard_map/pallas_call | solution.py:356
  389.2 2.4 collective-permute-start.54
  391.5 2.0 collective-permute-start.58
  394.5 24.3 %shard_map.255 = (bf16[2,256,2048]{2,1,0:T(8,128)(2,1)S(1)}, f32[2,8,2048]{2,1,0:T(8,128)S(1)}, f32[2,8,2048]{2,1,0:T(8,128)S(1)}, f32[2,4,2048]{2,1,0:T(4,128)S...) custom-call(s32[2]{0:T(128)S(1)} %copy-done.70, bf16[2,264,2048]{2,1,0:T(8,128)(2,1)S(1)} %bitcast.249, ...), custom_call_target="tpu_custom_call" | custom-call | flops 24000000000 | tf_op jit(solution)/shard_map/pallas_call | solution.py:715
  420.5 3.7 shard_map.260
  432.5 2.2 fusion.7
  434.8 4.9 fusion.6
  441.7 2.7 shard_map.261
  445.8 5.0 shard_map.262
  454.2 4.4 collective-permute-done.64
  462.1 2.9 collective-permute-start.73
  465.0 11.1 %collective-permute-done.67 = bf16[152,1024]{1,0:T(8,128)(2,1)S(1)} collective-permute-done((bf16[152,1024]{1,0:T(8,128)(2,1)S(1)}, bf16[152,1024]{1,0:T(8,128)(2,1)S(1)}, u32[]{:S(2)}, u32[]{:S(2)}) %collective-permute-start.67) | collective-permute-done | bytes 311328 | tf_op jit(solution)/shard_map/ppermute | solution.py:41
  477.9 2.7 collective-permute-start.70
  483.5 2.1 convert_add_fusion
  493.0 3.5 collective-permute-start.75
  500.0 8.6 %collective-permute-done.75 = bf16[32,2048]{1,0:T(8,128)(2,1)S(1)} collective-permute-done((bf16[32,2048]{1,0:T(8,128)(2,1)S(1)}, bf16[32,2048]{1,0:T(8,128)(2,1)S(1)}, u32[]{:S(2)}, u32[]{:S(2)}) %collective-permute-start.75) | collective-permute-done | bytes 131104 | tf_op jit(solution)/shard_map/ppermute | solution.py:41
  (470 shorter events, 128.4 us)
Async XLA Ops:
  2.6 9.4 %collective-permute-start.1 = (bf16[32,2048]{1,0:T(8,128)(2,1)S(1)}, bf16[32,2048]{1,0:T(8,128)(2,1)S(1)}, u32[]{:S(2)}, u32[]{:S(2)}) collective-permute-start(bf16[32,2048]{1,0:T(8,128)(2,1)S(1)} %bitcast.286), channel_id=1, source_target_pairs={{0,8},{1,9},{2,10},{3,11},{4,12},{5,13},{6,14},{7,15},{8,0},{9,1},... | collective-permute-start | bytes 393224 | tf_op jit(solution)/shard_map/ppermute | solution.py:41
  5.7 12.9 %collective-permute-start.2 = (bf16[32,2048]{1,0:T(8,128)(2,1)S(1)}, bf16[32,2048]{1,0:T(8,128)(2,1)S(1)}, u32[]{:S(2)}, u32[]{:S(2)}) collective-permute-start(bf16[32,2048]{1,0:T(8,128)(2,1)S(1)} %bitcast.287), channel_id=1, source_target_pairs={{0,16},{1,17},{2,18},{3,19},{4,20},{5,21},{6,22},{7,23},{8,24},{9,... | collective-permute-start | bytes 393224 | tf_op jit(solution)/shard_map/ppermute | solution.py:41
  8.3 10.3 %collective-permute-start.3 = (bf16[32,2048]{1,0:T(8,128)(2,1)S(1)}, bf16[32,2048]{1,0:T(8,128)(2,1)S(1)}, u32[]{:S(2)}, u32[]{:S(2)}) collective-permute-start(bf16[32,2048]{1,0:T(8,128)(2,1)S(1)} %bitcast.288), channel_id=1, source_target_pairs={{0,24},{1,25},{2,26},{3,27},{4,28},{5,29},{6,30},{7,31},{8,16},{9,... | collective-permute-start | bytes 393224 | tf_op jit(solution)/shard_map/ppermute | solution.py:41
  21.9 8.3 %collective-permute-start.6 = (bf16[152,1024]{1,0:T(8,128)(2,1)S(1)}, bf16[152,1024]{1,0:T(8,128)(2,1)S(1)}, u32[]{:S(2)}, u32[]{:S(2)}) collective-permute-start(bf16[152,1024]{1,0:T(8,128)(2,1)S(1)} %pad_maximum_fusion.22), channel_id=1, source_target_pairs={{0,8},{1,9},{2,10},{3,11},{4,12},{5,13},{6,14},{7,15},{8,0},{9,1},... | collective-permute-start | bytes 933896 | tf_op jit(solution)/shard_map/ppermute | solution.py:41
  31.1 15.2 %collective-permute-start.8 = (bf16[2,4,32,1024]{3,2,1,0:T(8,128)(2,1)S(1)}, bf16[2,4,32,1024]{3,2,1,0:T(8,128)(2,1)S(1)}, u32[]{:S(2)}, u32[]{:S(2)}) collective-permute-start(bf16[2,4,32,1024]{3,2,1,0:T(8,128)(2,1)S(1)} %pad_maximum_fusion.17), channel_id=1, source_target_pairs={{0,2},{1,3},{2,0},{3,1},{4,6},{5,7},{6,4},{7,5},{8,10},{9,11},{10,... | collective-permute-start | bytes 1572872 | tf_op jit(solution)/shard_map/ppermute | solution.py:41
  31.5 14.7 %collective-permute-start.7 = (bf16[2,4,32,1024]{3,2,1,0:T(8,128)(2,1)S(1)}, bf16[2,4,32,1024]{3,2,1,0:T(8,128)(2,1)S(1)}, u32[]{:S(2)}, u32[]{:S(2)}) collective-permute-start(bf16[2,4,32,1024]{3,2,1,0:T(8,128)(2,1)S(1)} %pad_maximum_fusion.16), channel_id=1, source_target_pairs={{0,4},{1,5},{2,6},{3,7},{4,0},{5,1},{6,2},{7,3},{8,12},{9,13},{10,... | collective-permute-start | bytes 1572872 | tf_op jit(solution)/shard_map/ppermute | solution.py:41
  31.9 14.4 %collective-permute-start.9 = (bf16[152,1024]{1,0:T(8,128)(2,1)S(1)}, bf16[152,1024]{1,0:T(8,128)(2,1)S(1)}, u32[]{:S(2)}, u32[]{:S(2)}) collective-permute-start(bf16[152,1024]{1,0:T(8,128)(2,1)S(1)} %pad_maximum_fusion.22), channel_id=1, source_target_pairs={{0,16},{1,17},{2,18},{3,19},{4,20},{5,21},{6,22},{7,23},{8,24},{9,... | collective-permute-start | bytes 933896 | tf_op jit(solution)/shard_map/ppermute | solution.py:41
  49.3 12.3 %collective-permute-start.12 = (bf16[152,1024]{1,0:T(8,128)(2,1)}, bf16[152,1024]{1,0:T(8,128)(2,1)S(1)}, u32[]{:S(2)}, u32[]{:S(2)}) collective-permute-start(bf16[152,1024]{1,0:T(8,128)(2,1)} %copy-done.91), channel_id=1, source_target_pairs={{0,24},{1,25},{2,26},{3,27},{4,28},{5,29},{6,30},{7,31},{8,16},{9,... | collective-permute-start | bytes 933896 | tf_op jit(solution)/shard_map/ppermute | solution.py:41
  50.6 28.0 %collective-permute-start.15 = (bf16[32,5632]{1,0:T(8,128)(2,1)}, bf16[32,5632]{1,0:T(8,128)(2,1)S(1)}, u32[]{:S(2)}, u32[]{:S(2)}) collective-permute-start(bf16[32,5632]{1,0:T(8,128)(2,1)} %param.25), channel_id=1, source_target_pairs={{0,8},{1,9},{2,10},{3,11},{4,12},{5,13},{6,14},{7,15},{8,0},{9,1},... | collective-permute-start | bytes 1081352 | tf_op jit(solution)/shard_map/ppermute | solution.py:41
  61.8 16.7 %collective-permute-start.13 = (bf16[4,152,512]{2,1,0:T(8,128)(2,1)S(1)}, bf16[4,152,512]{2,1,0:T(8,128)(2,1)S(1)}, u32[]{:S(2)}, u32[]{:S(2)}) collective-permute-start(bf16[4,152,512]{2,1,0:T(8,128)(2,1)S(1)} %get-tuple-element.341), channel_id=1, source_target_pairs={{0,2},{1,3},{2,0},{3,1},{4,6},{5,7},{6,4},{7,5},{8,10},{9,11},{10,... | collective-permute-start | bytes 1867784 | tf_op jit(solution)/shard_map/ppermute | solution.py:41
  63.6 15.0 %collective-permute-start.14 = (bf16[4,152,512]{2,1,0:T(8,128)(2,1)S(1)}, bf16[4,152,512]{2,1,0:T(8,128)(2,1)S(1)}, u32[]{:S(2)}, u32[]{:S(2)}) collective-permute-start(bf16[4,152,512]{2,1,0:T(8,128)(2,1)S(1)} %get-tuple-element.343), channel_id=1, source_target_pairs={{0,4},{1,5},{2,6},{3,7},{4,0},{5,1},{6,2},{7,3},{8,12},{9,13},{10,... | collective-permute-start | bytes 1867784 | tf_op jit(solution)/shard_map/ppermute | solution.py:41
  80.4 9.1 %collective-permute-start.17 = (bf16[2,2,144,256]{3,2,1,0:T(8,128)(2,1)S(1)}, bf16[2,2,144,256]{3,2,1,0:T(8,128)(2,1)S(1)}, u32[]{:S(2)}, u32[]{:S(2)}) collective-permute-start(bf16[2,2,144,256]{3,2,1,0:T(8,128)(2,1)S(1)} %get-tuple-element.622), channel_id=1, source_target_pairs={{0,2},{1,3},{2,0},{3,1},{4,6},{5,7},{6,4},{7,5},{8,10},{9,11},{10,... | collective-permute-start | bytes 884744 | tf_op jit(solution)/shard_map/ppermute | solution.py:41
  89.5 8.3 %collective-permute-start.18 = (bf16[2,2,144,256]{3,2,1,0:T(8,128)(2,1)S(1)}, bf16[2,2,144,256]{3,2,1,0:T(8,128)(2,1)S(1)}, u32[]{:S(2)}, u32[]{:S(2)}) collective-permute-start(bf16[2,2,144,256]{3,2,1,0:T(8,128)(2,1)S(1)} %get-tuple-element.620), channel_id=1, source_target_pairs={{0,4},{1,5},{2,6},{3,7},{4,0},{5,1},{6,2},{7,3},{8,12},{9,13},{10,... | collective-permute-start | bytes 884744 | tf_op jit(solution)/shard_map/ppermute | solution.py:41
  99.8 29.8 %collective-permute-start.21 = (bf16[2,4,152,512]{3,2,1,0:T(8,128)(2,1)}, bf16[2,4,152,512]{3,2,1,0:T(8,128)(2,1)}, u32[]{:S(2)}, u32[]{:S(2)}) collective-permute-start(bf16[2,4,152,512]{3,2,1,0:T(8,128)(2,1)} %pad_maximum_fusion.9), channel_id=1, source_target_pairs={{0,2},{1,3},{2,0},{3,1},{4,6},{5,7},{6,4},{7,5},{8,10},{9,11},{10,... | collective-permute-start | bytes 3735560 | tf_op jit(solution)/shard_map/ppermute | solution.py:41
  101.3 28.3 %collective-permute-start.20 = (bf16[2,4,152,512]{3,2,1,0:T(8,128)(2,1)}, bf16[2,4,152,512]{3,2,1,0:T(8,128)(2,1)}, u32[]{:S(2)}, u32[]{:S(2)}) collective-permute-start(bf16[2,4,152,512]{3,2,1,0:T(8,128)(2,1)} %pad_maximum_fusion.8), channel_id=1, source_target_pairs={{0,4},{1,5},{2,6},{3,7},{4,0},{5,1},{6,2},{7,3},{8,12},{9,13},{10,... | collective-permute-start | bytes 3735560 | tf_op jit(solution)/shard_map/ppermute | solution.py:41
  102.2 27.4 %collective-permute-start.22 = (bf16[32,5632]{1,0:T(8,128)(2,1)S(1)}, bf16[32,5632]{1,0:T(8,128)(2,1)S(1)}, u32[]{:S(2)}, u32[]{:S(2)}) collective-permute-start(bf16[32,5632]{1,0:T(8,128)(2,1)S(1)} %copy-done.96), channel_id=1, source_target_pairs={{0,16},{1,17},{2,18},{3,19},{4,20},{5,21},{6,22},{7,23},{8,24},{9,... | collective-permute-start | bytes 1081352 | tf_op jit(solution)/shard_map/ppermute | solution.py:41
  106.6 23.0 %collective-permute-start.23 = (bf16[32,5632]{1,0:T(8,128)(2,1)S(1)}, bf16[32,5632]{1,0:T(8,128)(2,1)}, u32[]{:S(2)}, u32[]{:S(2)}) collective-permute-start(bf16[32,5632]{1,0:T(8,128)(2,1)S(1)} %copy-done.96), channel_id=1, source_target_pairs={{0,24},{1,25},{2,26},{3,27},{4,28},{5,29},{6,30},{7,31},{8,16},{9,... | collective-permute-start | bytes 1081352 | tf_op jit(solution)/shard_map/ppermute | solution.py:41
  109.8 11.8 %collective-permute-start.19 = (bf16[128,256]{1,0:T(8,128)(2,1)}, bf16[128,256]{1,0:T(8,128)(2,1)S(1)}, u32[]{:S(2)}, u32[]{:S(2)}) collective-permute-start(bf16[128,256]{1,0:T(8,128)(2,1)} %shard_map.239), channel_id=1, source_target_pairs={{0,8},{1,9},{2,10},{3,11},{4,12},{5,13},{6,14},{7,15},{8,16},{9,17... | collective-permute-start | bytes 196616 | tf_op jit(solution)/shard_map/ppermute | solution.py:47
  131.7 34.4 %collective-permute-start.28 = (bf16[2,2,4,152,512]{4,3,2,1,0:T(8,128)(2,1)S(1)}, bf16[2,2,4,152,512]{4,3,2,1,0:T(8,128)(2,1)S(1)}, u32[]{:S(2)}, u32[]{:S(2)}) collective-permute-start(bf16[2,2,4,152,512]{4,3,2,1,0:T(8,128)(2,1)S(1)} %pad_maximum_fusion.1.refs_0_), channel_id=1, source_target_pairs={{0,1},{1,0},{2,3},{3,2},{4,5},{5,4},{6,7},{7,6},{8,9},{9,8},{10,11... | collective-permute-start | bytes 7471112 | tf_op jit(solution)/shard_map/ppermute | solution.py:41
  133.8 32.3 %collective-permute-start.27 = (bf16[2,2,4,152,512]{4,3,2,1,0:T(8,128)(2,1)S(1)}, bf16[2,2,4,152,512]{4,3,2,1,0:T(8,128)(2,1)S(1)}, u32[]{:S(2)}, u32[]{:S(2)}) collective-permute-start(bf16[2,2,4,152,512]{4,3,2,1,0:T(8,128)(2,1)S(1)} %pad_maximum_fusion.refs_0_), channel_id=1, source_target_pairs={{0,1},{1,0},{2,3},{3,2},{4,5},{5,4},{6,7},{7,6},{8,9},{9,8},{10,11... | collective-permute-start | bytes 7471112 | tf_op jit(solution)/shard_map/ppermute | solution.py:41
  140.4 9.2 %collective-permute-start.25 = (bf16[2,2,128,256]{3,2,1,0:T(8,128)(2,1)S(1)}, bf16[2,2,128,256]{3,2,1,0:T(8,128)(2,1)S(1)}, u32[]{:S(2)}, u32[]{:S(2)}) collective-permute-start(bf16[2,2,128,256]{3,2,1,0:T(8,128)(2,1)S(1)} %get-tuple-element.634), channel_id=1, source_target_pairs={{0,2},{1,3},{2,0},{3,1},{4,6},{5,7},{6,4},{7,5},{8,10},{9,11},{10,... | collective-permute-start | bytes 786440 | tf_op jit(solution)/shard_map/ppermute | solution.py:41
  142.3 23.8 %collective-permute-start.29 = (bf16[4,32,2816]{2,1,0:T(8,128)(2,1)S(1)}, bf16[4,32,2816]{2,1,0:T(8,128)(2,1)S(1)}, u32[]{:S(2)}, u32[]{:S(2)}) collective-permute-start(bf16[4,32,2816]{2,1,0:T(8,128)(2,1)S(1)} %get-tuple-element.366), channel_id=1, source_target_pairs={{0,2},{1,3},{2,0},{3,1},{4,6},{5,7},{6,4},{7,5},{8,10},{9,11},{10,... | collective-permute-start | bytes 2162696 | tf_op jit(solution)/shard_map/ppermute | solution.py:41
  142.7 23.3 %collective-permute-start.30 = (bf16[4,32,2816]{2,1,0:T(8,128)(2,1)S(1)}, bf16[4,32,2816]{2,1,0:T(8,128)(2,1)S(1)}, u32[]{:S(2)}, u32[]{:S(2)}) collective-permute-start(bf16[4,32,2816]{2,1,0:T(8,128)(2,1)S(1)} %get-tuple-element.368), channel_id=1, source_target_pairs={{0,4},{1,5},{2,6},{3,7},{4,0},{5,1},{6,2},{7,3},{8,12},{9,13},{10,... | collective-permute-start | bytes 2162696 | tf_op jit(solution)/shard_map/ppermute | solution.py:41
  149.7 16.3 %collective-permute-start.26 = (bf16[2,2,128,256]{3,2,1,0:T(8,128)(2,1)S(1)}, bf16[2,2,128,256]{3,2,1,0:T(8,128)(2,1)S(1)}, u32[]{:S(2)}, u32[]{:S(2)}) collective-permute-start(bf16[2,2,128,256]{3,2,1,0:T(8,128)(2,1)S(1)} %get-tuple-element.632), channel_id=1, source_target_pairs={{0,4},{1,5},{2,6},{3,7},{4,0},{5,1},{6,2},{7,3},{8,12},{9,13},{10,... | collective-permute-start | bytes 786440 | tf_op jit(solution)/shard_map/ppermute | solution.py:41
  166.2 32.4 %collective-permute-start.32 = (bf16[2,4,32,2816]{3,2,1,0:T(8,128)(2,1)S(1)}, bf16[2,4,32,2816]{3,2,1,0:T(8,128)(2,1)}, u32[]{:S(2)}, u32[]{:S(2)}) collective-permute-start(bf16[2,4,32,2816]{3,2,1,0:T(8,128)(2,1)S(1)} %pad_maximum_fusion.6), channel_id=1, source_target_pairs={{0,2},{1,3},{2,0},{3,1},{4,6},{5,7},{6,4},{7,5},{8,10},{9,11},{10,... | collective-permute-start | bytes 4325384 | tf_op jit(solution)/shard_map/ppermute | solution.py:41
  167.9 30.7 %collective-permute-start.34 = (bf16[2,4,32,2816]{3,2,1,0:T(8,128)(2,1)S(1)}, bf16[2,4,32,2816]{3,2,1,0:T(8,128)(2,1)}, u32[]{:S(2)}, u32[]{:S(2)}) collective-permute-start(bf16[2,4,32,2816]{3,2,1,0:T(8,128)(2,1)S(1)} %pad_maximum_fusion.6), channel_id=1, source_target_pairs={{0,1},{1,0},{2,3},{3,2},{4,5},{5,4},{6,7},{7,6},{8,9},{9,8},{10,11... | collective-permute-start | bytes 4325384 | tf_op jit(solution)/shard_map/ppermute | solution.py:41
  168.1 34.2 %collective-permute-start.31 = (bf16[2,4,32,2816]{3,2,1,0:T(8,128)(2,1)S(1)}, bf16[2,4,32,2816]{3,2,1,0:T(8,128)(2,1)}, u32[]{:S(2)}, u32[]{:S(2)}) collective-permute-start(bf16[2,4,32,2816]{3,2,1,0:T(8,128)(2,1)S(1)} %pad_maximum_fusion.5), channel_id=1, source_target_pairs={{0,4},{1,5},{2,6},{3,7},{4,0},{5,1},{6,2},{7,3},{8,12},{9,13},{10,... | collective-permute-start | bytes 4325384 | tf_op jit(solution)/shard_map/ppermute | solution.py:41
  168.5 33.7 %collective-permute-start.33 = (bf16[2,4,32,2816]{3,2,1,0:T(8,128)(2,1)S(1)}, bf16[2,4,32,2816]{3,2,1,0:T(8,128)(2,1)}, u32[]{:S(2)}, u32[]{:S(2)}) collective-permute-start(bf16[2,4,32,2816]{3,2,1,0:T(8,128)(2,1)S(1)} %pad_maximum_fusion.5), channel_id=1, source_target_pairs={{0,1},{1,0},{2,3},{3,2},{4,5},{5,4},{6,7},{7,6},{8,9},{9,8},{10,11... | collective-permute-start | bytes 4325384 | tf_op jit(solution)/shard_map/ppermute | solution.py:41
  255.8 12.9 %collective-permute-start.38 = (bf16[2,2,144,256]{3,2,1,0:T(8,128)(2,1)S(1)}, bf16[2,2,144,256]{3,2,1,0:T(8,128)(2,1)S(1)}, u32[]{:S(2)}, u32[]{:S(2)}) collective-permute-start(bf16[2,2,144,256]{3,2,1,0:T(8,128)(2,1)S(1)} %get-tuple-element.615), channel_id=1, source_target_pairs={{0,2},{1,3},{2,0},{3,1},{4,6},{5,7},{6,4},{7,5},{8,10},{9,11},{10,... | collective-permute-start | bytes 884744 | tf_op jit(solution)/shard_map/ppermute | solution.py:41
  268.7 15.0 %collective-permute-start.40 = (bf16[2,2,4,32,2816]{4,3,2,1,0:T(8,128)(2,1)}, bf16[2,2,4,32,2816]{4,3,2,1,0:T(8,128)(2,1)}, u32[]{:S(2)}, u32[]{:S(2)}) collective-permute-start(bf16[2,2,4,32,2816]{4,3,2,1,0:T(8,128)(2,1)} %get-tuple-element.412), channel_id=1, source_target_pairs={{0,1},{1,0},{2,3},{3,2},{4,5},{5,4},{6,7},{7,6},{8,9},{9,8},{10,11... | collective-permute-start | bytes 8650760 | tf_op jit(solution)/shard_map/ppermute | solution.py:41
  268.8 15.0 %collective-permute-start.41 = (bf16[2,2,4,32,2816]{4,3,2,1,0:T(8,128)(2,1)}, bf16[2,2,4,32,2816]{4,3,2,1,0:T(8,128)(2,1)}, u32[]{:S(2)}, u32[]{:S(2)}) collective-permute-start(bf16[2,2,4,32,2816]{4,3,2,1,0:T(8,128)(2,1)} %get-tuple-element.414), channel_id=1, source_target_pairs={{0,1},{1,0},{2,3},{3,2},{4,5},{5,4},{6,7},{7,6},{8,9},{9,8},{10,11... | collective-permute-start | bytes 8650760 | tf_op jit(solution)/shard_map/ppermute | solution.py:41
  269.4 11.5 %collective-permute-start.39 = (bf16[2,2,144,256]{3,2,1,0:T(8,128)(2,1)S(1)}, bf16[2,2,144,256]{3,2,1,0:T(8,128)(2,1)S(1)}, u32[]{:S(2)}, u32[]{:S(2)}) collective-permute-start(bf16[2,2,144,256]{3,2,1,0:T(8,128)(2,1)S(1)} %get-tuple-element.613), channel_id=1, source_target_pairs={{0,4},{1,5},{2,6},{3,7},{4,0},{5,1},{6,2},{7,3},{8,12},{9,13},{10,... | collective-permute-start | bytes 884744 | tf_op jit(solution)/shard_map/ppermute | solution.py:41
  292.0 13.4 %collective-permute-start.42 = (bf16[128,256]{1,0:T(8,128)(2,1)S(1)}, bf16[128,256]{1,0:T(8,128)(2,1)S(1)}, u32[]{:S(2)}, u32[]{:S(2)}) collective-permute-start(bf16[128,256]{1,0:T(8,128)(2,1)S(1)} %copy-done.120), channel_id=1, source_target_pairs={{8,0},{9,1},{10,2},{11,3},{12,4},{13,5},{14,6},{15,7},{16,8},{17,9... | collective-permute-start | bytes 196616 | tf_op jit(solution)/shard_map/ppermute | solution.py:47
  307.2 42.1 %collective-permute-start.48 = (bf16[2,2,4,152,512]{4,3,2,1,0:T(8,128)(2,1)}, bf16[2,2,4,152,512]{4,3,2,1,0:T(8,128)(2,1)}, u32[]{:S(2)}, u32[]{:S(2)}) collective-permute-start(bf16[2,2,4,152,512]{4,3,2,1,0:T(8,128)(2,1)} %pad_maximum_fusion.3), channel_id=1, source_target_pairs={{0,1},{1,0},{2,3},{3,2},{4,5},{5,4},{6,7},{7,6},{8,9},{9,8},{10,11... | collective-permute-start | bytes 7471112 | tf_op jit(solution)/shard_map/ppermute | solution.py:41
  309.4 39.9 %collective-permute-start.47 = (bf16[2,2,4,152,512]{4,3,2,1,0:T(8,128)(2,1)}, bf16[2,2,4,152,512]{4,3,2,1,0:T(8,128)(2,1)}, u32[]{:S(2)}, u32[]{:S(2)}) collective-permute-start(bf16[2,2,4,152,512]{4,3,2,1,0:T(8,128)(2,1)} %pad_maximum_fusion.2), channel_id=1, source_target_pairs={{0,1},{1,0},{2,3},{3,2},{4,5},{5,4},{6,7},{7,6},{8,9},{9,8},{10,11... | collective-permute-start | bytes 7471112 | tf_op jit(solution)/shard_map/ppermute | solution.py:41
  309.5 39.8 %collective-permute-start.45 = (bf16[2,4,32,2816]{3,2,1,0:T(8,128)(2,1)}, bf16[2,4,32,2816]{3,2,1,0:T(8,128)(2,1)}, u32[]{:S(2)}, u32[]{:S(2)}) collective-permute-start(bf16[2,4,32,2816]{3,2,1,0:T(8,128)(2,1)} %get-tuple-element.434), channel_id=1, source_target_pairs={{0,2},{1,3},{2,0},{3,1},{4,6},{5,7},{6,4},{7,5},{8,10},{9,11},{10,... | collective-permute-start | bytes 4325384 | tf_op jit(solution)/shard_map/ppermute | solution.py:41
  311.1 38.2 %collective-permute-start.46 = (bf16[2,4,32,2816]{3,2,1,0:T(8,128)(2,1)}, bf16[2,4,32,2816]{3,2,1,0:T(8,128)(2,1)}, u32[]{:S(2)}, u32[]{:S(2)}) collective-permute-start(bf16[2,4,32,2816]{3,2,1,0:T(8,128)(2,1)} %get-tuple-element.437), channel_id=1, source_target_pairs={{0,4},{1,5},{2,6},{3,7},{4,0},{5,1},{6,2},{7,3},{8,12},{9,13},{10,... | collective-permute-start | bytes 4325384 | tf_op jit(solution)/shard_map/ppermute | solution.py:41
  320.5 28.8 %collective-permute-start.44 = (bf16[2,2,128,256]{3,2,1,0:T(8,128)(2,1)S(1)}, bf16[2,2,128,256]{3,2,1,0:T(8,128)(2,1)S(1)}, u32[]{:S(2)}, u32[]{:S(2)}) collective-permute-start(bf16[2,2,128,256]{3,2,1,0:T(8,128)(2,1)S(1)} %get-tuple-element.628), channel_id=1, source_target_pairs={{0,2},{1,3},{2,0},{3,1},{4,6},{5,7},{6,4},{7,5},{8,10},{9,11},{10,... | collective-permute-start | bytes 786440 | tf_op jit(solution)/shard_map/ppermute | solution.py:41
  352.4 23.4 %collective-permute-start.50 = (bf16[4,32,2816]{2,1,0:T(8,128)(2,1)S(1)}, bf16[4,32,2816]{2,1,0:T(8,128)(2,1)S(1)}, u32[]{:S(2)}, u32[]{:S(2)}) collective-permute-start(bf16[4,32,2816]{2,1,0:T(8,128)(2,1)S(1)} %get-tuple-element.457), channel_id=1, source_target_pairs={{0,4},{1,5},{2,6},{3,7},{4,0},{5,1},{6,2},{7,3},{8,12},{9,13},{10,... | collective-permute-start | bytes 2162696 | tf_op jit(solution)/shard_map/ppermute | solution.py:41
  354.2 21.7 %collective-permute-start.51 = (bf16[4,32,2816]{2,1,0:T(8,128)(2,1)S(1)}, bf16[4,32,2816]{2,1,0:T(8,128)(2,1)S(1)}, u32[]{:S(2)}, u32[]{:S(2)}) collective-permute-start(bf16[4,32,2816]{2,1,0:T(8,128)(2,1)S(1)} %get-tuple-element.458), channel_id=1, source_target_pairs={{0,2},{1,3},{2,0},{3,1},{4,6},{5,7},{6,4},{7,5},{8,10},{9,11},{10,... | collective-permute-start | bytes 2162696 | tf_op jit(solution)/shard_map/ppermute | solution.py:41
  357.9 17.9 %collective-permute-start.49 = (bf16[2,2,128,256]{3,2,1,0:T(8,128)(2,1)S(1)}, bf16[2,2,128,256]{3,2,1,0:T(8,128)(2,1)S(1)}, u32[]{:S(2)}, u32[]{:S(2)}) collective-permute-start(bf16[2,2,128,256]{3,2,1,0:T(8,128)(2,1)S(1)} %get-tuple-element.626), channel_id=1, source_target_pairs={{0,4},{1,5},{2,6},{3,7},{4,0},{5,1},{6,2},{7,3},{8,12},{9,13},{10,... | collective-permute-start | bytes 786440 | tf_op jit(solution)/shard_map/ppermute | solution.py:41
  385.8 33.0 %collective-permute-start.52 = (bf16[2,4,152,512]{3,2,1,0:T(8,128)(2,1)S(1)}, bf16[2,4,152,512]{3,2,1,0:T(8,128)(2,1)S(1)}, u32[]{:S(2)}, u32[]{:S(2)}) collective-permute-start(bf16[2,4,152,512]{3,2,1,0:T(8,128)(2,1)S(1)} %get-tuple-element.495), channel_id=1, source_target_pairs={{0,2},{1,3},{2,0},{3,1},{4,6},{5,7},{6,4},{7,5},{8,10},{9,11},{10,... | collective-permute-start | bytes 3735560 | tf_op jit(solution)/shard_map/ppermute | solution.py:41
  387.5 31.4 %collective-permute-start.53 = (bf16[2,4,152,512]{3,2,1,0:T(8,128)(2,1)S(1)}, bf16[2,4,152,512]{3,2,1,0:T(8,128)(2,1)S(1)}, u32[]{:S(2)}, u32[]{:S(2)}) collective-permute-start(bf16[2,4,152,512]{3,2,1,0:T(8,128)(2,1)S(1)} %get-tuple-element.496), channel_id=1, source_target_pairs={{0,4},{1,5},{2,6},{3,7},{4,0},{5,1},{6,2},{7,3},{8,12},{9,13},{10,... | collective-permute-start | bytes 3735560 | tf_op jit(solution)/shard_map/ppermute | solution.py:41
  389.2 29.7 %collective-permute-start.54 = (bf16[32,5632]{1,0:T(8,128)(2,1)S(1)}, bf16[32,5632]{1,0:T(8,128)(2,1)S(1)}, u32[]{:S(2)}, u32[]{:S(2)}) collective-permute-start(bf16[32,5632]{1,0:T(8,128)(2,1)S(1)} %get-tuple-element.497), channel_id=1, source_target_pairs={{0,8},{1,9},{2,10},{3,11},{4,12},{5,13},{6,14},{7,15},{8,0},{9,1},... | collective-permute-start | bytes 1081352 | tf_op jit(solution)/shard_map/ppermute | solution.py:41
  391.5 48.2 %collective-permute-start.58 = (bf16[32,5632]{1,0:T(8,128)(2,1)}, bf16[32,5632]{1,0:T(8,128)(2,1)}, u32[]{:S(2)}, u32[]{:S(2)}) collective-permute-start(bf16[32,5632]{1,0:T(8,128)(2,1)} %get-tuple-element.525), channel_id=1, source_target_pairs={{0,16},{1,17},{2,18},{3,19},{4,20},{5,21},{6,22},{7,23},{8,24},{9,... | collective-permute-start | bytes 1081352 | tf_op jit(solution)/shard_map/ppermute | solution.py:41
  393.5 57.2 %collective-permute-start.61 = (bf16[32,5632]{1,0:T(8,128)(2,1)}, bf16[32,5632]{1,0:T(8,128)(2,1)}, u32[]{:S(2)}, u32[]{:S(2)}) collective-permute-start(bf16[32,5632]{1,0:T(8,128)(2,1)} %get-tuple-element.552), channel_id=1, source_target_pairs={{0,24},{1,25},{2,26},{3,27},{4,28},{5,29},{6,30},{7,31},{8,16},{9,... | collective-permute-start | bytes 1081352 | tf_op jit(solution)/shard_map/ppermute | solution.py:41
  418.9 8.4 %collective-permute-start.55 = (bf16[2,8,2048]{2,1,0:T(8,128)(2,1)S(1)}, bf16[2,8,2048]{2,1,0:T(8,128)(2,1)S(1)}, u32[]{:S(2)}, u32[]{:S(2)}) collective-permute-start(bf16[2,8,2048]{2,1,0:T(8,128)(2,1)S(1)} %convert_element_type.49), channel_id=1, source_target_pairs={{1,0},{2,1},{3,2},{4,3},{5,4},{6,5},{7,6},{8,7},{9,8},{10,9},{11,1... | collective-permute-start | bytes 196616 | tf_op jit(solution)/shard_map/ppermute | solution.py:47
  424.2 17.1 %collective-permute-start.56 = (bf16[4,152,512]{2,1,0:T(8,128)(2,1)}, bf16[4,152,512]{2,1,0:T(8,128)(2,1)}, u32[]{:S(2)}, u32[]{:S(2)}) collective-permute-start(bf16[4,152,512]{2,1,0:T(8,128)(2,1)} %get-tuple-element.522), channel_id=1, source_target_pairs={{0,4},{1,5},{2,6},{3,7},{4,0},{5,1},{6,2},{7,3},{8,12},{9,13},{10,... | collective-permute-start | bytes 1867784 | tf_op jit(solution)/shard_map/ppermute | solution.py:41
  425.2 16.5 %collective-permute-start.57 = (bf16[4,152,512]{2,1,0:T(8,128)(2,1)}, bf16[4,152,512]{2,1,0:T(8,128)(2,1)}, u32[]{:S(2)}, u32[]{:S(2)}) collective-permute-start(bf16[4,152,512]{2,1,0:T(8,128)(2,1)} %get-tuple-element.523), channel_id=1, source_target_pairs={{0,2},{1,3},{2,0},{3,1},{4,6},{5,7},{6,4},{7,5},{8,10},{9,11},{10,... | collective-permute-start | bytes 1867784 | tf_op jit(solution)/shard_map/ppermute | solution.py:41
  445.3 6.7 %collective-permute-start.60 = (f32[40,1024]{1,0:T(8,128)S(1)}, f32[40,1024]{1,0:T(8,128)S(1)}, u32[]{:S(2)}, u32[]{:S(2)}) collective-permute-start(f32[40,1024]{1,0:T(8,128)S(1)} %add.161), channel_id=1, source_target_pairs={{0,2},{1,3},{2,0},{3,1},{4,6},{5,7},{6,4},{7,5},{8,10},{9,11},{10,... | collective-permute-start | bytes 491528 | tf_op jit(solution)/shard_map/ppermute | solution.py:41
  451.9 6.7 %collective-permute-start.62 = (bf16[2,2,4,32,1024]{4,3,2,1,0:T(8,128)(2,1)S(1)}, bf16[2,2,4,32,1024]{4,3,2,1,0:T(8,128)(2,1)S(1)}, u32[]{:S(2)}, u32[]{:S(2)}) collective-permute-start(bf16[2,2,4,32,1024]{4,3,2,1,0:T(8,128)(2,1)S(1)} %get-tuple-element.554), channel_id=1, source_target_pairs={{0,1},{1,0},{2,3},{3,2},{4,5},{5,4},{6,7},{7,6},{8,9},{9,8},{10,11... | collective-permute-start | bytes 3145736 | tf_op jit(solution)/shard_map/ppermute | solution.py:41
  451.9 6.7 %collective-permute-start.63 = (bf16[2,2,4,32,1024]{4,3,2,1,0:T(8,128)(2,1)S(1)}, bf16[2,2,4,32,1024]{4,3,2,1,0:T(8,128)(2,1)S(1)}, u32[]{:S(2)}, u32[]{:S(2)}) collective-permute-start(bf16[2,2,4,32,1024]{4,3,2,1,0:T(8,128)(2,1)S(1)} %get-tuple-element.556), channel_id=1, source_target_pairs={{0,1},{1,0},{2,3},{3,2},{4,5},{5,4},{6,7},{7,6},{8,9},{9,8},{10,11... | collective-permute-start | bytes 3145736 | tf_op jit(solution)/shard_map/ppermute | solution.py:41
  459.0 17.1 %collective-permute-start.65 = (bf16[2,4,32,1024]{3,2,1,0:T(8,128)(2,1)S(1)}, bf16[2,4,32,1024]{3,2,1,0:T(8,128)(2,1)S(1)}, u32[]{:S(2)}, u32[]{:S(2)}) collective-permute-start(bf16[2,4,32,1024]{3,2,1,0:T(8,128)(2,1)S(1)} %get-tuple-element.563), channel_id=1, source_target_pairs={{0,2},{1,3},{2,0},{3,1},{4,6},{5,7},{6,4},{7,5},{8,10},{9,11},{10,... | collective-permute-start | bytes 1572872 | tf_op jit(solution)/shard_map/ppermute | solution.py:41
  459.8 16.3 %collective-permute-start.66 = (bf16[2,4,32,1024]{3,2,1,0:T(8,128)(2,1)S(1)}, bf16[2,4,32,1024]{3,2,1,0:T(8,128)(2,1)S(1)}, u32[]{:S(2)}, u32[]{:S(2)}) collective-permute-start(bf16[2,4,32,1024]{3,2,1,0:T(8,128)(2,1)S(1)} %get-tuple-element.564), channel_id=1, source_target_pairs={{0,4},{1,5},{2,6},{3,7},{4,0},{5,1},{6,2},{7,3},{8,12},{9,13},{10,... | collective-permute-start | bytes 1572872 | tf_op jit(solution)/shard_map/ppermute | solution.py:41
  461.5 14.6 %collective-permute-start.67 = (bf16[152,1024]{1,0:T(8,128)(2,1)S(1)}, bf16[152,1024]{1,0:T(8,128)(2,1)S(1)}, u32[]{:S(2)}, u32[]{:S(2)}) collective-permute-start(bf16[152,1024]{1,0:T(8,128)(2,1)S(1)} %get-tuple-element.567), channel_id=1, source_target_pairs={{0,8},{1,9},{2,10},{3,11},{4,12},{5,13},{6,14},{7,15},{8,0},{9,1},... | collective-permute-start | bytes 933896 | tf_op jit(solution)/shard_map/ppermute | solution.py:41
  462.1 26.9 %collective-permute-start.73 = (bf16[152,1024]{1,0:T(8,128)(2,1)}, bf16[152,1024]{1,0:T(8,128)(2,1)}, u32[]{:S(2)}, u32[]{:S(2)}) collective-permute-start(bf16[152,1024]{1,0:T(8,128)(2,1)} %get-tuple-element.578), channel_id=1, source_target_pairs={{0,16},{1,17},{2,18},{3,19},{4,20},{5,21},{6,22},{7,23},{8,24},{9,... | collective-permute-start | bytes 933896 | tf_op jit(solution)/shard_map/ppermute | solution.py:41
  476.2 9.4 %collective-permute-start.69 = (bf16[40,1024]{1,0:T(8,128)(2,1)S(1)}, bf16[40,1024]{1,0:T(8,128)(2,1)S(1)}, u32[]{:S(2)}, u32[]{:S(2)}) collective-permute-start(bf16[40,1024]{1,0:T(8,128)(2,1)S(1)} %add.163.refs_0_), channel_id=1, source_target_pairs={{0,16},{1,17},{2,18},{3,19},{4,20},{5,21},{6,22},{7,23},{8,24},{9,... | collective-permute-start | bytes 245768 | tf_op jit(solution)/shard_map/ppermute | solution.py:41
  477.9 9.4 %collective-permute-start.70 = (bf16[40,1024]{1,0:T(8,128)(2,1)S(1)}, bf16[40,1024]{1,0:T(8,128)(2,1)}, u32[]{:S(2)}, u32[]{:S(2)}) collective-permute-start(bf16[40,1024]{1,0:T(8,128)(2,1)S(1)} %add.163.refs_0_), channel_id=1, source_target_pairs={{0,24},{1,25},{2,26},{3,27},{4,28},{5,29},{6,30},{7,31},{8,16},{9,... | collective-permute-start | bytes 245768 | tf_op jit(solution)/shard_map/ppermute | solution.py:41
  482.1 6.9 %collective-permute-start.71 = (bf16[4,32,1024]{2,1,0:T(8,128)(2,1)}, bf16[4,32,1024]{2,1,0:T(8,128)(2,1)S(1)}, u32[]{:S(2)}, u32[]{:S(2)}) collective-permute-start(bf16[4,32,1024]{2,1,0:T(8,128)(2,1)} %get-tuple-element.576), channel_id=1, source_target_pairs={{0,4},{1,5},{2,6},{3,7},{4,0},{5,1},{6,2},{7,3},{8,12},{9,13},{10,... | collective-permute-start | bytes 786440 | tf_op jit(solution)/shard_map/ppermute | solution.py:41
  482.5 6.7 %collective-permute-start.72 = (bf16[4,32,1024]{2,1,0:T(8,128)(2,1)}, bf16[4,32,1024]{2,1,0:T(8,128)(2,1)}, u32[]{:S(2)}, u32[]{:S(2)}) collective-permute-start(bf16[4,32,1024]{2,1,0:T(8,128)(2,1)} %get-tuple-element.577), channel_id=1, source_target_pairs={{0,2},{1,3},{2,0},{3,1},{4,6},{5,7},{6,4},{7,5},{8,10},{9,11},{10,... | collective-permute-start | bytes 786440 | tf_op jit(solution)/shard_map/ppermute | solution.py:41
  485.6 11.7 %collective-permute-start.77 = (bf16[152,1024]{1,0:T(8,128)(2,1)}, bf16[152,1024]{1,0:T(8,128)(2,1)}, u32[]{:S(2)}, u32[]{:S(2)}) collective-permute-start(bf16[152,1024]{1,0:T(8,128)(2,1)} %get-tuple-element.594), channel_id=1, source_target_pairs={{0,24},{1,25},{2,26},{3,27},{4,28},{5,29},{6,30},{7,31},{8,16},{9,... | collective-permute-start | bytes 933896 | tf_op jit(solution)/shard_map/ppermute | solution.py:41
  492.9 7.1 %collective-permute-start.74 = (bf16[32,2048]{1,0:T(8,128)(2,1)S(1)}, bf16[32,2048]{1,0:T(8,128)(2,1)S(1)}, u32[]{:S(2)}, u32[]{:S(2)}) collective-permute-start(bf16[32,2048]{1,0:T(8,128)(2,1)S(1)} %get-tuple-element.588), channel_id=1, source_target_pairs={{0,8},{1,9},{2,10},{3,11},{4,12},{5,13},{6,14},{7,15},{8,0},{9,1},... | collective-permute-start | bytes 393224 | tf_op jit(solution)/shard_map/ppermute | solution.py:41
  493.0 15.6 %collective-permute-start.75 = (bf16[32,2048]{1,0:T(8,128)(2,1)S(1)}, bf16[32,2048]{1,0:T(8,128)(2,1)S(1)}, u32[]{:S(2)}, u32[]{:S(2)}) collective-permute-start(bf16[32,2048]{1,0:T(8,128)(2,1)S(1)} %get-tuple-element.589), channel_id=1, source_target_pairs={{0,16},{1,17},{2,18},{3,19},{4,20},{5,21},{6,22},{7,23},{8,24},{9,... | collective-permute-start | bytes 393224 | tf_op jit(solution)/shard_map/ppermute | solution.py:41
  496.4 12.2 %collective-permute-start.76 = (bf16[32,2048]{1,0:T(8,128)(2,1)S(1)}, bf16[32,2048]{1,0:T(8,128)(2,1)S(1)}, u32[]{:S(2)}, u32[]{:S(2)}) collective-permute-start(bf16[32,2048]{1,0:T(8,128)(2,1)S(1)} %get-tuple-element.590), channel_id=1, source_target_pairs={{0,24},{1,25},{2,26},{3,27},{4,28},{5,29},{6,30},{7,31},{8,16},{9,... | collective-permute-start | bytes 393224 | tf_op jit(solution)/shard_map/ppermute | solution.py:41
  (137 other events, 1074.9 us)
